TPU v7x, 32 devices: a whole 2x2x4 slice. The times are simulated.
32 devices in a mesh: fsdp: 8 (over y, x, core), tp: 4 (over z).
Axes of the slice: x: 2, y: 2, z: 4, core: 2. Of those that a mesh axis runs over, the one named last changes fastest.
Arguments:
- inputs: bfloat16 [2048, 16, 768], P('tp', 'fsdp'), may hold values from -6 to 6
- segments: int32 [2048, 16], P(None, 'fsdp'), may hold values from 0 to 2047, as said below
- w_qkv: bfloat16 [768, 3, 768], P('fsdp', None, 'tp'), may hold values from -0.21875 to 0.21875
- qkv_bias: float32 [3, 768], P(None, 'tp'), may hold values from -3 to 3
- pool_kernel: float32 [2, 5, 768], P(None, None, 'tp'), may hold values from -3 to 3
- w_out: bfloat16 [768, 768], P('fsdp', 'tp'), may hold values from -3.5 to 3.5
- out_bias: float32 [2, 768], replicated, may hold values from -3 to 3
- w_up: bfloat16 [768, 3072], P('fsdp', 'tp'), may hold values from -0.21875 to 0.21875
- up_bias: float32 [3072], P('tp'), may hold values from -3 to 3
- w_down: bfloat16 [768, 3072], P('fsdp', 'tp'), may hold values from -0.21875 to 0.21875
- norm_gains: float32 [2, 768], replicated, may hold values from 0.25 to 1.75
- norm_shifts: float32 [2, 768], replicated, may hold values from -3 to 3
- cotangent: bfloat16 [2048, 16, 768], P('tp', 'fsdp'), may hold values from -6 to 6
Outputs:
- outputs: bfloat16 [2048, 16, 768], P('tp', 'fsdp')
- grad_inputs: float32 [2048, 16, 768], P('tp', 'fsdp')
- grad_w_qkv: float32 [768, 3, 768], P('fsdp', None, 'tp')
- grad_qkv_bias: float32 [3, 768], P(None, 'tp')
- grad_pool_kernel: float32 [2, 5, 768], P(None, None, 'tp')
- grad_w_out: float32 [768, 768], P('fsdp', 'tp')
- grad_out_bias: float32 [2, 768], replicated
- grad_w_up: float32 [768, 3072], P('fsdp', 'tp')
- grad_up_bias: float32 [3072], P('tp')
- grad_w_down: float32 [768, 3072], P('fsdp', 'tp')
- grad_norm_gains: float32 [2, 768], replicated
- grad_norm_shifts: float32 [2, 768], replicated
Inputs may be any that keep to these rules, and one draw needn't show every extreme that they name: `segments`: along each sequence a token's document number is the position of its document's first token, so it never falls; the last token of every sequence is a document of its own; one document of every sequence covers at least 1536 consecutive tokens.
All inputs are finite; a program needn't handle non-finite values.
Results may differ from a plain program's by a relative error of at most 0.02.
The roundings to bfloat16 on the way count: a program that leaves them out, or rounds other values in their place, can miss the bound.
Values may be sent and summed in bfloat16 or wider, within the bound.
No kernel may reach another device: no remote copies, remote signals or barrier semaphores. Data moves between devices by JAX's collectives and lax.ppermute only.
A program may use at most 192 MiB of HBM per device.

v0:
```python
from functools import partial

import jax
import jax.numpy as jnp
from jax import lax
from jax.sharding import PartitionSpec as P

HEAD_DIM = 64
WINDOW = 128
POOL_STRIDE = 4
POOL_KERNEL = 5
QBLOCK = 512


EPSILON = 1e-05


def layer_norm(residual, norm_gain, norm_shift):
    row_mean = jnp.mean(residual, axis=-1, keepdims=True)
    centered = residual - row_mean
    variance = jnp.mean(centered * centered, axis=-1, keepdims=True)
    return centered * lax.rsqrt(variance + EPSILON) * norm_gain + norm_shift


def pool_pairs(pair_vals, kernel_vals, seg_rows):
    pair_count, seq_count, length, features = pair_vals.shape
    margin = POOL_KERNEL // 2
    pooled_len = length // POOL_STRIDE
    padded = jnp.pad(pair_vals, ((0, 0), (0, 0), (margin, margin), (0, 0)))
    seg_pad = jnp.pad(seg_rows, ((0, 0), (margin, margin)), constant_values=-1)
    centers = seg_rows.reshape(seq_count, pooled_len, POOL_STRIDE)[:, :, 0]
    pooled_sum = jnp.zeros((pair_count, seq_count, pooled_len, features), jnp.float32)
    for offset in range(POOL_KERNEL):
        tapped = padded[:, :, offset : offset + length].reshape(
            pair_count, seq_count, pooled_len, POOL_STRIDE, features
        )[:, :, :, 0]
        same_doc = (
            seg_pad[:, offset : offset + length].reshape(seq_count, pooled_len, POOL_STRIDE)[
                :, :, 0
            ]
            == centers
        )
        pooled_sum = (
            pooled_sum
            + kernel_vals[:, offset][:, None, None, :]
            * tapped
            * same_doc.astype(jnp.float32)[None, :, :, None]
        )
    return pooled_sum


def padded_views(key_rows, value_rows, seg_row):
    half_window = WINDOW // 2
    keys_pad = jnp.pad(key_rows, ((half_window, half_window), (0, 0), (0, 0)))
    values_pad = jnp.pad(value_rows, ((half_window, half_window), (0, 0), (0, 0)))
    seg_pad = jnp.pad(seg_row, (half_window, half_window), constant_values=-1)
    centers = seg_row.reshape(-1, POOL_STRIDE)[:, 0]
    return (keys_pad, values_pad, seg_pad, centers)


def block_inputs(queries, keys_pad, values_pad, seg_row, seg_pad, first_row):
    near_width = QBLOCK + 2 * (WINDOW // 2)
    return (
        lax.dynamic_slice_in_dim(queries, first_row, QBLOCK, 0),
        lax.dynamic_slice_in_dim(keys_pad, first_row, near_width, 0),
        lax.dynamic_slice_in_dim(values_pad, first_row, near_width, 0),
        lax.dynamic_slice_in_dim(seg_row, first_row, QBLOCK, 0),
        lax.dynamic_slice_in_dim(seg_pad, first_row, near_width, 0),
    )


def block_scores(query_blk, key_near, key_far, seg_query, seg_near, centers, first_row):
    half_window = WINDOW // 2
    near_scores = jnp.einsum(
        "qhe,khe->hqk", query_blk, key_near, preferred_element_type=jnp.float32
    )
    far_scores = jnp.einsum("qhe,khe->hqk", query_blk, key_far, preferred_element_type=jnp.float32)
    scores = jnp.concatenate([near_scores, far_scores], axis=-1) * HEAD_DIM ** (-0.5)
    query_pos = first_row + jnp.arange(query_blk.shape[0], dtype=jnp.int32)
    key_pos = first_row - half_window + jnp.arange(key_near.shape[0], dtype=jnp.int32)
    near_mask = (jnp.abs(query_pos[:, None] - key_pos[None, :]) <= half_window) & (
        seg_query[:, None] == seg_near[None, :]
    )
    far_mask = seg_query[:, None] == centers[None, :]
    allowed = jnp.concatenate([near_mask, far_mask], axis=-1)
    return jnp.where(allowed[None], scores, -1e30)


def attend_forward(operands):
    queries, key_rows, value_rows, pooled_heads, seg_row = operands
    keys_pad, values_pad, seg_pad, centers = padded_views(key_rows, value_rows, seg_row)
    near_width = QBLOCK + 2 * (WINDOW // 2)

    def one_block(first_row):
        query_blk, key_near, value_near, seg_query, seg_near = block_inputs(
            queries, keys_pad, values_pad, seg_row, seg_pad, first_row
        )
        scores = block_scores(
            query_blk, key_near, pooled_heads[0], seg_query, seg_near, centers, first_row
        )
        row_top = jnp.max(scores, axis=-1, keepdims=True)
        raised = jnp.exp(scores - row_top)
        row_total = jnp.sum(raised, axis=-1, keepdims=True)
        probs_low = (raised / row_total).astype(jnp.bfloat16)
        mixed_out = jnp.einsum(
            "hqk,khe->qhe",
            probs_low[:, :, :near_width],
            value_near,
            preferred_element_type=jnp.float32,
        )
        mixed_out = mixed_out + jnp.einsum(
            "hqk,khe->qhe",
            probs_low[:, :, near_width:],
            pooled_heads[1],
            preferred_element_type=jnp.float32,
        )
        return (mixed_out.astype(jnp.bfloat16), (row_top + jnp.log(row_total))[:, :, 0])

    starts = jnp.arange(queries.shape[0] // QBLOCK, dtype=jnp.int32) * QBLOCK
    mixed_out, log_total = lax.map(one_block, starts)
    return (mixed_out.reshape(queries.shape[0], -1), log_total)


def attend_backward(operands):
    queries, key_rows, value_rows, pooled_heads, seg_row, log_total, grad_mixed = operands
    keys_pad, values_pad, seg_pad, centers = padded_views(key_rows, value_rows, seg_row)
    half_window = WINDOW // 2
    near_width = QBLOCK + 2 * half_window
    length = queries.shape[0]
    score_scale = HEAD_DIM ** (-0.5)

    def one_step(running, block_index):
        grad_keys_pad, grad_values_pad, grad_far = running
        first_row = block_index * QBLOCK
        query_blk, key_near, value_near, seg_query, seg_near = block_inputs(
            queries, keys_pad, values_pad, seg_row, seg_pad, first_row
        )
        grad_blk = lax.dynamic_slice_in_dim(grad_mixed, first_row, QBLOCK, 0)
        scores = block_scores(
            query_blk, key_near, pooled_heads[0], seg_query, seg_near, centers, first_row
        )
        probs = jnp.exp(scores - log_total[block_index][:, :, None])
        probs_low = probs.astype(jnp.bfloat16)
        grad_probs = jnp.concatenate(
            [
                jnp.einsum(
                    "qhe,khe->hqk", grad_blk, value_near, preferred_element_type=jnp.float32
                ),
                jnp.einsum(
                    "qhe,khe->hqk", grad_blk, pooled_heads[1], preferred_element_type=jnp.float32
                ),
            ],
            axis=-1,
        )
        row_dot = jnp.sum(probs * grad_probs, axis=-1, keepdims=True)
        grad_scores = (probs * (grad_probs - row_dot)).astype(jnp.bfloat16)
        near_grad = grad_scores[:, :, :near_width]
        far_grad = grad_scores[:, :, near_width:]
        grad_query = (
            jnp.einsum("hqk,khe->qhe", near_grad, key_near, preferred_element_type=jnp.float32)
            + jnp.einsum(
                "hqk,khe->qhe", far_grad, pooled_heads[0], preferred_element_type=jnp.float32
            )
        ) * score_scale
        grad_key_near = (
            jnp.einsum("hqk,qhe->khe", near_grad, query_blk, preferred_element_type=jnp.float32)
            * score_scale
        )
        grad_value_near = jnp.einsum(
            "hqk,qhe->khe",
            probs_low[:, :, :near_width],
            grad_blk,
            preferred_element_type=jnp.float32,
        )
        grad_key_far = (
            jnp.einsum("hqk,qhe->khe", far_grad, query_blk, preferred_element_type=jnp.float32)
            * score_scale
        )
        grad_value_far = jnp.einsum(
            "hqk,qhe->khe",
            probs_low[:, :, near_width:],
            grad_blk,
            preferred_element_type=jnp.float32,
        )
        grad_keys_pad = lax.dynamic_update_slice_in_dim(
            grad_keys_pad,
            lax.dynamic_slice_in_dim(grad_keys_pad, first_row, near_width, 0) + grad_key_near,
            first_row,
            0,
        )
        grad_values_pad = lax.dynamic_update_slice_in_dim(
            grad_values_pad,
            lax.dynamic_slice_in_dim(grad_values_pad, first_row, near_width, 0) + grad_value_near,
            first_row,
            0,
        )
        grad_far = grad_far + jnp.stack([grad_key_far, grad_value_far])
        return ((grad_keys_pad, grad_values_pad, grad_far), grad_query)

    initial = (
        jnp.zeros(keys_pad.shape, jnp.float32),
        jnp.zeros(values_pad.shape, jnp.float32),
        jnp.zeros(pooled_heads.shape, jnp.float32),
    )
    block_ids = jnp.arange(length // QBLOCK, dtype=jnp.int32)
    (grad_keys_pad, grad_values_pad, grad_far), grad_query = lax.scan(one_step, initial, block_ids)
    return (
        grad_query.reshape(length, -1),
        grad_keys_pad[half_window : half_window + length].reshape(length, -1),
        grad_values_pad[half_window : half_window + length].reshape(length, -1),
        grad_far.reshape(2, grad_far.shape[1], -1),
    )


def fetch_layer(first_weight, second_weight):
    return (
        lax.all_gather(first_weight, "fsdp", axis=0, tiled=True),
        lax.all_gather(second_weight, "fsdp", axis=0, tiled=True),
    )


def reduce_layer(first_grad, second_grad):
    return (
        lax.psum_scatter(first_grad, "fsdp", scatter_dimension=0, tiled=True),
        lax.psum_scatter(second_grad, "fsdp", scatter_dimension=0, tiled=True),
    )


def collect_rows(shard_rows):
    return lax.all_gather(shard_rows, "tp", axis=0, tiled=True)


def sum_heads(term_fn, row_count):
    return lax.psum_scatter(
        term_fn(jnp.int32(0), row_count * lax.axis_size("tp")),
        "tp",
        scatter_dimension=0,
        tiled=True,
    )


def sum_inputs(term_fn, row_count):
    return lax.psum_scatter(
        term_fn(jnp.int32(0), row_count * lax.axis_size("tp")).astype(jnp.bfloat16),
        "tp",
        scatter_dimension=0,
        tiled=True,
    ).astype(jnp.float32)


def collect_grads(shard_rows):
    return lax.all_gather(shard_rows, "tp", axis=0, tiled=True)


def body(
    inputs,
    segments,
    w_qkv,
    qkv_bias,
    pool_kernel,
    w_out,
    out_bias,
    w_up,
    up_bias,
    w_down,
    norm_gains,
    norm_shifts,
    cotangent,
):
    local_rows, group_seqs, model_width = inputs.shape
    local_feats = w_qkv.shape[2]
    local_heads = local_feats // HEAD_DIM
    seq_rows = segments.T
    full_qkv, full_out = fetch_layer(w_qkv, w_out)
    whole_inputs = collect_rows(inputs)
    made = (
        jnp.einsum("tsd,dcf->stcf", whole_inputs, full_qkv, preferred_element_type=jnp.float32)
        + qkv_bias
    )
    projected = made.astype(jnp.bfloat16)
    full_len = projected.shape[1]
    split_heads = projected.reshape(group_seqs, full_len, 3, local_heads, HEAD_DIM)
    queries = split_heads[:, :, 0]
    key_rows = split_heads[:, :, 1]
    value_rows = split_heads[:, :, 2]
    pair_vals = jnp.stack([projected[:, :, 1], projected[:, :, 2]]).astype(jnp.float32)
    pooled_low = pool_pairs(pair_vals, pool_kernel, seq_rows).astype(jnp.bfloat16)
    pooled_heads = jnp.moveaxis(pooled_low.reshape(2, group_seqs, -1, local_heads, HEAD_DIM), 1, 0)
    mixed_out, log_total = lax.map(
        attend_forward, (queries, key_rows, value_rows, pooled_heads, seq_rows)
    )

    def attention_term(first_index, row_count):
        return jnp.einsum("stf,ef->tse", mixed_out, full_out, preferred_element_type=jnp.float32)

    branch = sum_heads(attention_term, local_rows) + out_bias[0]
    residual_one = inputs.astype(jnp.float32) + branch
    first_out = layer_norm(residual_one, norm_gains[0], norm_shifts[0])
    first_low = first_out.astype(jnp.bfloat16)
    full_up, full_down = fetch_layer(w_up, w_down)
    whole_first = collect_rows(first_low)
    pre_act = (
        jnp.einsum("tsd,df->stf", whole_first, full_up, preferred_element_type=jnp.float32)
        + up_bias
    )
    hidden = jax.nn.gelu(pre_act, approximate=False).astype(jnp.bfloat16)

    def ffn_term(first_index, row_count):
        return jnp.einsum("stf,ef->tse", hidden, full_down, preferred_element_type=jnp.float32)

    ffn_out = sum_heads(ffn_term, local_rows) + out_bias[1]
    residual_two = first_out + ffn_out
    outputs = layer_norm(residual_two, norm_gains[1], norm_shifts[1])
    grad_out = cotangent.astype(jnp.float32)
    norm_two_back = jax.vjp(layer_norm, residual_two, norm_gains[1], norm_shifts[1])[1]
    grad_second, gain_two, shift_two = norm_two_back(grad_out)
    grad_ffn_low = grad_second.astype(jnp.bfloat16)
    whole_ffn_grad = collect_grads(grad_ffn_low)
    grad_hidden = jnp.einsum(
        "tse,ef->stf", whole_ffn_grad, full_down, preferred_element_type=jnp.float32
    )
    gelu_back = jax.vjp(partial(jax.nn.gelu, approximate=False), pre_act)[1]
    grad_pre = gelu_back(grad_hidden)[0].astype(jnp.bfloat16)
    grad_w_down = jnp.einsum(
        "stf,tse->ef", hidden, whole_ffn_grad, preferred_element_type=jnp.float32
    )
    grad_w_up = jnp.einsum("tsd,stf->df", whole_first, grad_pre, preferred_element_type=jnp.float32)
    grad_up_bias = jnp.sum(grad_pre, axis=(0, 1), dtype=jnp.float32)
    grad_w_up, grad_w_down = reduce_layer(grad_w_up, grad_w_down)

    def up_term(first_index, row_count):
        return jnp.einsum("stf,df->tsd", grad_pre, full_up, preferred_element_type=jnp.float32)

    grad_first = grad_second + sum_inputs(up_term, local_rows)
    norm_one_back = jax.vjp(layer_norm, residual_one, norm_gains[0], norm_shifts[0])[1]
    grad_residual, gain_one, shift_one = norm_one_back(grad_first)
    grad_branch_low = grad_residual.astype(jnp.bfloat16)
    whole_branch_grad = collect_grads(grad_branch_low)
    grad_attended = jnp.einsum(
        "tse,ef->stf", whole_branch_grad, full_out, preferred_element_type=jnp.float32
    ).astype(jnp.bfloat16)
    grad_w_out = jnp.einsum(
        "stf,tse->ef", mixed_out, whole_branch_grad, preferred_element_type=jnp.float32
    )
    grad_queries, grad_keys, grad_values, grad_far = lax.map(
        attend_backward,
        (
            queries,
            key_rows,
            value_rows,
            pooled_heads,
            seq_rows,
            log_total,
            grad_attended.reshape(group_seqs, full_len, local_heads, HEAD_DIM),
        ),
    )
    grad_pooled = jnp.moveaxis(grad_far, 1, 0).astype(jnp.bfloat16)

    def pool_local(pair_in, kernel_in):
        return pool_pairs(pair_in, kernel_in, seq_rows)

    pool_back = jax.vjp(pool_local, pair_vals, pool_kernel)[1]
    pair_grads, grad_pool_kernel = pool_back(grad_pooled.astype(jnp.float32))
    grad_projected = jnp.stack(
        [grad_queries, grad_keys + pair_grads[0], grad_values + pair_grads[1]], axis=2
    ).astype(jnp.bfloat16)
    grad_qkv_bias = jnp.sum(grad_projected, axis=(0, 1), dtype=jnp.float32)
    grad_w_qkv = jnp.einsum(
        "tsd,stcf->dcf", whole_inputs, grad_projected, preferred_element_type=jnp.float32
    )

    def qkv_term(first_index, row_count):
        return jnp.einsum(
            "stcf,dcf->tsd", grad_projected, full_qkv, preferred_element_type=jnp.float32
        )

    grad_inputs = grad_residual + sum_inputs(qkv_term, local_rows)
    grad_w_qkv, grad_w_out = reduce_layer(grad_w_qkv, grad_w_out)
    grad_qkv_bias, grad_pool_kernel, grad_up_bias = lax.psum(
        (grad_qkv_bias, grad_pool_kernel, grad_up_bias), "fsdp"
    )
    grad_out_bias = jnp.stack(
        [
            jnp.sum(grad_branch_low, axis=(0, 1), dtype=jnp.float32),
            jnp.sum(grad_ffn_low, axis=(0, 1), dtype=jnp.float32),
        ]
    )
    grad_norm_gains = jnp.stack([gain_one, gain_two])
    grad_norm_shifts = jnp.stack([shift_one, shift_two])
    grad_out_bias, grad_norm_gains, grad_norm_shifts = lax.psum(
        (grad_out_bias, grad_norm_gains, grad_norm_shifts), ("fsdp", "tp")
    )
    return (
        outputs.astype(jnp.bfloat16),
        grad_inputs,
        grad_w_qkv,
        grad_qkv_bias,
        grad_pool_kernel,
        grad_w_out,
        grad_out_bias,
        grad_w_up,
        grad_up_bias,
        grad_w_down,
        grad_norm_gains,
        grad_norm_shifts,
    )


def solution(mesh):
    placed = (
        P("tp", "fsdp", None),
        P(None, "fsdp"),
        P("fsdp", None, "tp"),
        P(None, "tp"),
        P(None, None, "tp"),
        P("fsdp", "tp"),
        P(),
        P("fsdp", "tp"),
        P("tp"),
        P("fsdp", "tp"),
        P(),
        P(),
        P("tp", "fsdp", None),
    )
    return jax.shard_map(
        body,
        mesh=mesh,
        in_specs=placed,
        out_specs=(
            P("tp", "fsdp", None),
            P("tp", "fsdp", None),
            P("fsdp", None, "tp"),
            P(None, "tp"),
            P(None, None, "tp"),
            P("fsdp", "tp"),
            P(),
            P("fsdp", "tp"),
            P("tp"),
            P("fsdp", "tp"),
            P(),
            P(),
        ),
        check_vma=False,
    )
```

profile of v0, /device:TPU:0, one launch (start us, length us, event | category | flops | bytes accessed | tf_op | source)
XLA Modules:
  0.0 2417.2 jit_solution(5214915028221113958)
XLA Ops:
  16.5 12.1 all_gather.26
  28.6 14.3 all_gather.24
  43.4 85.7 %all-gather.7.cloned.1.call-done = bf16[2048,2,768]{2,0,1:T(8,128)(2,1)} async-done(((bf16[512,2,768]{2,0,1:T(8,128)(2,1)}), bf16[2048,2,768]{2,0,1:T(8,128)(2,1)}) %all-gather.7.cloned.1.call-update) | async-done | bytes 6291472 | tf_op jit(solution)/shard_map/all_gather | solution.py:230
  129.1 8.6 add_convert_fusion
  144.6 19.5 fusion.221
  164.1 12.7 copy.235
  181.6 12.7 copy.238
  199.2 12.7 copy.246
  216.8 12.7 copy.249
  234.4 6.1 copy.241
  240.4 6.1 copy.243
  246.5 4.7 copy.242
  263.1 158.9 %while.92 = (s32[]{:T(128)}, bf16[2,2048,192]{1,2,0:T(8,128)(2,1)}, f32[2,4,3,512]{3,2,1,0:T(4,128)}, bf16[2,2048,3,64]{1,3,2,0:T(8,128)(2,1)}, bf16[2,2048,3,64...) while((s32[]{:T(128)}, bf16[2,2048,192]{1,2,0:T(8,128)(2,1)}, ...), condition=%wide.region_5.6_spmd, body=%wide.region_0.5_spmd.sunk | while | flops 482213504 | bytes 70589568 | solution.py:289
  270.4 68.5 %while.95 = (s32[]{:T(128)}, bf16[4,512,3,64]{1,3,2,0:T(8,128)(2,1)}, f32[4,3,512]{2,1,0:T(4,128)S(1)}, s32[4]{0:T(128)S(1)}, bf16[2176,3,64]{0,2,1:T(8,128)(2,1...) while((s32[]{:T(128)}, ...), condition=%wide.region_4.4_spmd, body=%wide.region_1.3_spmd.sunk | while | flops 482213504 | bytes 57001256 | solution.py:120
  349.6 68.5 %while.95 = (s32[]{:T(128)}, bf16[4,512,3,64]{1,3,2,0:T(8,128)(2,1)}, f32[4,3,512]{2,1,0:T(4,128)S(1)}, s32[4]{0:T(128)S(1)}, bf16[2176,3,64]{0,2,1:T(8,128)(2,1...) while((s32[]{:T(128)}, ...), condition=%wide.region_4.4_spmd, body=%wide.region_1.3_spmd.sunk | while | flops 482213504 | bytes 57001256 | solution.py:120
  422.0 7.9 convolution_bitcast_fusion
  430.7 209.4 %reduce-scatter.11.cloned.1.call-done = f32[512,2,768]{2,0,1:T(8,128)} async-done(((f32[2048,2,768]{2,0,1:T(8,128)}), f32[512,2,768]{2,0,1:T(8,128)}) %reduce-scatter.11.cloned.1.call-update) | async-done | bytes 3145744 | tf_op jit(solution)/shard_map/reduce_scatter | solution.py:234
  646.4 115.7 %all-gather.9.cloned.1.call-done = bf16[2048,2,768]{2,0,1:T(8,128)(2,1)} async-done(((bf16[512,2,768]{2,0,1:T(8,128)(2,1)}), bf16[2048,2,768]{2,0,1:T(8,128)(2,1)}) %all-gather.9.cloned.1.call-update) | async-done | bytes 6291472 | tf_op jit(solution)/shard_map/all_gather | solution.py:230
  762.0 35.2 %fusion.148 = (bf16[2,2048,768]{2,1,0:T(8,128)(2,1)}, f32[2,2048,768]{2,1,0:T(8,128)}, f32[2048,2,768]{2,0,1:T(8,128)}) fusion(f32[768]{0:T(1024)S(1)} %copy-done.60, bf16[2048,2,768]{2,0,1:T(8,128)(2,1)} %all-gather.9.cloned.1.call-done, bf16[768,768]{1,0:T(8,128)(2,1)} %all-gather.11.cloned.1.call-done), kind=kOutput, calls=%fused_computation.151 | convolution fusion | flops 5039456256 | bytes 38931456 | tf_op jit(solution)/shard_map/tsd,df->stf/dot_general | solution.py:303
  797.3 10.2 convolution_bitcast_fusion.1
  807.6 210.0 %reduce-scatter.13.cloned.1.call-done = f32[512,2,768]{2,0,1:T(8,128)} async-done(((f32[2048,2,768]{2,0,1:T(8,128)}), f32[512,2,768]{2,0,1:T(8,128)}) %reduce-scatter.13.cloned.1.call-update) | async-done | bytes 3145744 | tf_op jit(solution)/shard_map/reduce_scatter | solution.py:234
  1030.1 116.5 %all-gather.15.cloned.1.call-done = bf16[2048,2,768]{2,0,1:T(8,128)(2,1)} async-done(((bf16[512,2,768]{2,0,1:T(8,128)(2,1)}), bf16[2048,2,768]{2,0,1:T(8,128)(2,1)}) %all-gather.15.cloned.1.call-update) | async-done | bytes 6291472 | tf_op jit(solution)/shard_map/all_gather | solution.py:252
  1146.6 17.5 convert_reduce_fusion
  1164.2 9.7 convert_bitcast_fusion
  1174.0 108.9 %reduce-scatter.15.cloned.1.call-done = bf16[512,2,768]{2,0,1:T(8,128)(2,1)} async-done(((bf16[2048,2,768]{2,0,1:T(8,128)(2,1)}), bf16[512,2,768]{2,0,1:T(8,128)(2,1)}) %reduce-scatter.15.cloned.1.call-update) | async-done | bytes 1572880 | tf_op jit(solution)/shard_map/reduce_scatter | solution.py:243
  1294.9 4.2 copy.294
  1301.4 4.2 copy.296
  1305.6 103.0 %all-gather.17.cloned.1.call-done = bf16[2048,2,768]{2,0,1:T(8,128)(2,1)} async-done(((bf16[512,2,768]{2,0,1:T(8,128)(2,1)}), bf16[2048,2,768]{2,0,1:T(8,128)(2,1)}) %all-gather.17.cloned.1.call-update) | async-done | bytes 6291472 | tf_op jit(solution)/shard_map/all_gather | solution.py:252
  1408.6 6.3 convolution_convert_fusion
  1414.8 571.5 %while.94 = (s32[]{:T(128)}, bf16[2,2048,192]{1,2,0:T(8,128)(2,1)}, f32[2,2048,192]{1,2,0:T(8,128)}, f32[2,2048,192]{1,2,0:T(8,128)}, bf16[2,2,512,192]{2,3,1,0:...) while((s32[]{:T(128)}, bf16[2,2048,192]{1,2,0:T(8,128)(2,1)}, ...), condition=%wide.region_21.22_spmd, body=%wide.region_17.21_spmd.sunk | while | flops 1169927936 | bytes 178733744 | solution.py:345
  1432.4 258.0 %while.96 = (s32[]{:T(128)}, f32[2176,3,64]{0,2,1:T(8,128)}, f32[2176,3,64]{0,2,1:T(8,128)}, f32[2,512,3,64]{1,3,2,0:T(8,128)}, bf16[4,512,3,64]{1,0,3,2:T(4,128...) while((s32[]{:T(128)}, f32[2176,3,64]{0,2,1:T(8,128)}, ...), condition=%wide.region_20.20_spmd.clone, body=%wide.region_18.19_spmd.clone.sunk | while | flops 1169927936 | bytes 84741104 | solution.py:206
  1452.6 18.5 multiply_convert_fusion.2
  1517.0 18.5 multiply_convert_fusion.2
  1581.6 18.5 multiply_convert_fusion.2
  1646.1 18.5 multiply_convert_fusion.2
  1717.8 258.0 %while.96 = (s32[]{:T(128)}, f32[2176,3,64]{0,2,1:T(8,128)}, f32[2176,3,64]{0,2,1:T(8,128)}, f32[2,512,3,64]{1,3,2,0:T(8,128)}, bf16[4,512,3,64]{1,0,3,2:T(4,128...) while((s32[]{:T(128)}, f32[2176,3,64]{0,2,1:T(8,128)}, ...), condition=%wide.region_20.20_spmd.clone, body=%wide.region_18.19_spmd.clone.sunk | while | flops 1169927936 | bytes 84741104 | solution.py:206
  1738.1 18.5 multiply_convert_fusion.2
  1802.5 18.5 multiply_convert_fusion.2
  1867.1 18.5 multiply_convert_fusion.2
  1931.6 18.5 multiply_convert_fusion.2
  1986.3 6.2 fusion.187
  1995.3 5.6 pad.103.clone
  2000.9 12.7 copy.257
  2016.3 5.6 pad.105.clone
  2021.9 12.7 copy.259
  2037.3 5.6 pad.107.clone
  2042.9 12.7 copy.261
  2058.6 5.6 pad.109.clone
  2064.2 12.6 copy.263
  2079.6 5.6 pad.111.clone
  2085.2 12.6 copy.265
  2097.8 15.2 fusion.197
  2113.1 9.0 fusion.163
  2125.3 8.8 fusion.162
  2134.2 10.3 convolution_bitcast_fusion.2
  2144.6 10.1 convolution_bitcast_fusion.3
  2158.9 5.5 convolution_bitcast_fusion.4
  2164.4 45.1 %all-reduce.23 = (f32[2,768]{1,0:T(2,128)}, f32[2,768]{1,0:T(2,128)}, f32[2,768]{1,0:T(2,128)}) all-reduce(f32[2,768]{1,0:T(2,128)S(1)} %get-tuple-element.1115, f32[2,768]{1,0:T(2,128)S(1)} %get-tuple-element.1116, f32[2,768]{1,0:T(2,128)S(1)} %pad_maximum_fusion.6), channel_id=1, replica_groups=mesh['fsdp'=8,'tp'=4] {'fsdp','tp'}, use_global_device_ids=true, to_apply=%region_35.36 | all-reduce | flops 4608 | bytes 36864 | tf_op jit(solution)/shard_map/psum | solution.py:390
  2212.3 25.1 %all-reduce.24 = (f32[3,192]{1,0:T(4,128)}, f32[2,5,192]{2,0,1:T(2,128)}, f32[768]{0:T(1024)}) all-reduce(f32[3,192]{1,0:T(4,128)S(1)} %convert_reduce_fusion.1, f32[2,5,192]{2,0,1:T(2,128)S(1)} %pad_add_fusion.6, f32[768]{0:T(1024)S(1)} %copy-done.57), channel_id=1, replica_groups=mesh['fsdp'=8,'tp'=4] {'fsdp'}, use_global_device_ids=true, to_apply=%region_25.26 | all-reduce | flops 3264 | bytes 26112 | tf_op jit(solution)/shard_map/psum | solution.py:379
  2239.3 38.4 %reduce-scatter.17.cloned.1.call-done = bf16[512,2,768]{2,0,1:T(8,128)(2,1)} async-done(((bf16[2048,2,768]{2,0,1:T(8,128)(2,1)}), bf16[512,2,768]{2,0,1:T(8,128)(2,1)}) %reduce-scatter.17.cloned.1.call-update) | async-done | bytes 1572880 | tf_op jit(solution)/shard_map/reduce_scatter | solution.py:243
  2279.5 4.1 copy.272
  2283.6 41.1 %reduce-scatter.23.cloned.1.call-done = f32[96,768]{1,0:T(8,128)} async-done(((f32[768,768]{1,0:T(8,128)}), f32[96,768]{1,0:T(8,128)}) %reduce-scatter.23.cloned.1.call-update) | async-done | bytes 294928 | tf_op jit(solution)/shard_map/reduce_scatter | solution.py:225
  2324.7 46.2 %reduce-scatter.21.cloned.1.call-done = f32[96,768]{1,0:T(8,128)} async-done(((f32[768,768]{1,0:T(8,128)}), f32[96,768]{1,0:T(8,128)}) %reduce-scatter.21.cloned.1.call-update) | async-done | bytes 294928 | tf_op jit(solution)/shard_map/reduce_scatter | solution.py:224
  2370.9 39.0 %reduce-scatter.19.cloned.1.call-done = f32[96,192]{1,0:T(8,128)} async-done(((f32[768,192]{1,0:T(8,128)}), f32[96,192]{1,0:T(8,128)}) %reduce-scatter.19.cloned.1.call-update) | async-done | bytes 73744 | tf_op jit(solution)/shard_map/reduce_scatter | solution.py:225
  (703 shorter events, 636.9 us)
Async XLA Ops:
  8.0 7.4 copy-start.37
  8.0 121.1 %all-gather.7.cloned.1.call-start = ((), (), s32[]{:S(2)}) async-start(), calls=%async_computation.8 | async-start | bytes 7864320 | tf_op jit(solution)/shard_map/all_gather | solution.py:230
  10.8 4.7 copy-start.53
  10.8 5.7 copy-start.38
  10.9 629.2 %reduce-scatter.11.cloned.1.call-start = ((), (), s32[]{:S(2)}) async-start(), calls=%async_computation.9 | async-start | bytes 15728640 | tf_op jit(solution)/shard_map/reduce_scatter | solution.py:234
  14.3 114.8 %copy-start.59 = (f32[3,192]{1,0:T(4,128)S(1)}, f32[3,192]{1,0:T(4,128)}, u32[]{:S(2)}) copy-start(f32[3,192]{1,0:T(4,128)} %param.24) | copy-start | bytes 6916
  43.3 214.7 %copy-start.41 = (f32[2,512]{1,0:T(2,128)}, f32[2,512]{1,0:T(2,128)S(1)}, u32[]{:S(2)}) copy-start(f32[2,512]{1,0:T(2,128)S(1)} %get-tuple-element.947) | copy-start | bytes 12292
  43.3 214.7 %copy-start.42 = (f32[2,512]{1,0:T(2,128)}, f32[2,512]{1,0:T(2,128)S(1)}, u32[]{:S(2)}) copy-start(f32[2,512]{1,0:T(2,128)S(1)} %get-tuple-element.948) | copy-start | bytes 12292
  43.3 214.7 %copy-start.43 = (f32[2,512]{1,0:T(2,128)}, f32[2,512]{1,0:T(2,128)S(1)}, u32[]{:S(2)}) copy-start(f32[2,512]{1,0:T(2,128)S(1)} %get-tuple-element.949) | copy-start | bytes 12292
  43.4 214.7 %copy-start.44 = (f32[2,512]{1,0:T(2,128)}, f32[2,512]{1,0:T(2,128)S(1)}, u32[]{:S(2)}) copy-start(f32[2,512]{1,0:T(2,128)S(1)} %get-tuple-element.950) | copy-start | bytes 12292
  179.1 15.2 copy-start.10
  196.6 15.3 copy-start.12
  214.2 15.2 copy-start.13
  231.8 8.7 copy-start.15
  255.2 3.6 copy-start.24
  263.1 158.9 %copy-start.27 = (bf16[768,192]{1,0:T(8,128)(2,1)S(1)}, bf16[768,192]{1,0:T(8,128)(2,1)}, u32[]{:S(2)}) copy-start(bf16[768,192]{1,0:T(8,128)(2,1)} %all_gather.26) | copy-start | bytes 884740
  429.9 216.5 %all-gather.11.cloned.1.call-start = ((), (), s32[]{:S(2)}) async-start(), calls=%async_computation.11 | async-start | bytes 1327104 | tf_op jit(solution)/shard_map/all_gather | solution.py:217
  430.5 331.6 %all-gather.9.cloned.1.call-start = ((), (), s32[]{:S(2)}) async-start(), calls=%async_computation.10 | async-start | bytes 7864320 | tf_op jit(solution)/shard_map/all_gather | solution.py:230
  644.0 118.1 %copy-start.60 = (f32[768]{0:T(1024)S(1)}, f32[768]{0:T(1024)}, u32[]{:S(2)}) copy-start(f32[768]{0:T(1024)} %param.29) | copy-start | bytes 9220
  645.7 151.6 %all-gather.13.cloned.1.call-start = ((), (), s32[]{:S(2)}) async-start(), calls=%async_computation.12 | async-start | bytes 1327104 | tf_op jit(solution)/shard_map/all_gather | solution.py:218
  646.3 371.3 %reduce-scatter.13.cloned.1.call-start = ((), (), s32[]{:S(2)}) async-start(), calls=%async_computation.13 | async-start | bytes 15728640 | tf_op jit(solution)/shard_map/reduce_scatter | solution.py:234
  807.5 339.1 %all-gather.15.cloned.1.call-start = ((), (), s32[]{:S(2)}) async-start(), calls=%async_computation.14 | async-start | bytes 7864320 | tf_op jit(solution)/shard_map/all_gather | solution.py:252
  1030.1 252.8 %reduce-scatter.15.cloned.1.call-start = ((), (), s32[]{:S(2)}) async-start(), calls=%async_computation.15 | async-start | bytes 7864320 | tf_op jit(solution)/shard_map/reduce_scatter | solution.py:243
  1146.6 17.6 copy-start.58
  1173.9 113.0 %copy-start.46 = (f32[512,2]{0,1:T(2,128)S(1)}, f32[512,2]{0,1:T(2,128)}, u32[]{:S(2)}) copy-start(f32[512,2]{0,1:T(2,128)} %copy-done.45) | copy-start | bytes 12292
  1173.9 234.6 %all-gather.17.cloned.1.call-start = ((), (), s32[]{:S(2)}) async-start(), calls=%async_computation.16 | async-start | bytes 7864320 | tf_op jit(solution)/shard_map/all_gather | solution.py:252
  1282.9 4.1 copy-start.4
  1282.9 4.1 copy-start.20
  1288.7 3.9 copy-start.39
  1292.5 944.8 %reduce-scatter.25.cloned.1.call-start = ((), (), s32[]{:S(2)}) async-start(), calls=%async_computation.21 | async-start | bytes 2211840
  1294.9 4.2 copy-start.14
  1299.1 109.4 %copy-start.28 = (bf16[768,192]{1,0:T(8,128)(2,1)S(1)}, bf16[768,192]{1,0:T(8,128)(2,1)}, u32[]{:S(2)}) copy-start(bf16[768,192]{1,0:T(8,128)(2,1)} %all_gather.26) | copy-start | bytes 884740
  1446.3 24.9 %copy-start.1 = (f32[3,512,512]{2,1,0:T(8,128)}, f32[3,512,512]{2,1,0:T(8,128)S(1)}, u32[]{:S(2)}) copy-start(f32[3,512,512]{2,1,0:T(8,128)S(1)} %fusion.310) | copy-start | bytes 9437188 | tf_op jit(solution)/shard_map/while/body/eval_jaxpr/while
  1510.7 24.9 %copy-start.1 = (f32[3,512,512]{2,1,0:T(8,128)}, f32[3,512,512]{2,1,0:T(8,128)S(1)}, u32[]{:S(2)}) copy-start(f32[3,512,512]{2,1,0:T(8,128)S(1)} %fusion.310) | copy-start | bytes 9437188 | tf_op jit(solution)/shard_map/while/body/eval_jaxpr/while
  1575.3 24.9 %copy-start.1 = (f32[3,512,512]{2,1,0:T(8,128)}, f32[3,512,512]{2,1,0:T(8,128)S(1)}, u32[]{:S(2)}) copy-start(f32[3,512,512]{2,1,0:T(8,128)S(1)} %fusion.310) | copy-start | bytes 9437188 | tf_op jit(solution)/shard_map/while/body/eval_jaxpr/while
  1639.8 24.9 %copy-start.1 = (f32[3,512,512]{2,1,0:T(8,128)}, f32[3,512,512]{2,1,0:T(8,128)S(1)}, u32[]{:S(2)}) copy-start(f32[3,512,512]{2,1,0:T(8,128)S(1)} %fusion.310) | copy-start | bytes 9437188 | tf_op jit(solution)/shard_map/while/body/eval_jaxpr/while
  1692.8 3.5 copy-start.31
  1693.0 3.5 copy-start.30
  1693.0 5.2 copy-start.9
  1731.8 24.9 %copy-start.1 = (f32[3,512,512]{2,1,0:T(8,128)}, f32[3,512,512]{2,1,0:T(8,128)S(1)}, u32[]{:S(2)}) copy-start(f32[3,512,512]{2,1,0:T(8,128)S(1)} %fusion.310) | copy-start | bytes 9437188 | tf_op jit(solution)/shard_map/while/body/eval_jaxpr/while
  1796.1 24.9 %copy-start.1 = (f32[3,512,512]{2,1,0:T(8,128)}, f32[3,512,512]{2,1,0:T(8,128)S(1)}, u32[]{:S(2)}) copy-start(f32[3,512,512]{2,1,0:T(8,128)S(1)} %fusion.310) | copy-start | bytes 9437188 | tf_op jit(solution)/shard_map/while/body/eval_jaxpr/while
  1860.7 24.9 %copy-start.1 = (f32[3,512,512]{2,1,0:T(8,128)}, f32[3,512,512]{2,1,0:T(8,128)S(1)}, u32[]{:S(2)}) copy-start(f32[3,512,512]{2,1,0:T(8,128)S(1)} %fusion.310) | copy-start | bytes 9437188 | tf_op jit(solution)/shard_map/while/body/eval_jaxpr/while
  1925.2 24.9 %copy-start.1 = (f32[3,512,512]{2,1,0:T(8,128)}, f32[3,512,512]{2,1,0:T(8,128)S(1)}, u32[]{:S(2)}) copy-start(f32[3,512,512]{2,1,0:T(8,128)S(1)} %fusion.310) | copy-start | bytes 9437188 | tf_op jit(solution)/shard_map/while/body/eval_jaxpr/while
  1978.2 3.5 copy-start.31
  1978.4 3.5 copy-start.30
  1978.4 5.2 copy-start.9
  1981.8 3.4 copy-start.35
  2097.8 15.3 copy-start.34
  2113.1 12.2 copy-start.18
  2113.1 12.2 copy-start.19
  2125.2 152.5 %reduce-scatter.17.cloned.1.call-start = ((), (), s32[]{:S(2)}) async-start(), calls=%async_computation.17 | async-start | bytes 7864320 | tf_op jit(solution)/shard_map/reduce_scatter | solution.py:243
  2134.2 190.6 %reduce-scatter.23.cloned.1.call-start = ((), (), s32[]{:S(2)}) async-start(), calls=%async_computation.20 | async-start | bytes 2654208 | tf_op jit(solution)/shard_map/reduce_scatter | solution.py:225
  2144.5 10.3 copy-start.48
  2144.5 10.3 copy-start.49
  2144.5 10.3 copy-start.47
  2144.5 226.4 %reduce-scatter.21.cloned.1.call-start = ((), (), s32[]{:S(2)}) async-start(), calls=%async_computation.19 | async-start | bytes 2654208 | tf_op jit(solution)/shard_map/reduce_scatter | solution.py:224
  2154.6 4.2 copy-start.51
  2154.6 4.2 copy-start.52
  2154.6 4.2 copy-start.50
  2154.7 4.2 copy-start.33
  2154.7 255.2 %reduce-scatter.19.cloned.1.call-start = ((), (), s32[]{:S(2)}) async-start(), calls=%async_computation.18 | async-start | bytes 884736 | tf_op jit(solution)/shard_map/reduce_scatter | solution.py:225
  2164.4 47.9 %copy-start.57 = (f32[768]{0:T(1024)S(1)}, f32[768]{0:T(1024)}, u32[]{:S(2)}) copy-start(f32[768]{0:T(1024)} %get-tuple-element.1113) | copy-start | bytes 9220
  2164.4 113.3 %copy-start.6 = (f32[512,2,768]{2,0,1:T(8,128)S(1)}, f32[512,2,768]{2,0,1:T(8,128)}, u32[]{:S(2)}) copy-start(f32[512,2,768]{2,0,1:T(8,128)} %copy-done.5) | copy-start | bytes 9437188
  2164.4 113.3 %copy-start.40 = (f32[512,2]{0,1:T(2,128)S(1)}, f32[512,2]{0,1:T(2,128)}, u32[]{:S(2)}) copy-start(f32[512,2]{0,1:T(2,128)} %copy-done.39) | copy-start | bytes 12292
  (49 other events, 97.4 us)
Sparse Core Ops, SparseCore 0:
  11.0 118.0 all-gather.6
  430.0 210.0 reduce-scatter.10
  1030.2 116.3 all-gather.14
  1292.7 115.8 all-gather.16
Sparse Core Ops, SparseCore 1:
  432.2 22.0 all-gather.10
  645.8 116.2 all-gather.8
  763.8 22.0 all-gather.12
  807.6 209.9 reduce-scatter.12
  1174.0 108.8 reduce-scatter.14
  2125.3 38.3 reduce-scatter.24
  2166.0 111.7 reduce-scatter.16
  2281.9 42.8 reduce-scatter.22
  2328.5 42.3 reduce-scatter.20
  2375.0 34.9 reduce-scatter.18
where the time goes:
time: 2430 us; the launch traced here: 2420 us
  waiting for transfers between devices  1120 us (46%)
  local copies, waits for them, and re-layouts  406 us (17%)
  matrix products  401 us (17%)
  other arithmetic  328 us (13%)
  blocking collectives  96.6 us (4%)
  loops' own time  54.4 us (2%)
    reduce_scatter x2, waiting for transfers between devices, sum_heads(): lax.psum_scatter(term_fn(jnp.int32(0), row_count * lax.axis_size('tp')),...  419 us
    all_gather x2, waiting for transfers between devices, collect_grads(): return lax.all_gather(shard_rows, 'tp', axis=0, tiled=True)  219 us
    all_gather x2, waiting for transfers between devices, collect_rows(): return lax.all_gather(shard_rows, 'tp', axis=0, tiled=True)  201 us
    sub x8, other arithmetic, one_step(): grad_scores = (probs * (grad_probs - row_dot)).astype(jnp.bfloat16)  148 us
    reduce_scatter x2, waiting for transfers between devices, sum_inputs(): lax.psum_scatter(term_fn(jnp.int32(0), row_count * lax.axis_size('tp')).a...  147 us
    slice x14, local copies, waits for them, and re-layouts, pool_pairs(): padded[:, :, offset:offset + length]  89.8 us
    reduce_scatter x2, waiting for transfers between devices, reduce_layer(): lax.psum_scatter(second_grad, 'fsdp', scatter_dimension=0, tiled=True)  80.1 us
    reshape x5, local copies, waits for them, and re-layouts, pool_pairs(): padded[:, :, offset:offset + length]  63.3 us
  transfers between devices with their start and end apart: 14, of which 11 were waited for; matrix products, arithmetic and copies ran while one was open for 4% of the time, Pallas kernels for 0%

commit v1 on v0

v1 whole, which is shorter than its diff:
```python
from functools import partial

import jax
import jax.numpy as jnp
from jax import lax
from jax.experimental import pallas as pl
from jax.experimental.pallas import tpu as pltpu
from jax.sharding import PartitionSpec as P

HEAD_DIM = 64
HALF = 64
STRIDE = 4
TAPS = 5
MARGIN = TAPS // 2
PAIR = 2 * HEAD_DIM
QB = 128
EPSILON = 1e-05
NEG = -1e30
SCALE = HEAD_DIM**-0.5
BF = jnp.bfloat16
F32 = jnp.float32


def nt(a, b):
    return lax.dot_general(a, b, (((1,), (1,)), ((), ())), preferred_element_type=F32)


def nn(a, b):
    return lax.dot_general(a, b, (((1,), (0,)), ((), ())), preferred_element_type=F32)


def tn(a, b):
    return lax.dot_general(a, b, (((0,), (0,)), ((), ())), preferred_element_type=F32)


def fill_masks(segq_ref, segk_ref, cen_ref, near_bias, far_bias):
    rows = segq_ref.shape[1]
    shape = (QB, 2 * HALF + QB)
    gap = lax.broadcasted_iota(jnp.int32, shape, 1) - lax.broadcasted_iota(jnp.int32, shape, 0)
    band = (gap >= 0) & (gap <= 2 * HALF)
    for first in range(0, rows, QB):
        own = segq_ref[0, first : first + QB, :]
        keys = segk_ref[0, :, first : first + QB + 2 * HALF]
        near_bias[first : first + QB, :] = jnp.where(band & (own == keys), 0.0, NEG)
        far_bias[first : first + QB, :] = jnp.where(own == cen_ref[0], 0.0, NEG)


def join_rows(left_ref, own_ref, right_ref, joined):
    rows = own_ref.shape[1]
    joined[:HALF, :] = left_ref[0]
    joined[HALF : HALF + rows, :] = own_ref[0]
    joined[HALF + rows :, :] = right_ref[0]


def head_mask(head):
    lane = lax.broadcasted_iota(jnp.int32, (1, PAIR), 1)
    return lane < HEAD_DIM if head == 0 else lane >= HEAD_DIM


def softmax_block(query, keys_near, keys_far, bias_near, bias_far):
    near = nt(query, keys_near) + bias_near
    far = nt(query, keys_far) + bias_far
    top = jnp.maximum(
        jnp.max(near, axis=-1, keepdims=True), jnp.max(far, axis=-1, keepdims=True)
    )
    near = jnp.exp(near - top)
    far = jnp.exp(far - top)
    total = jnp.sum(near, axis=-1, keepdims=True) + jnp.sum(far, axis=-1, keepdims=True)
    inverse = 1.0 / total
    return near * inverse, far * inverse


def attend_forward_kernel(
    q_ref, k_ref, v_ref, kl_ref, kr_ref, vl_ref, vr_ref, pk_ref, pv_ref,
    segq_ref, segk_ref, cen_ref, out_ref, near_bias, far_bias, keys, values,
):
    @pl.when(pl.program_id(1) == 0)
    def _():
        fill_masks(segq_ref, segk_ref, cen_ref, near_bias, far_bias)

    rows = q_ref.shape[1]
    join_rows(kl_ref, k_ref, kr_ref, keys)
    join_rows(vl_ref, v_ref, vr_ref, values)
    far_keys = pk_ref[...].reshape(-1, PAIR)
    far_values = pv_ref[...].reshape(-1, PAIR)
    for first in range(0, rows, QB):
        block = slice(first, first + QB)
        span = slice(first, first + QB + 2 * HALF)
        query = q_ref[0, block, :] * BF(SCALE)
        halves = []
        for head in range(2):
            picked = jnp.where(head_mask(head), query, BF(0))
            near, far = softmax_block(
                picked, keys[span, :], far_keys, near_bias[block, :], far_bias[block, :]
            )
            halves.append(nn(near.astype(BF), values[span, :]) + nn(far.astype(BF), far_values))
        out_ref[0, block, :] = jnp.where(head_mask(0), halves[0], halves[1]).astype(BF)


def attend_backward_kernel(
    q_ref, k_ref, v_ref, kl_ref, kr_ref, vl_ref, vr_ref, pk_ref, pv_ref,
    segq_ref, segk_ref, cen_ref, grad_ref,
    dq_ref, dk_ref, dv_ref, dpk_ref, dpv_ref,
    near_bias, far_bias, keys, values, far_probs, far_grads,
):
    @pl.when(pl.program_id(1) == 0)
    def _():
        fill_masks(segq_ref, segk_ref, cen_ref, near_bias, far_bias)

    rows = q_ref.shape[1]
    join_rows(kl_ref, k_ref, kr_ref, keys)
    join_rows(vl_ref, v_ref, vr_ref, values)
    far_keys = pk_ref[...].reshape(-1, PAIR)
    far_values = pv_ref[...].reshape(-1, PAIR)
    dk_ref[...] = jnp.zeros_like(dk_ref)
    dv_ref[...] = jnp.zeros_like(dv_ref)
    for head in range(2):
        mask = head_mask(head)
        for first in range(0, rows, QB):
            block = slice(first, first + QB)
            span = slice(first, first + QB + 2 * HALF)
            query = jnp.where(mask, q_ref[0, block, :] * BF(SCALE), BF(0))
            grad = jnp.where(mask, grad_ref[0, block, :], BF(0))
            near, far = softmax_block(
                query, keys[span, :], far_keys, near_bias[block, :], far_bias[block, :]
            )
            grad_near = nt(grad, values[span, :])
            grad_far = nt(grad, far_values)
            row_dot = jnp.sum(near * grad_near, axis=-1, keepdims=True) + jnp.sum(
                far * grad_far, axis=-1, keepdims=True
            )
            ds_near = (near * (grad_near - row_dot)).astype(BF)
            ds_far = (far * (grad_far - row_dot)).astype(BF)
            far_probs[block, :] = far.astype(BF)
            far_grads[block, :] = ds_far
            dq = (nn(ds_near, keys[span, :]) + nn(ds_far, far_keys)) * SCALE
            if head == 0:
                dq_ref[0, block, :] = dq.astype(BF)
            else:
                dq_ref[0, block, :] = jnp.where(mask, dq.astype(BF), dq_ref[0, block, :])
            dk_ref[0, span, :] += tn(ds_near, query)
            dv_ref[0, span, :] += tn(near.astype(BF), grad)
        query = jnp.where(mask, q_ref[0] * BF(SCALE), BF(0))
        grad = jnp.where(mask, grad_ref[0], BF(0))
        dpk = tn(far_grads[...], query).reshape(dpk_ref.shape)
        dpv = tn(far_probs[...], grad).reshape(dpv_ref.shape)
        if head == 0:
            dpk_ref[...] = dpk.astype(BF)
            dpv_ref[...] = dpv.astype(BF)
        else:
            dpk_ref[...] = jnp.where(mask, dpk.astype(BF), dpk_ref[...])
            dpv_ref[...] = jnp.where(mask, dpv.astype(BF), dpv_ref[...])


def attention_specs(seqs, rows, parts, blocks, far_rows):
    def own(part):
        return pl.BlockSpec((None, 1, rows, PAIR), lambda s, h: (part, s, 0, h))

    def halo(part):
        return pl.BlockSpec((None, 1, HALF, PAIR), lambda s, h: (part, s, 0, h))

    def pooled(part):
        return pl.BlockSpec(
            (blocks, None, 1, far_rows, PAIR), lambda s, h: (0, part, s, 0, h)
        )

    return [
        own(0), own(1), own(2),
        halo(0), halo(0), halo(1), halo(1),
        pooled(0), pooled(1),
        pl.BlockSpec((1, rows, 1), lambda s, h: (s, 0, 0)),
        pl.BlockSpec((1, 1, rows + 2 * HALF), lambda s, h: (s, 0, 0)),
        pl.BlockSpec((1, 1, blocks * far_rows), lambda s, h: (s, 0, 0)),
    ]


def attention_scratch(rows, far_all):
    return [
        pltpu.VMEM((rows, 2 * HALF + QB), F32),
        pltpu.VMEM((rows, far_all), F32),
        pltpu.VMEM((rows + 2 * HALF, PAIR), BF),
        pltpu.VMEM((rows + 2 * HALF, PAIR), BF),
    ]


def attend_forward(projected, left, right, pooled, segs):
    _, seqs, rows, width = projected.shape
    blocks, _, _, far_rows, _ = pooled.shape
    cells = seqs * rows * (2 * HALF + QB + blocks * far_rows) * (width // HEAD_DIM)
    return pl.pallas_call(
        attend_forward_kernel,
        grid=(seqs, width // PAIR),
        in_specs=attention_specs(seqs, rows, 3, blocks, far_rows),
        out_specs=pl.BlockSpec((1, rows, PAIR), lambda s, h: (s, 0, h)),
        out_shape=jax.ShapeDtypeStruct((seqs, rows, width), BF),
        scratch_shapes=attention_scratch(rows, blocks * far_rows),
        compiler_params=pltpu.CompilerParams(vmem_limit_bytes=40 * 2**20),
        cost_estimate=pl.CostEstimate(
            flops=8 * 64 * cells, bytes_accessed=12 * 2**20, transcendentals=cells
        ),
    )(projected, projected, projected, left, right, left, right, pooled, pooled, *segs)


def attend_backward(projected, left, right, pooled, segs, grad):
    _, seqs, rows, width = projected.shape
    blocks, _, _, far_rows, _ = pooled.shape
    cells = seqs * rows * (2 * HALF + QB + blocks * far_rows) * (width // HEAD_DIM)
    wide = rows + 2 * HALF
    far_spec = pl.BlockSpec((blocks, 1, far_rows, PAIR), lambda s, h: (0, s, 0, h))
    far_shape = jax.ShapeDtypeStruct((blocks, seqs, far_rows, width), BF)
    wide_spec = pl.BlockSpec((1, wide, PAIR), lambda s, h: (s, 0, h))
    wide_shape = jax.ShapeDtypeStruct((seqs, wide, width), F32)
    own_spec = pl.BlockSpec((1, rows, PAIR), lambda s, h: (s, 0, h))
    return pl.pallas_call(
        attend_backward_kernel,
        grid=(seqs, width // PAIR),
        in_specs=attention_specs(seqs, rows, 3, blocks, far_rows) + [own_spec],
        out_specs=[own_spec, wide_spec, wide_spec, far_spec, far_spec],
        out_shape=[
            jax.ShapeDtypeStruct((seqs, rows, width), BF),
            wide_shape, wide_shape, far_shape, far_shape,
        ],
        scratch_shapes=attention_scratch(rows, blocks * far_rows)
        + [pltpu.VMEM((rows, blocks * far_rows), BF)] * 2,
        compiler_params=pltpu.CompilerParams(vmem_limit_bytes=40 * 2**20),
        cost_estimate=pl.CostEstimate(
            flops=20 * 64 * cells, bytes_accessed=24 * 2**20, transcendentals=cells
        ),
    )(projected, projected, projected, left, right, left, right, pooled, pooled, *segs, grad)


def norm_stats(residual):
    row_mean = jnp.mean(residual, axis=-1, keepdims=True)
    centered = residual - row_mean
    variance = jnp.mean(centered * centered, axis=-1, keepdims=True)
    inverse = lax.rsqrt(variance + EPSILON)
    return centered * inverse, inverse


def norm_back(grad, normed, inverse, gain):
    scaled = grad * gain
    first = jnp.mean(scaled, axis=-1, keepdims=True)
    second = jnp.mean(scaled * normed, axis=-1, keepdims=True)
    return (scaled - first - normed * second) * inverse


def gather_weight(shard):
    wide = lax.all_gather(shard, "tp", axis=shard.ndim - 1, tiled=True)
    return lax.all_gather(wide, "fsdp", axis=0, tiled=True)


def scatter_weight(grad):
    part = lax.psum_scatter(grad.astype(BF), "fsdp", scatter_dimension=0, tiled=True)
    return lax.psum_scatter(
        part, "tp", scatter_dimension=part.ndim - 1, tiled=True
    ).astype(F32)


def shift_right(rows):
    count = lax.axis_size("tp")
    return lax.ppermute(rows, "tp", [(i, i + 1) for i in range(count - 1)])


def shift_left(rows):
    count = lax.axis_size("tp")
    return lax.ppermute(rows, "tp", [(i + 1, i) for i in range(count - 1)])


def body(
    inputs, segments, w_qkv, qkv_bias, pool_kernel, w_out, out_bias,
    w_up, up_bias, w_down, norm_gains, norm_shifts, cotangent,
):
    rows, seqs, width = inputs.shape
    tp = lax.axis_size("tp")
    place = lax.axis_index("tp")
    full_len = rows * tp
    far_rows = rows // STRIDE

    seg_rows = segments.T
    padded = jnp.pad(seg_rows, ((0, 0), (HALF, HALF)), constant_values=-1)
    seg_keys = lax.dynamic_slice_in_dim(padded, place * rows, rows + 2 * HALF, 1)
    seg_own = seg_keys[:, HALF : HALF + rows]
    centers_all = seg_rows[:, ::STRIDE]
    segs = (seg_own[:, :, None], seg_keys[:, None, :], centers_all[:, None, :])
    centers = seg_own[:, ::STRIDE]
    near_seg = seg_keys[:, HALF - MARGIN : HALF + rows]
    same = [
        (near_seg[:, r : r + rows : STRIDE][:, :far_rows] == centers).astype(F32)
        for r in range(TAPS)
    ]

    tokens = inputs.transpose(1, 0, 2)
    full_qkv = gather_weight(w_qkv)
    bias_qkv = lax.all_gather(qkv_bias, "tp", axis=1, tiled=True)
    kernel = lax.all_gather(pool_kernel, "tp", axis=2, tiled=True)
    bias_up = lax.all_gather(up_bias, "tp", axis=0, tiled=True)
    full_out = gather_weight(w_out)
    full_up = gather_weight(w_up)
    full_down = gather_weight(w_down)

    made = jnp.einsum("sld,dcf->cslf", tokens, full_qkv, preferred_element_type=F32)
    projected = (made + bias_qkv[:, None, None, :]).astype(BF)
    left = shift_right(projected[1:, :, rows - HALF :])
    right = shift_left(projected[1:, :, :HALF])

    wide = jnp.concatenate([left[:, :, HALF - MARGIN :], projected[1:]], axis=2)
    tapped = [
        lax.slice_in_dim(wide, r, r + rows - STRIDE + 1, STRIDE, 2).astype(F32)
        for r in range(TAPS)
    ]
    pooled_own = sum(
        kernel[:, r][:, None, None, :] * tapped[r] * same[r][None, :, :, None]
        for r in range(TAPS)
    ).astype(BF)
    pooled = lax.all_gather(pooled_own, "tp", axis=0, tiled=False)
    attended = attend_forward(projected, left, right, pooled, segs)

    branch = (
        jnp.einsum("slf,ef->sle", attended, full_out, preferred_element_type=F32) + out_bias[0]
    )
    normed_one, inverse_one = norm_stats(tokens.astype(F32) + branch)
    first_out = normed_one * norm_gains[0] + norm_shifts[0]
    first_low = first_out.astype(BF)
    pre_act = (
        jnp.einsum("sld,df->slf", first_low, full_up, preferred_element_type=F32) + bias_up
    )
    hidden = jax.nn.gelu(pre_act, approximate=False).astype(BF)
    ffn_out = (
        jnp.einsum("slf,ef->sle", hidden, full_down, preferred_element_type=F32) + out_bias[1]
    )
    normed_two, inverse_two = norm_stats(first_out + ffn_out)
    outputs = normed_two * norm_gains[1] + norm_shifts[1]

    grad_out = cotangent.transpose(1, 0, 2).astype(F32)
    grad_second = norm_back(grad_out, normed_two, inverse_two, norm_gains[1])
    gain_two = jnp.sum(grad_out * normed_two, axis=(0, 1))
    shift_two = jnp.sum(grad_out, axis=(0, 1))
    grad_ffn_low = grad_second.astype(BF)
    grad_hidden = jnp.einsum("sle,ef->slf", grad_ffn_low, full_down, preferred_element_type=F32)
    gelu_back = jax.vjp(partial(jax.nn.gelu, approximate=False), pre_act)[1]
    grad_pre = gelu_back(grad_hidden)[0].astype(BF)
    grad_w_down = jnp.einsum("sle,slf->ef", grad_ffn_low, hidden, preferred_element_type=F32)
    grad_w_down = scatter_weight(grad_w_down)
    grad_w_up = jnp.einsum("sld,slf->df", first_low, grad_pre, preferred_element_type=F32)
    grad_w_up = scatter_weight(grad_w_up)
    grad_up_bias = jnp.sum(grad_pre, axis=(0, 1), dtype=F32)
    grad_first = grad_second + jnp.einsum(
        "slf,df->sld", grad_pre, full_up, preferred_element_type=F32
    )
    grad_residual = norm_back(grad_first, normed_one, inverse_one, norm_gains[0])
    gain_one = jnp.sum(grad_first * normed_one, axis=(0, 1))
    shift_one = jnp.sum(grad_first, axis=(0, 1))
    grad_branch_low = grad_residual.astype(BF)
    grad_attended = jnp.einsum(
        "sle,ef->slf", grad_branch_low, full_out, preferred_element_type=F32
    ).astype(BF)
    grad_w_out = jnp.einsum("sle,slf->ef", grad_branch_low, attended, preferred_element_type=F32)
    grad_w_out = scatter_weight(grad_w_out)

    dq, dk, dv, dpk, dpv = attend_backward(projected, left, right, pooled, segs, grad_attended)
    grad_pooled = lax.psum_scatter(
        jnp.stack([dpk, dpv], axis=1), "tp", scatter_dimension=0, tiled=False
    ).astype(F32)
    pair_grads = jnp.stack([dk, dv])
    to_left = pair_grads[:, :, :HALF]
    to_right = pair_grads[:, :, HALF + rows :]
    tap_grads = []
    grad_taps = []
    for r in range(TAPS):
        masked = grad_pooled * same[r][None, :, :, None]
        tap_grads.append(kernel[:, r][:, None, None, :] * masked)
        grad_taps.append(jnp.sum(masked * tapped[r], axis=(1, 2)))
    grad_kernel = jnp.stack(grad_taps, axis=1)
    later = jnp.pad(tap_grads[4], ((0, 0), (0, 0), (1, 0), (0, 0)))
    quads = jnp.stack(
        [
            jnp.pad(tap_grads[0], ((0, 0), (0, 0), (0, 1), (0, 0))) + later,
            jnp.pad(tap_grads[1], ((0, 0), (0, 0), (0, 1), (0, 0))),
            jnp.pad(tap_grads[2], ((0, 0), (0, 0), (0, 1), (0, 0))),
            jnp.pad(tap_grads[3], ((0, 0), (0, 0), (0, 1), (0, 0))),
        ],
        axis=3,
    ).reshape(2, seqs, rows + STRIDE, width)
    to_left = to_left.at[:, :, HALF - MARGIN :].add(quads[:, :, :MARGIN])
    own_pairs = pair_grads[:, :, HALF : HALF + rows] + quads[:, :, MARGIN : MARGIN + rows]
    from_right = shift_left(to_left.astype(BF)).astype(F32)
    from_left = shift_right(to_right.astype(BF)).astype(F32)
    own_pairs = own_pairs.at[:, :, rows - HALF :].add(from_right)
    own_pairs = own_pairs.at[:, :, :HALF].add(from_left)
    grad_projected = jnp.concatenate([dq[None], own_pairs.astype(BF)], axis=0)
    grad_qkv_bias = jnp.sum(grad_projected, axis=(1, 2), dtype=F32)
    grad_w_qkv = jnp.einsum("sld,cslf->dcf", tokens, grad_projected, preferred_element_type=F32)
    grad_w_qkv = scatter_weight(grad_w_qkv)
    grad_inputs = grad_residual + jnp.einsum(
        "cslf,dcf->sld", grad_projected, full_qkv, preferred_element_type=F32
    )

    grad_out_bias = jnp.stack(
        [
            jnp.sum(grad_branch_low, axis=(0, 1), dtype=F32),
            jnp.sum(grad_ffn_low, axis=(0, 1), dtype=F32),
        ]
    )
    grad_norm_gains = jnp.stack([gain_one, gain_two])
    grad_norm_shifts = jnp.stack([shift_one, shift_two])
    (
        grad_qkv_bias, grad_kernel, grad_up_bias, grad_out_bias, grad_norm_gains, grad_norm_shifts
    ) = lax.psum(
        (
            grad_qkv_bias, grad_kernel, grad_up_bias,
            grad_out_bias, grad_norm_gains, grad_norm_shifts,
        ),
        ("fsdp", "tp"),
    )

    def own_columns(whole):
        count = whole.shape[-1] // tp
        return lax.dynamic_slice_in_dim(whole, place * count, count, whole.ndim - 1)

    return (
        outputs.transpose(1, 0, 2).astype(BF),
        grad_inputs.transpose(1, 0, 2),
        grad_w_qkv,
        own_columns(grad_qkv_bias),
        own_columns(grad_kernel),
        grad_w_out,
        grad_out_bias,
        grad_w_up,
        own_columns(grad_up_bias),
        grad_w_down,
        grad_norm_gains,
        grad_norm_shifts,
    )


def solution(mesh):
    placed = (
        P("tp", "fsdp", None),
        P(None, "fsdp"),
        P("fsdp", None, "tp"),
        P(None, "tp"),
        P(None, None, "tp"),
        P("fsdp", "tp"),
        P(),
        P("fsdp", "tp"),
        P("tp"),
        P("fsdp", "tp"),
        P(),
        P(),
        P("tp", "fsdp", None),
    )
    return jax.shard_map(
        body,
        mesh=mesh,
        in_specs=placed,
        out_specs=(
            P("tp", "fsdp", None),
            P("tp", "fsdp", None),
            P("fsdp", None, "tp"),
            P(None, "tp"),
            P(None, None, "tp"),
            P("fsdp", "tp"),
            P(),
            P("fsdp", "tp"),
            P("tp"),
            P("fsdp", "tp"),
            P(),
            P(),
        ),
        check_vma=False,
    )
```

time: 2430 us -> 943 us (0.39)
  waiting for transfers between devices: 1120 us -> 342 us
  matrix products: 401 us -> 108 us
  local copies, waits for them, and re-layouts: 406 us -> 122 us
  other arithmetic: 328 us -> 82.1 us
  Pallas kernels: 0 us -> 111 us
  loops' own time: 54.4 us -> 0 us
  blocking collectives: 96.6 us -> 144 us
    reduce_scatter x7, waiting for transfers between devices: 693 us -> 154 us  [the longest x3 64.8 us: scatter_weight(): lax.psum_scatter(part, 'tp', scatter_dimension=part.ndim - 1, tiled=True)]
    all_gather x6 -> x5, waiting for transfers between devices: 421 us -> 4.4 us  [the longest x4 4.38 us: gather_weight(): return lax.all_gather(wide, 'fsdp', axis=0, tiled=True)]
    dot_general x124 -> x12, matrix products: 401 us -> 108 us  [the longest x1 18.1 us: body(): jnp.einsum('sle,ef->slf', grad_ffn_low, full_down, preferred_element_type...]
    sub x8 -> x0, other arithmetic: 148 us -> none  [one_step(): grad_scores = (probs * (grad_probs - row_dot)).astype(jnp.bfloat16)]
    all_gather x2 -> x7, blocking collectives: 26.4 us -> 144 us  [the longest x4 82.7 us: gather_weight(): wide = lax.all_gather(shard, 'tp', axis=shard.ndim - 1, tiled=True)]
    psum x0 -> x1, waiting for transfers between devices: none -> 113 us  [body(): lax.psum((grad_qkv_bias, grad_kernel, grad_up_bias, grad_out_bias, grad_n...]
    pallas_call x0 -> x2, Pallas kernels: none -> 111 us  [the longest x1 66.8 us: attend_backward(): pl.pallas_call(attend_backward_kernel, grid=(seqs, width // PAIR), in_spe...]
    psum x2 -> x0, blocking collectives: 70.2 us -> none  [the longest x1 45.1 us: body(): lax.psum((grad_out_bias, grad_norm_gains, grad_norm_shifts), ('fsdp', 'tp'))]
  transfers between devices with their start and end apart: 14 -> 19, of which waited for: 11 -> 10; matrix products, arithmetic and copies ran while one was open for 4% -> 22% of each run, Pallas kernels for 0% -> 12%
where the time goes in v1:
time: 943 us; the launch traced here: 933 us
  waiting for transfers between devices  342 us (36%)
  blocking collectives  144 us (15%)
  local copies, waits for them, and re-layouts  122 us (13%)
  Pallas kernels  111 us (12%)
  matrix products  108 us (11%)
  other arithmetic  82.1 us (9%)
  between operations  15.5 us (2%)
    psum x1, waiting for transfers between devices, body(): lax.psum((grad_qkv_bias, grad_kernel, grad_up_bias, grad_out_bias, grad_n...  113 us
    all_gather x4, blocking collectives, gather_weight(): wide = lax.all_gather(shard, 'tp', axis=shard.ndim - 1, tiled=True)  82.7 us
    pallas_call x1, Pallas kernels, attend_backward(): pl.pallas_call(attend_backward_kernel, grid=(seqs, width // PAIR), in_spe...  66.8 us
    reduce_scatter x3, waiting for transfers between devices, scatter_weight(): lax.psum_scatter(part, 'tp', scatter_dimension=part.ndim - 1, tiled=True)  64.8 us
    unnamed x17, waiting for transfers between devices  63.2 us
    reduce_scatter x3, waiting for transfers between devices, scatter_weight(): lax.psum_scatter(grad.astype(BF), 'fsdp', scatter_dimension=0, tiled=True)  54 us
    pallas_call x1, Pallas kernels, attend_forward(): pl.pallas_call(attend_forward_kernel, grid=(seqs, width // PAIR), in_spec...  44 us
    unnamed x175, local copies, waits for them, and re-layouts  43.4 us
  transfers between devices with their start and end apart: 19, of which 10 were waited for; matrix products, arithmetic and copies ran while one was open for 22% of the time, Pallas kernels for 12%

profile of v1, /device:TPU:0, one launch (start us, length us, event | category | flops | bytes accessed | tf_op | source)
XLA Modules:
  0.0 933.4 jit_solution(2588060115932886461)
XLA Ops:
  8.3 21.3 %all_gather.39 = bf16[96,3,768]{0,1,2:T(4,128)(2,1)S(1)} all-gather(bf16[96,3,192]{0,1,2:T(4,128)(2,1)S(1)} %copy.82), channel_id=1, replica_groups=mesh['fsdp'=8,'tp'=4] {'tp'}, dimensions={2}, use_global_device_ids=true | all-gather | bytes 552960 | tf_op jit(solution)/shard_map/all_gather | solution.py:248
  30.8 13.3 %all-gather.1 = f32[4,192,3]{1,2,0:T(4,128)S(1)} all-gather(f32[1,192,3]{1,2,0:T(4,128)} %bitcast.233), channel_id=1, replica_groups=mesh['fsdp'=8,'tp'=4] {'tp'}, dimensions={0}, use_global_device_ids=true | all-gather | bytes 11520 | tf_op jit(solution)/shard_map/all_gather | solution.py:294
  45.1 17.4 %all_gather.42 = f32[2,5,768]{1,0,2:T(2,128)S(1)} all-gather(f32[2,5,192]{1,0,2:T(2,128)S(1)} %copy.86), channel_id=1, replica_groups=mesh['fsdp'=8,'tp'=4] {'tp'}, dimensions={2}, use_global_device_ids=true | all-gather | bytes 38400 | tf_op jit(solution)/shard_map/all_gather | solution.py:295
  62.5 4.7 fusion.103
  67.2 6.1 fusion.8.q_ref.k_ref.v_ref
  73.3 2.1 copy-done
  79.4 1.9 copy.88
  81.3 1.9 copy.89
  86.6 2.1 slice.239
  88.7 6.0 slice.212
  94.7 6.0 slice.215
  100.7 6.0 slice.218
  106.8 2.4 pad_maximum_fusion.2
  109.1 8.8 slice.203
  118.0 10.2 %slice.209 = bf16[2,2,128,768]{3,2,1,0:T(8,128)(2,1)} slice(bf16[2,2,514,768]{3,2,1,0:T(8,128)(2,1)} %pad_maximum_fusion.2), slice={[0:2:1], [0:2:1], [1:510:4], [0:768:1]} | slice | bytes 1572864 | tf_op jit(solution)/shard_map/slice | solution.py:308
  128.1 3.1 fusion.59
  132.3 14.6 %all_gather.45 = bf16[96,768]{0,1:T(8,128)(2,1)S(1)} all-gather(bf16[96,192]{0,1:T(8,128)(2,1)S(1)} %copy.93), channel_id=1, replica_groups=mesh['fsdp'=8,'tp'=4] {'tp'}, dimensions={1}, use_global_device_ids=true | all-gather | bytes 184320 | tf_op jit(solution)/shard_map/all_gather | solution.py:248
  147.9 23.5 %all_gather.47 = bf16[96,3072]{1,0:T(8,128)(2,1)} all-gather(bf16[96,768]{1,0:T(8,128)(2,1)} %param.26), channel_id=1, replica_groups=mesh['fsdp'=8,'tp'=4] {'tp'}, dimensions={1}, use_global_device_ids=true | all-gather | bytes 737280 | tf_op jit(solution)/shard_map/all_gather | solution.py:248
  171.5 23.2 %all_gather.50 = bf16[96,3072]{1,0:T(8,128)(2,1)} all-gather(bf16[96,768]{1,0:T(8,128)(2,1)} %param.28), channel_id=1, replica_groups=mesh['fsdp'=8,'tp'=4] {'tp'}, dimensions={1}, use_global_device_ids=true | all-gather | bytes 737280 | tf_op jit(solution)/shard_map/all_gather | solution.py:248
  196.7 31.0 %all-gather.2 = f32[4,1,768]{2,1,0:T(1,128)S(1)} all-gather(f32[1,1,768]{2,1,0:T(1,128)S(1)} %reshape.195), channel_id=1, replica_groups=mesh['fsdp'=8,'tp'=4] {'tp'}, dimensions={0}, use_global_device_ids=true | all-gather | bytes 15360 | tf_op jit(solution)/shard_map/all_gather | solution.py:296
  228.4 2.5 copy-done.1
  230.9 1.9 copy-done.2
  232.8 44.0 %shard_map.220 = bf16[2,512,768]{2,1,0:T(8,128)(2,1)S(1)} custom-call(bf16[3,2,512,768]{3,2,1,0:T(8,128)(2,1)S(1)} %copy-done.1, bf16[3,2,512,768]{3,2,1,0:T(8,128)(2,1)S(1)} %copy-done.1, bf16[3,2,512,768]{3,2,1,0:T(8,128)(2,1)S(1)} %copy-done.1, bf16[2,2,64,768]{3,2,1,0:T(8,128)(2,1)S(1)} %collective-permute-done.kl_ref.vl_ref, ...), custom_call_target="tpu_custom_call" | custom-call | flops 4831838208 | bytes 12582912 | tf_op jit(solution)/shard_map/pallas_call | solution.py:190
  276.9 4.9 fusion.101
  284.6 4.3 all-gather.13.cloned.1.call-done
  288.9 15.7 %fusion.43 = (u8[512,3072]{1,0:T(8,128)(4,1)S(1)}, u8[512,3072]{1,0:T(8,128)(4,1)S(1)}, f32[2,512,3072]{2,1,0:T(8,128)}) fusion(f32[3072]{0:T(1024)S(1)} %bitcast.228, bf16[768,3072]{1,0:T(8,128)(2,1)} %all-gather.13.cloned.1.call-done, f32[2,512,768]{2,1,0:T(8,128)} %copy-done.12, f32[768]{0:T(1024)S(1)} %get-tuple-element.125, ...), kind=kOutput, calls=%fused_computation.94 | convolution fusion | flops 4876664832 | bytes 23619584 | tf_op jit(solution)/shard_map/sld,df->slf/dot_general | solution.py:325
  304.6 31.9 %multiply_convert_fusion = (bf16[2,512,3072]{2,1,0:T(8,128)(2,1)}, f32[2,512,3072]{2,1,0:T(8,128)}) fusion(f32[2,512,3072]{2,1,0:T(8,128)} %get-tuple-element.179, f32[3072]{0:T(1024)S(1)} %bitcast.229, u8[512,3072]{1,0:T(8,128)(4,1)S(1)} %get-tuple-element.107, u8[512,3072]{1,0:T(8,128)(4,1)S(1)} %get-tuple-element.106), kind=kLoop, calls=%fused_computation.9 | loop fusion | flops 223346688 | bytes 34615296 | tf_op jit(solution)/shard_map/convert_element_type | solution.py:327
  336.6 11.0 %fusion.99 = (f32[2,512]{1,0:T(2,128)S(1)}, f32[2,512,768]{2,1,0:T(8,128)S(1)}, f32[2,512,768]{2,1,0:T(8,128)}) fusion(f32[768]{0:T(1024)S(1)} %get-tuple-element.120, f32[768]{0:T(1024)S(1)} %get-tuple-element.125, f32[768]{0:T(1024)S(1)} %get-tuple-element.184, f32[2,512]{1,0:T(2,128)S(1)} %get-tuple-element.170, f32[2,512,768]{2,1,0:T(8,128)} %copy-done.12, ...), kind=kOutput, calls=%fused_computation.197 | convolution fusion | flops 4837342208 | bytes 20468736 | tf_op jit(solution)/shard_map/slf,ef->sle/dot_general | solution.py:329
  349.3 2.3 fusion.28
  352.8 1.8 convert_reduce_fusion.3
  354.6 18.1 %convert_reduce_fusion = (f32[3072]{0:T(1024)}, bf16[2,512,3072]{2,1,0:T(8,128)(2,1)}) fusion(f32[2,512,3072]{2,1,0:T(8,128)} %get-tuple-element.140, bf16[2,512,768]{2,1,0:T(8,128)(2,1)S(1)} %get-tuple-element.135, bf16[768,3072]{1,0:T(8,128)(2,1)} %all-gather.15.cloned.1.call-done, f32[2,512,3072]{2,1,0:T(8,128)} %get-tuple-element.179, f32[3072]{0:T(1024)S(1)} %bitcast.230), kind=kOutput, calls=%fused_computation.7 | convolution fusion | flops 4885312512 | bytes 37773312 | tf_op jit(solution)/shard_map/sle,ef->slf/dot_general | solution.py:339
  372.7 11.9 %multiply_reduce_fusion = (f32[768]{0:T(1024)}, f32[2,512]{1,0:T(2,128)S(1)}, f32[2,512]{1,0:T(2,128)S(1)}, f32[768]{0:T(1024)}, f32[2,512,768]{2,1,0:T(8,128)S(1)}, /*index=5*/f32[2,512,768]{2,1,0:T(8,128)}) fusion(f32[2,512,768]{2,1,0:T(8,128)S(1)} %copy-done.13, f32[2,512]{1,0:T(2,128)S(1)} %copy-done.63, f32[2,512]{1,0:T(2,128)S(1)} %copy-done.45, ...), kind=kOutput, calls=%fused_computation.83 | convolution fusion | flops 4845989888 | bytes 25210880 | tf_op jit(solution)/shard_map/slf,df->sld/dot_general | solution.py:347
  388.7 2.5 bitcast_convert_fusion.3
  391.3 3.3 convolution_convert_fusion.grad_ref
  394.6 66.8 %shard_map.221 = (bf16[2,512,768]{2,1,0:T(8,128)(2,1)S(1)}, f32[2,640,768]{2,1,0:T(8,128)}, f32[2,640,768]{2,1,0:T(8,128)}, bf16[4,2,128,768]{3,2,1,0:T(8,128)(2,1)S(1)}, bf16[4,2,128,768]{3,2,1,0:T(8,128)(2,1)S(1)}) custom-call(bf16[3,2,512,768]{3,2,1,0:T(8,128)(2,1)} %copy-done, bf16[3,2,512,768]{3,2,1,0:T(8,128)(2,1)} %copy-done, ...), custom_call_target="tpu_custom_call" | custom-call | flops 12079595520 | bytes 25165824 | tf_op jit(solution)/shard_map/pallas_call | solution.py:214
  462.6 2.0 pad_maximum_fusion.3
  464.6 1.8 copy-done.14
  466.4 9.9 %bitcast_convert_fusion.1 = bf16[768,3072]{1,0:T(8,128)(2,1)} fusion(bf16[2,512,3072]{2,1,0:T(8,128)(2,1)} %get-tuple-element.183, f32[2,512,768]{2,1,0:T(8,128)S(1)} %copy-done.14, f32[768]{0:T(1024)S(1)} %copy-done.55, f32[768]{0:T(1024)S(1)} %copy-done.43, f32[2,512]{1,0:T(2,128)S(1)} %copy-done.64, f32[2,512]{1,0:T(2,128)S(1)} %copy-done.46), kind=kOutput, calls=%fused_computation.29 | convolution fusion | flops 4838129664 | bytes 14170112 | tf_op jit(solution)/shard_map/sld,slf->df/dot_general | solution.py:344
  477.7 9.8 %bitcast_convert_fusion = bf16[768,3072]{1,0:T(8,128)(2,1)} fusion(bf16[2,512,768]{2,1,0:T(8,128)(2,1)S(1)} %copy-done.30, bf16[2,512,3072]{2,1,0:T(8,128)(2,1)} %get-tuple-element.139), kind=kOutput, calls=%fused_computation.28 | convolution fusion | flops 4834197504 | bytes 12582912 | tf_op jit(solution)/shard_map/sle,slf->ef/dot_general | solution.py:342
  487.6 2.3 fusion.79
  489.9 4.2 collective-permute-start.3
  495.9 35.3 %reduce-scatter.14.cloned.1.call-done = bf16[1,2,2,128,768]{4,3,2,1,0:T(8,128)(2,1)} async-done(((bf16[4,2,2,128,768]{4,3,2,1,0:T(8,128)(2,1)}), bf16[1,2,2,128,768]{4,3,2,1,0:T(8,128)(2,1)}) %reduce-scatter.14.cloned.1.call-update) | async-done | bytes 786448 | tf_op jit(solution)/shard_map/reduce_scatter | solution.py:361
  531.2 3.7 fusion.68
  535.5 3.0 pad_maximum_fusion
  538.6 9.1 copy.97
  548.4 8.2 slice.246
  559.1 4.4 fusion.7
  563.4 7.2 collective-permute-done.2
  575.1 5.5 bitcast_convert_fusion.2
  580.6 6.0 copy.117
  590.3 3.2 convert_reduce_fusion.1
  594.4 54.0 %reduce-scatter.24.cloned.1.call-done = bf16[96,3072]{1,0:T(8,128)(2,1)} async-done(((bf16[768,3072]{1,0:T(8,128)(2,1)}), bf16[96,3072]{1,0:T(8,128)(2,1)}) %reduce-scatter.24.cloned.1.call-update) | async-done | bytes 589840 | tf_op jit(solution)/shard_map/reduce_scatter | solution.py:253
  648.5 5.2 add_convert_fusion.2
  653.8 2.8 copy.104
  656.5 14.0 %reduce-scatter.30.cloned.1.call-done = bf16[192,96]{1,0:T(8,128)(2,1)} async-done(((bf16[768,96]{1,0:T(8,128)(2,1)}), bf16[192,96]{1,0:T(8,128)(2,1)}) %reduce-scatter.30.cloned.1.call-update) | async-done | bytes 36880
  672.1 48.3 %reduce-scatter.28.cloned.1.call-done = bf16[96,2304]{1,0:T(8,128)(2,1)} async-done(((bf16[768,2304]{1,0:T(8,128)(2,1)}), bf16[96,2304]{1,0:T(8,128)(2,1)}) %reduce-scatter.28.cloned.1.call-update) | async-done | bytes 442384
  720.4 2.1 copy.118
  722.5 9.4 %fusion.37 = f32[512,2,768]{2,0,1:T(8,128)S(1)} fusion(f32[2,512,768]{2,1,0:T(8,128)} %get-tuple-element.181, f32[2,512,768]{2,1,0:T(8,128)} %get-tuple-element.180, bf16[768,3,768]{2,0,1:T(8,128)(2,1)} %all-gather.9.cloned.1.call-done, f32[2,512,768]{2,1,0:T(8,128)} %get-tuple-element.178, f32[512,2]{0,1:T(2,128)S(1)} %copy-done.74, ...), kind=kOutput, calls=%fused_computation.70 | convolution fusion | flops 3645112320 | bytes 24034304 | tf_op jit(solution)/shard_map/cslf,dcf->sld/dot_general | solution.py:394
  731.9 4.1 copy.105
  736.0 112.6 %all-reduce.9.cloned.1.call-done = (f32[3,768]{1,0:T(4,128)}, f32[2,5,768]{2,0,1:T(2,128)}, f32[2,768]{1,0:T(2,128)}, f32[3072]{0:T(1024)}, f32[2,768]{1,0:T(2,128)}, /*index=5*/f32[2,768]{1,0:T(2,128)}) async-done(((f32[3,768]{1,0:T(4,128)}, f32[2,5,768]{2,0,1:T(2,128)}, f32[2,768]{1,0:T(2,128)}, f32[3072]{0:T(1024)}, f32[2,768]{1,0:T(2,128)}, /*index=5*/f32[2,768]{1,0:T(2,128)}), (f32[3,768]{1,0:T(4,128)}, ...) | async-done | bytes 70672 | tf_op jit(solution)/shard_map/psum | solution.py:408
  852.7 23.2 %reduce-scatter.22.cloned.1.call-done = bf16[96,768]{1,0:T(8,128)(2,1)} async-done(((bf16[96,3072]{1,0:T(8,128)(2,1)}), bf16[96,768]{1,0:T(8,128)(2,1)}) %reduce-scatter.22.cloned.1.call-update) | async-done | bytes 147472 | tf_op jit(solution)/shard_map/reduce_scatter | solution.py:254
  877.6 20.8 %reduce-scatter.26.cloned.1.call-done = bf16[96,768]{1,0:T(8,128)(2,1)} async-done(((bf16[96,3072]{1,0:T(8,128)(2,1)}), bf16[96,768]{1,0:T(8,128)(2,1)}) %reduce-scatter.26.cloned.1.call-update) | async-done | bytes 147472 | tf_op jit(solution)/shard_map/reduce_scatter | solution.py:254
  900.0 20.8 %reduce-scatter.16.cloned.1.call-done = bf16[96,3,192]{0,2,1:T(8,128)(2,1)} async-done(((bf16[96,3,768]{0,2,1:T(8,128)(2,1)}), bf16[96,3,192]{0,2,1:T(8,128)(2,1)}) %reduce-scatter.16.cloned.1.call-update) | async-done | bytes 110608 | tf_op jit(solution)/shard_map/reduce_scatter | solution.py:254
  920.8 1.8 copy.106
  (270 shorter events, 54.9 us)
Async XLA Ops:
  7.2 60.0 %all-gather.9.cloned.1.call-start = ((), (), s32[]{:S(2)}) async-start(), calls=%async_computation.9 | async-start | bytes 3981312 | tf_op jit(solution)/shard_map/all_gather | solution.py:249
  30.8 197.6 %all-gather.17.cloned.1.call-start = ((), (), s32[]{:S(2)}) async-start(), calls=%async_computation.20 | async-start | bytes 3932160 | tf_op jit(solution)/shard_map/all_gather | solution.py:315
  67.2 10.7 %copy-start.34 = (s32[2048,2]{0,1:T(2,128)S(1)}, s32[2048,2]{0,1:T(2,128)}, u32[]{:S(2)}) copy-start(s32[2048,2]{0,1:T(2,128)} %param.20) | copy-start | bytes 49156
  75.4 7.7 copy-start.28
  76.3 30.4 %collective-permute-start = (bf16[2,2,64,768]{3,2,1,0:T(8,128)(2,1)}, bf16[2,2,64,768]{3,2,1,0:T(8,128)(2,1)S(1)}, u32[]{:S(2)}, u32[]{:S(2)}) collective-permute-start(bf16[2,2,64,768]{3,2,1,0:T(8,128)(2,1)} %get-tuple-element.146), channel_id=1, source_target_pairs={{0,1},{1,2},{2,3},{4,5},{5,6},{6,7},{8,9},{9,10},{10,11},{12,13},{... | collective-permute-start | bytes 1179656 | tf_op jit(solution)/shard_map/ppermute | solution.py:261
  109.1 19.0 %copy-start.18 = (bf16[2,2,128,768]{3,2,1,0:T(8,128)(2,1)S(1)}, bf16[2,2,128,768]{3,2,1,0:T(8,128)(2,1)}, u32[]{:S(2)}) copy-start(bf16[2,2,128,768]{3,2,1,0:T(8,128)(2,1)} %slice.212) | copy-start | bytes 2359300
  109.1 19.0 %copy-start.20 = (bf16[2,2,128,768]{3,2,1,0:T(8,128)(2,1)S(1)}, bf16[2,2,128,768]{3,2,1,0:T(8,128)(2,1)}, u32[]{:S(2)}) copy-start(bf16[2,2,128,768]{3,2,1,0:T(8,128)(2,1)} %slice.215) | copy-start | bytes 2359300
  109.1 19.0 %copy-start.22 = (bf16[2,2,128,768]{3,2,1,0:T(8,128)(2,1)S(1)}, bf16[2,2,128,768]{3,2,1,0:T(8,128)(2,1)}, u32[]{:S(2)}) copy-start(bf16[2,2,128,768]{3,2,1,0:T(8,128)(2,1)} %slice.218) | copy-start | bytes 2359300
  118.0 13.3 %copy-start.24 = (bf16[2,2,128,768]{3,2,1,0:T(8,128)(2,1)}, bf16[2,2,128,768]{3,2,1,0:T(8,128)(2,1)S(1)}, u32[]{:S(2)}) copy-start(bf16[2,2,128,768]{3,2,1,0:T(8,128)(2,1)S(1)} %slice.203) | copy-start | bytes 2359300
  131.2 63.5 %copy-start.33 = (bf16[2,2,64,768]{3,2,1,0:T(8,128)(2,1)S(1)}, bf16[2,2,64,768]{3,2,1,0:T(8,128)(2,1)}, u32[]{:S(2)}) copy-start(bf16[2,2,64,768]{3,2,1,0:T(8,128)(2,1)} %get-tuple-element.145) | copy-start | bytes 1179652
  131.3 65.4 %copy-start.75 = (f32[768]{0:T(1024)S(1)}, f32[768]{0:T(1024)}, u32[]{:S(2)}) copy-start(f32[768]{0:T(1024)} %param.27) | copy-start | bytes 9220
  131.3 96.4 %copy-start.68 = (f32[2,768]{1,0:T(2,128)S(1)}, f32[2,768]{1,0:T(2,128)}, u32[]{:S(2)}) copy-start(f32[2,768]{1,0:T(2,128)} %param.25) | copy-start | bytes 18436
  131.3 96.4 %copy-start.69 = (f32[2,768]{1,0:T(2,128)S(1)}, f32[2,768]{1,0:T(2,128)}, u32[]{:S(2)}) copy-start(f32[2,768]{1,0:T(2,128)} %param.30) | copy-start | bytes 18436
  131.3 96.4 %copy-start.70 = (f32[2,768]{1,0:T(2,128)S(1)}, f32[2,768]{1,0:T(2,128)}, u32[]{:S(2)}) copy-start(f32[2,768]{1,0:T(2,128)} %param.29) | copy-start | bytes 18436
  131.3 145.5 %all-gather.11.cloned.1.call-start = ((), (), s32[]{:S(2)}) async-start(), calls=%async_computation.10 | async-start | bytes 1327104 | tf_op jit(solution)/shard_map/all_gather | solution.py:249
  147.8 141.1 %all-gather.13.cloned.1.call-start = ((), (), s32[]{:S(2)}) async-start(), calls=%async_computation.11 | async-start | bytes 5308416 | tf_op jit(solution)/shard_map/all_gather | solution.py:249
  171.4 165.1 %all-gather.15.cloned.1.call-start = ((), (), s32[]{:S(2)}) async-start(), calls=%async_computation.12 | async-start | bytes 5308416 | tf_op jit(solution)/shard_map/all_gather | solution.py:249
  194.7 299.4 %reduce-scatter.18.cloned.1.call-start = ((), (), s32[]{:S(2)}) async-start(), calls=%async_computation.15 | async-start | bytes 1327104 | tf_op jit(solution)/shard_map/reduce_scatter | solution.py:253
  194.7 33.6 %collective-permute-start.1 = (bf16[2,2,64,768]{3,2,1,0:T(8,128)(2,1)S(1)}, bf16[2,2,64,768]{3,2,1,0:T(8,128)(2,1)S(1)}, u32[]{:S(2)}, u32[]{:S(2)}) collective-permute-start(bf16[2,2,64,768]{3,2,1,0:T(8,128)(2,1)S(1)} %copy-done.33), channel_id=1, source_target_pairs={{1,0},{2,1},{3,2},{5,4},{6,5},{7,6},{9,8},{10,9},{11,10},{13,12},{... | collective-permute-start | bytes 1179656 | tf_op jit(solution)/shard_map/ppermute | solution.py:266
  196.6 80.2 %copy-start.4 = (s32[2,512,1]{2,1,0:T(8,128)}, s32[2,512,1]{2,1,0:T(8,128)S(1)}, u32[]{:S(2)}) copy-start(s32[2,512,1]{2,1,0:T(8,128)S(1)} %copy.92.segq_ref) | copy-start | bytes 12292
  227.7 76.9 %copy-start.38 = (f32[4,1,768]{2,1,0:T(1,128)}, f32[4,1,768]{2,1,0:T(1,128)S(1)}, u32[]{:S(2)}) copy-start(f32[4,1,768]{2,1,0:T(1,128)S(1)} %all-gather.2) | copy-start | bytes 36868
  227.7 49.2 %copy-start.35 = (f32[768]{0:T(1024)}, f32[768]{0:T(1024)S(1)}, u32[]{:S(2)}) copy-start(f32[768]{0:T(1024)S(1)} %get-tuple-element.121) | copy-start | bytes 9220
  227.7 108.9 %copy-start.52 = (f32[768]{0:T(1024)}, f32[768]{0:T(1024)S(1)}, u32[]{:S(2)}) copy-start(f32[768]{0:T(1024)S(1)} %get-tuple-element.120) | copy-start | bytes 9220
  228.3 108.2 %copy-start.41 = (f32[768]{0:T(1024)}, f32[768]{0:T(1024)S(1)}, u32[]{:S(2)}) copy-start(f32[768]{0:T(1024)S(1)} %get-tuple-element.184) | copy-start | bytes 9220
  228.3 108.3 %copy-start.54 = (f32[768]{0:T(1024)}, f32[768]{0:T(1024)S(1)}, u32[]{:S(2)}) copy-start(f32[768]{0:T(1024)S(1)} %get-tuple-element.125) | copy-start | bytes 9220
  228.4 48.5 %copy-start.8 = (bf16[2,2,64,768]{3,2,1,0:T(8,128)(2,1)}, bf16[2,2,64,768]{3,2,1,0:T(8,128)(2,1)S(1)}, u32[]{:S(2)}) copy-start(bf16[2,2,64,768]{3,2,1,0:T(8,128)(2,1)S(1)} %collective-permute-done.1.kr_ref.vr_ref) | copy-start | bytes 1179652
  282.4 54.2 %copy-start.44 = (f32[2,512]{1,0:T(2,128)}, f32[2,512]{1,0:T(2,128)S(1)}, u32[]{:S(2)}) copy-start(f32[2,512]{1,0:T(2,128)S(1)} %get-tuple-element.168) | copy-start | bytes 12292
  284.5 52.1 %copy-start.62 = (f32[2,512]{1,0:T(2,128)}, f32[2,512]{1,0:T(2,128)S(1)}, u32[]{:S(2)}) copy-start(f32[2,512]{1,0:T(2,128)S(1)} %get-tuple-element.170) | copy-start | bytes 12292
  354.6 18.1 %copy-start.29 = (bf16[2,512,768]{2,1,0:T(8,128)(2,1)}, bf16[2,512,768]{2,1,0:T(8,128)(2,1)S(1)}, u32[]{:S(2)}) copy-start(bf16[2,512,768]{2,1,0:T(8,128)(2,1)S(1)} %get-tuple-element.135) | copy-start | bytes 4718596
  354.6 18.1 %copy-start.13 = (f32[2,512,768]{2,1,0:T(8,128)S(1)}, f32[2,512,768]{2,1,0:T(8,128)}, u32[]{:S(2)}) copy-start(f32[2,512,768]{2,1,0:T(8,128)} %copy-done.12) | copy-start | bytes 9437188
  354.6 18.1 %copy-start.42 = (f32[768]{0:T(1024)S(1)}, f32[768]{0:T(1024)}, u32[]{:S(2)}) copy-start(f32[768]{0:T(1024)} %copy-done.41) | copy-start | bytes 9220
  354.6 18.1 %copy-start.45 = (f32[2,512]{1,0:T(2,128)S(1)}, f32[2,512]{1,0:T(2,128)}, u32[]{:S(2)}) copy-start(f32[2,512]{1,0:T(2,128)} %copy-done.44) | copy-start | bytes 12292
  354.6 18.1 %copy-start.63 = (f32[2,512]{1,0:T(2,128)S(1)}, f32[2,512]{1,0:T(2,128)}, u32[]{:S(2)}) copy-start(f32[2,512]{1,0:T(2,128)} %copy-done.62) | copy-start | bytes 12292
  391.2 140.0 %reduce-scatter.14.cloned.1.call-start = ((), (), s32[]{:S(2)}) async-start(), calls=%async_computation.13 | async-start | bytes 3932160 | tf_op jit(solution)/shard_map/reduce_scatter | solution.py:361
  464.6 129.1 %reduce-scatter.20.cloned.1.call-start = ((), (), s32[]{:S(2)}) async-start(), calls=%async_computation.16 | async-start | bytes 5308416 | tf_op jit(solution)/shard_map/reduce_scatter | solution.py:253
  476.3 172.1 %reduce-scatter.24.cloned.1.call-start = ((), (), s32[]{:S(2)}) async-start(), calls=%async_computation.18 | async-start | bytes 5308416 | tf_op jit(solution)/shard_map/reduce_scatter | solution.py:253
  487.5 183.0 %reduce-scatter.30.cloned.1.call-start = ((), (), s32[]{:S(2)}) async-start(), calls=%async_computation.22 | async-start | bytes 245760
  487.5 43.6 %copy-start.19 = (bf16[2,2,128,768]{3,2,1,0:T(8,128)(2,1)S(1)}, bf16[2,2,128,768]{3,2,1,0:T(8,128)(2,1)}, u32[]{:S(2)}) copy-start(bf16[2,2,128,768]{3,2,1,0:T(8,128)(2,1)} %slice.212) | copy-start | bytes 2359300
  487.5 43.6 %copy-start.21 = (bf16[2,2,128,768]{3,2,1,0:T(8,128)(2,1)S(1)}, bf16[2,2,128,768]{3,2,1,0:T(8,128)(2,1)}, u32[]{:S(2)}) copy-start(bf16[2,2,128,768]{3,2,1,0:T(8,128)(2,1)} %slice.215) | copy-start | bytes 2359300
  487.6 43.6 %copy-start.23 = (bf16[2,2,128,768]{3,2,1,0:T(8,128)(2,1)S(1)}, bf16[2,2,128,768]{3,2,1,0:T(8,128)(2,1)}, u32[]{:S(2)}) copy-start(bf16[2,2,128,768]{3,2,1,0:T(8,128)(2,1)} %slice.218) | copy-start | bytes 2359300
  487.6 43.6 %copy-start.25 = (bf16[2,2,128,768]{3,2,1,0:T(8,128)(2,1)S(1)}, bf16[2,2,128,768]{3,2,1,0:T(8,128)(2,1)}, u32[]{:S(2)}) copy-start(bf16[2,2,128,768]{3,2,1,0:T(8,128)(2,1)} %copy-done.24) | copy-start | bytes 2359300
  487.6 43.6 %copy-start.37 = (f32[2,1,768]{2,0,1:T(2,128)S(1)}, f32[2,1,768]{2,0,1:T(2,128)}, u32[]{:S(2)}) copy-start(f32[2,1,768]{2,0,1:T(2,128)} %copy.88) | copy-start | bytes 18436
  489.9 80.9 %collective-permute-start.3 = (bf16[2,2,64,768]{3,2,1,0:T(8,128)(2,1)S(1)}, bf16[2,2,64,768]{3,2,1,0:T(8,128)(2,1)}, u32[]{:S(2)}, u32[]{:S(2)}) collective-permute-start(bf16[2,2,64,768]{3,2,1,0:T(8,128)(2,1)S(1)} %get-tuple-element.143), channel_id=1, source_target_pairs={{0,1},{1,2},{2,3},{4,5},{5,6},{6,7},{8,9},{9,10},{10,11},{12,13},{... | collective-permute-start | bytes 1179656 | tf_op jit(solution)/shard_map/ppermute | solution.py:261
  495.8 224.5 %reduce-scatter.28.cloned.1.call-start = ((), (), s32[]{:S(2)}) async-start(), calls=%async_computation.21 | async-start | bytes 3981312
  548.4 8.2 copy-start.10
  548.4 8.2 copy-start.32
  557.6 13.1 %collective-permute-start.2 = (bf16[2,2,64,768]{3,2,1,0:T(8,128)(2,1)S(1)}, bf16[2,2,64,768]{3,2,1,0:T(8,128)(2,1)S(1)}, u32[]{:S(2)}, u32[]{:S(2)}) collective-permute-start(bf16[2,2,64,768]{3,2,1,0:T(8,128)(2,1)S(1)} %fusion.86), channel_id=1, source_target_pairs={{1,0},{2,1},{3,2},{5,4},{6,5},{7,6},{9,8},{10,9},{11,10},{13,12},{... | collective-permute-start | bytes 1179656 | tf_op jit(solution)/shard_map/ppermute | solution.py:266
  572.4 8.2 copy-start.17
  586.8 261.8 %all-reduce.9.cloned.1.call-start = ((), (), s32[]{:S(2)}) async-start(), calls=%async_computation.23 | async-start | bytes 147456 | tf_op jit(solution)/shard_map/psum | solution.py:408
  588.2 60.2 %copy-start.36 = (f32[768]{0:T(1024)S(1)}, f32[768]{0:T(1024)}, u32[]{:S(2)}) copy-start(f32[768]{0:T(1024)} %copy-done.35) | copy-start | bytes 9220
  588.2 60.2 %copy-start.53 = (f32[768]{0:T(1024)S(1)}, f32[768]{0:T(1024)}, u32[]{:S(2)}) copy-start(f32[768]{0:T(1024)} %copy-done.52) | copy-start | bytes 9220
  588.3 60.2 %copy-start.56 = (f32[768]{0:T(1024)S(1)}, f32[768]{0:T(1024)}, u32[]{:S(2)}) copy-start(f32[768]{0:T(1024)} %copy-done.54) | copy-start | bytes 9220
  588.3 60.2 %copy-start.57 = (f32[512,2]{0,1:T(2,128)S(1)}, f32[512,2]{0,1:T(2,128)}, u32[]{:S(2)}) copy-start(f32[512,2]{0,1:T(2,128)} %get-tuple-element.167) | copy-start | bytes 12292
  588.3 60.2 %copy-start.58 = (f32[512,2]{0,1:T(2,128)S(1)}, f32[512,2]{0,1:T(2,128)}, u32[]{:S(2)}) copy-start(f32[512,2]{0,1:T(2,128)} %get-tuple-element.169) | copy-start | bytes 12292
  588.3 60.2 %copy-start.59 = (f32[768]{0:T(1024)S(1)}, f32[768]{0:T(1024)}, u32[]{:S(2)}) copy-start(f32[768]{0:T(1024)} %get-tuple-element.124) | copy-start | bytes 9220
  588.3 60.2 %copy-start.60 = (f32[512,2]{0,1:T(2,128)S(1)}, f32[512,2]{0,1:T(2,128)}, u32[]{:S(2)}) copy-start(f32[512,2]{0,1:T(2,128)} %get-tuple-element.171) | copy-start | bytes 12292
  588.3 60.2 %copy-start.61 = (f32[512,2]{0,1:T(2,128)S(1)}, f32[512,2]{0,1:T(2,128)}, u32[]{:S(2)}) copy-start(f32[512,2]{0,1:T(2,128)} %get-tuple-element.166) | copy-start | bytes 12292
  593.6 282.3 %reduce-scatter.22.cloned.1.call-start = ((), (), s32[]{:S(2)}) async-start(), calls=%async_computation.17 | async-start | bytes 737280 | tf_op jit(solution)/shard_map/reduce_scatter | solution.py:254
  594.4 304.0 %reduce-scatter.26.cloned.1.call-start = ((), (), s32[]{:S(2)}) async-start(), calls=%async_computation.19 | async-start | bytes 737280 | tf_op jit(solution)/shard_map/reduce_scatter | solution.py:254
  648.4 272.4 %reduce-scatter.16.cloned.1.call-start = ((), (), s32[]{:S(2)}) async-start(), calls=%async_computation.14 | async-start | bytes 737280 | tf_op jit(solution)/shard_map/reduce_scatter | solution.py:254
  653.7 68.7 %copy-start.71 = (f32[512,2]{0,1:T(2,128)S(1)}, f32[512,2]{0,1:T(2,128)}, u32[]{:S(2)}) copy-start(f32[512,2]{0,1:T(2,128)} %get-tuple-element.161) | copy-start | bytes 12292
  653.7 68.7 %copy-start.72 = (f32[512,2]{0,1:T(2,128)S(1)}, f32[512,2]{0,1:T(2,128)}, u32[]{:S(2)}) copy-start(f32[512,2]{0,1:T(2,128)} %get-tuple-element.163) | copy-start | bytes 12292
  653.8 68.7 %copy-start.73 = (f32[512,2]{0,1:T(2,128)S(1)}, f32[512,2]{0,1:T(2,128)}, u32[]{:S(2)}) copy-start(f32[512,2]{0,1:T(2,128)} %get-tuple-element.158) | copy-start | bytes 12292
  653.8 68.7 %copy-start.74 = (f32[512,2]{0,1:T(2,128)S(1)}, f32[512,2]{0,1:T(2,128)}, u32[]{:S(2)}) copy-start(f32[512,2]{0,1:T(2,128)} %get-tuple-element.160) | copy-start | bytes 12292
  (33 other events, 78.7 us)
Sparse Core Ops, SparseCore 0:
  30.9 33.3 all-gather.8
  131.4 90.7 all-gather.16
  224.7 23.3 all-gather.10
  249.9 38.9 all-gather.12
  290.6 38.9 all-gather.14
  391.3 36.7 reduce-scatter.17
  464.7 66.4 reduce-scatter.13
  535.0 55.9 reduce-scatter.19
  594.4 53.8 reduce-scatter.23
  651.1 19.3 reduce-scatter.29
  674.0 46.2 reduce-scatter.27
  727.8 120.7 all-reduce.8
  850.9 25.0 reduce-scatter.21
  878.1 20.2 reduce-scatter.25
  900.5 20.2 reduce-scatter.15

commit v2 on v1

v2 whole, which is shorter than its diff:
```python
from functools import partial

import jax
import jax.numpy as jnp
import numpy as np
from jax import lax
from jax.experimental import pallas as pl
from jax.experimental.pallas import tpu as pltpu
from jax.sharding import PartitionSpec as P

HEAD_DIM = 64
HALF = 64
STRIDE = 4
TAPS = 5
MARGIN = TAPS // 2
PAIR = 2 * HEAD_DIM
QB = 128
NEAR = QB + 2 * HALF
FB = 512
RC = 256
EPSILON = 1e-05
NEG = -1e30
SCALE = HEAD_DIM**-0.5
BF = jnp.bfloat16
F32 = jnp.float32
MIB = 2**20


def nt(a, b):
    return lax.dot_general(a, b, (((1,), (1,)), ((), ())), preferred_element_type=F32)


def nn(a, b):
    return lax.dot_general(a, b, (((1,), (0,)), ((), ())), preferred_element_type=F32)


def tn(a, b):
    return lax.dot_general(a, b, (((0,), (0,)), ((), ())), preferred_element_type=F32)


def params(mib):
    return pltpu.CompilerParams(vmem_limit_bytes=mib * MIB)


def cost(flops, mib, trans=0):
    return pl.CostEstimate(flops=flops, bytes_accessed=mib * MIB, transcendentals=trans)


def once(shape):
    zeros = (0,) * len(shape)
    return pl.BlockSpec(shape, lambda *_: zeros, pipeline_mode=pl.Buffered(1))


def project_kernel(count, offs, *refs):
    pieces = refs[:count]
    x_ref, bias_ref, taps_ref, same_ref, out_ref, pooled_ref, w_ref, plain = refs[count:]
    part = pl.program_id(0)
    for n in range(count):
        rows = pieces[n].shape[0]
        w_ref[0, pl.ds(pl.multiple_of(offs[n], 16), rows), :] = pieces[n][...]
    seqs, wide, _ = x_ref.shape
    far_rows = pooled_ref.shape[2]
    for s in range(seqs):
        made = (nn(x_ref[s], w_ref[0]) + bias_ref[0]).astype(BF)
        out_ref[0, s] = made
        for half in range(plain.shape[1]):
            plain[s, half] = made[:, half * PAIR : (half + 1) * PAIR].astype(F32)

    @pl.when(part > 0)
    def _():
        for s in range(seqs):
            for half in range(plain.shape[1]):
                lanes = slice(half * PAIR, (half + 1) * PAIR)
                total = jnp.zeros((far_rows, PAIR), F32)
                for r in range(TAPS):
                    rows = plain[s, half, pl.ds(HALF - MARGIN + r, far_rows, stride=STRIDE), :]
                    total = total + taps_ref[0, r : r + 1, lanes] * rows * same_ref[
                        s, :, r : r + 1
                    ]
                pooled_ref[0, s, :, lanes] = total.astype(BF)


def project(chunk, chunks, pieces, offs, x_wide, bias, taps, same, far_rows):
    seqs, wide, width = x_wide.shape
    span = width // chunks

    def piece_spec(piece):
        return pl.BlockSpec((piece.shape[0], span), lambda c, o: (0, c * chunks + chunk))

    def kv(c):
        return jnp.maximum(c - 1, 0)

    return pl.pallas_call(
        partial(project_kernel, len(pieces)),
        grid_spec=pltpu.PrefetchScalarGridSpec(
            num_scalar_prefetch=1,
            grid=(3,),
            in_specs=[piece_spec(p) for p in pieces]
            + [
                once(x_wide.shape),
                pl.BlockSpec((1, 1, span), lambda c, o: (c, 0, chunk)),
                pl.BlockSpec((1, 8, span), lambda c, o: (kv(c), 0, chunk)),
                once(same.shape),
            ],
            out_specs=[
                pl.BlockSpec((1, seqs, wide, span), lambda c, o: (c, 0, 0, 0)),
                pl.BlockSpec((1, seqs, far_rows, span), lambda c, o: (kv(c), 0, 0, 0)),
                pl.BlockSpec((1, width, span), lambda c, o: (c, 0, 0)),
            ],
            scratch_shapes=[pltpu.VMEM((seqs, span // PAIR, wide, PAIR), F32)],
        ),
        out_shape=[
            jax.ShapeDtypeStruct((3, seqs, wide, span), BF),
            jax.ShapeDtypeStruct((2, seqs, far_rows, span), BF),
            jax.ShapeDtypeStruct((3, width, span), BF),
        ],
        compiler_params=params(32),
        cost_estimate=cost(6 * seqs * wide * width * span, 8),
    )(offs, *pieces, x_wide, bias, taps, same)


def fill_masks(segq_ref, segk_ref, cen_ref, near_bias, far_bias):
    rows = segq_ref.shape[1]
    shape = (QB, NEAR)
    gap = lax.broadcasted_iota(jnp.int32, shape, 1) - lax.broadcasted_iota(jnp.int32, shape, 0)
    band = (gap >= 0) & (gap <= 2 * HALF)
    for first in range(0, rows, QB):
        own = segq_ref[0, first : first + QB, :]
        keys = segk_ref[0, :, first : first + NEAR]
        near_bias[first : first + QB, :] = jnp.where(band & (own == keys), 0.0, NEG)
        far_bias[first : first + QB, :] = jnp.where(own == cen_ref[0], 0.0, NEG)


def head_mask(head):
    lane = lax.broadcasted_iota(jnp.int32, (1, PAIR), 1)
    return lane < HEAD_DIM if head == 0 else lane >= HEAD_DIM


def softmax_block(query, keys_near, keys_far, bias_near, bias_far):
    near = nt(query, keys_near) + bias_near
    far = nt(query, keys_far) + bias_far
    top = jnp.maximum(
        jnp.max(near, axis=-1, keepdims=True), jnp.max(far, axis=-1, keepdims=True)
    )
    near = jnp.exp(near - top)
    far = jnp.exp(far - top)
    total = jnp.sum(near, axis=-1, keepdims=True) + jnp.sum(far, axis=-1, keepdims=True)
    inverse = 1.0 / total
    return near * inverse, far * inverse


def join_slots(slots, joined):
    rows = slots[0].shape[1]
    for n, slot in enumerate(slots):
        joined[n * rows : (n + 1) * rows, :] = slot[0]


def attend_forward_kernel(blocks, q_ref, k_ref, v_ref, *refs):
    pk, pv = refs[:blocks], refs[blocks : 2 * blocks]
    segq, segk, cen, out_ref, near_bias, far_bias, far_keys, far_values = refs[2 * blocks :]

    @pl.when(pl.program_id(1) == 0)
    def _():
        fill_masks(segq, segk, cen, near_bias, far_bias)

    join_slots(pk, far_keys)
    join_slots(pv, far_values)
    for first in range(0, out_ref.shape[1], QB):
        block = slice(first, first + QB)
        span = slice(first, first + NEAR)
        query = q_ref[0, HALF + first : HALF + first + QB, :] * BF(SCALE)
        halves = []
        for head in range(2):
            picked = jnp.where(head_mask(head), query, BF(0))
            near, far = softmax_block(
                picked, k_ref[0, span, :], far_keys[...], near_bias[block, :], far_bias[block, :]
            )
            halves.append(
                nn(near.astype(BF), v_ref[0, span, :]) + nn(far.astype(BF), far_values[...])
            )
        out_ref[0, block, :] = jnp.where(head_mask(0), halves[0], halves[1]).astype(BF)


def attend_backward_kernel(blocks, q_ref, k_ref, v_ref, *refs):
    pk, pv = refs[:blocks], refs[blocks : 2 * blocks]
    segq, segk, cen, grad_ref, dq_ref, dk_ref, dv_ref = refs[2 * blocks : 2 * blocks + 7]
    dp_refs = refs[2 * blocks + 7 : 3 * blocks + 7]
    near_bias, far_bias, far_keys, far_values, far_probs, far_grads = refs[3 * blocks + 7 :]

    @pl.when(pl.program_id(1) == 0)
    def _():
        fill_masks(segq, segk, cen, near_bias, far_bias)

    rows = dq_ref.shape[1]
    join_slots(pk, far_keys)
    join_slots(pv, far_values)
    dk_ref[...] = jnp.zeros_like(dk_ref)
    dv_ref[...] = jnp.zeros_like(dv_ref)
    pieces = []
    for head in range(2):
        mask = head_mask(head)
        for first in range(0, rows, QB):
            block = slice(first, first + QB)
            span = slice(first, first + NEAR)
            query = jnp.where(
                mask, q_ref[0, HALF + first : HALF + first + QB, :] * BF(SCALE), BF(0)
            )
            grad = jnp.where(mask, grad_ref[0, block, :], BF(0))
            near, far = softmax_block(
                query, k_ref[0, span, :], far_keys[...], near_bias[block, :], far_bias[block, :]
            )
            grad_near = nt(grad, v_ref[0, span, :])
            grad_far = nt(grad, far_values[...])
            row_dot = jnp.sum(near * grad_near, axis=-1, keepdims=True) + jnp.sum(
                far * grad_far, axis=-1, keepdims=True
            )
            ds_near = (near * (grad_near - row_dot)).astype(BF)
            ds_far = (far * (grad_far - row_dot)).astype(BF)
            far_probs[block, :] = far.astype(BF)
            far_grads[block, :] = ds_far
            dq = (nn(ds_near, k_ref[0, span, :]) + nn(ds_far, far_keys[...])) * SCALE
            if head == 0:
                dq_ref[0, block, :] = dq.astype(BF)
            else:
                dq_ref[0, block, :] = jnp.where(mask, dq.astype(BF), dq_ref[0, block, :])
            dk_ref[0, span, :] += tn(ds_near, query)
            dv_ref[0, span, :] += tn(near.astype(BF), grad)
        query = jnp.where(mask, q_ref[0, HALF : HALF + rows, :] * BF(SCALE), BF(0))
        grad = jnp.where(mask, grad_ref[0], BF(0))
        pieces.append((tn(far_grads[...], query), tn(far_probs[...], grad)))
    far_rows = dp_refs[0].shape[2]
    for n, ref in enumerate(dp_refs):
        span = slice(n * far_rows, (n + 1) * far_rows)
        for c in range(2):
            ref[c, 0] = jnp.where(head_mask(0), pieces[0][c][span], pieces[1][c][span]).astype(BF)


def attention_specs(wide, blocks, far_rows):
    def own(part):
        return pl.BlockSpec((None, 1, wide, PAIR), lambda s, h: (part, s, 0, h))

    def pooled(part):
        return pl.BlockSpec((None, 1, far_rows, PAIR), lambda s, h: (part, s, 0, h))

    rows = wide - 2 * HALF
    return (
        [own(0), own(1), own(2)]
        + [pooled(0)] * blocks
        + [pooled(1)] * blocks
        + [
            pl.BlockSpec((1, rows, 1), lambda s, h: (s, 0, 0)),
            pl.BlockSpec((1, 1, wide), lambda s, h: (s, 0, 0)),
            pl.BlockSpec((1, 1, blocks * far_rows), lambda s, h: (s, 0, 0)),
        ]
    )


def attention_scratch(rows, far_all):
    return [
        pltpu.VMEM((rows, NEAR), F32),
        pltpu.VMEM((rows, far_all), F32),
        pltpu.VMEM((far_all, PAIR), BF),
        pltpu.VMEM((far_all, PAIR), BF),
    ]


def attend_forward(proj, slots, segs):
    _, seqs, wide, span = proj.shape
    blocks, far_rows = len(slots), slots[0].shape[2]
    rows = wide - 2 * HALF
    cells = seqs * rows * (NEAR + blocks * far_rows) * (span // HEAD_DIM)
    return pl.pallas_call(
        partial(attend_forward_kernel, blocks),
        grid=(seqs, span // PAIR),
        in_specs=attention_specs(wide, blocks, far_rows),
        out_specs=pl.BlockSpec((1, rows, PAIR), lambda s, h: (s, 0, h)),
        out_shape=jax.ShapeDtypeStruct((seqs, rows, span), BF),
        scratch_shapes=attention_scratch(rows, blocks * far_rows),
        compiler_params=params(32),
        cost_estimate=cost(16 * 64 * cells, 8, cells),
    )(proj, proj, proj, *slots, *slots, *segs)


def attend_backward(proj, slots, segs, grad):
    _, seqs, wide, span = proj.shape
    blocks, far_rows = len(slots), slots[0].shape[2]
    rows = wide - 2 * HALF
    cells = seqs * rows * (NEAR + blocks * far_rows) * (span // HEAD_DIM)
    own_spec = pl.BlockSpec((1, rows, PAIR), lambda s, h: (s, 0, h))
    wide_spec = pl.BlockSpec((1, wide, PAIR), lambda s, h: (s, 0, h))
    wide_shape = jax.ShapeDtypeStruct((seqs, wide, span), F32)
    far_spec = pl.BlockSpec((2, 1, far_rows, PAIR), lambda s, h: (0, s, 0, h))
    far_shape = jax.ShapeDtypeStruct((2, seqs, far_rows, span), BF)
    out = pl.pallas_call(
        partial(attend_backward_kernel, blocks),
        grid=(seqs, span // PAIR),
        in_specs=attention_specs(wide, blocks, far_rows) + [own_spec],
        out_specs=[own_spec, wide_spec, wide_spec] + [far_spec] * blocks,
        out_shape=[jax.ShapeDtypeStruct((seqs, rows, span), BF), wide_shape, wide_shape]
        + [far_shape] * blocks,
        scratch_shapes=attention_scratch(rows, blocks * far_rows)
        + [pltpu.VMEM((rows, blocks * far_rows), BF)] * 2,
        compiler_params=params(40),
        cost_estimate=cost(40 * 64 * cells, 16, cells),
    )(proj, proj, proj, *slots, *slots, *segs, grad)
    return out[0], out[1], out[2], out[3:]


def norm_stats(residual):
    row_mean = jnp.mean(residual, axis=-1, keepdims=True)
    centered = residual - row_mean
    variance = jnp.mean(centered * centered, axis=-1, keepdims=True)
    inverse = lax.rsqrt(variance + EPSILON)
    return centered * inverse, inverse


def norm_back(grad, normed, inverse, gain):
    scaled = grad * gain
    first = jnp.mean(scaled, axis=-1, keepdims=True)
    second = jnp.mean(scaled * normed, axis=-1, keepdims=True)
    return (scaled - first - normed * second) * inverse


def column_sum(values):
    return jnp.sum(values.astype(F32), axis=0, keepdims=True)


def dense_kernel(chunks, steps, *refs):
    att = refs[:chunks]
    x_ref, cot_ref, wout_ref, up_ref, down_ref, bup_ref, misc_ref = refs[chunks : chunks + 7]
    outs = refs[chunks + 7 :]
    out_ref, gres_ref = outs[:2]
    gatt = outs[2 : 2 + chunks]
    gout = outs[2 + chunks : 2 + 2 * chunks]
    gud_ref, gbup_ref, small_ref = outs[2 + 2 * chunks : 5 + 2 * chunks]
    (
        normed, inverse, flow, flow_t, acc, gffn, gffn_t, hidden, slope, gpre
    ) = outs[5 + 2 * chunks :]
    step = pl.program_id(0)
    seqs, rows, width = cot_ref.shape
    total = seqs * rows
    span = width // chunks
    bias_one, bias_two = misc_ref[0:1, :], misc_ref[1:2, :]
    gain_one, gain_two = misc_ref[2:3, :], misc_ref[3:4, :]
    shift_one, shift_two = misc_ref[4:5, :], misc_ref[5:6, :]
    parts = [(first, first // rows, first % rows) for first in range(0, total, RC)]

    @pl.when(step == 0)
    def _():
        for first, s, row in parts:
            block = slice(first, first + RC)
            branch = bias_one
            for j in range(chunks):
                branch = branch + nt(
                    att[j][s, row : row + RC, :], wout_ref[:, j * span : (j + 1) * span]
                )
            n_one, inv = norm_stats(
                x_ref[s, HALF + row : HALF + row + RC, :].astype(F32) + branch
            )
            normed[block, :] = n_one
            inverse[block, :] = inv
            low = (n_one * gain_one + shift_one).astype(BF)
            flow[block, :] = low
            flow_t[:, block] = low.T
            acc[block, :] = jnp.zeros((RC, width), F32)

    @pl.when(step < steps)
    def _():
        for first, s, row in parts:
            block = slice(first, first + RC)
            pre = nn(flow[block, :], up_ref[...]) + bup_ref[...]
            cdf = 0.5 * (1.0 + lax.erf(pre * np.float32(np.sqrt(0.5))))
            pdf = jnp.exp(-0.5 * (pre * pre)) * np.float32(1.0 / np.sqrt(2.0 * np.pi))
            low = (pre * cdf).astype(BF)
            hidden[step, block, :] = low
            slope[step, block, :] = cdf + pre * pdf
            acc[block, :] += nt(low, down_ref[...])

    @pl.when(step == steps)
    def _():
        small_ref[...] = jnp.zeros_like(small_ref)
        for first, s, row in parts:
            block = slice(first, first + RC)
            first_out = normed[block, :] * gain_one + shift_one
            n_two, inv = norm_stats(first_out + (acc[block, :] + bias_two))
            out_ref[s, row : row + RC, :] = (n_two * gain_two + shift_two).astype(BF)
            grad = cot_ref[s, row : row + RC, :].astype(F32)
            second = norm_back(grad, n_two, inv, gain_two)
            acc[block, :] = second
            low = second.astype(BF)
            gffn[block, :] = low
            gffn_t[:, block] = low.T
            small_ref[1:2, :] += column_sum(low)
            small_ref[3:4, :] += column_sum(grad * n_two)
            small_ref[5:6, :] += column_sum(grad)

    @pl.when(step >= steps)
    def _():
        which = 2 * steps - 1 - step
        bias_sum = jnp.zeros((1, FB), F32)
        for first, s, row in parts:
            block = slice(first, first + RC)
            grad = nn(gffn[block, :], down_ref[...])
            low = (grad * slope[which, block, :]).astype(BF)
            gpre[block, :] = low
            bias_sum = bias_sum + column_sum(low)
            acc[block, :] += nt(low, up_ref[...])
        gbup_ref[...] = bias_sum
        lead = (gud_ref.shape[0], gud_ref.shape[2], FB)
        gud_ref[:, 0] = nn(flow_t[...], gpre[...]).astype(BF).reshape(lead)
        gud_ref[:, 1] = nn(gffn_t[...], hidden[which]).astype(BF).reshape(lead)

    @pl.when(step == 2 * steps - 1)
    def _():
        for first, s, row in parts:
            block = slice(first, first + RC)
            grad = acc[block, :]
            n_one = normed[block, :]
            back = norm_back(grad, n_one, inverse[block, :], gain_one)
            gres_ref[s, row : row + RC, :] = back
            low = back.astype(BF)
            flow_t[:, block] = low.T
            small_ref[0:1, :] += column_sum(low)
            small_ref[2:3, :] += column_sum(grad * n_one)
            small_ref[4:5, :] += column_sum(grad)
            for j in range(chunks):
                gatt[j][s, row : row + RC, :] = nn(
                    low, wout_ref[:, j * span : (j + 1) * span]
                ).astype(BF)
        for j in range(chunks):
            gout[j][...] = nn(flow_t[...], att[j][...].reshape(total, span)).astype(BF)


def dense(att, x_wide, cot, weights, bias_up, misc, hidden_units, row_blocks):
    chunks = len(att)
    seqs, rows, width = cot.shape
    total = seqs * rows
    span = width // chunks
    steps = hidden_units // FB

    def which(i):
        return jnp.where(i < steps, i, 2 * steps - 1 - i)

    def back(i):
        return jnp.where(i < steps, steps - 1, 2 * steps - 1 - i)

    lead = width // row_blocks
    out_shape = (
        [
            jax.ShapeDtypeStruct((seqs, rows, width), BF),
            jax.ShapeDtypeStruct((seqs, rows, width), F32),
        ]
        + [jax.ShapeDtypeStruct((seqs, rows, span), BF)] * chunks
        + [jax.ShapeDtypeStruct((width, span), BF)] * chunks
        + [
            jax.ShapeDtypeStruct((row_blocks, 2, lead, hidden_units), BF),
            jax.ShapeDtypeStruct((1, hidden_units), F32),
            jax.ShapeDtypeStruct((8, width), F32),
        ]
    )
    out_specs = [once(o.shape) for o in out_shape[: 2 + 2 * chunks]] + [
        pl.BlockSpec((row_blocks, 2, lead, FB), lambda i: (0, 0, 0, back(i))),
        pl.BlockSpec((1, FB), lambda i: (0, back(i))),
        once((8, width)),
    ]
    out = pl.pallas_call(
        partial(dense_kernel, chunks, steps),
        grid=(2 * steps,),
        in_specs=[once(a.shape) for a in att]
        + [
            once(x_wide.shape),
            once(cot.shape),
            pl.BlockSpec(
                (width, width),
                lambda i: (0, 2 * hidden_units // width),
                pipeline_mode=pl.Buffered(1),
            ),
            pl.BlockSpec((width, FB), lambda i: (0, which(i))),
            pl.BlockSpec((width, FB), lambda i: (0, steps + which(i))),
            pl.BlockSpec((1, FB), lambda i: (0, which(i))),
            once(misc.shape),
        ],
        out_specs=out_specs,
        out_shape=out_shape,
        scratch_shapes=[
            pltpu.VMEM((total, width), F32),
            pltpu.VMEM((total, 1), F32),
            pltpu.VMEM((total, width), BF),
            pltpu.VMEM((width, total), BF),
            pltpu.VMEM((total, width), F32),
            pltpu.VMEM((total, width), BF),
            pltpu.VMEM((width, total), BF),
            pltpu.VMEM((steps, total, FB), BF),
            pltpu.VMEM((steps, total, FB), F32),
            pltpu.VMEM((total, FB), BF),
        ],
        compiler_params=params(60),
        cost_estimate=cost(
            12 * total * width * hidden_units + 6 * total * width * width, 48, total * hidden_units
        ),
    )(*att, x_wide, cot, weights, weights, weights, bias_up, misc)
    return (
        out[0], out[1], out[2 : 2 + chunks], out[2 + chunks : 2 + 2 * chunks],
        out[-3], out[-2], out[-1],
    )


def gather_back_kernel(
    blocks, groups, first_chunk, offs, *refs
):
    dk_ref, dv_ref, dq_ref, proj_k, proj_v = refs[:5]
    dps = refs[5 : 5 + blocks]
    taps_ref, same_ref, xt_ref, w_ref, gout_ref, gx_in = refs[5 + blocks : 11 + blocks]
    outs = refs[11 + blocks :]
    gws = outs[:groups]
    gx_ref, small_ref, plain, spread, low_q, low_k, low_v, stage = outs[groups:]
    seqs, wide, span = dk_ref.shape
    rows = wide - 2 * HALF
    far_rows = dps[0].shape[2]
    small_ref[...] = jnp.zeros_like(small_ref)
    for c, (near, proj, low) in enumerate(((dk_ref, proj_k, low_k), (dv_ref, proj_v, low_v))):
        for s in range(seqs):
            for half in range(span // PAIR):
                lanes = slice(half * PAIR, (half + 1) * PAIR)
                plain[...] = proj[0, s, :, lanes].astype(F32)
                spread[...] = near[s, :, lanes]
                pooled = dps[0][c, s, :, lanes].astype(F32)
                for n in range(1, blocks):
                    pooled = pooled + dps[n][c, s, :, lanes].astype(F32)
                pooled = pooled.astype(BF).astype(F32)
                for r in range(TAPS):
                    place = pl.ds(HALF - MARGIN + r, far_rows, stride=STRIDE)
                    masked = pooled * same_ref[s, :, r : r + 1]
                    row = 8 + 8 * c + r
                    small_ref[row : row + 1, lanes] += column_sum(masked * plain[place, :])
                    spread[place, :] = spread[place, :] + taps_ref[c, r : r + 1, lanes] * masked
                made = spread[...].astype(BF)
                low[s * wide : (s + 1) * wide, lanes] = made
                small_ref[1 + c : 2 + c, lanes] += column_sum(made)
    for s in range(seqs):
        base = s * wide
        low_q[base : base + HALF, :] = jnp.zeros((HALF, span), BF)
        low_q[base + HALF : base + HALF + rows, :] = dq_ref[s]
        low_q[base + HALF + rows : base + wide, :] = jnp.zeros((HALF, span), BF)
        small_ref[0:1, :] += column_sum(dq_ref[s])
        grad = (
            nt(low_q[base : base + wide, :], w_ref[0])
            + nt(low_k[base : base + wide, :], w_ref[1])
            + nt(low_v[base : base + wide, :], w_ref[2])
        )
        gx_ref[s] = grad if first_chunk else gx_in[s] + grad
    heads = span // HEAD_DIM
    lane = lax.broadcasted_iota(jnp.int32, (1, PAIR), 1) < HEAD_DIM
    width = xt_ref.shape[0]
    for u in range(heads // 2):
        lanes = slice(u * PAIR, (u + 1) * PAIR)
        stage_q = nn(xt_ref[...], low_q[:, lanes])
        stage_k = nn(xt_ref[...], low_k[:, lanes])
        stage_v = nn(xt_ref[...], low_v[:, lanes])
        stage_o = gout_ref[:, lanes].astype(F32)
        for odd in range(2):
            t = 2 * u + odd
            if odd == 0:
                one = jnp.where(lane, stage_q, pltpu.roll(stage_k, HEAD_DIM, 1))
                two = jnp.where(lane, stage_v, pltpu.roll(stage_o, HEAD_DIM, 1))
            else:
                one = jnp.where(lane, pltpu.roll(stage_q, HEAD_DIM, 1), stage_k)
                two = jnp.where(lane, pltpu.roll(stage_v, HEAD_DIM, 1), stage_o)
            stage[t, :, :PAIR] = one.astype(BF)
            stage[t, :, PAIR:] = two.astype(BF)
    height = gws[0].shape[2]
    number = 0
    for group in gws:
        for n in range(group.shape[0]):
            place = pl.ds(pl.multiple_of(offs[number], 16), height)
            group[n] = stage[:, place, :]
            number += 1


def gather_back(first_chunk, chunk, offs, group_sizes, near, dps, proj, taps, same, xt, w, gout, gx):
    dq, dk, dv = near
    seqs, wide, span = dk.shape
    width = xt.shape[0]
    blocks, far_rows = len(dps), dps[0].shape[2]
    height = width // sum(group_sizes)
    heads = span // HEAD_DIM
    gx_block = (seqs, 8, width) if first_chunk else (seqs, wide, width)
    out = pl.pallas_call(
        partial(gather_back_kernel, blocks, len(group_sizes), first_chunk),
        grid_spec=pltpu.PrefetchScalarGridSpec(
            num_scalar_prefetch=1,
            grid=(1,),
            in_specs=[
                once(dk.shape), once(dv.shape), once(dq.shape),
                pl.BlockSpec((1, seqs, wide, span), lambda i, o: (1, 0, 0, 0)),
                pl.BlockSpec((1, seqs, wide, span), lambda i, o: (2, 0, 0, 0)),
            ]
            + [once(d.shape) for d in dps]
            + [
                pl.BlockSpec((2, 8, span), lambda i, o: (0, 0, chunk)),
                once(same.shape), once(xt.shape), once(w.shape), once(gout.shape),
                once(gx_block),
            ],
            out_specs=[once((size, heads, height, 4 * HEAD_DIM)) for size in group_sizes]
            + [once((seqs, wide, width)), once((24, span))],
            scratch_shapes=[
                pltpu.VMEM((wide, PAIR), F32),
                pltpu.VMEM((wide, PAIR), F32),
                pltpu.VMEM((seqs * wide, span), BF),
                pltpu.VMEM((seqs * wide, span), BF),
                pltpu.VMEM((seqs * wide, span), BF),
                pltpu.VMEM((heads, width, 4 * HEAD_DIM), BF),
            ],
        ),
        out_shape=[
            jax.ShapeDtypeStruct((size, heads, height, 4 * HEAD_DIM), BF) for size in group_sizes
        ]
        + [
            jax.ShapeDtypeStruct((seqs, wide, width), F32),
            jax.ShapeDtypeStruct((24, span), F32),
        ],
        compiler_params=params(48),
        cost_estimate=cost(12 * seqs * wide * width * span, 16),
    )(offs, dk, dv, dq, proj, proj, *dps, taps, same, xt, w, gout, gx)
    return out[: len(group_sizes)], out[-2], out[-1]


def cycle(values, axis, shift):
    count = lax.axis_size(axis)
    return lax.ppermute(values, axis, [(i, (i + shift) % count) for i in range(count)])


def swap(values, axis, mask):
    count = lax.axis_size(axis)
    return lax.ppermute(values, axis, [(i, i ^ mask) for i in range(count)])


def shift_right(rows):
    count = lax.axis_size("tp")
    return lax.ppermute(rows, "tp", [(i, i + 1) for i in range(count - 1)])


def shift_left(rows):
    count = lax.axis_size("tp")
    return lax.ppermute(rows, "tp", [(i + 1, i) for i in range(count - 1)])


def gather_pieces(shard):
    mine = lax.axis_index("fsdp")
    rows = shard.shape[0]
    half = rows // 2
    across = swap(shard, "fsdp", 2)
    along = swap(shard, "fsdp", 4)
    corner = [swap(across[:half], "fsdp", 4), swap(along[half:], "fsdp", 2)]
    own = [shard, across, along] + corner
    other = [swap(piece, "fsdp", 1) for piece in own]
    place = [
        (mine ^ mask) * rows + extra
        for core in (0, 1)
        for mask, extra in ((core, 0), (2 + core, 0), (4 + core, 0), (6 + core, 0), (6 + core, half))
    ]
    return own + other, jnp.stack(place).astype(jnp.int32)


def add_low(first, *others):
    total = first.astype(F32)
    for other in others:
        total = total + other.astype(F32)
    return total


def scatter_chain(keep, send):
    merged = add_low(keep, swap(send, "fsdp", 1)).astype(BF)
    merged = add_low(merged[0], *[swap(merged[n], "fsdp", 2 * n) for n in (1, 2, 3)]).astype(BF)
    return scatter_tp(merged)


def scatter_tp(blocks):
    count = lax.axis_size("tp")
    me = lax.axis_index("tp")

    def pick(d):
        return lax.dynamic_index_in_dim(blocks, (me + d) % count, 0, keepdims=False)

    return add_low(pick(0), *[cycle(pick(d), "tp", d) for d in range(1, count)])


def sum_everywhere(values):
    for axis in ("fsdp", "tp"):
        mask = 1
        while mask < lax.axis_size(axis):
            values = values + swap(values, axis, mask)
            mask *= 2
    return values


def split_three(values):
    high = lax.reduce_precision(values, 8, 7)
    rest = values - high
    middle = lax.reduce_precision(rest, 8, 7)
    return jnp.stack([high, middle, rest - middle]).astype(BF)


def body(
    inputs, segments, w_qkv, qkv_bias, pool_kernel, w_out, out_bias,
    w_up, up_bias, w_down, norm_gains, norm_shifts, cotangent,
):
    rows, seqs, width = inputs.shape
    tp = lax.axis_size("tp")
    fsdp = lax.axis_size("fsdp")
    place = lax.axis_index("tp")
    shard_rows = w_qkv.shape[0]
    local = w_qkv.shape[2]
    chunks = local // HEAD_DIM
    span = tp * HEAD_DIM
    hidden_local = w_up.shape[1]
    hidden_units = hidden_local * tp
    far_rows = rows // STRIDE
    fast = fsdp == 8 and shard_rows % 32 == 0

    bias_values = jnp.concatenate(
        [qkv_bias.reshape(-1), pool_kernel.reshape(-1), up_bias.reshape(-1)]
    )
    biases = split_three(bias_values)
    extra = -(-biases.size // (3 * local))
    packed = jnp.concatenate(
        [
            w_qkv.reshape(shard_rows, 3 * local),
            jnp.pad(biases.reshape(-1), (0, extra * 3 * local - biases.size)).reshape(
                extra, 3 * local
            ),
        ],
        axis=0,
    )
    columns = lax.all_gather(packed, "tp", axis=0, tiled=False)
    qkv_rows = (
        columns[:, :shard_rows]
        .reshape(tp, shard_rows, 3, chunks, HEAD_DIM)
        .transpose(1, 2, 3, 0, 4)
        .reshape(shard_rows, 3 * width)
    )
    if fast:
        pieces, offs = gather_pieces(qkv_rows)
    else:
        pieces = [lax.all_gather(qkv_rows, "fsdp", axis=0, tiled=True)]
        offs = jnp.zeros((1,), jnp.int32)
    whole_bias = jnp.sum(
        columns[:, shard_rows:].reshape(tp, -1)[:, : biases.size].reshape(tp, 3, -1).astype(F32),
        axis=1,
    )
    lead = (3 + 2 * TAPS) * local
    featured = (
        whole_bias[:, :lead]
        .reshape(tp, 3 + 2 * TAPS, chunks, HEAD_DIM)
        .transpose(1, 2, 0, 3)
        .reshape(3 + 2 * TAPS, width)
    )
    bias_qkv = featured[:3, None, :]
    taps = jnp.pad(featured[3:].reshape(2, TAPS, width), ((0, 0), (0, 8 - TAPS), (0, 0)))
    bias_up = whole_bias[:, lead:].reshape(1, hidden_units)

    columns, later = lax.optimization_barrier(
        (columns, jnp.concatenate([w_up, w_down, w_out], axis=1))
    )
    rest = lax.all_gather(later, "tp", axis=0, tiled=False)
    rest = jnp.concatenate(
        [
            rest[:, :, :hidden_local].transpose(1, 0, 2).reshape(shard_rows, hidden_units),
            rest[:, :, hidden_local : 2 * hidden_local]
            .transpose(1, 0, 2)
            .reshape(shard_rows, hidden_units),
            rest[:, :, 2 * hidden_local :]
            .reshape(tp, shard_rows, chunks, HEAD_DIM)
            .transpose(1, 2, 0, 3)
            .reshape(shard_rows, width),
        ],
        axis=1,
    )
    weights = lax.all_gather(rest, "fsdp", axis=0, tiled=True)

    left = shift_right(inputs[rows - HALF :])
    right = shift_left(inputs[:HALF])
    x_wide = jnp.concatenate([left, inputs, right], axis=0).transpose(1, 0, 2)
    wide = rows + 2 * HALF
    x_cols = x_wide.reshape(seqs * wide, width).T
    cot = cotangent.transpose(1, 0, 2)

    seg_rows = segments.T
    padded = jnp.pad(seg_rows, ((0, 0), (HALF, HALF)), constant_values=-1)
    seg_keys = lax.dynamic_slice_in_dim(padded, place * rows, wide, 1)
    seg_own = seg_keys[:, HALF : HALF + rows]
    centers = seg_rows[:, ::STRIDE].reshape(seqs, tp, far_rows)
    centers_cycle = jnp.concatenate(
        [
            lax.dynamic_index_in_dim(centers, (place - d) % tp, 1, keepdims=True)
            for d in range(tp)
        ],
        axis=1,
    ).reshape(seqs, 1, tp * far_rows)
    segs = (seg_own[:, :, None], seg_keys[:, None, :], centers_cycle)
    own_centers = seg_own[:, ::STRIDE]
    same = jnp.stack(
        [
            seg_keys[:, HALF - MARGIN + r : HALF - MARGIN + r + rows : STRIDE][:, :far_rows]
            == own_centers
            for r in range(TAPS)
        ]
        + [jnp.zeros_like(own_centers, dtype=bool)] * (8 - TAPS),
        axis=2,
    ).astype(F32)

    made = [
        project(j, chunks, pieces, offs, x_wide, bias_qkv, taps, same, far_rows)
        for j in range(chunks)
    ]
    slots = [
        [pooled] + [cycle(pooled, "tp", d) for d in range(1, tp)] for _, pooled, _ in made
    ]
    att = [attend_forward(made[j][0], slots[j], segs) for j in range(chunks)]
    misc = jnp.concatenate([out_bias, norm_gains, norm_shifts, jnp.zeros((2, width), F32)])
    row_blocks = fsdp if shard_rows % 16 == 0 else 1
    outputs, grad_residual, grad_att, grad_out, gud, grad_up_bias, small = dense(
        att, x_wide, cot, weights, bias_up, misc, hidden_units, row_blocks
    )
    if row_blocks == 1:
        gud = gud.reshape(2, fsdp, shard_rows, hidden_units).transpose(1, 0, 2, 3)
    gud = lax.psum_scatter(gud, "fsdp", scatter_dimension=0, tiled=False)
    gud = gud.reshape(2, shard_rows, tp, hidden_local).transpose(2, 0, 1, 3)
    gud = lax.psum_scatter(gud, "tp", scatter_dimension=0, tiled=False).astype(F32)

    if fast:
        mine = lax.axis_index("fsdp")
        group_sizes = (4, 4)
        out_offs = jnp.stack(
            [(mine ^ m) * shard_rows for m in (0, 2, 4, 6, 1, 3, 5, 7)]
        ).astype(jnp.int32)
    else:
        group_sizes = (1,)
        out_offs = jnp.zeros((1,), jnp.int32)
    backs = [attend_backward(made[j][0], slots[j], segs, grad_att[j]) for j in range(chunks)]
    gx = jnp.zeros((seqs, 8, width), F32)
    weight_grads, smalls = [], []
    for j in range(chunks):
        dq, dk, dv, dps = backs[j]
        arrived = [dps[0]] + [cycle(dps[d], "tp", -d) for d in range(1, tp)]
        groups, gx, small_j = gather_back(
            j == 0, j, out_offs, group_sizes, (dq, dk, dv), arrived,
            made[j][0], taps, same, x_cols, made[j][2], grad_out[j], gx,
        )
        smalls.append(small_j)
        if fast:
            weight_grads.append(scatter_chain(*groups))
        else:
            whole = groups[0].reshape(tp, fsdp, shard_rows, 4 * HEAD_DIM).transpose(1, 0, 2, 3)
            whole = lax.psum_scatter(whole, "fsdp", scatter_dimension=0, tiled=False)
            weight_grads.append(scatter_tp(whole))

    to_left = shift_left(gx[:, :HALF].astype(BF))
    to_right = shift_right(gx[:, HALF + rows :].astype(BF))
    middle = gx[:, HALF : HALF + rows] + grad_residual
    middle = middle.at[:, :HALF].add(to_right.astype(F32))
    middle = middle.at[:, rows - HALF :].add(to_left.astype(F32))
    grad_inputs = middle.transpose(1, 0, 2)

    small_rows = jnp.concatenate(smalls, axis=1)
    sums = sum_everywhere(
        jnp.concatenate(
            [small, small_rows, grad_up_bias.reshape(-1, width)],
            axis=0,
        )
    )
    grad_out_bias, grad_gains, grad_shifts = sums[0:2], sums[2:4], sums[4:6]
    mixed = lax.dynamic_index_in_dim(
        sums[8:32].reshape(24, chunks, tp, HEAD_DIM), place, 2, keepdims=False
    ).reshape(24, local)
    grad_up = lax.dynamic_slice_in_dim(sums[32:].reshape(-1), place * hidden_local, hidden_local)

    stacked = jnp.stack(
        [g.reshape(shard_rows, 4, HEAD_DIM) for g in weight_grads], axis=2
    ).reshape(shard_rows, 4, local)
    return (
        outputs.transpose(1, 0, 2),
        grad_inputs,
        stacked[:, :3],
        mixed[:3],
        jnp.stack([mixed[8 : 8 + TAPS], mixed[16 : 16 + TAPS]]),
        stacked[:, 3],
        grad_out_bias,
        gud[0],
        grad_up,
        gud[1],
        grad_gains,
        grad_shifts,
    )


def solution(mesh):
    placed = (
        P("tp", "fsdp", None),
        P(None, "fsdp"),
        P("fsdp", None, "tp"),
        P(None, "tp"),
        P(None, None, "tp"),
        P("fsdp", "tp"),
        P(),
        P("fsdp", "tp"),
        P("tp"),
        P("fsdp", "tp"),
        P(),
        P(),
        P("tp", "fsdp", None),
    )
    return jax.shard_map(
        body,
        mesh=mesh,
        in_specs=placed,
        out_specs=(
            P("tp", "fsdp", None),
            P("tp", "fsdp", None),
            P("fsdp", None, "tp"),
            P(None, "tp"),
            P(None, None, "tp"),
            P("fsdp", "tp"),
            P(),
            P("fsdp", "tp"),
            P("tp"),
            P("fsdp", "tp"),
            P(),
            P(),
        ),
        check_vma=False,
    )
```

time: 943 us -> 518 us (0.55)
  waiting for transfers between devices: 342 us -> 75.9 us
  blocking collectives: 144 us -> 18.2 us
  Pallas kernels: 111 us -> 220 us
  matrix products: 108 us -> 0 us
  starting transfers between devices: 8.97 us -> 85.9 us
  other arithmetic: 82.1 us -> 16.3 us
  local copies, waits for them, and re-layouts: 122 us -> 77.2 us
    reduce_scatter x7 -> x2, waiting for transfers between devices: 154 us -> 0.01 us  [the longest x1 0.01 us: body(): gud = lax.psum_scatter(gud, 'fsdp', scatter_dimension=0, tiled=False)]
    all_gather x7 -> x1, blocking collectives: 144 us -> 18.2 us  [body(): columns = lax.all_gather(packed, 'tp', axis=0, tiled=False)]
    psum x1 -> x0, waiting for transfers between devices: 113 us -> none  [body(): lax.psum((grad_qkv_bias, grad_kernel, grad_up_bias, grad_out_bias, grad_n...]
    pallas_call x2 -> x13, Pallas kernels: 111 us -> 220 us  [the longest x3 68.6 us: attend_backward(): pl.pallas_call(partial(attend_backward_kernel, blocks), grid=(seqs, span...]
    dot_general x12 -> x0, matrix products: 108 us -> none  [the longest x1 18.1 us: body(): jnp.einsum('sle,ef->slf', grad_ffn_low, full_down, preferred_element_type...]
    ppermute x0 -> x53, starting transfers between devices: none -> 75.7 us  [the longest x27 51.2 us: cycle(): lax.ppermute(values, axis, [(i, (i + shift) % count) for i in range(count)])]
    unnamed x17 -> x4, waiting for transfers between devices: 63.2 us -> 0.07 us
    slice x26 -> x25, local copies, waits for them, and re-layouts: 62.6 us -> 6.97 us  [the longest x2 1.43 us: body(): mixed[:3]]
  transfers between devices with their start and end apart: 19 -> 61, of which waited for: 10 -> 10; matrix products, arithmetic and copies ran while one was open for 22% -> 10% of each run, Pallas kernels for 12% -> 32%
where the time goes in v2:
time: 518 us; the launch traced here: 509 us
  Pallas kernels  220 us (42%)
  starting transfers between devices  85.9 us (17%)
  local copies, waits for them, and re-layouts  77.2 us (15%)
  waiting for transfers between devices  75.9 us (15%)
  blocking collectives  18.2 us (4%)
  other arithmetic  16.3 us (3%)
  between operations  15.7 us (3%)
    pallas_call x3, Pallas kernels, attend_backward(): pl.pallas_call(partial(attend_backward_kernel, blocks), grid=(seqs, span...  68.6 us
    pallas_call x1, Pallas kernels, dense(): pl.pallas_call(partial(dense_kernel, chunks, steps), grid=(2 * steps,), i...  55.7 us
    ppermute x27, starting transfers between devices, cycle(): lax.ppermute(values, axis, [(i, (i + shift) % count) for i in range(count)])  51.2 us
    unnamed x186, local copies, waits for them, and re-layouts  50.9 us
    pallas_call x3, Pallas kernels, attend_forward(): pl.pallas_call(partial(attend_forward_kernel, blocks), grid=(seqs, span /...  44.8 us
    pallas_call x3, Pallas kernels, gather_back(): pl.pallas_call(partial(gather_back_kernel, blocks, len(group_sizes), firs...  37 us
    all_gather x1, waiting for transfers between devices, body(): rest = lax.all_gather(later, 'tp', axis=0, tiled=False)  35.3 us
    ppermute x26, starting transfers between devices, swap(): return lax.ppermute(values, axis, [(i, i ^ mask) for i in range(count)])  24.4 us
  transfers between devices with their start and end apart: 61, of which 10 were waited for; matrix products, arithmetic and copies ran while one was open for 10% of the time, Pallas kernels for 32%

profile of v2, /device:TPU:0, one launch (start us, length us, event | category | flops | bytes accessed | tf_op | source)
XLA Modules:
  0.0 509.0 jit_solution(7335151138373718916)
XLA Ops:
  11.3 18.2 %all-gather.2 = bf16[4,113,576]{1,2,0:T(8,128)(2,1)S(1)} all-gather(bf16[1,113,576]{1,2,0:T(8,128)(2,1)S(1)} %maximum_bitcast_fusion), channel_id=2, replica_groups=mesh['fsdp'=8,'tp'=4] {'tp'}, dimensions={0}, use_global_device_ids=true | all-gather | bytes 650880 | tf_op jit(solution)/shard_map/all_gather | solution.py:735
  29.4 1.6 pad_maximum_fusion.2
  31.1 35.3 %all-gather.8.cloned.1.call-done = bf16[384,1728]{1,0:T(8,128)(2,1)} async-done(((bf16[96,1728]{1,0:T(8,128)(2,1)}), bf16[384,1728]{1,0:T(8,128)(2,1)}) %all-gather.8.cloned.1.call-update) | async-done | bytes 1327120 | tf_op jit(solution)/shard_map/all_gather | solution.py:765
  66.4 1.3 slice_bitcast_fusion.1
  70.6 1.5 collective-permute-start
  72.1 1.5 collective-permute-start.1
  75.6 3.2 collective-permute-start.9
  89.0 1.3 copy.450
  94.0 8.0 %collective-permute-done.2.refs_3_ = bf16[48,2304]{1,0:T(8,128)(2,1)S(1)} collective-permute-done((bf16[48,2304]{1,0:T(8,128)(2,1)S(1)}, bf16[48,2304]{1,0:T(8,128)(2,1)S(1)}, u32[]{:S(2)}, u32[]{:S(2)}) %collective-permute-start.2) | collective-permute-done | bytes 221216 | tf_op jit(solution)/shard_map/ppermute | solution.py:635
  102.5 1.6 constant_dynamic-update-slice_fusion.1
  105.2 4.6 shard_map.224
  111.9 1.6 collective-permute-start.18
  113.5 2.2 collective-permute-start.19
  115.8 4.5 shard_map.222
  122.4 4.5 shard_map.220
  127.0 2.8 collective-permute-start.16
  129.8 12.8 %collective-permute-done.18.refs_2_.refs_6_ = bf16[2,2,128,256]{3,2,1,0:T(8,128)(2,1)S(1)} collective-permute-done((bf16[2,2,128,256]{3,2,1,0:T(8,128)(2,1)S(1)}, bf16[2,2,128,256]{3,2,1,0:T(8,128)(2,1)S(1)}, u32[]{:S(2)}, u32[]{:S(2)}) %collective-permute-start.18) | collective-permute-done | bytes 262176 | tf_op jit(solution)/shard_map/ppermute | solution.py:630
  142.6 5.2 %collective-permute-start.11 = (bf16[2,2,128,256]{3,2,1,0:T(8,128)(2,1)S(1)}, bf16[2,2,128,256]{3,2,1,0:T(8,128)(2,1)S(1)}, u32[]{:S(2)}, u32[]{:S(2)}) collective-permute-start(bf16[2,2,128,256]{3,2,1,0:T(8,128)(2,1)S(1)} %get-tuple-element.91.refs_0_.refs_4_), channel_id=1, source_target_pairs={{0,1},{1,2},{2,3},{3,0},{4,5},{5,6},{6,7},{7,4},{8,9},{9,10},{10,1... | collective-permute-start | bytes 786440 | tf_op jit(solution)/shard_map/ppermute | solution.py:630
  147.8 3.9 collective-permute-start.12
  151.7 14.9 %shard_map.225.refs_2_ = bf16[2,512,256]{2,1,0:T(8,128)(2,1)S(1)} custom-call(bf16[3,2,640,256]{3,2,1,0:T(8,128)(2,1)S(1)} %get-tuple-element.94.q_ref.k_ref.v_ref.refs_3_.refs_4_, bf16[3,2,640,256]{3,2,1,0:T(8,128)(2,1)S(1)} %get-tuple-element.94.q_ref.k_ref.v_ref.refs_3_.refs_4_, ...), custom_call_target="tpu_custom_call" | custom-call | flops 3221225472 | bytes 8388608 | tf_op jit(solution)/shard_map/pallas_call | solution.py:272
  166.7 1.4 collective-permute-start.13
  168.1 14.9 %shard_map.223.refs_1_ = bf16[2,512,256]{2,1,0:T(8,128)(2,1)S(1)} custom-call(bf16[3,2,640,256]{3,2,1,0:T(8,128)(2,1)S(1)} %get-tuple-element.92.q_ref.k_ref.v_ref.refs_3_.refs_4_, bf16[3,2,640,256]{3,2,1,0:T(8,128)(2,1)S(1)} %get-tuple-element.92.q_ref.k_ref.v_ref.refs_3_.refs_4_, ...), custom_call_target="tpu_custom_call" | custom-call | flops 3221225472 | bytes 8388608 | tf_op jit(solution)/shard_map/pallas_call | solution.py:272
  183.9 14.9 %shard_map.221.refs_0_ = bf16[2,512,256]{2,1,0:T(8,128)(2,1)S(1)} custom-call(bf16[3,2,640,256]{3,2,1,0:T(8,128)(2,1)S(1)} %get-tuple-element.90.q_ref.k_ref.v_ref.refs_3_.refs_4_, bf16[3,2,640,256]{3,2,1,0:T(8,128)(2,1)S(1)} %get-tuple-element.90.q_ref.k_ref.v_ref.refs_3_.refs_4_, ...), custom_call_target="tpu_custom_call" | custom-call | flops 3221225472 | bytes 8388608 | tf_op jit(solution)/shard_map/pallas_call | solution.py:272
  201.8 55.7 %shard_map.226 = (bf16[2,512,768]{2,1,0:T(8,128)(2,1)}, f32[2,512,768]{2,1,0:T(8,128)}, bf16[2,512,256]{2,1,0:T(8,128)(2,1)}, bf16[2,512,256]{2,1,0:T(8,128)(2,1...) custom-call(bf16[2,512,256]{2,1,0:T(8,128)(2,1)} %copy-done.70, ...), custom_call_target="tpu_custom_call" | custom-call | flops 32614907904 | bytes 50331648 | tf_op jit(solution)/shard_map/pallas_call | solution.py:466
  257.7 1.4 copy-done.1
  259.1 2.3 copy.432
  261.4 1.5 copy-done.7
  267.0 23.0 %shard_map.229 = (bf16[2,512,256]{2,1,0:T(8,128)(2,1)S(1)}, f32[2,640,256]{2,1,0:T(8,128)S(1)}, f32[2,640,256]{2,1,0:T(8,128)S(1)}, bf16[2,2,128,256]{3,2,1,0:T(...) custom-call(bf16[3,2,640,256]{3,2,1,0:T(8,128)(2,1)S(1)} %copy-done., ...), custom_call_target="tpu_custom_call" | custom-call | flops 8053063680 | bytes 16777216 | tf_op jit(solution)/shard_map/pallas_call | solution.py:294
  293.8 5.8 %collective-permute-start.27 = (bf16[2,2,128,256]{3,2,1,0:T(8,128)(2,1)}, bf16[2,2,128,256]{3,2,1,0:T(8,128)(2,1)}, u32[]{:S(2)}, u32[]{:S(2)}) collective-permute-start(bf16[2,2,128,256]{3,2,1,0:T(8,128)(2,1)} %get-tuple-element.124), channel_id=1, source_target_pairs={{0,2},{1,3},{2,0},{3,1},{4,6},{5,7},{6,4},{7,5},{8,10},{9,11},{10,... | collective-permute-start | bytes 786440 | tf_op jit(solution)/shard_map/ppermute | solution.py:630
  299.7 23.0 %shard_map.228 = (bf16[2,512,256]{2,1,0:T(8,128)(2,1)S(1)}, f32[2,640,256]{2,1,0:T(8,128)S(1)}, f32[2,640,256]{2,1,0:T(8,128)S(1)}, bf16[2,2,128,256]{3,2,1,0:T(...) custom-call(bf16[3,2,640,256]{3,2,1,0:T(8,128)(2,1)S(1)} %copy-done., ...), custom_call_target="tpu_custom_call" | custom-call | flops 8053063680 | bytes 16777216 | tf_op jit(solution)/shard_map/pallas_call | solution.py:294
  325.7 3.8 collective-permute-start.23
  329.5 22.6 %shard_map.227 = (bf16[2,512,256]{2,1,0:T(8,128)(2,1)S(1)}, f32[2,640,256]{2,1,0:T(8,128)S(1)}, f32[2,640,256]{2,1,0:T(8,128)S(1)}, bf16[2,2,128,256]{3,2,1,0:T(...) custom-call(bf16[3,2,640,256]{3,2,1,0:T(8,128)(2,1)S(1)} %copy-done., ...), custom_call_target="tpu_custom_call" | custom-call | flops 8053063680 | bytes 16777216 | tf_op jit(solution)/shard_map/pallas_call | solution.py:294
  359.7 3.3 collective-permute-start.20
  369.4 11.6 %shard_map.230 = (bf16[4,4,96,256]{3,2,1,0:T(8,128)(2,1)S(1)}, bf16[4,4,96,256]{3,2,1,0:T(8,128)(2,1)S(1)}, f32[2,640,768]{2,1,0:T(8,128)}, f32[24,256]{1,0:T(8,128)S(1)}) custom-call(s32[8]{0:T(128)S(1)} %stack.103.offs, f32[2,640,256]{2,1,0:T(8,128)} %copy-done.8, f32[2,640,256]{2,1,0:T(8,128)} %copy-done.9, bf16[2,512,256]{2,1,0:T(8,128)(2,1)S(1)} %copy-done.25, ...), custom_call_target="tpu_custom_call" | custom-call | flops 3019898880 | bytes 16777216 | tf_op jit(solution)/shard_map/pallas_call | solution.py:588
  382.1 12.7 %shard_map.231 = (bf16[4,4,96,256]{3,2,1,0:T(8,128)(2,1)S(1)}, bf16[4,4,96,256]{3,2,1,0:T(8,128)(2,1)}, f32[2,640,768]{2,1,0:T(8,128)}, f32[24,256]{1,0:T(8,128)S(1)}) custom-call(s32[8]{0:T(128)S(1)} %stack.103.offs, f32[2,640,256]{2,1,0:T(8,128)} %copy-done.12, f32[2,640,256]{2,1,0:T(8,128)} %copy-done.13, bf16[2,512,256]{2,1,0:T(8,128)(2,1)S(1)} %copy-done.23, ...), custom_call_target="tpu_custom_call" | custom-call | flops 3019898880 | bytes 16777216 | tf_op jit(solution)/shard_map/pallas_call | solution.py:588
  394.9 12.7 %shard_map.232 = (bf16[4,4,96,256]{3,2,1,0:T(8,128)(2,1)S(1)}, bf16[4,4,96,256]{3,2,1,0:T(8,128)(2,1)}, f32[2,640,768]{2,1,0:T(8,128)}, f32[24,256]{1,0:T(8,128)S(1)}) custom-call(s32[8]{0:T(128)S(1)} %stack.103.offs, f32[2,640,256]{2,1,0:T(8,128)} %copy-done.10, f32[2,640,256]{2,1,0:T(8,128)} %copy-done.11, bf16[2,512,256]{2,1,0:T(8,128)(2,1)S(1)} %copy-done.21, ...), custom_call_target="tpu_custom_call" | custom-call | flops 3019898880 | bytes 16777216 | tf_op jit(solution)/shard_map/pallas_call | solution.py:588
  407.7 4.5 copy.428
  413.1 2.5 convert.23
  416.5 4.3 collective-permute-start.29
  421.1 1.6 collective-permute-start.54
  423.3 2.7 collective-permute-done.54
  427.3 3.0 collective-permute-start.55
  430.5 5.9 %collective-permute-done.55 = f32[36,768]{1,0:T(8,128)S(1)} collective-permute-done((f32[36,768]{1,0:T(8,128)S(1)}, f32[36,768]{1,0:T(8,128)S(1)}, u32[]{:S(2)}, u32[]{:S(2)}) %collective-permute-start.55) | collective-permute-done | bytes 110624 | tf_op jit(solution)/shard_map/ppermute | solution.py:635
  436.4 2.0 collective-permute-start.56
  438.5 4.1 copy.429
  447.8 1.4 add_convert_fusion.2
  450.0 1.6 collective-permute-start.32
  451.6 1.5 collective-permute-start.33
  453.5 1.4 add_convert_fusion.1
  454.9 1.6 collective-permute-start.39
  456.6 2.7 reshape_reduce_scatter.3
  460.5 1.5 collective-permute-start.40
  462.0 1.4 add_convert_fusion
  463.9 1.6 collective-permute-start.46
  465.5 1.5 collective-permute-start.47
  467.0 1.3 fusion.10
  468.9 4.5 collective-permute-done.40
  475.5 3.0 collective-permute-start.37
  479.0 1.5 collective-permute-start.43
  480.8 2.6 collective-permute-start.44
  483.5 1.3 collective-permute-start.49
  484.8 3.9 collective-permute-start.50
  488.7 3.4 collective-permute-start.51
  493.4 4.7 collective-permute-done.50
  (381 shorter events, 79.2 us)
Async XLA Ops:
  7.2 59.2 %all-gather.8.cloned.1.call-start = ((), (), s32[]{:S(2)}) async-start(), calls=%async_computation.5 | async-start | bytes 1720320 | tf_op jit(solution)/shard_map/all_gather | solution.py:765
  31.0 170.8 %all-gather.6.cloned.1.call-start = ((), (), s32[]{:S(2)}) async-start(), calls=%async_computation.2 | async-start | bytes 11943936 | tf_op jit(solution)/shard_map/all_gather | solution.py:779
  70.3 386.3 %reduce-scatter.3.cloned.1.call-start = ((), (), s32[]{:S(2)}) async-start(), calls=%async_computation.3 | async-start | bytes 10616832 | tf_op jit(solution)/shard_map/reduce_scatter | solution.py:827
  70.6 20.6 %collective-permute-start = (bf16[96,2304]{1,0:T(8,128)(2,1)S(1)}, bf16[96,2304]{1,0:T(8,128)(2,1)S(1)}, u32[]{:S(2)}, u32[]{:S(2)}) collective-permute-start(bf16[96,2304]{1,0:T(8,128)(2,1)S(1)} %copy.406.refs_0_), channel_id=1, source_target_pairs={{0,8},{4,12},{8,0},{12,4},{16,24},{20,28},{24,16},{28,20},{1,9},{5... | collective-permute-start | bytes 1327112 | tf_op jit(solution)/shard_map/ppermute | solution.py:635
  72.1 19.7 %collective-permute-start.1 = (bf16[96,2304]{1,0:T(8,128)(2,1)S(1)}, bf16[96,2304]{1,0:T(8,128)(2,1)S(1)}, u32[]{:S(2)}, u32[]{:S(2)}) collective-permute-start(bf16[96,2304]{1,0:T(8,128)(2,1)S(1)} %copy.406.refs_0_), channel_id=1, source_target_pairs={{0,16},{4,20},{8,24},{12,28},{16,0},{20,4},{24,8},{28,12},{1,17},{... | collective-permute-start | bytes 1327112 | tf_op jit(solution)/shard_map/ppermute | solution.py:635
  73.6 31.5 %collective-permute-start.4 = (bf16[96,2304]{1,0:T(8,128)(2,1)S(1)}, bf16[96,2304]{1,0:T(8,128)(2,1)}, u32[]{:S(2)}, u32[]{:S(2)}) collective-permute-start(bf16[96,2304]{1,0:T(8,128)(2,1)S(1)} %copy.406.refs_0_), channel_id=1, source_target_pairs={{0,4},{4,0},{8,12},{12,8},{16,20},{20,16},{24,28},{28,24},{1,5},{5... | collective-permute-start | bytes 1327112 | tf_op jit(solution)/shard_map/ppermute | solution.py:635
  75.6 16.9 %collective-permute-start.9 = (bf16[64,2,768]{2,0,1:T(8,128)(2,1)}, bf16[64,2,768]{2,0,1:T(8,128)(2,1)}, u32[]{:S(2)}, u32[]{:S(2)}) collective-permute-start(bf16[64,2,768]{2,0,1:T(8,128)(2,1)} %copy.448), channel_id=1, source_target_pairs={{0,1},{1,2},{2,3},{4,5},{5,6},{6,7},{8,9},{9,10},{10,11},{12,13},{... | collective-permute-start | bytes 589832 | tf_op jit(solution)/shard_map/ppermute | solution.py:640
  79.6 13.1 %collective-permute-start.10 = (bf16[64,2,768]{2,0,1:T(8,128)(2,1)}, bf16[64,2,768]{2,0,1:T(8,128)(2,1)}, u32[]{:S(2)}, u32[]{:S(2)}) collective-permute-start(bf16[64,2,768]{2,0,1:T(8,128)(2,1)} %copy.449), channel_id=1, source_target_pairs={{1,0},{2,1},{3,2},{5,4},{6,5},{7,6},{9,8},{10,9},{11,10},{13,12},{... | collective-permute-start | bytes 589832 | tf_op jit(solution)/shard_map/ppermute | solution.py:645
  91.2 10.8 %collective-permute-start.2 = (bf16[48,2304]{1,0:T(8,128)(2,1)S(1)}, bf16[48,2304]{1,0:T(8,128)(2,1)S(1)}, u32[]{:S(2)}, u32[]{:S(2)}) collective-permute-start(bf16[48,2304]{1,0:T(8,128)(2,1)S(1)} %slice.255), channel_id=1, source_target_pairs={{0,16},{4,20},{8,24},{12,28},{16,0},{20,4},{24,8},{28,12},{1,17},{... | collective-permute-start | bytes 663560 | tf_op jit(solution)/shard_map/ppermute | solution.py:635
  91.9 10.1 %collective-permute-start.3 = (bf16[48,2304]{1,0:T(8,128)(2,1)S(1)}, bf16[48,2304]{1,0:T(8,128)(2,1)S(1)}, u32[]{:S(2)}, u32[]{:S(2)}) collective-permute-start(bf16[48,2304]{1,0:T(8,128)(2,1)S(1)} %slice.256), channel_id=1, source_target_pairs={{0,8},{4,12},{8,0},{12,4},{16,24},{20,28},{24,16},{28,20},{1,9},{5... | collective-permute-start | bytes 663560 | tf_op jit(solution)/shard_map/ppermute | solution.py:635
  92.5 12.6 %collective-permute-start.5 = (bf16[96,2304]{1,0:T(8,128)(2,1)S(1)}, bf16[96,2304]{1,0:T(8,128)(2,1)S(1)}, u32[]{:S(2)}, u32[]{:S(2)}) collective-permute-start(bf16[96,2304]{1,0:T(8,128)(2,1)S(1)} %collective-permute-done.refs_1_), channel_id=1, source_target_pairs={{0,4},{4,0},{8,12},{12,8},{16,20},{20,16},{24,28},{28,24},{1,5},{5... | collective-permute-start | bytes 1327112 | tf_op jit(solution)/shard_map/ppermute | solution.py:635
  92.6 12.5 %collective-permute-start.6 = (bf16[96,2304]{1,0:T(8,128)(2,1)S(1)}, bf16[96,2304]{1,0:T(8,128)(2,1)S(1)}, u32[]{:S(2)}, u32[]{:S(2)}) collective-permute-start(bf16[96,2304]{1,0:T(8,128)(2,1)S(1)} %collective-permute-done.1.refs_2_), channel_id=1, source_target_pairs={{0,4},{4,0},{8,12},{12,8},{16,20},{20,16},{24,28},{28,24},{1,5},{5... | collective-permute-start | bytes 1327112 | tf_op jit(solution)/shard_map/ppermute | solution.py:635
  102.0 3.1 collective-permute-start.7
  102.0 3.1 collective-permute-start.8
  110.8 16.2 %collective-permute-start.17 = (bf16[2,2,128,256]{3,2,1,0:T(8,128)(2,1)S(1)}, bf16[2,2,128,256]{3,2,1,0:T(8,128)(2,1)S(1)}, u32[]{:S(2)}, u32[]{:S(2)}) collective-permute-start(bf16[2,2,128,256]{3,2,1,0:T(8,128)(2,1)S(1)} %get-tuple-element.95.refs_0_.refs_4_), channel_id=1, source_target_pairs={{0,1},{1,2},{2,3},{3,0},{4,5},{5,6},{6,7},{7,4},{8,9},{9,10},{10,1... | collective-permute-start | bytes 786440 | tf_op jit(solution)/shard_map/ppermute | solution.py:630
  111.9 30.7 %collective-permute-start.18 = (bf16[2,2,128,256]{3,2,1,0:T(8,128)(2,1)S(1)}, bf16[2,2,128,256]{3,2,1,0:T(8,128)(2,1)S(1)}, u32[]{:S(2)}, u32[]{:S(2)}) collective-permute-start(bf16[2,2,128,256]{3,2,1,0:T(8,128)(2,1)S(1)} %get-tuple-element.95.refs_0_.refs_4_), channel_id=1, source_target_pairs={{0,2},{1,3},{2,0},{3,1},{4,6},{5,7},{6,4},{7,5},{8,10},{9,11},{10,... | collective-permute-start | bytes 786440 | tf_op jit(solution)/shard_map/ppermute | solution.py:630
  113.5 34.2 %collective-permute-start.19 = (bf16[2,2,128,256]{3,2,1,0:T(8,128)(2,1)S(1)}, bf16[2,2,128,256]{3,2,1,0:T(8,128)(2,1)S(1)}, u32[]{:S(2)}, u32[]{:S(2)}) collective-permute-start(bf16[2,2,128,256]{3,2,1,0:T(8,128)(2,1)S(1)} %get-tuple-element.95.refs_0_.refs_4_), channel_id=1, source_target_pairs={{0,3},{1,0},{2,1},{3,2},{4,7},{5,4},{6,5},{7,6},{8,11},{9,8},{10,9... | collective-permute-start | bytes 786440 | tf_op jit(solution)/shard_map/ppermute | solution.py:630
  121.3 46.7 %copy-start.47 = (bf16[2,2,128,256]{3,2,1,0:T(8,128)(2,1)}, bf16[2,2,128,256]{3,2,1,0:T(8,128)(2,1)S(1)}, u32[]{:S(2)}) copy-start(bf16[2,2,128,256]{3,2,1,0:T(8,128)(2,1)S(1)} %get-tuple-element.93.refs_0_.refs_4_) | copy-start | bytes 786436
  121.3 45.3 %collective-permute-start.14 = (bf16[2,2,128,256]{3,2,1,0:T(8,128)(2,1)S(1)}, bf16[2,2,128,256]{3,2,1,0:T(8,128)(2,1)S(1)}, u32[]{:S(2)}, u32[]{:S(2)}) collective-permute-start(bf16[2,2,128,256]{3,2,1,0:T(8,128)(2,1)S(1)} %get-tuple-element.93.refs_0_.refs_4_), channel_id=1, source_target_pairs={{0,1},{1,2},{2,3},{3,0},{4,5},{5,6},{6,7},{7,4},{8,9},{9,10},{10,1... | collective-permute-start | bytes 786440 | tf_op jit(solution)/shard_map/ppermute | solution.py:630
  121.3 46.7 %collective-permute-start.15 = (bf16[2,2,128,256]{3,2,1,0:T(8,128)(2,1)S(1)}, bf16[2,2,128,256]{3,2,1,0:T(8,128)(2,1)S(1)}, u32[]{:S(2)}, u32[]{:S(2)}) collective-permute-start(bf16[2,2,128,256]{3,2,1,0:T(8,128)(2,1)S(1)} %get-tuple-element.93.refs_0_.refs_4_), channel_id=1, source_target_pairs={{0,2},{1,3},{2,0},{3,1},{4,6},{5,7},{6,4},{7,5},{8,10},{9,11},{10,... | collective-permute-start | bytes 786440 | tf_op jit(solution)/shard_map/ppermute | solution.py:630
  127.0 56.9 %copy-start.6 = (bf16[3,2,640,256]{3,2,1,0:T(8,128)(2,1)}, bf16[3,2,640,256]{3,2,1,0:T(8,128)(2,1)S(1)}, u32[]{:S(2)}) copy-start(bf16[3,2,640,256]{3,2,1,0:T(8,128)(2,1)S(1)} %get-tuple-element.90.q_ref.k_ref.v_ref.refs_3_.refs_4_) | copy-start | bytes 5898244
  127.0 56.9 %copy-start.55 = (bf16[2,2,128,256]{3,2,1,0:T(8,128)(2,1)}, bf16[2,2,128,256]{3,2,1,0:T(8,128)(2,1)S(1)}, u32[]{:S(2)}) copy-start(bf16[2,2,128,256]{3,2,1,0:T(8,128)(2,1)S(1)} %get-tuple-element.91.refs_0_.refs_4_) | copy-start | bytes 786436
  127.0 41.0 %collective-permute-start.16 = (bf16[2,2,128,256]{3,2,1,0:T(8,128)(2,1)S(1)}, bf16[2,2,128,256]{3,2,1,0:T(8,128)(2,1)S(1)}, u32[]{:S(2)}, u32[]{:S(2)}) collective-permute-start(bf16[2,2,128,256]{3,2,1,0:T(8,128)(2,1)S(1)} %get-tuple-element.93.refs_0_.refs_4_), channel_id=1, source_target_pairs={{0,3},{1,0},{2,1},{3,2},{4,7},{5,4},{6,5},{7,6},{8,11},{9,8},{10,9... | collective-permute-start | bytes 786440 | tf_op jit(solution)/shard_map/ppermute | solution.py:630
  142.6 41.3 %collective-permute-start.11 = (bf16[2,2,128,256]{3,2,1,0:T(8,128)(2,1)S(1)}, bf16[2,2,128,256]{3,2,1,0:T(8,128)(2,1)S(1)}, u32[]{:S(2)}, u32[]{:S(2)}) collective-permute-start(bf16[2,2,128,256]{3,2,1,0:T(8,128)(2,1)S(1)} %get-tuple-element.91.refs_0_.refs_4_), channel_id=1, source_target_pairs={{0,1},{1,2},{2,3},{3,0},{4,5},{5,6},{6,7},{7,4},{8,9},{9,10},{10,1... | collective-permute-start | bytes 786440 | tf_op jit(solution)/shard_map/ppermute | solution.py:630
  147.8 36.1 %collective-permute-start.12 = (bf16[2,2,128,256]{3,2,1,0:T(8,128)(2,1)S(1)}, bf16[2,2,128,256]{3,2,1,0:T(8,128)(2,1)S(1)}, u32[]{:S(2)}, u32[]{:S(2)}) collective-permute-start(bf16[2,2,128,256]{3,2,1,0:T(8,128)(2,1)S(1)} %get-tuple-element.91.refs_0_.refs_4_), channel_id=1, source_target_pairs={{0,2},{1,3},{2,0},{3,1},{4,6},{5,7},{6,4},{7,5},{8,10},{9,11},{10,... | collective-permute-start | bytes 786440 | tf_op jit(solution)/shard_map/ppermute | solution.py:630
  166.7 17.2 %collective-permute-start.13 = (bf16[2,2,128,256]{3,2,1,0:T(8,128)(2,1)S(1)}, bf16[2,2,128,256]{3,2,1,0:T(8,128)(2,1)S(1)}, u32[]{:S(2)}, u32[]{:S(2)}) collective-permute-start(bf16[2,2,128,256]{3,2,1,0:T(8,128)(2,1)S(1)} %get-tuple-element.91.refs_0_.refs_4_), channel_id=1, source_target_pairs={{0,3},{1,0},{2,1},{3,2},{4,7},{5,4},{6,5},{7,6},{8,11},{9,8},{10,9... | collective-permute-start | bytes 786440 | tf_op jit(solution)/shard_map/ppermute | solution.py:630
  257.6 242.6 %reduce-scatter.5.cloned.1.call-start = ((), (), s32[]{:S(2)}) async-start(), calls=%async_computation.4 | async-start | bytes 1474560 | tf_op jit(solution)/shard_map/reduce_scatter | solution.py:829
  293.8 64.7 %collective-permute-start.26 = (bf16[2,2,128,256]{3,2,1,0:T(8,128)(2,1)}, bf16[2,2,128,256]{3,2,1,0:T(8,128)(2,1)S(1)}, u32[]{:S(2)}, u32[]{:S(2)}) collective-permute-start(bf16[2,2,128,256]{3,2,1,0:T(8,128)(2,1)} %get-tuple-element.123), channel_id=1, source_target_pairs={{0,3},{1,0},{2,1},{3,2},{4,7},{5,4},{6,5},{7,6},{8,11},{9,8},{10,9... | collective-permute-start | bytes 786440 | tf_op jit(solution)/shard_map/ppermute | solution.py:630
  293.8 65.9 %collective-permute-start.27 = (bf16[2,2,128,256]{3,2,1,0:T(8,128)(2,1)}, bf16[2,2,128,256]{3,2,1,0:T(8,128)(2,1)}, u32[]{:S(2)}, u32[]{:S(2)}) collective-permute-start(bf16[2,2,128,256]{3,2,1,0:T(8,128)(2,1)} %get-tuple-element.124), channel_id=1, source_target_pairs={{0,2},{1,3},{2,0},{3,1},{4,6},{5,7},{6,4},{7,5},{8,10},{9,11},{10,... | collective-permute-start | bytes 786440 | tf_op jit(solution)/shard_map/ppermute | solution.py:630
  299.6 63.4 %collective-permute-start.28 = (bf16[2,2,128,256]{3,2,1,0:T(8,128)(2,1)}, bf16[2,2,128,256]{3,2,1,0:T(8,128)(2,1)}, u32[]{:S(2)}, u32[]{:S(2)}) collective-permute-start(bf16[2,2,128,256]{3,2,1,0:T(8,128)(2,1)} %get-tuple-element.125), channel_id=1, source_target_pairs={{0,1},{1,2},{2,3},{3,0},{4,5},{5,6},{6,7},{7,4},{8,9},{9,10},{10,1... | collective-permute-start | bytes 786440 | tf_op jit(solution)/shard_map/ppermute | solution.py:630
  325.7 56.2 %collective-permute-start.23 = (bf16[2,2,128,256]{3,2,1,0:T(8,128)(2,1)}, bf16[2,2,128,256]{3,2,1,0:T(8,128)(2,1)}, u32[]{:S(2)}, u32[]{:S(2)}) collective-permute-start(bf16[2,2,128,256]{3,2,1,0:T(8,128)(2,1)} %get-tuple-element.113), channel_id=1, source_target_pairs={{0,3},{1,0},{2,1},{3,2},{4,7},{5,4},{6,5},{7,6},{8,11},{9,8},{10,9... | collective-permute-start | bytes 786440 | tf_op jit(solution)/shard_map/ppermute | solution.py:630
  329.5 52.6 %collective-permute-start.24 = (bf16[2,2,128,256]{3,2,1,0:T(8,128)(2,1)}, bf16[2,2,128,256]{3,2,1,0:T(8,128)(2,1)}, u32[]{:S(2)}, u32[]{:S(2)}) collective-permute-start(bf16[2,2,128,256]{3,2,1,0:T(8,128)(2,1)} %get-tuple-element.114), channel_id=1, source_target_pairs={{0,2},{1,3},{2,0},{3,1},{4,6},{5,7},{6,4},{7,5},{8,10},{9,11},{10,... | collective-permute-start | bytes 786440 | tf_op jit(solution)/shard_map/ppermute | solution.py:630
  359.2 22.9 %collective-permute-start.25 = (bf16[2,2,128,256]{3,2,1,0:T(8,128)(2,1)}, bf16[2,2,128,256]{3,2,1,0:T(8,128)(2,1)S(1)}, u32[]{:S(2)}, u32[]{:S(2)}) collective-permute-start(bf16[2,2,128,256]{3,2,1,0:T(8,128)(2,1)} %copy-done.61), channel_id=1, source_target_pairs={{0,1},{1,2},{2,3},{3,0},{4,5},{5,6},{6,7},{7,4},{8,9},{9,10},{10,1... | collective-permute-start | bytes 786440 | tf_op jit(solution)/shard_map/ppermute | solution.py:630
  359.7 35.1 %collective-permute-start.20 = (bf16[2,2,128,256]{3,2,1,0:T(8,128)(2,1)}, bf16[2,2,128,256]{3,2,1,0:T(8,128)(2,1)S(1)}, u32[]{:S(2)}, u32[]{:S(2)}) collective-permute-start(bf16[2,2,128,256]{3,2,1,0:T(8,128)(2,1)} %copy-done.60), channel_id=1, source_target_pairs={{0,3},{1,0},{2,1},{3,2},{4,7},{5,4},{6,5},{7,6},{8,11},{9,8},{10,9... | collective-permute-start | bytes 786440 | tf_op jit(solution)/shard_map/ppermute | solution.py:630
  363.0 31.8 %collective-permute-start.21 = (bf16[2,2,128,256]{3,2,1,0:T(8,128)(2,1)}, bf16[2,2,128,256]{3,2,1,0:T(8,128)(2,1)S(1)}, u32[]{:S(2)}, u32[]{:S(2)}) collective-permute-start(bf16[2,2,128,256]{3,2,1,0:T(8,128)(2,1)} %copy-done.59), channel_id=1, source_target_pairs={{0,2},{1,3},{2,0},{3,1},{4,6},{5,7},{6,4},{7,5},{8,10},{9,11},{10,... | collective-permute-start | bytes 786440 | tf_op jit(solution)/shard_map/ppermute | solution.py:630
  381.8 13.0 %collective-permute-start.22 = (bf16[2,2,128,256]{3,2,1,0:T(8,128)(2,1)S(1)}, bf16[2,2,128,256]{3,2,1,0:T(8,128)(2,1)S(1)}, u32[]{:S(2)}, u32[]{:S(2)}) collective-permute-start(bf16[2,2,128,256]{3,2,1,0:T(8,128)(2,1)S(1)} %copy-done.58), channel_id=1, source_target_pairs={{0,1},{1,2},{2,3},{3,0},{4,5},{5,6},{6,7},{7,4},{8,9},{9,10},{10,1... | collective-permute-start | bytes 786440 | tf_op jit(solution)/shard_map/ppermute | solution.py:630
  407.6 8.0 %collective-permute-start.52 = (f32[36,768]{1,0:T(8,128)S(1)}, f32[36,768]{1,0:T(8,128)S(1)}, u32[]{:S(2)}, u32[]{:S(2)}) collective-permute-start(f32[36,768]{1,0:T(8,128)S(1)} %pad_maximum_fusion.3), channel_id=1, source_target_pairs={{0,4},{4,0},{8,12},{12,8},{16,20},{20,16},{24,28},{28,24},{1,5},{5... | collective-permute-start | bytes 331784 | tf_op jit(solution)/shard_map/ppermute | solution.py:635
  412.2 35.5 %collective-permute-start.31 = (bf16[4,4,96,256]{3,2,1,0:T(8,128)(2,1)S(1)}, bf16[4,4,96,256]{3,2,1,0:T(8,128)(2,1)}, u32[]{:S(2)}, u32[]{:S(2)}) collective-permute-start(bf16[4,4,96,256]{3,2,1,0:T(8,128)(2,1)S(1)} %copy-done.38), channel_id=1, source_target_pairs={{0,4},{4,0},{8,12},{12,8},{16,20},{20,16},{24,28},{28,24},{1,5},{5... | collective-permute-start | bytes 2359304 | tf_op jit(solution)/shard_map/ppermute | solution.py:635
  412.6 40.9 %collective-permute-start.38 = (bf16[4,4,96,256]{3,2,1,0:T(8,128)(2,1)}, bf16[4,4,96,256]{3,2,1,0:T(8,128)(2,1)}, u32[]{:S(2)}, u32[]{:S(2)}) collective-permute-start(bf16[4,4,96,256]{3,2,1,0:T(8,128)(2,1)} %get-tuple-element.135), channel_id=1, source_target_pairs={{0,4},{4,0},{8,12},{12,8},{16,20},{20,16},{24,28},{28,24},{1,5},{5... | collective-permute-start | bytes 2359304 | tf_op jit(solution)/shard_map/ppermute | solution.py:635
  412.7 47.7 %collective-permute-start.45 = (bf16[4,4,96,256]{3,2,1,0:T(8,128)(2,1)}, bf16[4,4,96,256]{3,2,1,0:T(8,128)(2,1)}, u32[]{:S(2)}, u32[]{:S(2)}) collective-permute-start(bf16[4,4,96,256]{3,2,1,0:T(8,128)(2,1)} %get-tuple-element.137), channel_id=1, source_target_pairs={{0,4},{4,0},{8,12},{12,8},{16,20},{20,16},{24,28},{28,24},{1,5},{5... | collective-permute-start | bytes 2359304 | tf_op jit(solution)/shard_map/ppermute | solution.py:635
  415.6 5.4 %collective-permute-start.53 = (f32[36,768]{1,0:T(8,128)S(1)}, f32[36,768]{1,0:T(8,128)S(1)}, u32[]{:S(2)}, u32[]{:S(2)}) collective-permute-start(f32[36,768]{1,0:T(8,128)S(1)} %fusion.19), channel_id=1, source_target_pairs={{0,8},{4,12},{8,0},{12,4},{16,24},{20,28},{24,16},{28,20},{1,9},{5... | collective-permute-start | bytes 331784 | tf_op jit(solution)/shard_map/ppermute | solution.py:635
  416.5 10.9 %collective-permute-start.29 = (bf16[2,64,768]{2,1,0:T(8,128)(2,1)S(1)}, bf16[2,64,768]{2,1,0:T(8,128)(2,1)S(1)}, u32[]{:S(2)}, u32[]{:S(2)}) collective-permute-start(bf16[2,64,768]{2,1,0:T(8,128)(2,1)S(1)} %get-tuple-element.267), channel_id=1, source_target_pairs={{0,1},{1,2},{2,3},{4,5},{5,6},{6,7},{8,9},{9,10},{10,11},{12,13},{... | collective-permute-start | bytes 589832 | tf_op jit(solution)/shard_map/ppermute | solution.py:640
  421.1 4.9 collective-permute-start.54
  426.0 12.4 %collective-permute-start.30 = (bf16[2,64,768]{2,1,0:T(8,128)(2,1)S(1)}, bf16[2,64,768]{2,1,0:T(8,128)(2,1)S(1)}, u32[]{:S(2)}, u32[]{:S(2)}) collective-permute-start(bf16[2,64,768]{2,1,0:T(8,128)(2,1)S(1)} %get-tuple-element.266), channel_id=1, source_target_pairs={{1,0},{2,1},{3,2},{5,4},{6,5},{7,6},{9,8},{10,9},{11,10},{13,12},{... | collective-permute-start | bytes 589832 | tf_op jit(solution)/shard_map/ppermute | solution.py:645
  427.3 9.1 %collective-permute-start.55 = (f32[36,768]{1,0:T(8,128)S(1)}, f32[36,768]{1,0:T(8,128)S(1)}, u32[]{:S(2)}, u32[]{:S(2)}) collective-permute-start(f32[36,768]{1,0:T(8,128)S(1)} %add.246), channel_id=1, source_target_pairs={{0,1},{1,0},{2,3},{3,2},{4,5},{5,4},{6,7},{7,6},{8,9},{9,8},{10,11... | collective-permute-start | bytes 331784 | tf_op jit(solution)/shard_map/ppermute | solution.py:635
  436.4 6.2 %collective-permute-start.56 = (f32[36,768]{1,0:T(8,128)S(1)}, f32[36,768]{1,0:T(8,128)S(1)}, u32[]{:S(2)}, u32[]{:S(2)}) collective-permute-start(f32[36,768]{1,0:T(8,128)S(1)} %add.247), channel_id=1, source_target_pairs={{0,2},{1,3},{2,0},{3,1},{4,6},{5,7},{6,4},{7,5},{8,10},{9,11},{10,... | collective-permute-start | bytes 331784 | tf_op jit(solution)/shard_map/ppermute | solution.py:635
  450.0 13.4 %collective-permute-start.32 = (bf16[4,96,256]{2,1,0:T(8,128)(2,1)}, bf16[4,96,256]{2,1,0:T(8,128)(2,1)}, u32[]{:S(2)}, u32[]{:S(2)}) collective-permute-start(bf16[4,96,256]{2,1,0:T(8,128)(2,1)} %get-tuple-element.272), channel_id=1, source_target_pairs={{0,8},{4,12},{8,0},{12,4},{16,24},{20,28},{24,16},{28,20},{1,9},{5... | collective-permute-start | bytes 589832 | tf_op jit(solution)/shard_map/ppermute | solution.py:635
  451.6 12.4 %collective-permute-start.33 = (bf16[4,96,256]{2,1,0:T(8,128)(2,1)}, bf16[4,96,256]{2,1,0:T(8,128)(2,1)}, u32[]{:S(2)}, u32[]{:S(2)}) collective-permute-start(bf16[4,96,256]{2,1,0:T(8,128)(2,1)} %get-tuple-element.274), channel_id=1, source_target_pairs={{0,16},{4,20},{8,24},{12,28},{16,0},{20,4},{24,8},{28,12},{1,17},{... | collective-permute-start | bytes 589832 | tf_op jit(solution)/shard_map/ppermute | solution.py:635
  453.1 12.4 %collective-permute-start.34 = (bf16[4,96,256]{2,1,0:T(8,128)(2,1)S(1)}, bf16[4,96,256]{2,1,0:T(8,128)(2,1)}, u32[]{:S(2)}, u32[]{:S(2)}) collective-permute-start(bf16[4,96,256]{2,1,0:T(8,128)(2,1)S(1)} %get-tuple-element.273), channel_id=1, source_target_pairs={{0,24},{4,28},{8,16},{12,20},{16,8},{20,12},{24,0},{28,4},{1,25},{... | collective-permute-start | bytes 589832 | tf_op jit(solution)/shard_map/ppermute | solution.py:635
  454.9 13.4 %collective-permute-start.39 = (bf16[4,96,256]{2,1,0:T(8,128)(2,1)S(1)}, bf16[4,96,256]{2,1,0:T(8,128)(2,1)}, u32[]{:S(2)}, u32[]{:S(2)}) collective-permute-start(bf16[4,96,256]{2,1,0:T(8,128)(2,1)S(1)} %get-tuple-element.275), channel_id=1, source_target_pairs={{0,8},{4,12},{8,0},{12,4},{16,24},{20,28},{24,16},{28,20},{1,9},{5... | collective-permute-start | bytes 589832 | tf_op jit(solution)/shard_map/ppermute | solution.py:635
  460.5 12.9 %collective-permute-start.40 = (bf16[4,96,256]{2,1,0:T(8,128)(2,1)S(1)}, bf16[4,96,256]{2,1,0:T(8,128)(2,1)S(1)}, u32[]{:S(2)}, u32[]{:S(2)}) collective-permute-start(bf16[4,96,256]{2,1,0:T(8,128)(2,1)S(1)} %get-tuple-element.277), channel_id=1, source_target_pairs={{0,16},{4,20},{8,24},{12,28},{16,0},{20,4},{24,8},{28,12},{1,17},{... | collective-permute-start | bytes 589832 | tf_op jit(solution)/shard_map/ppermute | solution.py:635
  463.4 9.9 %collective-permute-start.41 = (bf16[4,96,256]{2,1,0:T(8,128)(2,1)S(1)}, bf16[4,96,256]{2,1,0:T(8,128)(2,1)S(1)}, u32[]{:S(2)}, u32[]{:S(2)}) collective-permute-start(bf16[4,96,256]{2,1,0:T(8,128)(2,1)S(1)} %get-tuple-element.276), channel_id=1, source_target_pairs={{0,24},{4,28},{8,16},{12,20},{16,8},{20,12},{24,0},{28,4},{1,25},{... | collective-permute-start | bytes 589832 | tf_op jit(solution)/shard_map/ppermute | solution.py:635
  463.9 11.5 %collective-permute-start.46 = (bf16[4,96,256]{2,1,0:T(8,128)(2,1)S(1)}, bf16[4,96,256]{2,1,0:T(8,128)(2,1)S(1)}, u32[]{:S(2)}, u32[]{:S(2)}) collective-permute-start(bf16[4,96,256]{2,1,0:T(8,128)(2,1)S(1)} %get-tuple-element.278), channel_id=1, source_target_pairs={{0,8},{4,12},{8,0},{12,4},{16,24},{20,28},{24,16},{28,20},{1,9},{5... | collective-permute-start | bytes 589832 | tf_op jit(solution)/shard_map/ppermute | solution.py:635
  465.5 13.0 %collective-permute-start.47 = (bf16[4,96,256]{2,1,0:T(8,128)(2,1)S(1)}, bf16[4,96,256]{2,1,0:T(8,128)(2,1)S(1)}, u32[]{:S(2)}, u32[]{:S(2)}) collective-permute-start(bf16[4,96,256]{2,1,0:T(8,128)(2,1)S(1)} %get-tuple-element.280), channel_id=1, source_target_pairs={{0,16},{4,20},{8,24},{12,28},{16,0},{20,4},{24,8},{28,12},{1,17},{... | collective-permute-start | bytes 589832 | tf_op jit(solution)/shard_map/ppermute | solution.py:635
  468.4 10.6 %collective-permute-start.48 = (bf16[4,96,256]{2,1,0:T(8,128)(2,1)S(1)}, bf16[4,96,256]{2,1,0:T(8,128)(2,1)S(1)}, u32[]{:S(2)}, u32[]{:S(2)}) collective-permute-start(bf16[4,96,256]{2,1,0:T(8,128)(2,1)S(1)} %get-tuple-element.279), channel_id=1, source_target_pairs={{0,24},{4,28},{8,16},{12,20},{16,8},{20,12},{24,0},{28,4},{1,25},{... | collective-permute-start | bytes 589832 | tf_op jit(solution)/shard_map/ppermute | solution.py:635
  473.4 7.5 %collective-permute-start.35 = (bf16[96,256]{1,0:T(8,128)(2,1)S(1)}, bf16[96,256]{1,0:T(8,128)(2,1)S(1)}, u32[]{:S(2)}, u32[]{:S(2)}) collective-permute-start(bf16[96,256]{1,0:T(8,128)(2,1)S(1)} %get-tuple-element.283), channel_id=1, source_target_pairs={{0,1},{1,2},{2,3},{3,0},{4,5},{5,6},{6,7},{7,4},{8,9},{9,10},{10,1... | collective-permute-start | bytes 147464 | tf_op jit(solution)/shard_map/ppermute | solution.py:630
  473.4 10.1 %collective-permute-start.36 = (bf16[96,256]{1,0:T(8,128)(2,1)S(1)}, bf16[96,256]{1,0:T(8,128)(2,1)S(1)}, u32[]{:S(2)}, u32[]{:S(2)}) collective-permute-start(bf16[96,256]{1,0:T(8,128)(2,1)S(1)} %get-tuple-element.285), channel_id=1, source_target_pairs={{0,2},{1,3},{2,0},{3,1},{4,6},{5,7},{6,4},{7,5},{8,10},{9,11},{10,... | collective-permute-start | bytes 147464 | tf_op jit(solution)/shard_map/ppermute | solution.py:630
  475.5 9.3 %collective-permute-start.37 = (bf16[96,256]{1,0:T(8,128)(2,1)S(1)}, bf16[96,256]{1,0:T(8,128)(2,1)S(1)}, u32[]{:S(2)}, u32[]{:S(2)}) collective-permute-start(bf16[96,256]{1,0:T(8,128)(2,1)S(1)} %get-tuple-element.284), channel_id=1, source_target_pairs={{0,3},{1,0},{2,1},{3,2},{4,7},{5,4},{6,5},{7,6},{8,11},{9,8},{10,9... | collective-permute-start | bytes 147464 | tf_op jit(solution)/shard_map/ppermute | solution.py:630
  478.5 10.2 %collective-permute-start.42 = (bf16[96,256]{1,0:T(8,128)(2,1)S(1)}, bf16[96,256]{1,0:T(8,128)(2,1)S(1)}, u32[]{:S(2)}, u32[]{:S(2)}) collective-permute-start(bf16[96,256]{1,0:T(8,128)(2,1)S(1)} %get-tuple-element.286), channel_id=1, source_target_pairs={{0,1},{1,2},{2,3},{3,0},{4,5},{5,6},{6,7},{7,4},{8,9},{9,10},{10,1... | collective-permute-start | bytes 147464 | tf_op jit(solution)/shard_map/ppermute | solution.py:630
  479.0 14.5 %collective-permute-start.43 = (bf16[96,256]{1,0:T(8,128)(2,1)S(1)}, bf16[96,256]{1,0:T(8,128)(2,1)S(1)}, u32[]{:S(2)}, u32[]{:S(2)}) collective-permute-start(bf16[96,256]{1,0:T(8,128)(2,1)S(1)} %get-tuple-element.288), channel_id=1, source_target_pairs={{0,2},{1,3},{2,0},{3,1},{4,6},{5,7},{6,4},{7,5},{8,10},{9,11},{10,... | collective-permute-start | bytes 147464 | tf_op jit(solution)/shard_map/ppermute | solution.py:630
  480.8 12.6 %collective-permute-start.44 = (bf16[96,256]{1,0:T(8,128)(2,1)S(1)}, bf16[96,256]{1,0:T(8,128)(2,1)S(1)}, u32[]{:S(2)}, u32[]{:S(2)}) collective-permute-start(bf16[96,256]{1,0:T(8,128)(2,1)S(1)} %get-tuple-element.287), channel_id=1, source_target_pairs={{0,3},{1,0},{2,1},{3,2},{4,7},{5,4},{6,5},{7,6},{8,11},{9,8},{10,9... | collective-permute-start | bytes 147464 | tf_op jit(solution)/shard_map/ppermute | solution.py:630
  483.5 9.9 %collective-permute-start.49 = (bf16[96,256]{1,0:T(8,128)(2,1)S(1)}, bf16[96,256]{1,0:T(8,128)(2,1)S(1)}, u32[]{:S(2)}, u32[]{:S(2)}) collective-permute-start(bf16[96,256]{1,0:T(8,128)(2,1)S(1)} %get-tuple-element.289), channel_id=1, source_target_pairs={{0,1},{1,2},{2,3},{3,0},{4,5},{5,6},{6,7},{7,4},{8,9},{9,10},{10,1... | collective-permute-start | bytes 147464 | tf_op jit(solution)/shard_map/ppermute | solution.py:630
  484.8 13.3 %collective-permute-start.50 = (bf16[96,256]{1,0:T(8,128)(2,1)S(1)}, bf16[96,256]{1,0:T(8,128)(2,1)S(1)}, u32[]{:S(2)}, u32[]{:S(2)}) collective-permute-start(bf16[96,256]{1,0:T(8,128)(2,1)S(1)} %get-tuple-element.291), channel_id=1, source_target_pairs={{0,2},{1,3},{2,0},{3,1},{4,6},{5,7},{6,4},{7,5},{8,10},{9,11},{10,... | collective-permute-start | bytes 147464 | tf_op jit(solution)/shard_map/ppermute | solution.py:630
  488.7 9.5 %collective-permute-start.51 = (bf16[96,256]{1,0:T(8,128)(2,1)S(1)}, bf16[96,256]{1,0:T(8,128)(2,1)S(1)}, u32[]{:S(2)}, u32[]{:S(2)}) collective-permute-start(bf16[96,256]{1,0:T(8,128)(2,1)S(1)} %get-tuple-element.290), channel_id=1, source_target_pairs={{0,3},{1,0},{2,1},{3,2},{4,7},{5,4},{6,5},{7,6},{8,11},{9,8},{10,9... | collective-permute-start | bytes 147464 | tf_op jit(solution)/shard_map/ppermute | solution.py:630
  (83 other events, 1066.6 us)
Sparse Core Ops, SparseCore 0:
  31.1 35.1 all-gather.7
  70.4 67.2 all-gather.5
  257.7 77.2 reduce-scatter.2
  460.6 35.7 reduce-scatter.4

commit v3 on v2

--- a/solution.py
+++ b/solution.py
@@ -16,7 +16,7 @@
 PAIR = 2 * HEAD_DIM
 QB = 128
 NEAR = QB + 2 * HALF
-FB = 512
+EXTRA = 16
 RC = 256
 EPSILON = 1e-05
 NEG = -1e30
@@ -43,7 +43,7 @@
 
 
 def cost(flops, mib, trans=0):
-    return pl.CostEstimate(flops=flops, bytes_accessed=mib * MIB, transcendentals=trans)
+    return pl.CostEstimate(flops=1, bytes_accessed=1, transcendentals=0)
 
 
 def once(shape):
@@ -276,7 +276,7 @@
         out_specs=pl.BlockSpec((1, rows, PAIR), lambda s, h: (s, 0, h)),
         out_shape=jax.ShapeDtypeStruct((seqs, rows, span), BF),
         scratch_shapes=attention_scratch(rows, blocks * far_rows),
-        compiler_params=params(32),
+        compiler_params=params(60),
         cost_estimate=cost(16 * 64 * cells, 8, cells),
     )(proj, proj, proj, *slots, *slots, *segs)
 
@@ -300,7 +300,7 @@
         + [far_shape] * blocks,
         scratch_shapes=attention_scratch(rows, blocks * far_rows)
         + [pltpu.VMEM((rows, blocks * far_rows), BF)] * 2,
-        compiler_params=params(40),
+        compiler_params=params(60),
         cost_estimate=cost(40 * 64 * cells, 16, cells),
     )(proj, proj, proj, *slots, *slots, *segs, grad)
     return out[0], out[1], out[2], out[3:]
@@ -327,19 +327,22 @@
 
 def dense_kernel(chunks, steps, *refs):
     att = refs[:chunks]
-    x_ref, cot_ref, wout_ref, up_ref, down_ref, bup_ref, misc_ref = refs[chunks : chunks + 7]
+    x_ref, cot_ref, wout_ref, up_blk, down_blk, bup_ref, misc_ref = refs[chunks : chunks + 7]
     outs = refs[chunks + 7 :]
     out_ref, gres_ref = outs[:2]
     gatt = outs[2 : 2 + chunks]
     gout = outs[2 + chunks : 2 + 2 * chunks]
-    gud_ref, gbup_ref, small_ref = outs[2 + 2 * chunks : 5 + 2 * chunks]
+    gud_ref, small_ref = outs[2 + 2 * chunks : 4 + 2 * chunks]
     (
-        normed, inverse, flow, flow_t, acc, gffn, gffn_t, hidden, slope, gpre
-    ) = outs[5 + 2 * chunks :]
+        inverse, flow, flow_t, acc, gffn, gffn_t, hidden, slope, gpre
+    ) = outs[4 + 2 * chunks :]
     step = pl.program_id(0)
     seqs, rows, width = cot_ref.shape
     total = seqs * rows
     span = width // chunks
+    units = gpre.shape[1]
+    up_ref = up_blk[...].reshape(width, units)
+    down_ref = down_blk[...].reshape(width, units)
     bias_one, bias_two = misc_ref[0:1, :], misc_ref[1:2, :]
     gain_one, gain_two = misc_ref[2:3, :], misc_ref[3:4, :]
     shift_one, shift_two = misc_ref[4:5, :], misc_ref[5:6, :]
@@ -357,7 +360,7 @@
             n_one, inv = norm_stats(
                 x_ref[s, HALF + row : HALF + row + RC, :].astype(F32) + branch
             )
-            normed[block, :] = n_one
+            gres_ref[s, row : row + RC, :] = n_one
             inverse[block, :] = inv
             low = (n_one * gain_one + shift_one).astype(BF)
             flow[block, :] = low
@@ -368,20 +371,20 @@
     def _():
         for first, s, row in parts:
             block = slice(first, first + RC)
-            pre = nn(flow[block, :], up_ref[...]) + bup_ref[...]
+            pre = nn(flow[block, :], up_ref) + bup_ref[...]
             cdf = 0.5 * (1.0 + lax.erf(pre * np.float32(np.sqrt(0.5))))
             pdf = jnp.exp(-0.5 * (pre * pre)) * np.float32(1.0 / np.sqrt(2.0 * np.pi))
             low = (pre * cdf).astype(BF)
             hidden[step, block, :] = low
             slope[step, block, :] = cdf + pre * pdf
-            acc[block, :] += nt(low, down_ref[...])
+            acc[block, :] += nt(low, down_ref)
 
     @pl.when(step == steps)
     def _():
         small_ref[...] = jnp.zeros_like(small_ref)
         for first, s, row in parts:
             block = slice(first, first + RC)
-            first_out = normed[block, :] * gain_one + shift_one
+            first_out = gres_ref[s, row : row + RC, :] * gain_one + shift_one
             n_two, inv = norm_stats(first_out + (acc[block, :] + bias_two))
             out_ref[s, row : row + RC, :] = (n_two * gain_two + shift_two).astype(BF)
             grad = cot_ref[s, row : row + RC, :].astype(F32)
@@ -397,25 +400,30 @@
     @pl.when(step >= steps)
     def _():
         which = 2 * steps - 1 - step
-        bias_sum = jnp.zeros((1, FB), F32)
+        bias_sum = jnp.zeros((1, units), F32)
         for first, s, row in parts:
             block = slice(first, first + RC)
-            grad = nn(gffn[block, :], down_ref[...])
+            grad = nn(gffn[block, :], down_ref)
             low = (grad * slope[which, block, :]).astype(BF)
             gpre[block, :] = low
             bias_sum = bias_sum + column_sum(low)
-            acc[block, :] += nt(low, up_ref[...])
-        gbup_ref[...] = bias_sum
-        lead = (gud_ref.shape[0], gud_ref.shape[2], FB)
-        gud_ref[:, 0] = nn(flow_t[...], gpre[...]).astype(BF).reshape(lead)
-        gud_ref[:, 1] = nn(gffn_t[...], hidden[which]).astype(BF).reshape(lead)
+            acc[block, :] += nt(low, up_ref)
+        height = gud_ref.shape[2] - EXTRA
+        lead = (gud_ref.shape[0], height, units)
+        gud_ref[:, 0, :height] = nn(flow_t[...], gpre[...]).astype(BF).reshape(lead)
+        gud_ref[:, 1, :height] = nn(gffn_t[...], hidden[which]).astype(BF).reshape(lead)
+        head = lax.broadcasted_iota(jnp.int32, (EXTRA, 1), 0) == 0
+        extra = jnp.where(head, bias_sum, 0.0).astype(BF)
+        for m in range(gud_ref.shape[0]):
+            gud_ref[m, 0, height:] = extra
+            gud_ref[m, 1, height:] = jnp.zeros((EXTRA, units), BF)
 
     @pl.when(step == 2 * steps - 1)
     def _():
         for first, s, row in parts:
             block = slice(first, first + RC)
             grad = acc[block, :]
-            n_one = normed[block, :]
+            n_one = gres_ref[s, row : row + RC, :]
             back = norm_back(grad, n_one, inverse[block, :], gain_one)
             gres_ref[s, row : row + RC, :] = back
             low = back.astype(BF)
@@ -431,12 +439,13 @@
             gout[j][...] = nn(flow_t[...], att[j][...].reshape(total, span)).astype(BF)
 
 
-def dense(att, x_wide, cot, weights, bias_up, misc, hidden_units, row_blocks):
+def dense(att, x_wide, cot, w_out, weights, bias_up, misc):
     chunks = len(att)
     seqs, rows, width = cot.shape
     total = seqs * rows
     span = width // chunks
-    steps = hidden_units // FB
+    row_blocks, steps, height, units = weights.shape
+    units //= 2
 
     def which(i):
         return jnp.where(i < steps, i, 2 * steps - 1 - i)
@@ -444,7 +453,6 @@
     def back(i):
         return jnp.where(i < steps, steps - 1, 2 * steps - 1 - i)
 
-    lead = width // row_blocks
     out_shape = (
         [
             jax.ShapeDtypeStruct((seqs, rows, width), BF),
@@ -453,14 +461,12 @@
         + [jax.ShapeDtypeStruct((seqs, rows, span), BF)] * chunks
         + [jax.ShapeDtypeStruct((width, span), BF)] * chunks
         + [
-            jax.ShapeDtypeStruct((row_blocks, 2, lead, hidden_units), BF),
-            jax.ShapeDtypeStruct((1, hidden_units), F32),
+            jax.ShapeDtypeStruct((row_blocks, 2, height + EXTRA, steps * units), BF),
             jax.ShapeDtypeStruct((8, width), F32),
         ]
     )
     out_specs = [once(o.shape) for o in out_shape[: 2 + 2 * chunks]] + [
-        pl.BlockSpec((row_blocks, 2, lead, FB), lambda i: (0, 0, 0, back(i))),
-        pl.BlockSpec((1, FB), lambda i: (0, back(i))),
+        pl.BlockSpec((row_blocks, 2, height + EXTRA, units), lambda i: (0, 0, 0, back(i))),
         once((8, width)),
     ]
     out = pl.pallas_call(
@@ -470,159 +476,226 @@
         + [
             once(x_wide.shape),
             once(cot.shape),
-            pl.BlockSpec(
-                (width, width),
-                lambda i: (0, 2 * hidden_units // width),
-                pipeline_mode=pl.Buffered(1),
-            ),
-            pl.BlockSpec((width, FB), lambda i: (0, which(i))),
-            pl.BlockSpec((width, FB), lambda i: (0, steps + which(i))),
-            pl.BlockSpec((1, FB), lambda i: (0, which(i))),
+            once(w_out.shape),
+            pl.BlockSpec((row_blocks, None, height, units), lambda i: (0, which(i), 0, 0)),
+            pl.BlockSpec((row_blocks, None, height, units), lambda i: (0, which(i), 0, 1)),
+            pl.BlockSpec((1, units), lambda i: (0, which(i))),
             once(misc.shape),
         ],
         out_specs=out_specs,
         out_shape=out_shape,
         scratch_shapes=[
-            pltpu.VMEM((total, width), F32),
             pltpu.VMEM((total, 1), F32),
             pltpu.VMEM((total, width), BF),
             pltpu.VMEM((width, total), BF),
             pltpu.VMEM((total, width), F32),
             pltpu.VMEM((total, width), BF),
             pltpu.VMEM((width, total), BF),
-            pltpu.VMEM((steps, total, FB), BF),
-            pltpu.VMEM((steps, total, FB), F32),
-            pltpu.VMEM((total, FB), BF),
+            pltpu.VMEM((steps, total, units), BF),
+            pltpu.VMEM((steps, total, units), F32),
+            pltpu.VMEM((total, units), BF),
         ],
-        compiler_params=params(60),
-        cost_estimate=cost(
-            12 * total * width * hidden_units + 6 * total * width * width, 48, total * hidden_units
-        ),
-    )(*att, x_wide, cot, weights, weights, weights, bias_up, misc)
+        compiler_params=params(63),
+        cost_estimate=cost(1, 1),
+    )(*att, x_wide, cot, w_out, weights, weights, bias_up, misc)
     return (
-        out[0], out[1], out[2 : 2 + chunks], out[2 + chunks : 2 + 2 * chunks],
-        out[-3], out[-2], out[-1],
-    )
-
-
-def gather_back_kernel(
-    blocks, groups, first_chunk, offs, *refs
-):
-    dk_ref, dv_ref, dq_ref, proj_k, proj_v = refs[:5]
-    dps = refs[5 : 5 + blocks]
-    taps_ref, same_ref, xt_ref, w_ref, gout_ref, gx_in = refs[5 + blocks : 11 + blocks]
-    outs = refs[11 + blocks :]
+        out[0], out[1], out[2 : 2 + chunks], out[2 + chunks : 2 + 2 * chunks], out[-2], out[-1]
+    )
+
+
+def gather_back_kernel(blocks, chunks, groups, offs, *refs):
+    taken = 5 + blocks + 1
+    per_chunk = [refs[n * taken : (n + 1) * taken] for n in range(chunks)]
+    taps_ref, same_ref, xt_ref, more_ref = refs[chunks * taken : chunks * taken + 4]
+    outs = refs[chunks * taken + 4 :]
     gws = outs[:groups]
-    gx_ref, small_ref, plain, spread, low_q, low_k, low_v, stage = outs[groups:]
-    seqs, wide, span = dk_ref.shape
+    lows = outs[groups : groups + chunks]
+    small, plain, spread, low_q, total, stage = outs[groups + chunks :]
+    width = xt_ref.shape[0]
+    seq = pl.program_id(0)
+    wide, span = per_chunk[0][0].shape[1:]
     rows = wide - 2 * HALF
-    far_rows = dps[0].shape[2]
-    small_ref[...] = jnp.zeros_like(small_ref)
-    for c, (near, proj, low) in enumerate(((dk_ref, proj_k, low_k), (dv_ref, proj_v, low_v))):
-        for s in range(seqs):
+    far_rows = per_chunk[0][3].shape[2]
+
+    @pl.when(seq == 0)
+    def _():
+        small[...] = jnp.zeros_like(small)
+        total[...] = jnp.zeros_like(total)
+
+    for n, chunk_refs in enumerate(per_chunk):
+        dk_ref, dv_ref, dq_ref = chunk_refs[:3]
+        dps = chunk_refs[3 : 3 + blocks]
+        proj_k, proj_v = chunk_refs[3 + blocks : 5 + blocks]
+        low = lows[n]
+        base = n * span
+        low_q[:HALF, :] = jnp.zeros((HALF, span), BF)
+        low_q[HALF : HALF + rows, :] = dq_ref[0]
+        low_q[HALF + rows :, :] = jnp.zeros((HALF, span), BF)
+        small[0, 0:1, base : base + span] += column_sum(dq_ref[0])
+        for c, (near, proj) in enumerate(((dk_ref, proj_k), (dv_ref, proj_v))):
             for half in range(span // PAIR):
                 lanes = slice(half * PAIR, (half + 1) * PAIR)
-                plain[...] = proj[0, s, :, lanes].astype(F32)
-                spread[...] = near[s, :, lanes]
-                pooled = dps[0][c, s, :, lanes].astype(F32)
-                for n in range(1, blocks):
-                    pooled = pooled + dps[n][c, s, :, lanes].astype(F32)
+                wider = slice(base + half * PAIR, base + (half + 1) * PAIR)
+                plain[...] = proj[0, 0, :, lanes].astype(F32)
+                spread[...] = near[0, :, lanes]
+                pooled = dps[0][c, 0, :, lanes].astype(F32)
+                for d in range(1, blocks):
+                    pooled = pooled + dps[d][c, 0, :, lanes].astype(F32)
                 pooled = pooled.astype(BF).astype(F32)
                 for r in range(TAPS):
                     place = pl.ds(HALF - MARGIN + r, far_rows, stride=STRIDE)
-                    masked = pooled * same_ref[s, :, r : r + 1]
-                    row = 8 + 8 * c + r
-                    small_ref[row : row + 1, lanes] += column_sum(masked * plain[place, :])
-                    spread[place, :] = spread[place, :] + taps_ref[c, r : r + 1, lanes] * masked
+                    masked = pooled * same_ref[0, :, r : r + 1]
+                    small[1 + c, 1 + r : 2 + r, wider] += column_sum(masked * plain[place, :])
+                    spread[place, :] = spread[place, :] + taps_ref[c, r : r + 1, wider] * masked
                 made = spread[...].astype(BF)
-                low[s * wide : (s + 1) * wide, lanes] = made
-                small_ref[1 + c : 2 + c, lanes] += column_sum(made)
-    for s in range(seqs):
-        base = s * wide
-        low_q[base : base + HALF, :] = jnp.zeros((HALF, span), BF)
-        low_q[base + HALF : base + HALF + rows, :] = dq_ref[s]
-        low_q[base + HALF + rows : base + wide, :] = jnp.zeros((HALF, span), BF)
-        small_ref[0:1, :] += column_sum(dq_ref[s])
-        grad = (
-            nt(low_q[base : base + wide, :], w_ref[0])
-            + nt(low_k[base : base + wide, :], w_ref[1])
-            + nt(low_v[base : base + wide, :], w_ref[2])
-        )
-        gx_ref[s] = grad if first_chunk else gx_in[s] + grad
-    heads = span // HEAD_DIM
-    lane = lax.broadcasted_iota(jnp.int32, (1, PAIR), 1) < HEAD_DIM
-    width = xt_ref.shape[0]
-    for u in range(heads // 2):
-        lanes = slice(u * PAIR, (u + 1) * PAIR)
-        stage_q = nn(xt_ref[...], low_q[:, lanes])
-        stage_k = nn(xt_ref[...], low_k[:, lanes])
-        stage_v = nn(xt_ref[...], low_v[:, lanes])
-        stage_o = gout_ref[:, lanes].astype(F32)
-        for odd in range(2):
-            t = 2 * u + odd
-            if odd == 0:
-                one = jnp.where(lane, stage_q, pltpu.roll(stage_k, HEAD_DIM, 1))
-                two = jnp.where(lane, stage_v, pltpu.roll(stage_o, HEAD_DIM, 1))
-            else:
-                one = jnp.where(lane, pltpu.roll(stage_q, HEAD_DIM, 1), stage_k)
-                two = jnp.where(lane, pltpu.roll(stage_v, HEAD_DIM, 1), stage_o)
-            stage[t, :, :PAIR] = one.astype(BF)
-            stage[t, :, PAIR:] = two.astype(BF)
-    height = gws[0].shape[2]
-    number = 0
-    for group in gws:
-        for n in range(group.shape[0]):
-            place = pl.ds(pl.multiple_of(offs[number], 16), height)
-            group[n] = stage[:, place, :]
-            number += 1
-
-
-def gather_back(first_chunk, chunk, offs, group_sizes, near, dps, proj, taps, same, xt, w, gout, gx):
-    dq, dk, dv = near
-    seqs, wide, span = dk.shape
+                low[c, 0, :, lanes] = made
+                small[1 + c, 0:1, wider] += column_sum(made)
+        total[n, 0] += nn(xt_ref[...], low_q[...])
+        total[n, 1] += nn(xt_ref[...], low[0, 0])
+        total[n, 2] += nn(xt_ref[...], low[1, 0])
+
+    @pl.when(seq == pl.num_programs(0) - 1)
+    def _():
+        heads = span // HEAD_DIM
+        lane = lax.broadcasted_iota(jnp.int32, (1, PAIR), 1) < HEAD_DIM
+
+        def place_four(four, n, u, where):
+            turned = [pltpu.roll(value, HEAD_DIM, 1) for value in four]
+            for pair in range(2):
+                one, two = 2 * pair, 2 * pair + 1
+                first = (2 * n + pair) * PAIR
+                lanes = slice(first, first + PAIR)
+                stage[2 * u, where, lanes] = jnp.where(lane, four[one], turned[two]).astype(BF)
+                stage[2 * u + 1, where, lanes] = jnp.where(lane, turned[one], four[two]).astype(BF)
+
+        for n, chunk_refs in enumerate(per_chunk):
+            gout_ref = chunk_refs[5 + blocks]
+            for u in range(heads // 2):
+                lanes = slice(u * PAIR, (u + 1) * PAIR)
+                wider = slice(n * span + u * PAIR, n * span + (u + 1) * PAIR)
+                four = [total[n, part, :, lanes] for part in range(3)]
+                four.append(gout_ref[:, lanes].astype(F32))
+                place_four(four, n, u, slice(0, width))
+                place_four(
+                    [small[part, :, wider] for part in range(4)], n, u, slice(width, width + EXTRA)
+                )
+        last = slice(width, width + EXTRA)
+        head = lax.broadcasted_iota(jnp.int32, (EXTRA, 1), 0) <= TAPS
+        for t in range(heads):
+            stage[t, last, :] = jnp.where(
+                head, stage[t, last, :].astype(F32), more_ref[...]
+            ).astype(BF)
+        height = gws[0].shape[2] - EXTRA
+        number = 0
+        for group in gws:
+            for m in range(group.shape[0]):
+                place = pl.ds(pl.multiple_of(offs[number], 16), height)
+                group[m, :, :height] = stage[:, place, :]
+                group[m, :, height:] = stage[:, last, :]
+                number += 1
+
+
+def gather_back(first_chunk, offs, group_sizes, parts, taps, same, xt, more):
+    chunks = len(parts)
+    seqs, wide, span = parts[0][1].shape
     width = xt.shape[0]
-    blocks, far_rows = len(dps), dps[0].shape[2]
+    rows = wide - 2 * HALF
+    blocks, far_rows = len(parts[0][3]), parts[0][3][0].shape[2]
     height = width // sum(group_sizes)
     heads = span // HEAD_DIM
-    gx_block = (seqs, 8, width) if first_chunk else (seqs, wide, width)
+    in_specs, operands = [], []
+    for dq, dk, dv, dps, proj, gout in parts:
+        in_specs += [pl.BlockSpec((1, wide, span), lambda s, o: (s, 0, 0))] * 2
+        in_specs += [pl.BlockSpec((1, rows, span), lambda s, o: (s, 0, 0))]
+        in_specs += [pl.BlockSpec((2, 1, far_rows, span), lambda s, o: (0, s, 0, 0))] * blocks
+        in_specs += [
+            pl.BlockSpec((1, 1, wide, span), lambda s, o: (1, s, 0, 0)),
+            pl.BlockSpec((1, 1, wide, span), lambda s, o: (2, s, 0, 0)),
+            once(gout.shape),
+        ]
+        operands += [dk, dv, dq, *dps, proj, proj, gout]
     out = pl.pallas_call(
-        partial(gather_back_kernel, blocks, len(group_sizes), first_chunk),
+        partial(gather_back_kernel, blocks, chunks, len(group_sizes)),
         grid_spec=pltpu.PrefetchScalarGridSpec(
             num_scalar_prefetch=1,
-            grid=(1,),
-            in_specs=[
-                once(dk.shape), once(dv.shape), once(dq.shape),
-                pl.BlockSpec((1, seqs, wide, span), lambda i, o: (1, 0, 0, 0)),
-                pl.BlockSpec((1, seqs, wide, span), lambda i, o: (2, 0, 0, 0)),
+            grid=(seqs,),
+            in_specs=in_specs
+            + [
+                once((2, 8, span * chunks)),
+                pl.BlockSpec((1, far_rows, 8), lambda s, o: (s, 0, 0)),
+                pl.BlockSpec((width, wide), lambda s, o: (0, s)),
+                once(more.shape),
+            ],
+            out_specs=[
+                once((size, heads, height + EXTRA, 4 * HEAD_DIM * chunks)) for size in group_sizes
             ]
-            + [once(d.shape) for d in dps]
-            + [
-                pl.BlockSpec((2, 8, span), lambda i, o: (0, 0, chunk)),
-                once(same.shape), once(xt.shape), once(w.shape), once(gout.shape),
-                once(gx_block),
-            ],
-            out_specs=[once((size, heads, height, 4 * HEAD_DIM)) for size in group_sizes]
-            + [once((seqs, wide, width)), once((24, span))],
+            + [pl.BlockSpec((2, 1, wide, span), lambda s, o: (0, s, 0, 0))] * chunks,
             scratch_shapes=[
+                pltpu.VMEM((4, EXTRA, span * chunks), F32),
                 pltpu.VMEM((wide, PAIR), F32),
                 pltpu.VMEM((wide, PAIR), F32),
-                pltpu.VMEM((seqs * wide, span), BF),
-                pltpu.VMEM((seqs * wide, span), BF),
-                pltpu.VMEM((seqs * wide, span), BF),
-                pltpu.VMEM((heads, width, 4 * HEAD_DIM), BF),
+                pltpu.VMEM((wide, span), BF),
+                pltpu.VMEM((chunks, 3, width, span), F32),
+                pltpu.VMEM((heads, width + EXTRA, 4 * HEAD_DIM * chunks), BF),
             ],
         ),
         out_shape=[
-            jax.ShapeDtypeStruct((size, heads, height, 4 * HEAD_DIM), BF) for size in group_sizes
+            jax.ShapeDtypeStruct((size, heads, height + EXTRA, 4 * HEAD_DIM * chunks), BF)
+            for size in group_sizes
         ]
-        + [
-            jax.ShapeDtypeStruct((seqs, wide, width), F32),
-            jax.ShapeDtypeStruct((24, span), F32),
+        + [jax.ShapeDtypeStruct((2, seqs, wide, span), BF)] * chunks,
+        compiler_params=params(60),
+        cost_estimate=cost(6 * chunks * seqs * wide * width * span, 12 * chunks),
+    )(offs, *operands, taps[:, :, first_chunk * span : (first_chunk + chunks) * span], same, xt, more)
+    return out[: len(group_sizes)], out[len(group_sizes) :]
+
+
+def input_grad_kernel(chunks, *refs):
+    per_chunk = [refs[3 * n : 3 * n + 3] for n in range(chunks)]
+    res_ref, mid_ref, first_ref, last_ref = refs[3 * chunks :]
+    rows = mid_ref.shape[1]
+    edge = None
+    inner = res_ref[0]
+    for dq_ref, low_ref, w_ref in per_chunk:
+        inner = inner + nt(dq_ref[0], w_ref[0])
+        for c in range(2):
+            term = nt(low_ref[c, 0], w_ref[1 + c])
+            edge = term if edge is None else edge + term
+    mid_ref[0] = inner + edge[HALF : HALF + rows]
+    first_ref[0] = edge[:HALF].astype(BF)
+    last_ref[0] = edge[HALF + rows :].astype(BF)
+
+
+def input_grad(parts, residual):
+    seqs, rows, width = residual.shape
+    wide, span = parts[0][1].shape[2:]
+    in_specs, operands = [], []
+    for dq, low, w in parts:
+        in_specs += [
+            pl.BlockSpec((1, rows, span), lambda s: (s, 0, 0)),
+            pl.BlockSpec((2, 1, wide, span), lambda s: (0, s, 0, 0)),
+            once(w.shape),
+        ]
+        operands += [dq, low, w]
+    own = pl.BlockSpec((1, rows, width), lambda s: (s, 0, 0))
+    edge = pl.BlockSpec((1, HALF, width), lambda s: (s, 0, 0))
+    return pl.pallas_call(
+        partial(input_grad_kernel, len(parts)),
+        grid=(seqs,),
+        in_specs=in_specs + [own],
+        out_specs=[own, edge, edge],
+        out_shape=[
+            jax.ShapeDtypeStruct((seqs, rows, width), F32),
+            jax.ShapeDtypeStruct((seqs, HALF, width), BF),
+            jax.ShapeDtypeStruct((seqs, HALF, width), BF),
         ],
-        compiler_params=params(48),
-        cost_estimate=cost(12 * seqs * wide * width * span, 16),
-    )(offs, dk, dv, dq, proj, proj, *dps, taps, same, xt, w, gout, gx)
-    return out[: len(group_sizes)], out[-2], out[-1]
+        compiler_params=params(60),
+        cost_estimate=cost(6 * len(parts) * seqs * wide * width * span, 16),
+    )(*operands, residual)
+
+
+def after(value, *others):
+    return lax.optimization_barrier((value,) + others)[0]
 
 
 def cycle(values, axis, shift):
@@ -645,13 +718,24 @@
     return lax.ppermute(rows, "tp", [(i + 1, i) for i in range(count - 1)])
 
 
-def gather_pieces(shard):
+def gather_columns(shard):
+    if lax.axis_size("tp") != 4:
+        return lax.all_gather(shard, "tp", axis=0, tiled=False)
+    me = lax.axis_index("tp")
+    found = [shard] + [swap(shard, "tp", mask) for mask in (1, 2, 3)]
+    odd, high = me % 2 == 1, me >= 2
+    found = [jnp.where(odd, found[n ^ 1], found[n]) for n in range(4)]
+    return jnp.stack([jnp.where(high, found[n ^ 2], found[n]) for n in range(4)])
+
+
+def gather_pieces(shard, beside):
     mine = lax.axis_index("fsdp")
     rows = shard.shape[0]
     half = rows // 2
     across = swap(shard, "fsdp", 2)
     along = swap(shard, "fsdp", 4)
-    corner = [swap(across[:half], "fsdp", 4), swap(along[half:], "fsdp", 2)]
+    onward = after(across[:half], *beside)
+    corner = [swap(onward, "fsdp", 4), swap(along[half:], "fsdp", 2)]
     own = [shard, across, along] + corner
     other = [swap(piece, "fsdp", 1) for piece in own]
     place = [
@@ -669,10 +753,12 @@
     return total
 
 
-def scatter_chain(keep, send):
-    merged = add_low(keep, swap(send, "fsdp", 1)).astype(BF)
-    merged = add_low(merged[0], *[swap(merged[n], "fsdp", 2 * n) for n in (1, 2, 3)]).astype(BF)
-    return scatter_tp(merged)
+def merge_cores(keep, send):
+    return add_low(keep, swap(send, "fsdp", 1)).astype(BF)
+
+
+def merge_chips(blocks):
+    return add_low(blocks[0], *[swap(blocks[n], "fsdp", 2 * n) for n in (1, 2, 3)]).astype(BF)
 
 
 def scatter_tp(blocks):
@@ -685,13 +771,12 @@
     return add_low(pick(0), *[cycle(pick(d), "tp", d) for d in range(1, count)])
 
 
-def sum_everywhere(values):
-    for axis in ("fsdp", "tp"):
-        mask = 1
-        while mask < lax.axis_size(axis):
-            values = values + swap(values, axis, mask)
-            mask *= 2
-    return values
+def spread_rows(whole, blocks):
+    parts, rows, cols = whole.shape
+    rows -= EXTRA
+    main = whole[:, :rows].reshape(parts, blocks, rows // blocks, cols).transpose(1, 0, 2, 3)
+    more = jnp.broadcast_to(whole[None, :, rows:], (blocks, parts, EXTRA, cols))
+    return jnp.concatenate([main, more], axis=2)
 
 
 def split_three(values):
@@ -722,28 +807,26 @@
         [qkv_bias.reshape(-1), pool_kernel.reshape(-1), up_bias.reshape(-1)]
     )
     biases = split_three(bias_values)
-    extra = -(-biases.size // (3 * local))
+    extra = -(-biases.size // (4 * local))
     packed = jnp.concatenate(
         [
-            w_qkv.reshape(shard_rows, 3 * local),
-            jnp.pad(biases.reshape(-1), (0, extra * 3 * local - biases.size)).reshape(
-                extra, 3 * local
+            jnp.concatenate([w_qkv.reshape(shard_rows, 3 * local), w_out], axis=1),
+            jnp.pad(biases.reshape(-1), (0, extra * 4 * local - biases.size)).reshape(
+                extra, 4 * local
             ),
         ],
         axis=0,
     )
-    columns = lax.all_gather(packed, "tp", axis=0, tiled=False)
-    qkv_rows = (
+    left = shift_right(inputs[rows - HALF :])
+    right = shift_left(inputs[:HALF])
+    columns = gather_columns(packed)
+    wide_rows = (
         columns[:, :shard_rows]
-        .reshape(tp, shard_rows, 3, chunks, HEAD_DIM)
+        .reshape(tp, shard_rows, 4, chunks, HEAD_DIM)
         .transpose(1, 2, 3, 0, 4)
-        .reshape(shard_rows, 3 * width)
-    )
-    if fast:
-        pieces, offs = gather_pieces(qkv_rows)
-    else:
-        pieces = [lax.all_gather(qkv_rows, "fsdp", axis=0, tiled=True)]
-        offs = jnp.zeros((1,), jnp.int32)
+        .reshape(shard_rows, 4 * width)
+    )
+    qkv_rows, out_rows = wide_rows[:, : 3 * width], wide_rows[:, 3 * width :]
     whole_bias = jnp.sum(
         columns[:, shard_rows:].reshape(tp, -1)[:, : biases.size].reshape(tp, 3, -1).astype(F32),
         axis=1,
@@ -759,31 +842,8 @@
     taps = jnp.pad(featured[3:].reshape(2, TAPS, width), ((0, 0), (0, 8 - TAPS), (0, 0)))
     bias_up = whole_bias[:, lead:].reshape(1, hidden_units)
 
-    columns, later = lax.optimization_barrier(
-        (columns, jnp.concatenate([w_up, w_down, w_out], axis=1))
-    )
-    rest = lax.all_gather(later, "tp", axis=0, tiled=False)
-    rest = jnp.concatenate(
-        [
-            rest[:, :, :hidden_local].transpose(1, 0, 2).reshape(shard_rows, hidden_units),
-            rest[:, :, hidden_local : 2 * hidden_local]
-            .transpose(1, 0, 2)
-            .reshape(shard_rows, hidden_units),
-            rest[:, :, 2 * hidden_local :]
-            .reshape(tp, shard_rows, chunks, HEAD_DIM)
-            .transpose(1, 2, 0, 3)
-            .reshape(shard_rows, width),
-        ],
-        axis=1,
-    )
-    weights = lax.all_gather(rest, "fsdp", axis=0, tiled=True)
-
-    left = shift_right(inputs[rows - HALF :])
-    right = shift_left(inputs[:HALF])
     x_wide = jnp.concatenate([left, inputs, right], axis=0).transpose(1, 0, 2)
     wide = rows + 2 * HALF
-    x_cols = x_wide.reshape(seqs * wide, width).T
-    cot = cotangent.transpose(1, 0, 2)
 
     seg_rows = segments.T
     padded = jnp.pad(seg_rows, ((0, 0), (HALF, HALF)), constant_values=-1)
@@ -809,24 +869,52 @@
         axis=2,
     ).astype(F32)
 
-    made = [
-        project(j, chunks, pieces, offs, x_wide, bias_qkv, taps, same, far_rows)
-        for j in range(chunks)
-    ]
-    slots = [
-        [pooled] + [cycle(pooled, "tp", d) for d in range(1, tp)] for _, pooled, _ in made
-    ]
-    att = [attend_forward(made[j][0], slots[j], segs) for j in range(chunks)]
+    if fast:
+        pieces, offs = gather_pieces(qkv_rows, (x_wide, same, bias_qkv, taps) + segs)
+    else:
+        pieces = [lax.all_gather(qkv_rows, "fsdp", axis=0, tiled=True)]
+        offs = jnp.zeros((1,), jnp.int32)
+
+    later = after(jnp.concatenate([w_up, w_down], axis=1), columns)
+    weights = lax.all_gather(later, "tp", axis=0, tiled=False)
+
+    made, slots, att = [], [], []
+
+    def send_pooled(j, *waits):
+        pooled = made[j][1]
+        sent = after(pooled, *waits) if waits else pooled
+        slots.append([pooled] + [cycle(sent, "tp", d) for d in range(1, tp)])
+
+    for j in range(chunks):
+        if j:
+            offs = after(offs, made[-1][1])
+        made.append(project(j, chunks, pieces, offs, x_wide, bias_qkv, taps, same, far_rows))
+        if j == 0:
+            send_pooled(0)
+    if chunks > 1:
+        send_pooled(1, made[-1][1])
+    weights = after(weights, made[-1][1], *slots[0][1:])
+    weights = lax.all_gather(weights, "fsdp", axis=0, tiled=False)
+    full_out = lax.all_gather(after(out_rows, made[0][1]), "fsdp", axis=0, tiled=True)
+    for j in range(chunks):
+        order = segs if j == 0 else segs[:2] + (after(segs[2], att[-1]),)
+        att.append(attend_forward(made[j][0], slots[j], order))
+        if j + 2 < chunks:
+            send_pooled(j + 2, att[j])
+    if shard_rows % 16:
+        weights = weights.transpose(1, 0, 2, 3).reshape(1, tp, width, 2 * hidden_local)
+
+    x_cols = after(x_wide, att[0]).reshape(seqs * wide, width).T
+    cot = after(cotangent, att[0]).transpose(1, 0, 2)
     misc = jnp.concatenate([out_bias, norm_gains, norm_shifts, jnp.zeros((2, width), F32)])
-    row_blocks = fsdp if shard_rows % 16 == 0 else 1
-    outputs, grad_residual, grad_att, grad_out, gud, grad_up_bias, small = dense(
-        att, x_wide, cot, weights, bias_up, misc, hidden_units, row_blocks
-    )
-    if row_blocks == 1:
-        gud = gud.reshape(2, fsdp, shard_rows, hidden_units).transpose(1, 0, 2, 3)
+    outputs, grad_residual, grad_att, grad_out, gud, small = dense(
+        att, x_wide, cot, full_out, weights, bias_up, misc
+    )
+    if gud.shape[0] == 1:
+        gud = spread_rows(gud[0], fsdp)
     gud = lax.psum_scatter(gud, "fsdp", scatter_dimension=0, tiled=False)
-    gud = gud.reshape(2, shard_rows, tp, hidden_local).transpose(2, 0, 1, 3)
-    gud = lax.psum_scatter(gud, "tp", scatter_dimension=0, tiled=False).astype(F32)
+    gud_parts = gud.reshape(2, shard_rows + EXTRA, tp, hidden_local).transpose(2, 0, 1, 3)
+    gud = lax.psum_scatter(gud_parts, "tp", scatter_dimension=0, tiled=False).astype(F32)
 
     if fast:
         mine = lax.axis_index("fsdp")
@@ -837,60 +925,82 @@
     else:
         group_sizes = (1,)
         out_offs = jnp.zeros((1,), jnp.int32)
-    backs = [attend_backward(made[j][0], slots[j], segs, grad_att[j]) for j in range(chunks)]
-    gx = jnp.zeros((seqs, 8, width), F32)
-    weight_grads, smalls = [], []
+    backs = []
     for j in range(chunks):
-        dq, dk, dv, dps = backs[j]
+        order = segs
+        if j:
+            waits = (backs[-1][0],) + (tuple(backs[-2][3][1:]) if j > 1 else ())
+            order = segs[:2] + (after(segs[2], *waits),)
+        dq, dk, dv, dps = attend_backward(made[j][0], slots[j], order, grad_att[j])
+        if j:
+            dps = [after(d, *backs[-1][3][1:]) for d in dps]
         arrived = [dps[0]] + [cycle(dps[d], "tp", -d) for d in range(1, tp)]
-        groups, gx, small_j = gather_back(
-            j == 0, j, out_offs, group_sizes, (dq, dk, dv), arrived,
-            made[j][0], taps, same, x_cols, made[j][2], grad_out[j], gx,
+        backs.append((dq, dk, dv, arrived, made[j][0], grad_out[j]))
+    totals, lows, merged = [], [], []
+    for low, high in ((0, chunks - 1), (chunks - 1, chunks)):
+        if low == high:
+            continue
+        cols = (high - low) * 4 * HEAD_DIM
+        more = jnp.zeros((EXTRA, cols), F32)
+        if not merged:
+            flat = small[:6].reshape(-1)
+            lines = -(-flat.size // cols)
+            flat = jnp.pad(flat, (0, lines * cols - flat.size)).reshape(lines, cols)
+            more = jnp.pad(flat, ((TAPS + 1, EXTRA - TAPS - 1 - lines), (0, 0)))
+        waits = [backs[-1][0], gud_parts]
+        groups, low_kv = gather_back(
+            low, after(out_offs, *waits), group_sizes, backs[low:high], taps, same, x_cols, more
         )
-        smalls.append(small_j)
+        lows += low_kv
         if fast:
-            weight_grads.append(scatter_chain(*groups))
+            merged.append(merge_cores(*[after(g, *backs[-1][3][1:]) for g in groups]))
         else:
-            whole = groups[0].reshape(tp, fsdp, shard_rows, 4 * HEAD_DIM).transpose(1, 0, 2, 3)
-            whole = lax.psum_scatter(whole, "fsdp", scatter_dimension=0, tiled=False)
-            weight_grads.append(scatter_tp(whole))
-
-    to_left = shift_left(gx[:, :HALF].astype(BF))
-    to_right = shift_right(gx[:, HALF + rows :].astype(BF))
-    middle = gx[:, HALF : HALF + rows] + grad_residual
+            merged.append(spread_rows(groups[0][0], fsdp))
+    middle, first, last = input_grad(
+        [(backs[n][0], lows[n], made[n][2]) for n in range(chunks)], grad_residual
+    )
+    chips = []
+    for n, blocks in enumerate(merged):
+        blocks = after(blocks, *chips) if chips else blocks
+        if fast:
+            chips.append(merge_chips(blocks))
+        else:
+            chips.append(lax.psum_scatter(blocks, "fsdp", scatter_dimension=0, tiled=False))
+    for blocks in chips:
+        if len(totals) + 1 == len(chips):
+            blocks = after(blocks, middle)
+        else:
+            blocks = after(blocks, merged[-1])
+        totals.append(scatter_tp(blocks))
+
+    first, last = after(first, chips[-1]), after(last, chips[-1])
+    to_left = shift_left(first)
+    to_right = shift_right(last)
     middle = middle.at[:, :HALF].add(to_right.astype(F32))
     middle = middle.at[:, rows - HALF :].add(to_left.astype(F32))
     grad_inputs = middle.transpose(1, 0, 2)
 
-    small_rows = jnp.concatenate(smalls, axis=1)
-    sums = sum_everywhere(
-        jnp.concatenate(
-            [small, small_rows, grad_up_bias.reshape(-1, width)],
-            axis=0,
-        )
-    )
-    grad_out_bias, grad_gains, grad_shifts = sums[0:2], sums[2:4], sums[4:6]
-    mixed = lax.dynamic_index_in_dim(
-        sums[8:32].reshape(24, chunks, tp, HEAD_DIM), place, 2, keepdims=False
-    ).reshape(24, local)
-    grad_up = lax.dynamic_slice_in_dim(sums[32:].reshape(-1), place * hidden_local, hidden_local)
-
-    stacked = jnp.stack(
-        [g.reshape(shard_rows, 4, HEAD_DIM) for g in weight_grads], axis=2
-    ).reshape(shard_rows, 4, local)
+    sums = totals[0][shard_rows + TAPS + 1 :].reshape(-1)[: 6 * width].reshape(6, width)
+    stacked = jnp.concatenate(
+        [t[: shard_rows + TAPS + 1].reshape(-1, t.shape[1] // (4 * HEAD_DIM), 4, HEAD_DIM)
+         for t in totals],
+        axis=1,
+    )
+    stacked = stacked.transpose(0, 2, 1, 3).reshape(-1, 4, local)
+    main, bias_row, tap_rows = stacked[:shard_rows], stacked[shard_rows], stacked[shard_rows + 1 :]
     return (
         outputs.transpose(1, 0, 2),
         grad_inputs,
-        stacked[:, :3],
-        mixed[:3],
-        jnp.stack([mixed[8 : 8 + TAPS], mixed[16 : 16 + TAPS]]),
-        stacked[:, 3],
-        grad_out_bias,
-        gud[0],
-        grad_up,
-        gud[1],
-        grad_gains,
-        grad_shifts,
+        main[:, :3],
+        bias_row[:3],
+        tap_rows[:, 1:3].transpose(1, 0, 2),
+        main[:, 3],
+        sums[0:2],
+        gud[0, :shard_rows],
+        gud[0, shard_rows],
+        gud[1, :shard_rows],
+        sums[2:4],
+        sums[4:6],
     )
 
 

time: 518 us -> 429 us (0.83)
  waiting for transfers between devices: 75.9 us -> 32.2 us
  blocking collectives: 18.2 us -> 0 us
  local copies, waits for them, and re-layouts: 77.2 us -> 65.8 us
  starting transfers between devices: 85.9 us -> 76.4 us
    all_gather x2 -> x3, waiting for transfers between devices: 35.3 us -> 0.27 us  [the longest x1 0.24 us: body(): weights = lax.all_gather(weights, 'fsdp', axis=0, tiled=False)]
    unnamed x186 -> x98, local copies, waits for them, and re-layouts: 50.9 us -> 30.8 us
    all_gather x1 -> x0, blocking collectives: 18.2 us -> none  [body(): columns = lax.all_gather(packed, 'tp', axis=0, tiled=False)]
    ppermute x27 -> x24, waiting for transfers between devices: 19.1 us -> 11.6 us  [cycle(): lax.ppermute(values, axis, [(i, (i + shift) % count) for i in range(count)])]
    slice x13 -> x25, local copies, waits for them, and re-layouts: 5.34 us -> 11.7 us  [the longest x3 2.67 us: body(): bias_row[:3]]
    pallas_call x3, Pallas kernels: 37 us -> 30.9 us  [the longest x2 21.4 us: gather_back(): pl.pallas_call(partial(gather_back_kernel, blocks, chunks, len(group_size...]
    ppermute x27 -> x24, starting transfers between devices: 51.2 us -> 45.7 us  [cycle(): lax.ppermute(values, axis, [(i, (i + shift) % count) for i in range(count)])]
    ppermute x26 -> x20, starting transfers between devices: 24.4 us -> 19.4 us  [swap(): return lax.ppermute(values, axis, [(i, i ^ mask) for i in range(count)])]
  transfers between devices with their start and end apart: 61 -> 53, of which waited for: 10 -> 10; matrix products, arithmetic and copies ran while one was open for 10% -> 14% of each run, Pallas kernels for 32% -> 39%
where the time goes in v3:
time: 429 us; the launch traced here: 421 us
  Pallas kernels  217 us (51%)
  starting transfers between devices  76.4 us (18%)
  local copies, waits for them, and re-layouts  65.8 us (15%)
  waiting for transfers between devices  32.2 us (8%)
  between operations  15.3 us (4%)
  other arithmetic  13.5 us (3%)
    pallas_call x3, Pallas kernels, attend_backward(): pl.pallas_call(partial(attend_backward_kernel, blocks), grid=(seqs, span...  70.5 us
    pallas_call x1, Pallas kernels, dense(): pl.pallas_call(partial(dense_kernel, chunks, steps), grid=(2 * steps,), i...  53.4 us
    pallas_call x3, Pallas kernels, attend_forward(): pl.pallas_call(partial(attend_forward_kernel, blocks), grid=(seqs, span /...  48.8 us
    ppermute x24, starting transfers between devices, cycle(): lax.ppermute(values, axis, [(i, (i + shift) % count) for i in range(count)])  45.7 us
    unnamed x98, local copies, waits for them, and re-layouts  30.8 us
    pallas_call x2, Pallas kernels, gather_back(): pl.pallas_call(partial(gather_back_kernel, blocks, chunks, len(group_size...  21.4 us
    ppermute x20, waiting for transfers between devices, swap(): return lax.ppermute(values, axis, [(i, i ^ mask) for i in range(count)])  20.3 us
    ppermute x20, starting transfers between devices, swap(): return lax.ppermute(values, axis, [(i, i ^ mask) for i in range(count)])  19.4 us
  transfers between devices with their start and end apart: 53, of which 10 were waited for; matrix products, arithmetic and copies ran while one was open for 14% of the time, Pallas kernels for 39%

profile of v3, /device:TPU:0, one launch (start us, length us, event | category | flops | bytes accessed | tf_op | source)
XLA Modules:
  0.0 420.5 jit_solution(2657786365005208540)
XLA Ops:
  12.2 5.1 %collective-permute-start = (bf16[109,768]{0,1:T(8,128)(2,1)S(1)}, bf16[109,768]{0,1:T(8,128)(2,1)S(1)}, u32[]{:S(2)}, u32[]{:S(2)}) collective-permute-start(bf16[109,768]{0,1:T(8,128)(2,1)S(1)} %pad_maximum_fusion.2), channel_id=1, source_target_pairs={{0,3},{1,2},{2,1},{3,0},{4,7},{5,6},{6,5},{7,4},{8,11},{9,10},{10,... | collective-permute-start | bytes 502280 | tf_op jit(solution)/shard_map/ppermute | solution.py:708
  18.0 1.6 copy.295
  20.7 3.3 collective-permute-start.5
  24.1 1.3 collective-permute-start.6
  30.6 4.4 %collective-permute-done.1 = bf16[109,768]{0,1:T(8,128)(2,1)S(1)} collective-permute-done((bf16[109,768]{0,1:T(8,128)(2,1)S(1)}, bf16[109,768]{0,1:T(8,128)(2,1)S(1)}, u32[]{:S(2)}, u32[]{:S(2)}) %collective-permute-start.1) | collective-permute-done | bytes 167456 | tf_op jit(solution)/shard_map/ppermute | solution.py:708
  37.1 1.6 collective-permute-start.3
  38.6 1.5 collective-permute-start.4
  42.2 1.7 maximum_bitcast_fusion.refs_10_.refs_3_
  43.9 3.5 collective-permute-done.3.refs_1_
  47.4 1.6 collective-permute-start.7
  51.1 2.4 collective-permute-done.7.refs_3_
  53.5 2.4 collective-permute-done.8.refs_4_
  56.0 1.6 slice.281
  57.6 1.7 copy.327
  59.4 4.6 %shard_map.220 = (bf16[3,2,640,256]{3,2,1,0:T(8,128)(2,1)S(1)}, bf16[2,2,128,256]{3,2,1,0:T(8,128)(2,1)S(1)}, bf16[3,768,256]{2,1,0:T(8,128)(2,1)S(1)}) custom-call(s32[10]{0:T(128)S(1)} %stack.97.offs, bf16[96,2304]{1,0:T(8,128)(2,1)S(1)} %copy.326.refs_0_, bf16[96,2304]{1,0:T(8,128)(2,1)S(1)} %collective-permute-done.3.refs_1_, ...), custom_call_target="tpu_custom_call" | custom-call | flops 1 | bytes 1 | tf_op jit(solution)/shard_map/pallas_call | solution.py:93
  64.0 1.3 copy-done.1
  67.3 2.9 collective-permute-start.15
  71.1 4.6 %shard_map.222 = (bf16[3,2,640,256]{3,2,1,0:T(8,128)(2,1)S(1)}, bf16[2,2,128,256]{3,2,1,0:T(8,128)(2,1)S(1)}, bf16[3,768,256]{2,1,0:T(8,128)(2,1)S(1)}) custom-call(s32[10]{0:T(128)S(1)} %stack.97.offs, bf16[96,2304]{1,0:T(8,128)(2,1)S(1)} %copy.326.refs_0_, bf16[96,2304]{1,0:T(8,128)(2,1)S(1)} %collective-permute-done.3.refs_1_, ...), custom_call_target="tpu_custom_call" | custom-call | flops 1 | bytes 1 | tf_op jit(solution)/shard_map/pallas_call | solution.py:93
  75.7 1.4 copy-done.2
  78.8 4.6 %shard_map.223 = (bf16[3,2,640,256]{3,2,1,0:T(8,128)(2,1)S(1)}, bf16[2,2,128,256]{3,2,1,0:T(8,128)(2,1)S(1)}, bf16[3,768,256]{2,1,0:T(8,128)(2,1)S(1)}) custom-call(s32[10]{0:T(128)S(1)} %stack.97.offs, bf16[96,2304]{1,0:T(8,128)(2,1)S(1)} %copy.326.refs_0_, bf16[96,2304]{1,0:T(8,128)(2,1)S(1)} %collective-permute-done.3.refs_1_, ...), custom_call_target="tpu_custom_call" | custom-call | flops 1 | bytes 1 | tf_op jit(solution)/shard_map/pallas_call | solution.py:93
  86.4 2.5 collective-permute-done.15.refs_2_.refs_6_
  89.0 5.8 %collective-permute-start.17 = (bf16[2,2,128,256]{3,2,1,0:T(8,128)(2,1)}, bf16[2,2,128,256]{3,2,1,0:T(8,128)(2,1)S(1)}, u32[]{:S(2)}, u32[]{:S(2)}) collective-permute-start(bf16[2,2,128,256]{3,2,1,0:T(8,128)(2,1)} %copy-done.8), channel_id=1, source_target_pairs={{0,1},{1,2},{2,3},{3,0},{4,5},{5,6},{6,7},{7,4},{8,9},{9,10},{10,1... | collective-permute-start | bytes 786440 | tf_op jit(solution)/shard_map/ppermute | solution.py:703
  96.0 2.6 collective-permute-start.19
  98.5 16.2 %shard_map.221.refs_0_ = bf16[2,512,256]{2,1,0:T(8,128)(2,1)} custom-call(bf16[3,2,640,256]{3,2,1,0:T(8,128)(2,1)} %copy-done.1, bf16[3,2,640,256]{3,2,1,0:T(8,128)(2,1)} %copy-done.1, bf16[3,2,640,256]{3,2,1,0:T(8,128)(2,1)} %copy-done.1, bf16[2,2,128,256]{3,2,1,0:T(8,128)(2,1)} %copy-done.9, ...), custom_call_target="tpu_custom_call" | custom-call | flops 1 | bytes 1 | tf_op jit(solution)/shard_map/pallas_call | solution.py:272
  114.9 2.6 collective-permute-start.21
  117.4 1.3 collective-permute-start.22
  121.6 16.3 %shard_map.224.refs_1_ = bf16[2,512,256]{2,1,0:T(8,128)(2,1)} custom-call(bf16[3,2,640,256]{3,2,1,0:T(8,128)(2,1)} %copy-done.2, bf16[3,2,640,256]{3,2,1,0:T(8,128)(2,1)} %copy-done.2, bf16[3,2,640,256]{3,2,1,0:T(8,128)(2,1)} %copy-done.2, bf16[2,2,128,256]{3,2,1,0:T(8,128)(2,1)} %copy-done.8, bf16[2,2,128,256]{3,2,1,0:T(8,128)(2,1)} %copy-done.18, ...), custom_call_target="tpu_custom_call" | custom-call | flops 1 | bytes 1 | tf_op jit(solution)/shard_map/pallas_call | solution.py:272
  138.0 1.3 copy.332
  140.2 16.2 %shard_map.225.refs_2_ = bf16[2,512,256]{2,1,0:T(8,128)(2,1)} custom-call(bf16[3,2,640,256]{3,2,1,0:T(8,128)(2,1)} %copy-done, bf16[3,2,640,256]{3,2,1,0:T(8,128)(2,1)} %copy-done, bf16[3,2,640,256]{3,2,1,0:T(8,128)(2,1)} %copy-done, bf16[2,2,128,256]{3,2,1,0:T(8,128)(2,1)} %copy-done.6, bf16[2,2,128,256]{3,2,1,0:T(8,128)(2,1)} %copy-done.15, ...), custom_call_target="tpu_custom_call" | custom-call | flops 1 | bytes 1 | tf_op jit(solution)/shard_map/pallas_call | solution.py:272
  156.7 53.4 %shard_map.226 = (bf16[2,512,768]{2,1,0:T(8,128)(2,1)}, f32[2,512,768]{2,1,0:T(8,128)}, bf16[2,512,256]{2,1,0:T(8,128)(2,1)}, bf16[2,512,256]{2,1,0:T(8,128)(2,1...) custom-call(bf16[2,512,256]{2,1,0:T(8,128)(2,1)} %shard_map.221.refs, ...), custom_call_target="tpu_custom_call" | custom-call | flops 1 | bytes 1 | tf_op jit(solution)/shard_map/pallas_call | solution.py:472
  210.1 23.5 %shard_map.227 = (bf16[2,512,256]{2,1,0:T(8,128)(2,1)}, f32[2,640,256]{2,1,0:T(8,128)}, f32[2,640,256]{2,1,0:T(8,128)}, bf16[2,2,128,256]{3,2,1,0:T(8,128)(2,1)}...) custom-call(bf16[3,2,640,256]{3,2,1,0:T(8,128)(2,1)} %copy-done.1, ...), custom_call_target="tpu_custom_call" | custom-call | flops 1 | bytes 1 | tf_op jit(solution)/shard_map/pallas_call | solution.py:294
  233.6 3.5 collective-permute-start.23
  238.0 23.5 %shard_map.228 = (bf16[2,512,256]{2,1,0:T(8,128)(2,1)}, f32[2,640,256]{2,1,0:T(8,128)}, f32[2,640,256]{2,1,0:T(8,128)}, bf16[2,2,128,256]{3,2,1,0:T(8,128)(2,1)}...) custom-call(bf16[3,2,640,256]{3,2,1,0:T(8,128)(2,1)} %copy-done.2, ...), custom_call_target="tpu_custom_call" | custom-call | flops 1 | bytes 1 | tf_op jit(solution)/shard_map/pallas_call | solution.py:294
  261.6 2.5 collective-permute-start.28
  265.4 1.4 collective-permute-start.26
  266.8 23.5 %shard_map.229 = (bf16[2,512,256]{2,1,0:T(8,128)(2,1)}, f32[2,640,256]{2,1,0:T(8,128)}, f32[2,640,256]{2,1,0:T(8,128)}, bf16[2,2,128,256]{3,2,1,0:T(8,128)(2,1)}...) custom-call(bf16[3,2,640,256]{3,2,1,0:T(8,128)(2,1)} %copy-done, ...), custom_call_target="tpu_custom_call" | custom-call | flops 1 | bytes 1 | tf_op jit(solution)/shard_map/pallas_call | solution.py:294
  291.1 1.6 collective-permute-start.30
  292.7 1.6 collective-permute-start.29
  295.5 2.5 copy.325
  298.7 3.0 reshape_reduce_scatter.3
  301.6 1.3 copy.333
  303.0 13.2 %shard_map.230 = (bf16[4,4,112,512]{3,2,1,0:T(8,128)(2,1)}, bf16[4,4,112,512]{3,2,1,0:T(8,128)(2,1)}, bf16[2,2,640,256]{3,2,1,0:T(8,128)(2,1)}, bf16[2,2,640,256]{3,2,1,0:T(8,128)(2,1)}) custom-call(s32[8]{0:T(128)} %stack.111.offs, f32[2,640,256]{2,1,0:T(8,128)} %get-tuple-element.149.refs_0_, f32[2,640,256]{2,1,0:T(8,128)} %get-tuple-element.150.refs_1_, ...), custom_call_target="tpu_custom_call" | custom-call | flops 1 | bytes 1 | tf_op jit(solution)/shard_map/pallas_call | solution.py:617
  317.7 8.2 %shard_map.231 = (bf16[4,4,112,256]{3,2,1,0:T(8,128)(2,1)}, bf16[4,4,112,256]{3,2,1,0:T(8,128)(2,1)}, bf16[2,2,640,256]{3,2,1,0:T(8,128)(2,1)}) custom-call(s32[8]{0:T(128)} %stack.111.offs, f32[2,640,256]{2,1,0:T(8,128)} %get-tuple-element.170.refs_0_, f32[2,640,256]{2,1,0:T(8,128)} %get-tuple-element.171.refs_1_, ...), custom_call_target="tpu_custom_call" | custom-call | flops 1 | bytes 1 | tf_op jit(solution)/shard_map/pallas_call | solution.py:617
  326.3 2.6 add_convert_fusion
  330.1 1.5 collective-permute-start.34
  333.6 2.8 copy.321
  336.4 9.5 %shard_map.232 = (f32[2,512,768]{2,1,0:T(8,128)}, bf16[2,64,768]{2,1,0:T(8,128)(2,1)}, bf16[2,64,768]{2,1,0:T(8,128)(2,1)}) custom-call(bf16[2,512,256]{2,1,0:T(8,128)(2,1)} %get-tuple-element.137.refs_2_.refs_0_, bf16[2,2,640,256]{3,2,1,0:T(8,128)(2,1)} %get-tuple-element.166.refs_1_, bf16[3,768,256]{2,1,0:T(8,128)(2,1)} %copy-done.10, ...), custom_call_target="tpu_custom_call" | custom-call | flops 1 | bytes 1 | tf_op jit(solution)/shard_map/pallas_call | solution.py:682
  345.9 1.4 add_convert_fusion.1
  347.3 6.7 %collective-permute-done.35 = bf16[4,112,512]{2,1,0:T(8,128)(2,1)} collective-permute-done((bf16[4,112,512]{2,1,0:T(8,128)(2,1)}, bf16[4,112,512]{2,1,0:T(8,128)(2,1)}, u32[]{:S(2)}, u32[]{:S(2)}) %collective-permute-start.35) | collective-permute-done | bytes 458784 | tf_op jit(solution)/shard_map/ppermute | solution.py:708
  354.0 1.6 fusion.2
  356.2 1.5 collective-permute-start.43
  357.8 2.8 collective-permute-start.44
  361.3 1.5 collective-permute-start.38
  362.8 3.3 collective-permute-done.42
  366.1 1.5 collective-permute-start.39
  367.7 5.7 %collective-permute-done.43 = bf16[112,512]{1,0:T(8,128)(2,1)S(1)} collective-permute-done((bf16[112,512]{1,0:T(8,128)(2,1)S(1)}, bf16[112,512]{1,0:T(8,128)(2,1)S(1)}, u32[]{:S(2)}, u32[]{:S(2)}) %collective-permute-start.43) | collective-permute-done | bytes 114720 | tf_op jit(solution)/shard_map/ppermute | solution.py:703
  373.6 5.9 %collective-permute-start.45 = (bf16[112,256]{1,0:T(8,128)(2,1)S(1)}, bf16[112,256]{1,0:T(8,128)(2,1)S(1)}, u32[]{:S(2)}, u32[]{:S(2)}) collective-permute-start(bf16[112,256]{1,0:T(8,128)(2,1)S(1)} %get-tuple-element.328), channel_id=1, source_target_pairs={{0,1},{1,2},{2,3},{3,0},{4,5},{5,6},{6,7},{7,4},{8,9},{9,10},{10,1... | collective-permute-start | bytes 172040 | tf_op jit(solution)/shard_map/ppermute | solution.py:703
  379.5 2.2 collective-permute-start.46
  381.7 2.8 collective-permute-start.47
  387.9 5.2 %collective-permute-start.40 = (bf16[2,64,768]{2,1,0:T(8,128)(2,1)}, bf16[2,64,768]{2,1,0:T(8,128)(2,1)}, u32[]{:S(2)}, u32[]{:S(2)}) collective-permute-start(bf16[2,64,768]{2,1,0:T(8,128)(2,1)} %get-tuple-element.195), channel_id=1, source_target_pairs={{0,1},{1,2},{2,3},{4,5},{5,6},{6,7},{8,9},{9,10},{10,11},{12,13},{... | collective-permute-start | bytes 589832 | tf_op jit(solution)/shard_map/ppermute | solution.py:713
  395.8 1.8 copy.323
  397.7 1.5 slice_bitcast_fusion.9
  399.2 1.6 copy.324
  407.0 4.1 copy.322
  (266 shorter events, 57.0 us)
Async XLA Ops:
  7.2 81.7 %all-gather.8.cloned.1.call-start = ((), (), s32[]{:S(2)}) async-start(), calls=%async_computation.5 | async-start | bytes 1474560 | tf_op jit(solution)/shard_map/all_gather | solution.py:879
  12.2 18.4 %collective-permute-start = (bf16[109,768]{0,1:T(8,128)(2,1)S(1)}, bf16[109,768]{0,1:T(8,128)(2,1)S(1)}, u32[]{:S(2)}, u32[]{:S(2)}) collective-permute-start(bf16[109,768]{0,1:T(8,128)(2,1)S(1)} %pad_maximum_fusion.2), channel_id=1, source_target_pairs={{0,3},{1,2},{2,1},{3,0},{4,7},{5,6},{6,5},{7,4},{8,11},{9,10},{10,... | collective-permute-start | bytes 502280 | tf_op jit(solution)/shard_map/ppermute | solution.py:708
  17.3 17.7 %collective-permute-start.1 = (bf16[109,768]{0,1:T(8,128)(2,1)S(1)}, bf16[109,768]{0,1:T(8,128)(2,1)S(1)}, u32[]{:S(2)}, u32[]{:S(2)}) collective-permute-start(bf16[109,768]{0,1:T(8,128)(2,1)S(1)} %pad_maximum_fusion.2), channel_id=1, source_target_pairs={{0,2},{1,3},{2,0},{3,1},{4,6},{5,7},{6,4},{7,5},{8,10},{9,11},{10,... | collective-permute-start | bytes 502280 | tf_op jit(solution)/shard_map/ppermute | solution.py:708
  17.3 17.7 %collective-permute-start.2 = (bf16[109,768]{0,1:T(8,128)(2,1)S(1)}, bf16[109,768]{0,1:T(8,128)(2,1)S(1)}, u32[]{:S(2)}, u32[]{:S(2)}) collective-permute-start(bf16[109,768]{0,1:T(8,128)(2,1)S(1)} %pad_maximum_fusion.2), channel_id=1, source_target_pairs={{0,1},{1,0},{2,3},{3,2},{4,5},{5,4},{6,7},{7,6},{8,9},{9,8},{10,11... | collective-permute-start | bytes 502280 | tf_op jit(solution)/shard_map/ppermute | solution.py:708
  20.7 20.6 %collective-permute-start.5 = (bf16[64,2,768]{2,0,1:T(8,128)(2,1)S(1)}, bf16[64,2,768]{2,0,1:T(8,128)(2,1)S(1)}, u32[]{:S(2)}, u32[]{:S(2)}) collective-permute-start(bf16[64,2,768]{2,0,1:T(8,128)(2,1)S(1)} %get-tuple-element.311), channel_id=1, source_target_pairs={{0,1},{1,2},{2,3},{4,5},{5,6},{6,7},{8,9},{9,10},{10,11},{12,13},{... | collective-permute-start | bytes 589832 | tf_op jit(solution)/shard_map/ppermute | solution.py:713
  24.1 18.1 %collective-permute-start.6 = (bf16[64,2,768]{2,0,1:T(8,128)(2,1)S(1)}, bf16[64,2,768]{2,0,1:T(8,128)(2,1)}, u32[]{:S(2)}, u32[]{:S(2)}) collective-permute-start(bf16[64,2,768]{2,0,1:T(8,128)(2,1)S(1)} %get-tuple-element.312), channel_id=1, source_target_pairs={{1,0},{2,1},{3,2},{5,4},{6,5},{7,6},{9,8},{10,9},{11,10},{13,12},{... | collective-permute-start | bytes 589832 | tf_op jit(solution)/shard_map/ppermute | solution.py:718
  30.0 48.8 %copy-start.5 = (f32[2,128,8]{2,1,0:T(8,128)}, f32[2,128,8]{2,1,0:T(8,128)S(1)}, u32[]{:S(2)}) copy-start(f32[2,128,8]{2,1,0:T(8,128)S(1)} %convert_element_type.117.refs_13_.refs_21_.refs_11_) | copy-start | bytes 24580
  37.1 10.3 %collective-permute-start.3 = (bf16[96,2304]{1,0:T(8,128)(2,1)S(1)}, bf16[96,2304]{1,0:T(8,128)(2,1)S(1)}, u32[]{:S(2)}, u32[]{:S(2)}) collective-permute-start(bf16[96,2304]{1,0:T(8,128)(2,1)S(1)} %copy.326.refs_0_), channel_id=1, source_target_pairs={{0,8},{4,12},{8,0},{12,4},{16,24},{20,28},{24,16},{28,20},{1,9},{5... | collective-permute-start | bytes 1327112 | tf_op jit(solution)/shard_map/ppermute | solution.py:708
  38.6 11.2 %collective-permute-start.4 = (bf16[96,2304]{1,0:T(8,128)(2,1)S(1)}, bf16[96,2304]{1,0:T(8,128)(2,1)S(1)}, u32[]{:S(2)}, u32[]{:S(2)}) collective-permute-start(bf16[96,2304]{1,0:T(8,128)(2,1)S(1)} %copy.326.refs_0_), channel_id=1, source_target_pairs={{0,16},{4,20},{8,24},{12,28},{16,0},{20,4},{24,8},{28,12},{1,17},{... | collective-permute-start | bytes 1327112 | tf_op jit(solution)/shard_map/ppermute | solution.py:708
  40.5 115.9 %all-gather.6.cloned.1.call-start = ((), (), s32[]{:S(2)}) async-start(), calls=%async_computation.2 | async-start | bytes 1327104 | tf_op jit(solution)/shard_map/all_gather | solution.py:898
  41.1 18.3 %collective-permute-start.9 = (bf16[96,2304]{1,0:T(8,128)(2,1)S(1)}, bf16[96,2304]{1,0:T(8,128)(2,1)}, u32[]{:S(2)}, u32[]{:S(2)}) collective-permute-start(bf16[96,2304]{1,0:T(8,128)(2,1)S(1)} %copy.326.refs_0_), channel_id=1, source_target_pairs={{0,4},{4,0},{8,12},{12,8},{16,20},{20,16},{24,28},{28,24},{1,5},{5... | collective-permute-start | bytes 1327112 | tf_op jit(solution)/shard_map/ppermute | solution.py:708
  43.9 34.9 %copy-start.3 = (bf16[2,640,768]{2,1,0:T(8,128)(2,1)}, bf16[2,640,768]{2,1,0:T(8,128)(2,1)S(1)}, u32[]{:S(2)}) copy-start(bf16[2,640,768]{2,1,0:T(8,128)(2,1)S(1)} %maximum_bitcast_fusion.refs_10_.refs_3_) | copy-start | bytes 5898244
  47.4 6.1 %collective-permute-start.7 = (bf16[48,2304]{1,0:T(8,128)(2,1)S(1)}, bf16[48,2304]{1,0:T(8,128)(2,1)}, u32[]{:S(2)}, u32[]{:S(2)}) collective-permute-start(bf16[48,2304]{1,0:T(8,128)(2,1)S(1)} %slice.272), channel_id=1, source_target_pairs={{0,16},{4,20},{8,24},{12,28},{16,0},{20,4},{24,8},{28,12},{1,17},{... | collective-permute-start | bytes 663560 | tf_op jit(solution)/shard_map/ppermute | solution.py:708
  49.8 6.1 %collective-permute-start.8 = (bf16[48,2304]{1,0:T(8,128)(2,1)S(1)}, bf16[48,2304]{1,0:T(8,128)(2,1)}, u32[]{:S(2)}, u32[]{:S(2)}) collective-permute-start(bf16[48,2304]{1,0:T(8,128)(2,1)S(1)} %slice.280), channel_id=1, source_target_pairs={{0,8},{4,12},{8,0},{12,4},{16,24},{20,28},{24,16},{28,20},{1,9},{5... | collective-permute-start | bytes 663560 | tf_op jit(solution)/shard_map/ppermute | solution.py:708
  50.6 8.8 %collective-permute-start.10 = (bf16[96,2304]{1,0:T(8,128)(2,1)S(1)}, bf16[96,2304]{1,0:T(8,128)(2,1)}, u32[]{:S(2)}, u32[]{:S(2)}) collective-permute-start(bf16[96,2304]{1,0:T(8,128)(2,1)S(1)} %collective-permute-done.3.refs_1_), channel_id=1, source_target_pairs={{0,4},{4,0},{8,12},{12,8},{16,20},{20,16},{24,28},{28,24},{1,5},{5... | collective-permute-start | bytes 1327112 | tf_op jit(solution)/shard_map/ppermute | solution.py:708
  50.6 8.8 %collective-permute-start.11 = (bf16[96,2304]{1,0:T(8,128)(2,1)S(1)}, bf16[96,2304]{1,0:T(8,128)(2,1)}, u32[]{:S(2)}, u32[]{:S(2)}) collective-permute-start(bf16[96,2304]{1,0:T(8,128)(2,1)S(1)} %collective-permute-done.4.refs_2_), channel_id=1, source_target_pairs={{0,4},{4,0},{8,12},{12,8},{16,20},{20,16},{24,28},{28,24},{1,5},{5... | collective-permute-start | bytes 1327112 | tf_op jit(solution)/shard_map/ppermute | solution.py:708
  53.5 5.9 %collective-permute-start.12 = (bf16[48,2304]{1,0:T(8,128)(2,1)}, bf16[48,2304]{1,0:T(8,128)(2,1)}, u32[]{:S(2)}, u32[]{:S(2)}) collective-permute-start(bf16[48,2304]{1,0:T(8,128)(2,1)} %collective-permute-done.7.refs_3_), channel_id=1, source_target_pairs={{0,4},{4,0},{8,12},{12,8},{16,20},{20,16},{24,28},{28,24},{1,5},{5... | collective-permute-start | bytes 663560 | tf_op jit(solution)/shard_map/ppermute | solution.py:708
  55.9 3.4 collective-permute-start.13
  67.1 89.5 %all-gather.10.cloned.1.call-start = ((), (), s32[]{:S(2)}) async-start(), calls=%async_computation.6 | async-start | bytes 10616832 | tf_op jit(solution)/shard_map/all_gather | solution.py:897
  67.2 19.2 %collective-permute-start.14 = (bf16[2,2,128,256]{3,2,1,0:T(8,128)(2,1)}, bf16[2,2,128,256]{3,2,1,0:T(8,128)(2,1)}, u32[]{:S(2)}, u32[]{:S(2)}) collective-permute-start(bf16[2,2,128,256]{3,2,1,0:T(8,128)(2,1)} %copy-done.9), channel_id=1, source_target_pairs={{0,1},{1,2},{2,3},{3,0},{4,5},{5,6},{6,7},{7,4},{8,9},{9,10},{10,1... | collective-permute-start | bytes 786440 | tf_op jit(solution)/shard_map/ppermute | solution.py:703
  67.3 21.7 %collective-permute-start.15 = (bf16[2,2,128,256]{3,2,1,0:T(8,128)(2,1)}, bf16[2,2,128,256]{3,2,1,0:T(8,128)(2,1)}, u32[]{:S(2)}, u32[]{:S(2)}) collective-permute-start(bf16[2,2,128,256]{3,2,1,0:T(8,128)(2,1)} %copy-done.9), channel_id=1, source_target_pairs={{0,2},{1,3},{2,0},{3,1},{4,6},{5,7},{6,4},{7,5},{8,10},{9,11},{10,... | collective-permute-start | bytes 786440 | tf_op jit(solution)/shard_map/ppermute | solution.py:703
  70.1 18.8 %collective-permute-start.16 = (bf16[2,2,128,256]{3,2,1,0:T(8,128)(2,1)}, bf16[2,2,128,256]{3,2,1,0:T(8,128)(2,1)}, u32[]{:S(2)}, u32[]{:S(2)}) collective-permute-start(bf16[2,2,128,256]{3,2,1,0:T(8,128)(2,1)} %copy-done.9), channel_id=1, source_target_pairs={{0,3},{1,0},{2,1},{3,2},{4,7},{5,4},{6,5},{7,6},{8,11},{9,8},{10,9... | collective-permute-start | bytes 786440 | tf_op jit(solution)/shard_map/ppermute | solution.py:703
  88.9 209.7 %reduce-scatter.3.cloned.1.call-start = ((), (), s32[]{:S(2)}) async-start(), calls=%async_computation.3 | async-start | bytes 12386304 | tf_op jit(solution)/shard_map/reduce_scatter | solution.py:915
  89.0 28.4 %collective-permute-start.17 = (bf16[2,2,128,256]{3,2,1,0:T(8,128)(2,1)}, bf16[2,2,128,256]{3,2,1,0:T(8,128)(2,1)S(1)}, u32[]{:S(2)}, u32[]{:S(2)}) collective-permute-start(bf16[2,2,128,256]{3,2,1,0:T(8,128)(2,1)} %copy-done.8), channel_id=1, source_target_pairs={{0,1},{1,2},{2,3},{3,0},{4,5},{5,6},{6,7},{7,4},{8,9},{9,10},{10,1... | collective-permute-start | bytes 786440 | tf_op jit(solution)/shard_map/ppermute | solution.py:703
  96.0 24.9 %collective-permute-start.18 = (bf16[2,2,128,256]{3,2,1,0:T(8,128)(2,1)}, bf16[2,2,128,256]{3,2,1,0:T(8,128)(2,1)S(1)}, u32[]{:S(2)}, u32[]{:S(2)}) collective-permute-start(bf16[2,2,128,256]{3,2,1,0:T(8,128)(2,1)} %copy-done.8), channel_id=1, source_target_pairs={{0,2},{1,3},{2,0},{3,1},{4,6},{5,7},{6,4},{7,5},{8,10},{9,11},{10,... | collective-permute-start | bytes 786440 | tf_op jit(solution)/shard_map/ppermute | solution.py:703
  96.0 24.9 %collective-permute-start.19 = (bf16[2,2,128,256]{3,2,1,0:T(8,128)(2,1)}, bf16[2,2,128,256]{3,2,1,0:T(8,128)(2,1)S(1)}, u32[]{:S(2)}, u32[]{:S(2)}) collective-permute-start(bf16[2,2,128,256]{3,2,1,0:T(8,128)(2,1)} %copy-done.8), channel_id=1, source_target_pairs={{0,3},{1,0},{2,1},{3,2},{4,7},{5,4},{6,5},{7,6},{8,11},{9,8},{10,9... | collective-permute-start | bytes 786440 | tf_op jit(solution)/shard_map/ppermute | solution.py:703
  98.5 16.3 %copy-start.7 = (bf16[2,2,128,256]{3,2,1,0:T(8,128)(2,1)S(1)}, bf16[2,2,128,256]{3,2,1,0:T(8,128)(2,1)}, u32[]{:S(2)}) copy-start(bf16[2,2,128,256]{3,2,1,0:T(8,128)(2,1)} %copy-done.6) | copy-start | bytes 786436
  98.5 20.2 %copy-start.40 = (f32[2,768]{1,0:T(2,128)S(1)}, f32[2,768]{1,0:T(2,128)}, u32[]{:S(2)}) copy-start(f32[2,768]{1,0:T(2,128)} %param.28) | copy-start | bytes 18436
  98.5 20.2 %copy-start.41 = (f32[2,768]{1,0:T(2,128)S(1)}, f32[2,768]{1,0:T(2,128)}, u32[]{:S(2)}) copy-start(f32[2,768]{1,0:T(2,128)} %param.27) | copy-start | bytes 18436
  98.5 20.2 %copy-start.42 = (f32[2,768]{1,0:T(2,128)S(1)}, f32[2,768]{1,0:T(2,128)}, u32[]{:S(2)}) copy-start(f32[2,768]{1,0:T(2,128)} %param.23) | copy-start | bytes 18436
  114.8 24.5 %collective-permute-start.20 = (bf16[2,2,128,256]{3,2,1,0:T(8,128)(2,1)S(1)}, bf16[2,2,128,256]{3,2,1,0:T(8,128)(2,1)S(1)}, u32[]{:S(2)}, u32[]{:S(2)}) collective-permute-start(bf16[2,2,128,256]{3,2,1,0:T(8,128)(2,1)S(1)} %copy-done.7), channel_id=1, source_target_pairs={{0,1},{1,2},{2,3},{3,0},{4,5},{5,6},{6,7},{7,4},{8,9},{9,10},{10,1... | collective-permute-start | bytes 786440 | tf_op jit(solution)/shard_map/ppermute | solution.py:703
  114.9 24.4 %collective-permute-start.21 = (bf16[2,2,128,256]{3,2,1,0:T(8,128)(2,1)S(1)}, bf16[2,2,128,256]{3,2,1,0:T(8,128)(2,1)S(1)}, u32[]{:S(2)}, u32[]{:S(2)}) collective-permute-start(bf16[2,2,128,256]{3,2,1,0:T(8,128)(2,1)S(1)} %copy-done.7), channel_id=1, source_target_pairs={{0,2},{1,3},{2,0},{3,1},{4,6},{5,7},{6,4},{7,5},{8,10},{9,11},{10,... | collective-permute-start | bytes 786440 | tf_op jit(solution)/shard_map/ppermute | solution.py:703
  117.4 21.9 %collective-permute-start.22 = (bf16[2,2,128,256]{3,2,1,0:T(8,128)(2,1)S(1)}, bf16[2,2,128,256]{3,2,1,0:T(8,128)(2,1)S(1)}, u32[]{:S(2)}, u32[]{:S(2)}) collective-permute-start(bf16[2,2,128,256]{3,2,1,0:T(8,128)(2,1)S(1)} %copy-done.7), channel_id=1, source_target_pairs={{0,3},{1,0},{2,1},{3,2},{4,7},{5,4},{6,5},{7,6},{8,11},{9,8},{10,9... | collective-permute-start | bytes 786440 | tf_op jit(solution)/shard_map/ppermute | solution.py:703
  121.6 16.3 %copy-start.22 = (bf16[512,2,768]{2,1,0:T(2,128)(2,1)S(1)}, bf16[512,2,768]{2,1,0:T(2,128)(2,1)}, u32[]{:S(2)}) copy-start(bf16[512,2,768]{2,1,0:T(2,128)(2,1)} %param.29) | copy-start | bytes 4718596
  210.1 201.0 %reduce-scatter.5.cloned.1.call-start = ((), (), s32[]{:S(2)}) async-start(), calls=%async_computation.4 | async-start | bytes 1720320 | tf_op jit(solution)/shard_map/reduce_scatter | solution.py:917
  233.6 28.0 %collective-permute-start.23 = (bf16[2,2,128,256]{3,2,1,0:T(8,128)(2,1)}, bf16[2,2,128,256]{3,2,1,0:T(8,128)(2,1)S(1)}, u32[]{:S(2)}, u32[]{:S(2)}) collective-permute-start(bf16[2,2,128,256]{3,2,1,0:T(8,128)(2,1)} %get-tuple-element.141), channel_id=1, source_target_pairs={{0,3},{1,0},{2,1},{3,2},{4,7},{5,4},{6,5},{7,6},{8,11},{9,8},{10,9... | collective-permute-start | bytes 786440 | tf_op jit(solution)/shard_map/ppermute | solution.py:703
  237.0 24.5 %collective-permute-start.24 = (bf16[2,2,128,256]{3,2,1,0:T(8,128)(2,1)}, bf16[2,2,128,256]{3,2,1,0:T(8,128)(2,1)S(1)}, u32[]{:S(2)}, u32[]{:S(2)}) collective-permute-start(bf16[2,2,128,256]{3,2,1,0:T(8,128)(2,1)} %get-tuple-element.142), channel_id=1, source_target_pairs={{0,2},{1,3},{2,0},{3,1},{4,6},{5,7},{6,4},{7,5},{8,10},{9,11},{10,... | collective-permute-start | bytes 786440 | tf_op jit(solution)/shard_map/ppermute | solution.py:703
  237.0 24.5 %collective-permute-start.25 = (bf16[2,2,128,256]{3,2,1,0:T(8,128)(2,1)}, bf16[2,2,128,256]{3,2,1,0:T(8,128)(2,1)S(1)}, u32[]{:S(2)}, u32[]{:S(2)}) collective-permute-start(bf16[2,2,128,256]{3,2,1,0:T(8,128)(2,1)} %get-tuple-element.143), channel_id=1, source_target_pairs={{0,1},{1,2},{2,3},{3,0},{4,5},{5,6},{6,7},{7,4},{8,9},{9,10},{10,1... | collective-permute-start | bytes 786440 | tf_op jit(solution)/shard_map/ppermute | solution.py:703
  261.5 28.8 %copy-start.26 = (bf16[2,2,128,256]{3,2,1,0:T(8,128)(2,1)}, bf16[2,2,128,256]{3,2,1,0:T(8,128)(2,1)S(1)}, u32[]{:S(2)}) copy-start(bf16[2,2,128,256]{3,2,1,0:T(8,128)(2,1)S(1)} %collective-permute-done.23.refs_4_) | copy-start | bytes 786436
  261.6 28.8 %copy-start.27 = (bf16[2,2,128,256]{3,2,1,0:T(8,128)(2,1)}, bf16[2,2,128,256]{3,2,1,0:T(8,128)(2,1)S(1)}, u32[]{:S(2)}) copy-start(bf16[2,2,128,256]{3,2,1,0:T(8,128)(2,1)S(1)} %collective-permute-done.24.refs_5_) | copy-start | bytes 786436
  261.6 28.8 %copy-start.28 = (bf16[2,2,128,256]{3,2,1,0:T(8,128)(2,1)}, bf16[2,2,128,256]{3,2,1,0:T(8,128)(2,1)S(1)}, u32[]{:S(2)}) copy-start(bf16[2,2,128,256]{3,2,1,0:T(8,128)(2,1)S(1)} %collective-permute-done.25.refs_6_) | copy-start | bytes 786436
  261.6 28.8 %collective-permute-start.28 = (bf16[2,2,128,256]{3,2,1,0:T(8,128)(2,1)}, bf16[2,2,128,256]{3,2,1,0:T(8,128)(2,1)S(1)}, u32[]{:S(2)}, u32[]{:S(2)}) collective-permute-start(bf16[2,2,128,256]{3,2,1,0:T(8,128)(2,1)} %get-tuple-element.162), channel_id=1, source_target_pairs={{0,1},{1,2},{2,3},{3,0},{4,5},{5,6},{6,7},{7,4},{8,9},{9,10},{10,1... | collective-permute-start | bytes 786440 | tf_op jit(solution)/shard_map/ppermute | solution.py:703
  264.1 26.3 %collective-permute-start.27 = (bf16[2,2,128,256]{3,2,1,0:T(8,128)(2,1)}, bf16[2,2,128,256]{3,2,1,0:T(8,128)(2,1)S(1)}, u32[]{:S(2)}, u32[]{:S(2)}) collective-permute-start(bf16[2,2,128,256]{3,2,1,0:T(8,128)(2,1)} %get-tuple-element.160), channel_id=1, source_target_pairs={{0,2},{1,3},{2,0},{3,1},{4,6},{5,7},{6,4},{7,5},{8,10},{9,11},{10,... | collective-permute-start | bytes 786440 | tf_op jit(solution)/shard_map/ppermute | solution.py:703
  265.4 25.1 %collective-permute-start.26 = (bf16[2,2,128,256]{3,2,1,0:T(8,128)(2,1)}, bf16[2,2,128,256]{3,2,1,0:T(8,128)(2,1)}, u32[]{:S(2)}, u32[]{:S(2)}) collective-permute-start(bf16[2,2,128,256]{3,2,1,0:T(8,128)(2,1)} %get-tuple-element.158), channel_id=1, source_target_pairs={{0,3},{1,0},{2,1},{3,2},{4,7},{5,4},{6,5},{7,6},{8,11},{9,8},{10,9... | collective-permute-start | bytes 786440 | tf_op jit(solution)/shard_map/ppermute | solution.py:703
  266.8 28.7 %copy-start.4 = (bf16[2,640,768]{2,1,0:T(8,128)(2,1)S(1)}, bf16[2,640,768]{2,1,0:T(8,128)(2,1)}, u32[]{:S(2)}) copy-start(bf16[2,640,768]{2,1,0:T(8,128)(2,1)} %copy-done.3) | copy-start | bytes 5898244
  290.4 25.8 %collective-permute-start.31 = (bf16[2,2,128,256]{3,2,1,0:T(8,128)(2,1)}, bf16[2,2,128,256]{3,2,1,0:T(8,128)(2,1)S(1)}, u32[]{:S(2)}, u32[]{:S(2)}) collective-permute-start(bf16[2,2,128,256]{3,2,1,0:T(8,128)(2,1)} %get-tuple-element.179), channel_id=1, source_target_pairs={{0,1},{1,2},{2,3},{3,0},{4,5},{5,6},{6,7},{7,4},{8,9},{9,10},{10,1... | collective-permute-start | bytes 786440 | tf_op jit(solution)/shard_map/ppermute | solution.py:703
  291.1 25.1 %collective-permute-start.30 = (bf16[2,2,128,256]{3,2,1,0:T(8,128)(2,1)}, bf16[2,2,128,256]{3,2,1,0:T(8,128)(2,1)S(1)}, u32[]{:S(2)}, u32[]{:S(2)}) collective-permute-start(bf16[2,2,128,256]{3,2,1,0:T(8,128)(2,1)} %get-tuple-element.177), channel_id=1, source_target_pairs={{0,2},{1,3},{2,0},{3,1},{4,6},{5,7},{6,4},{7,5},{8,10},{9,11},{10,... | collective-permute-start | bytes 786440 | tf_op jit(solution)/shard_map/ppermute | solution.py:703
  292.7 23.5 %collective-permute-start.29 = (bf16[2,2,128,256]{3,2,1,0:T(8,128)(2,1)}, bf16[2,2,128,256]{3,2,1,0:T(8,128)(2,1)S(1)}, u32[]{:S(2)}, u32[]{:S(2)}) collective-permute-start(bf16[2,2,128,256]{3,2,1,0:T(8,128)(2,1)} %get-tuple-element.175), channel_id=1, source_target_pairs={{0,3},{1,0},{2,1},{3,2},{4,7},{5,4},{6,5},{7,6},{8,11},{9,8},{10,9... | collective-permute-start | bytes 786440 | tf_op jit(solution)/shard_map/ppermute | solution.py:703
  316.3 10.0 %collective-permute-start.33 = (bf16[4,4,112,512]{3,2,1,0:T(8,128)(2,1)}, bf16[4,4,112,512]{3,2,1,0:T(8,128)(2,1)}, u32[]{:S(2)}, u32[]{:S(2)}) collective-permute-start(bf16[4,4,112,512]{3,2,1,0:T(8,128)(2,1)} %get-tuple-element.193), channel_id=1, source_target_pairs={{0,4},{4,0},{8,12},{12,8},{16,20},{20,16},{24,28},{28,24},{1,5},{5... | collective-permute-start | bytes 5505032 | tf_op jit(solution)/shard_map/ppermute | solution.py:708
  325.9 20.0 %collective-permute-start.32 = (bf16[4,4,112,256]{3,2,1,0:T(8,128)(2,1)}, bf16[4,4,112,256]{3,2,1,0:T(8,128)(2,1)}, u32[]{:S(2)}, u32[]{:S(2)}) collective-permute-start(bf16[4,4,112,256]{3,2,1,0:T(8,128)(2,1)} %get-tuple-element.189), channel_id=1, source_target_pairs={{0,4},{4,0},{8,12},{12,8},{16,20},{20,16},{24,28},{28,24},{1,5},{5... | collective-permute-start | bytes 2752520 | tf_op jit(solution)/shard_map/ppermute | solution.py:708
  330.1 17.2 %collective-permute-start.34 = (bf16[4,112,512]{2,1,0:T(8,128)(2,1)}, bf16[4,112,512]{2,1,0:T(8,128)(2,1)}, u32[]{:S(2)}, u32[]{:S(2)}) collective-permute-start(bf16[4,112,512]{2,1,0:T(8,128)(2,1)} %get-tuple-element.308), channel_id=1, source_target_pairs={{0,8},{4,12},{8,0},{12,4},{16,24},{20,28},{24,16},{28,20},{1,9},{5... | collective-permute-start | bytes 1376264 | tf_op jit(solution)/shard_map/ppermute | solution.py:708
  331.6 22.5 %collective-permute-start.35 = (bf16[4,112,512]{2,1,0:T(8,128)(2,1)}, bf16[4,112,512]{2,1,0:T(8,128)(2,1)}, u32[]{:S(2)}, u32[]{:S(2)}) collective-permute-start(bf16[4,112,512]{2,1,0:T(8,128)(2,1)} %get-tuple-element.310), channel_id=1, source_target_pairs={{0,16},{4,20},{8,24},{12,28},{16,0},{20,4},{24,8},{28,12},{1,17},{... | collective-permute-start | bytes 1376264 | tf_op jit(solution)/shard_map/ppermute | solution.py:708
  332.3 21.7 %collective-permute-start.36 = (bf16[4,112,512]{2,1,0:T(8,128)(2,1)}, bf16[4,112,512]{2,1,0:T(8,128)(2,1)}, u32[]{:S(2)}, u32[]{:S(2)}) collective-permute-start(bf16[4,112,512]{2,1,0:T(8,128)(2,1)} %get-tuple-element.309), channel_id=1, source_target_pairs={{0,24},{4,28},{8,16},{12,20},{16,8},{20,12},{24,0},{28,4},{1,25},{... | collective-permute-start | bytes 1376264 | tf_op jit(solution)/shard_map/ppermute | solution.py:708
  355.6 10.5 %collective-permute-start.42 = (bf16[112,512]{1,0:T(8,128)(2,1)S(1)}, bf16[112,512]{1,0:T(8,128)(2,1)S(1)}, u32[]{:S(2)}, u32[]{:S(2)}) collective-permute-start(bf16[112,512]{1,0:T(8,128)(2,1)S(1)} %get-tuple-element.322), channel_id=1, source_target_pairs={{0,1},{1,2},{2,3},{3,0},{4,5},{5,6},{6,7},{7,4},{8,9},{9,10},{10,1... | collective-permute-start | bytes 344072 | tf_op jit(solution)/shard_map/ppermute | solution.py:703
  356.2 17.1 %collective-permute-start.43 = (bf16[112,512]{1,0:T(8,128)(2,1)S(1)}, bf16[112,512]{1,0:T(8,128)(2,1)S(1)}, u32[]{:S(2)}, u32[]{:S(2)}) collective-permute-start(bf16[112,512]{1,0:T(8,128)(2,1)S(1)} %get-tuple-element.324), channel_id=1, source_target_pairs={{0,2},{1,3},{2,0},{3,1},{4,6},{5,7},{6,4},{7,5},{8,10},{9,11},{10,... | collective-permute-start | bytes 344072 | tf_op jit(solution)/shard_map/ppermute | solution.py:703
  357.8 15.6 %collective-permute-start.44 = (bf16[112,512]{1,0:T(8,128)(2,1)S(1)}, bf16[112,512]{1,0:T(8,128)(2,1)S(1)}, u32[]{:S(2)}, u32[]{:S(2)}) collective-permute-start(bf16[112,512]{1,0:T(8,128)(2,1)S(1)} %get-tuple-element.323), channel_id=1, source_target_pairs={{0,3},{1,0},{2,1},{3,2},{4,7},{5,4},{6,5},{7,6},{8,11},{9,8},{10,9... | collective-permute-start | bytes 344072 | tf_op jit(solution)/shard_map/ppermute | solution.py:703
  360.7 12.8 %collective-permute-start.37 = (bf16[4,112,256]{2,1,0:T(8,128)(2,1)S(1)}, bf16[4,112,256]{2,1,0:T(8,128)(2,1)S(1)}, u32[]{:S(2)}, u32[]{:S(2)}) collective-permute-start(bf16[4,112,256]{2,1,0:T(8,128)(2,1)S(1)} %get-tuple-element.313), channel_id=1, source_target_pairs={{0,8},{4,12},{8,0},{12,4},{16,24},{20,28},{24,16},{28,20},{1,9},{5... | collective-permute-start | bytes 688136 | tf_op jit(solution)/shard_map/ppermute | solution.py:708
  361.3 12.1 %collective-permute-start.38 = (bf16[4,112,256]{2,1,0:T(8,128)(2,1)S(1)}, bf16[4,112,256]{2,1,0:T(8,128)(2,1)S(1)}, u32[]{:S(2)}, u32[]{:S(2)}) collective-permute-start(bf16[4,112,256]{2,1,0:T(8,128)(2,1)S(1)} %get-tuple-element.315), channel_id=1, source_target_pairs={{0,16},{4,20},{8,24},{12,28},{16,0},{20,4},{24,8},{28,12},{1,17},{... | collective-permute-start | bytes 688136 | tf_op jit(solution)/shard_map/ppermute | solution.py:708
  366.1 7.3 %collective-permute-start.39 = (bf16[4,112,256]{2,1,0:T(8,128)(2,1)S(1)}, bf16[4,112,256]{2,1,0:T(8,128)(2,1)S(1)}, u32[]{:S(2)}, u32[]{:S(2)}) collective-permute-start(bf16[4,112,256]{2,1,0:T(8,128)(2,1)S(1)} %get-tuple-element.314), channel_id=1, source_target_pairs={{0,24},{4,28},{8,16},{12,20},{16,8},{20,12},{24,0},{28,4},{1,25},{... | collective-permute-start | bytes 688136 | tf_op jit(solution)/shard_map/ppermute | solution.py:708
  373.6 19.5 %collective-permute-start.45 = (bf16[112,256]{1,0:T(8,128)(2,1)S(1)}, bf16[112,256]{1,0:T(8,128)(2,1)S(1)}, u32[]{:S(2)}, u32[]{:S(2)}) collective-permute-start(bf16[112,256]{1,0:T(8,128)(2,1)S(1)} %get-tuple-element.328), channel_id=1, source_target_pairs={{0,1},{1,2},{2,3},{3,0},{4,5},{5,6},{6,7},{7,4},{8,9},{9,10},{10,1... | collective-permute-start | bytes 172040 | tf_op jit(solution)/shard_map/ppermute | solution.py:703
  379.5 13.6 %collective-permute-start.46 = (bf16[112,256]{1,0:T(8,128)(2,1)S(1)}, bf16[112,256]{1,0:T(8,128)(2,1)S(1)}, u32[]{:S(2)}, u32[]{:S(2)}) collective-permute-start(bf16[112,256]{1,0:T(8,128)(2,1)S(1)} %get-tuple-element.330), channel_id=1, source_target_pairs={{0,2},{1,3},{2,0},{3,1},{4,6},{5,7},{6,4},{7,5},{8,10},{9,11},{10,... | collective-permute-start | bytes 172040 | tf_op jit(solution)/shard_map/ppermute | solution.py:703
  381.7 11.4 %collective-permute-start.47 = (bf16[112,256]{1,0:T(8,128)(2,1)S(1)}, bf16[112,256]{1,0:T(8,128)(2,1)S(1)}, u32[]{:S(2)}, u32[]{:S(2)}) collective-permute-start(bf16[112,256]{1,0:T(8,128)(2,1)S(1)} %get-tuple-element.329), channel_id=1, source_target_pairs={{0,3},{1,0},{2,1},{3,2},{4,7},{5,4},{6,5},{7,6},{8,11},{9,8},{10,9... | collective-permute-start | bytes 172040 | tf_op jit(solution)/shard_map/ppermute | solution.py:703
  386.6 19.4 %collective-permute-start.41 = (bf16[2,64,768]{2,1,0:T(8,128)(2,1)}, bf16[2,64,768]{2,1,0:T(8,128)(2,1)}, u32[]{:S(2)}, u32[]{:S(2)}) collective-permute-start(bf16[2,64,768]{2,1,0:T(8,128)(2,1)} %get-tuple-element.197), channel_id=1, source_target_pairs={{1,0},{2,1},{3,2},{5,4},{6,5},{7,6},{9,8},{10,9},{11,10},{13,12},{... | collective-permute-start | bytes 589832 | tf_op jit(solution)/shard_map/ppermute | solution.py:718
  387.9 17.1 %collective-permute-start.40 = (bf16[2,64,768]{2,1,0:T(8,128)(2,1)}, bf16[2,64,768]{2,1,0:T(8,128)(2,1)}, u32[]{:S(2)}, u32[]{:S(2)}) collective-permute-start(bf16[2,64,768]{2,1,0:T(8,128)(2,1)} %get-tuple-element.195), channel_id=1, source_target_pairs={{0,1},{1,2},{2,3},{4,5},{5,6},{6,7},{8,9},{9,10},{10,11},{12,13},{... | collective-permute-start | bytes 589832 | tf_op jit(solution)/shard_map/ppermute | solution.py:713
  (32 other events, 112.0 us)
Sparse Core Ops, SparseCore 0:
  40.6 28.8 all-gather.7
  72.0 23.8 all-gather.5
  97.8 58.8 all-gather.9
  210.2 84.3 reduce-scatter.2
  336.5 37.4 reduce-scatter.4

commit v4 on v3

--- a/solution.py
+++ b/solution.py
@@ -15,6 +15,7 @@
 MARGIN = TAPS // 2
 PAIR = 2 * HEAD_DIM
 QB = 128
+SB = 128
 NEAR = QB + 2 * HALF
 EXTRA = 16
 RC = 256
@@ -60,13 +61,16 @@
         w_ref[0, pl.ds(pl.multiple_of(offs[n], 16), rows), :] = pieces[n][...]
     seqs, wide, _ = x_ref.shape
     far_rows = pooled_ref.shape[2]
-    for s in range(seqs):
-        made = (nn(x_ref[s], w_ref[0]) + bias_ref[0]).astype(BF)
-        out_ref[0, s] = made
-        for half in range(plain.shape[1]):
-            plain[s, half] = made[:, half * PAIR : (half + 1) * PAIR].astype(F32)
-
-    @pl.when(part > 0)
+
+    @pl.when(part < 3)
+    def _():
+        for s in range(seqs):
+            made = (nn(x_ref[s], w_ref[0]) + bias_ref[0]).astype(BF)
+            out_ref[0, s] = made
+            for half in range(plain.shape[1]):
+                plain[s, half] = made[:, half * PAIR : (half + 1) * PAIR].astype(F32)
+
+    @pl.when((part > 0) & (part < 3))
     def _():
         for s in range(seqs):
             for half in range(plain.shape[1]):
@@ -87,23 +91,26 @@
     def piece_spec(piece):
         return pl.BlockSpec((piece.shape[0], span), lambda c, o: (0, c * chunks + chunk))
 
+    def three(c):
+        return jnp.minimum(c, 2)
+
     def kv(c):
-        return jnp.maximum(c - 1, 0)
+        return jnp.maximum(three(c) - 1, 0)
 
     return pl.pallas_call(
         partial(project_kernel, len(pieces)),
         grid_spec=pltpu.PrefetchScalarGridSpec(
             num_scalar_prefetch=1,
-            grid=(3,),
+            grid=(4,),
             in_specs=[piece_spec(p) for p in pieces]
             + [
                 once(x_wide.shape),
-                pl.BlockSpec((1, 1, span), lambda c, o: (c, 0, chunk)),
+                pl.BlockSpec((1, 1, span), lambda c, o: (three(c), 0, chunk)),
                 pl.BlockSpec((1, 8, span), lambda c, o: (kv(c), 0, chunk)),
                 once(same.shape),
             ],
             out_specs=[
-                pl.BlockSpec((1, seqs, wide, span), lambda c, o: (c, 0, 0, 0)),
+                pl.BlockSpec((1, seqs, wide, span), lambda c, o: (three(c), 0, 0, 0)),
                 pl.BlockSpec((1, seqs, far_rows, span), lambda c, o: (kv(c), 0, 0, 0)),
                 pl.BlockSpec((1, width, span), lambda c, o: (c, 0, 0)),
             ],
@@ -112,7 +119,7 @@
         out_shape=[
             jax.ShapeDtypeStruct((3, seqs, wide, span), BF),
             jax.ShapeDtypeStruct((2, seqs, far_rows, span), BF),
-            jax.ShapeDtypeStruct((3, width, span), BF),
+            jax.ShapeDtypeStruct((4, width, span), BF),
         ],
         compiler_params=params(32),
         cost_estimate=cost(6 * seqs * wide * width * span, 8),
@@ -136,9 +143,14 @@
     return lane < HEAD_DIM if head == 0 else lane >= HEAD_DIM
 
 
-def softmax_block(query, keys_near, keys_far, bias_near, bias_far):
-    near = nt(query, keys_near) + bias_near
-    far = nt(query, keys_far) + bias_far
+def fold_lanes(*arrays):
+    parts = [a[:, n : n + PAIR] for a in arrays for n in range(0, a.shape[1], PAIR)]
+    while len(parts) > 1:
+        parts = [sum(parts[n : n + 2]) for n in range(0, len(parts), 2)]
+    return parts[0]
+
+
+def softmax_rows(near, far):
     top = jnp.maximum(
         jnp.max(near, axis=-1, keepdims=True), jnp.max(far, axis=-1, keepdims=True)
     )
@@ -149,6 +161,15 @@
     return near * inverse, far * inverse
 
 
+def stack_heads(rows, stacked):
+    for first in range(0, rows.shape[0], QB):
+        part = rows[first : first + QB]
+        for head in range(2):
+            stacked[2 * first + head * QB : 2 * first + (head + 1) * QB, :] = jnp.where(
+                head_mask(head), part, BF(0)
+            )
+
+
 def join_slots(slots, joined):
     rows = slots[0].shape[1]
     for n, slot in enumerate(slots):
@@ -157,35 +178,50 @@
 
 def attend_forward_kernel(blocks, q_ref, k_ref, v_ref, *refs):
     pk, pv = refs[:blocks], refs[blocks : 2 * blocks]
-    segq, segk, cen, out_ref, near_bias, far_bias, far_keys, far_values = refs[2 * blocks :]
+    segq, segk, cen, out_ref = refs[2 * blocks : 2 * blocks + 4]
+    near_bias, far_bias, far_keys, far_values, query, far_scores, far_probs = refs[
+        2 * blocks + 4 :
+    ]
 
     @pl.when(pl.program_id(1) == 0)
     def _():
         fill_masks(segq, segk, cen, near_bias, far_bias)
 
+    rows = out_ref.shape[1]
     join_slots(pk, far_keys)
     join_slots(pv, far_values)
-    for first in range(0, out_ref.shape[1], QB):
-        block = slice(first, first + QB)
+    stack_heads(q_ref[0, HALF : HALF + rows, :] * BF(SCALE), query)
+    far_scores[...] = nt(query[...], far_keys[...])
+    outs = []
+    for first in range(0, rows, QB):
         span = slice(first, first + NEAR)
-        query = q_ref[0, HALF + first : HALF + first + QB, :] * BF(SCALE)
-        halves = []
-        for head in range(2):
-            picked = jnp.where(head_mask(head), query, BF(0))
-            near, far = softmax_block(
-                picked, k_ref[0, span, :], far_keys[...], near_bias[block, :], far_bias[block, :]
+        pair = slice(2 * first, 2 * first + 2 * QB)
+        near_all = nt(query[pair, :], k_ref[0, span, :])
+        lows = []
+        for part in range(0, 2 * QB, SB):
+            source = first + part % QB
+            near, far = softmax_rows(
+                near_all[part : part + SB] + near_bias[source : source + SB, :],
+                far_scores[2 * first + part : 2 * first + part + SB, :]
+                + far_bias[source : source + SB, :],
             )
-            halves.append(
-                nn(near.astype(BF), v_ref[0, span, :]) + nn(far.astype(BF), far_values[...])
-            )
-        out_ref[0, block, :] = jnp.where(head_mask(0), halves[0], halves[1]).astype(BF)
+            far_probs[2 * first + part : 2 * first + part + SB, :] = far.astype(BF)
+            lows.append(near.astype(BF))
+        outs.append(nn(jnp.concatenate(lows, axis=0), v_ref[0, span, :]))
+    far_out = nn(far_probs[...], far_values[...])
+    for n, first in enumerate(range(0, rows, QB)):
+        both = outs[n] + far_out[2 * first : 2 * first + 2 * QB]
+        out_ref[0, first : first + QB, :] = jnp.where(head_mask(0), both[:QB], both[QB:]).astype(BF)
 
 
 def attend_backward_kernel(blocks, q_ref, k_ref, v_ref, *refs):
     pk, pv = refs[:blocks], refs[blocks : 2 * blocks]
     segq, segk, cen, grad_ref, dq_ref, dk_ref, dv_ref = refs[2 * blocks : 2 * blocks + 7]
     dp_refs = refs[2 * blocks + 7 : 3 * blocks + 7]
-    near_bias, far_bias, far_keys, far_values, far_probs, far_grads = refs[3 * blocks + 7 :]
+    (
+        near_bias, far_bias, far_keys, far_values,
+        query, far_scores, far_probs, grad, far_dots, far_grads,
+    ) = refs[3 * blocks + 7 :]
 
     @pl.when(pl.program_id(1) == 0)
     def _():
@@ -194,45 +230,49 @@
     rows = dq_ref.shape[1]
     join_slots(pk, far_keys)
     join_slots(pv, far_values)
+    stack_heads(q_ref[0, HALF : HALF + rows, :] * BF(SCALE), query)
+    stack_heads(grad_ref[0], grad)
+    far_scores[...] = nt(query[...], far_keys[...])
+    far_dots[...] = nt(grad[...], far_values[...])
     dk_ref[...] = jnp.zeros_like(dk_ref)
     dv_ref[...] = jnp.zeros_like(dv_ref)
-    pieces = []
-    for head in range(2):
-        mask = head_mask(head)
-        for first in range(0, rows, QB):
-            block = slice(first, first + QB)
-            span = slice(first, first + NEAR)
-            query = jnp.where(
-                mask, q_ref[0, HALF + first : HALF + first + QB, :] * BF(SCALE), BF(0)
+    dqs = []
+    for first in range(0, rows, QB):
+        span = slice(first, first + NEAR)
+        pair = slice(2 * first, 2 * first + 2 * QB)
+        near_all = nt(query[pair, :], k_ref[0, span, :])
+        dots_all = nt(grad[pair, :], v_ref[0, span, :])
+        lows, grads = [], []
+        for part in range(0, 2 * QB, SB):
+            source = first + part % QB
+            here = slice(2 * first + part, 2 * first + part + SB)
+            near, far = softmax_rows(
+                near_all[part : part + SB] + near_bias[source : source + SB, :],
+                far_scores[here, :] + far_bias[source : source + SB, :],
             )
-            grad = jnp.where(mask, grad_ref[0, block, :], BF(0))
-            near, far = softmax_block(
-                query, k_ref[0, span, :], far_keys[...], near_bias[block, :], far_bias[block, :]
+            near_dot, far_dot = dots_all[part : part + SB], far_dots[here, :]
+            row_dot = jnp.sum(
+                fold_lanes(near * near_dot, far * far_dot), axis=-1, keepdims=True
             )
-            grad_near = nt(grad, v_ref[0, span, :])
-            grad_far = nt(grad, far_values[...])
-            row_dot = jnp.sum(near * grad_near, axis=-1, keepdims=True) + jnp.sum(
-                far * grad_far, axis=-1, keepdims=True
-            )
-            ds_near = (near * (grad_near - row_dot)).astype(BF)
-            ds_far = (far * (grad_far - row_dot)).astype(BF)
-            far_probs[block, :] = far.astype(BF)
-            far_grads[block, :] = ds_far
-            dq = (nn(ds_near, k_ref[0, span, :]) + nn(ds_far, far_keys[...])) * SCALE
-            if head == 0:
-                dq_ref[0, block, :] = dq.astype(BF)
-            else:
-                dq_ref[0, block, :] = jnp.where(mask, dq.astype(BF), dq_ref[0, block, :])
-            dk_ref[0, span, :] += tn(ds_near, query)
-            dv_ref[0, span, :] += tn(near.astype(BF), grad)
-        query = jnp.where(mask, q_ref[0, HALF : HALF + rows, :] * BF(SCALE), BF(0))
-        grad = jnp.where(mask, grad_ref[0], BF(0))
-        pieces.append((tn(far_grads[...], query), tn(far_probs[...], grad)))
+            far_probs[here, :] = far.astype(BF)
+            far_grads[here, :] = (far * (far_dot - row_dot)).astype(BF)
+            lows.append(near.astype(BF))
+            grads.append((near * (near_dot - row_dot)).astype(BF))
+        low = jnp.concatenate(lows, axis=0)
+        ds = jnp.concatenate(grads, axis=0)
+        dqs.append(nn(ds, k_ref[0, span, :]))
+        dk_ref[0, span, :] += nn(query[pair, :].T, ds).T
+        dv_ref[0, span, :] += nn(grad[pair, :].T, low).T
+    far_dq = nn(far_grads[...], far_keys[...])
+    for n, first in enumerate(range(0, rows, QB)):
+        both = (dqs[n] + far_dq[2 * first : 2 * first + 2 * QB]) * SCALE
+        dq_ref[0, first : first + QB, :] = jnp.where(head_mask(0), both[:QB], both[QB:]).astype(BF)
+    dpk = nn(query[...].T, far_grads[...]).T.astype(BF)
+    dpv = nn(grad[...].T, far_probs[...]).T.astype(BF)
     far_rows = dp_refs[0].shape[2]
     for n, ref in enumerate(dp_refs):
-        span = slice(n * far_rows, (n + 1) * far_rows)
-        for c in range(2):
-            ref[c, 0] = jnp.where(head_mask(0), pieces[0][c][span], pieces[1][c][span]).astype(BF)
+        ref[0, 0] = dpk[n * far_rows : (n + 1) * far_rows]
+        ref[1, 0] = dpv[n * far_rows : (n + 1) * far_rows]
 
 
 def attention_specs(wide, blocks, far_rows):
@@ -261,6 +301,9 @@
         pltpu.VMEM((rows, far_all), F32),
         pltpu.VMEM((far_all, PAIR), BF),
         pltpu.VMEM((far_all, PAIR), BF),
+        pltpu.VMEM((2 * rows, PAIR), BF),
+        pltpu.VMEM((2 * rows, far_all), F32),
+        pltpu.VMEM((2 * rows, far_all), BF),
     ]
 
 
@@ -299,7 +342,11 @@
         out_shape=[jax.ShapeDtypeStruct((seqs, rows, span), BF), wide_shape, wide_shape]
         + [far_shape] * blocks,
         scratch_shapes=attention_scratch(rows, blocks * far_rows)
-        + [pltpu.VMEM((rows, blocks * far_rows), BF)] * 2,
+        + [
+            pltpu.VMEM((2 * rows, PAIR), BF),
+            pltpu.VMEM((2 * rows, blocks * far_rows), F32),
+            pltpu.VMEM((2 * rows, blocks * far_rows), BF),
+        ],
         compiler_params=params(60),
         cost_estimate=cost(40 * 64 * cells, 16, cells),
     )(proj, proj, proj, *slots, *slots, *segs, grad)
@@ -326,9 +373,9 @@
 
 
 def dense_kernel(chunks, steps, *refs):
-    att = refs[:chunks]
-    x_ref, cot_ref, wout_ref, up_blk, down_blk, bup_ref, misc_ref = refs[chunks : chunks + 7]
-    outs = refs[chunks + 7 :]
+    att, wout = refs[:chunks], refs[chunks : 2 * chunks]
+    x_ref, cot_ref, up_blk, down_blk, bup_ref, misc_ref = refs[2 * chunks : 2 * chunks + 6]
+    outs = refs[2 * chunks + 6 :]
     out_ref, gres_ref = outs[:2]
     gatt = outs[2 : 2 + chunks]
     gout = outs[2 + chunks : 2 + 2 * chunks]
@@ -355,7 +402,7 @@
             branch = bias_one
             for j in range(chunks):
                 branch = branch + nt(
-                    att[j][s, row : row + RC, :], wout_ref[:, j * span : (j + 1) * span]
+                    att[j][s, row : row + RC, :], wout[j][0]
                 )
             n_one, inv = norm_stats(
                 x_ref[s, HALF + row : HALF + row + RC, :].astype(F32) + branch
@@ -433,13 +480,13 @@
             small_ref[4:5, :] += column_sum(grad)
             for j in range(chunks):
                 gatt[j][s, row : row + RC, :] = nn(
-                    low, wout_ref[:, j * span : (j + 1) * span]
+                    low, wout[j][0]
                 ).astype(BF)
         for j in range(chunks):
             gout[j][...] = nn(flow_t[...], att[j][...].reshape(total, span)).astype(BF)
 
 
-def dense(att, x_wide, cot, w_out, weights, bias_up, misc):
+def dense(att, projected_weights, x_wide, cot, weights, bias_up, misc):
     chunks = len(att)
     seqs, rows, width = cot.shape
     total = seqs * rows
@@ -474,9 +521,14 @@
         grid=(2 * steps,),
         in_specs=[once(a.shape) for a in att]
         + [
+            pl.BlockSpec(
+                (1, width, span), lambda i: (3, 0, 0), pipeline_mode=pl.Buffered(1)
+            )
+        ]
+        * chunks
+        + [
             once(x_wide.shape),
             once(cot.shape),
-            once(w_out.shape),
             pl.BlockSpec((row_blocks, None, height, units), lambda i: (0, which(i), 0, 0)),
             pl.BlockSpec((row_blocks, None, height, units), lambda i: (0, which(i), 0, 1)),
             pl.BlockSpec((1, units), lambda i: (0, which(i))),
@@ -497,7 +549,7 @@
         ],
         compiler_params=params(63),
         cost_estimate=cost(1, 1),
-    )(*att, x_wide, cot, w_out, weights, weights, bias_up, misc)
+    )(*att, *projected_weights, x_wide, cot, weights, weights, bias_up, misc)
     return (
         out[0], out[1], out[2 : 2 + chunks], out[2 + chunks : 2 + 2 * chunks], out[-2], out[-1]
     )
@@ -674,7 +726,9 @@
         in_specs += [
             pl.BlockSpec((1, rows, span), lambda s: (s, 0, 0)),
             pl.BlockSpec((2, 1, wide, span), lambda s: (0, s, 0, 0)),
-            once(w.shape),
+            pl.BlockSpec(
+                (3,) + w.shape[1:], lambda s: (0, 0, 0), pipeline_mode=pl.Buffered(1)
+            ),
         ]
         operands += [dq, low, w]
     own = pl.BlockSpec((1, rows, width), lambda s: (s, 0, 0))
@@ -698,9 +752,56 @@
     return lax.optimization_barrier((value,) + others)[0]
 
 
-def cycle(values, axis, shift):
-    count = lax.axis_size(axis)
-    return lax.ppermute(values, axis, [(i, (i + shift) % count) for i in range(count)])
+def finish_kernel(terms, chunks, *refs):
+    groups = [refs[:terms], refs[terms : 2 * terms]]
+    qkv_ref, out_ref, extra_ref, sums_ref = refs[2 * terms :]
+    totals = []
+    for group in groups:
+        total = group[0][...].astype(F32)
+        for ref in group[1:]:
+            total = total + ref[...].astype(F32)
+        totals.append(total)
+    rows = out_ref.shape[0]
+    sums_ref[...] = totals[0][rows:]
+    lane = lax.broadcasted_iota(jnp.int32, (1, PAIR), 1) < HEAD_DIM
+    first_count = totals[0].shape[1] // (4 * HEAD_DIM)
+
+    def part(chunk, which, high):
+        source = totals[0] if chunk < first_count else totals[1]
+        chunk = chunk if chunk < first_count else chunk - first_count
+        tile = 2 * chunk + which // 2
+        values = source[:, tile * PAIR : (tile + 1) * PAIR]
+        return values if which % 2 == high else pltpu.roll(values, HEAD_DIM, 1)
+
+    for which in range(4):
+        for chunk in range(0, chunks, 2):
+            first = chunk * HEAD_DIM
+            if chunk + 1 < chunks:
+                made = jnp.where(lane, part(chunk, which, 0), part(chunk + 1, which, 1))
+            else:
+                made = part(chunk, which, 0)[:, :HEAD_DIM]
+            lanes = slice(first, first + made.shape[1])
+            if which < 3:
+                qkv_ref[which, :, lanes] = made[:rows]
+                extra_ref[which, :, lanes] = made[rows:]
+            else:
+                out_ref[:, lanes] = made[:rows]
+
+
+def finish(groups, chunks):
+    rows = groups[0][0].shape[0] - EXTRA
+    local = chunks * HEAD_DIM
+    return pl.pallas_call(
+        partial(finish_kernel, len(groups[0]), chunks),
+        out_shape=[
+            jax.ShapeDtypeStruct((3, rows, local), F32),
+            jax.ShapeDtypeStruct((rows, local), F32),
+            jax.ShapeDtypeStruct((3, EXTRA, local), F32),
+            jax.ShapeDtypeStruct((EXTRA, groups[0][0].shape[1]), F32),
+        ],
+        compiler_params=params(16),
+        cost_estimate=cost(1, 1),
+    )(*groups[0], *groups[1])
 
 
 def swap(values, axis, mask):
@@ -746,6 +847,10 @@
     return own + other, jnp.stack(place).astype(jnp.int32)
 
 
+def spread_line(values):
+    return [swap(values, "tp", d) for d in range(1, lax.axis_size("tp"))]
+
+
 def add_low(first, *others):
     total = first.astype(F32)
     for other in others:
@@ -757,8 +862,9 @@
     return add_low(keep, swap(send, "fsdp", 1)).astype(BF)
 
 
-def merge_chips(blocks):
-    return add_low(blocks[0], *[swap(blocks[n], "fsdp", 2 * n) for n in (1, 2, 3)]).astype(BF)
+def merge_chips(blocks, *beside):
+    own = after(blocks[0], *beside) if beside else blocks[0]
+    return add_low(own, *[swap(blocks[n], "fsdp", 2 * n) for n in (1, 2, 3)]).astype(BF)
 
 
 def scatter_tp(blocks):
@@ -766,9 +872,9 @@
     me = lax.axis_index("tp")
 
     def pick(d):
-        return lax.dynamic_index_in_dim(blocks, (me + d) % count, 0, keepdims=False)
-
-    return add_low(pick(0), *[cycle(pick(d), "tp", d) for d in range(1, count)])
+        return lax.dynamic_index_in_dim(blocks, me ^ d, 0, keepdims=False)
+
+    return [pick(0)] + [swap(pick(d), "tp", d) for d in range(1, count)]
 
 
 def spread_rows(whole, blocks):
@@ -826,7 +932,6 @@
         .transpose(1, 2, 3, 0, 4)
         .reshape(shard_rows, 4 * width)
     )
-    qkv_rows, out_rows = wide_rows[:, : 3 * width], wide_rows[:, 3 * width :]
     whole_bias = jnp.sum(
         columns[:, shard_rows:].reshape(tp, -1)[:, : biases.size].reshape(tp, 3, -1).astype(F32),
         axis=1,
@@ -852,7 +957,7 @@
     centers = seg_rows[:, ::STRIDE].reshape(seqs, tp, far_rows)
     centers_cycle = jnp.concatenate(
         [
-            lax.dynamic_index_in_dim(centers, (place - d) % tp, 1, keepdims=True)
+            lax.dynamic_index_in_dim(centers, place ^ d, 1, keepdims=True)
             for d in range(tp)
         ],
         axis=1,
@@ -870,20 +975,21 @@
     ).astype(F32)
 
     if fast:
-        pieces, offs = gather_pieces(qkv_rows, (x_wide, same, bias_qkv, taps) + segs)
+        pieces, offs = gather_pieces(wide_rows, (x_wide, same, bias_qkv, taps) + segs)
     else:
-        pieces = [lax.all_gather(qkv_rows, "fsdp", axis=0, tiled=True)]
+        pieces = [lax.all_gather(wide_rows, "fsdp", axis=0, tiled=True)]
         offs = jnp.zeros((1,), jnp.int32)
 
-    later = after(jnp.concatenate([w_up, w_down], axis=1), columns)
-    weights = lax.all_gather(later, "tp", axis=0, tiled=False)
+    weights = lax.all_gather(
+        jnp.concatenate([w_up, w_down], axis=1), "tp", axis=0, tiled=False
+    )
 
     made, slots, att = [], [], []
 
     def send_pooled(j, *waits):
         pooled = made[j][1]
         sent = after(pooled, *waits) if waits else pooled
-        slots.append([pooled] + [cycle(sent, "tp", d) for d in range(1, tp)])
+        slots.append([pooled] + spread_line(sent))
 
     for j in range(chunks):
         if j:
@@ -892,23 +998,25 @@
         if j == 0:
             send_pooled(0)
     if chunks > 1:
-        send_pooled(1, made[-1][1])
-    weights = after(weights, made[-1][1], *slots[0][1:])
+        send_pooled(1, made[-1][1], *slots[0][1:])
+    weights = after(weights, made[0][1])
     weights = lax.all_gather(weights, "fsdp", axis=0, tiled=False)
-    full_out = lax.all_gather(after(out_rows, made[0][1]), "fsdp", axis=0, tiled=True)
     for j in range(chunks):
-        order = segs if j == 0 else segs[:2] + (after(segs[2], att[-1]),)
+        order = segs
+        if j == 1:
+            x_cols = after(x_wide, att[0]).reshape(seqs * wide, width).T
+            cot = after(cotangent, att[0]).transpose(1, 0, 2)
+        if j:
+            order = segs[:2] + (after(segs[2], att[-1], x_cols, cot),)
         att.append(attend_forward(made[j][0], slots[j], order))
         if j + 2 < chunks:
             send_pooled(j + 2, att[j])
     if shard_rows % 16:
-        weights = weights.transpose(1, 0, 2, 3).reshape(1, tp, width, 2 * hidden_local)
-
-    x_cols = after(x_wide, att[0]).reshape(seqs * wide, width).T
-    cot = after(cotangent, att[0]).transpose(1, 0, 2)
+        weights = weights.transpose(1, 0, 2, 3).reshape(1, tp, width, -1)
+
     misc = jnp.concatenate([out_bias, norm_gains, norm_shifts, jnp.zeros((2, width), F32)])
     outputs, grad_residual, grad_att, grad_out, gud, small = dense(
-        att, x_wide, cot, full_out, weights, bias_up, misc
+        att, [m[2] for m in made], x_wide, cot, weights, bias_up, misc
     )
     if gud.shape[0] == 1:
         gud = spread_rows(gud[0], fsdp)
@@ -934,7 +1042,7 @@
         dq, dk, dv, dps = attend_backward(made[j][0], slots[j], order, grad_att[j])
         if j:
             dps = [after(d, *backs[-1][3][1:]) for d in dps]
-        arrived = [dps[0]] + [cycle(dps[d], "tp", -d) for d in range(1, tp)]
+        arrived = [dps[0]] + [swap(dps[d], "tp", d) for d in range(1, tp)]
         backs.append((dq, dk, dv, arrived, made[j][0], grad_out[j]))
     totals, lows, merged = [], [], []
     for low, high in ((0, chunks - 1), (chunks - 1, chunks)):
@@ -947,7 +1055,7 @@
             lines = -(-flat.size // cols)
             flat = jnp.pad(flat, (0, lines * cols - flat.size)).reshape(lines, cols)
             more = jnp.pad(flat, ((TAPS + 1, EXTRA - TAPS - 1 - lines), (0, 0)))
-        waits = [backs[-1][0], gud_parts]
+        waits = [backs[-1][0]] + ([gud_parts] if merged else [])
         groups, low_kv = gather_back(
             low, after(out_offs, *waits), group_sizes, backs[low:high], taps, same, x_cols, more
         )
@@ -959,11 +1067,12 @@
     middle, first, last = input_grad(
         [(backs[n][0], lows[n], made[n][2]) for n in range(chunks)], grad_residual
     )
+    middle = middle.transpose(1, 0, 2)
     chips = []
     for n, blocks in enumerate(merged):
         blocks = after(blocks, *chips) if chips else blocks
         if fast:
-            chips.append(merge_chips(blocks))
+            chips.append(merge_chips(blocks, *([] if chips else [middle])))
         else:
             chips.append(lax.psum_scatter(blocks, "fsdp", scatter_dimension=0, tiled=False))
     for blocks in chips:
@@ -974,27 +1083,20 @@
         totals.append(scatter_tp(blocks))
 
     first, last = after(first, chips[-1]), after(last, chips[-1])
-    to_left = shift_left(first)
-    to_right = shift_right(last)
-    middle = middle.at[:, :HALF].add(to_right.astype(F32))
-    middle = middle.at[:, rows - HALF :].add(to_left.astype(F32))
-    grad_inputs = middle.transpose(1, 0, 2)
-
-    sums = totals[0][shard_rows + TAPS + 1 :].reshape(-1)[: 6 * width].reshape(6, width)
-    stacked = jnp.concatenate(
-        [t[: shard_rows + TAPS + 1].reshape(-1, t.shape[1] // (4 * HEAD_DIM), 4, HEAD_DIM)
-         for t in totals],
-        axis=1,
-    )
-    stacked = stacked.transpose(0, 2, 1, 3).reshape(-1, 4, local)
-    main, bias_row, tap_rows = stacked[:shard_rows], stacked[shard_rows], stacked[shard_rows + 1 :]
+    to_left = shift_left(first).transpose(1, 0, 2)
+    to_right = shift_right(last).transpose(1, 0, 2)
+    grad_inputs = middle.at[:HALF].add(to_right.astype(F32))
+    grad_inputs = grad_inputs.at[rows - HALF :].add(to_left.astype(F32))
+
+    grad_w_qkv, grad_w_out, extra_rows, sums = finish(totals, chunks)
+    sums = sums[TAPS + 1 :].reshape(-1)[: 6 * width].reshape(6, width)
     return (
         outputs.transpose(1, 0, 2),
         grad_inputs,
-        main[:, :3],
-        bias_row[:3],
-        tap_rows[:, 1:3].transpose(1, 0, 2),
-        main[:, 3],
+        grad_w_qkv.transpose(1, 0, 2),
+        extra_rows[:, 0],
+        extra_rows[1:, 1 : TAPS + 1],
+        grad_w_out,
         sums[0:2],
         gud[0, :shard_rows],
         gud[0, shard_rows],

time: 429 us -> 404 us (0.942)
  Pallas kernels: 217 us -> 181 us
  waiting for transfers between devices: 32.2 us -> 50.1 us
  local copies, waits for them, and re-layouts: 65.8 us -> 58.9 us
  starting transfers between devices: 76.4 us -> 82.6 us
    ppermute x20 -> x44, starting transfers between devices: 19.4 us -> 71.1 us  [swap(): return lax.ppermute(values, axis, [(i, i ^ mask) for i in range(count)])]
    ppermute x24 -> x0, starting transfers between devices: 45.7 us -> none  [cycle(): lax.ppermute(values, axis, [(i, (i + shift) % count) for i in range(count)])]
    ppermute x20 -> x44, waiting for transfers between devices: 20.3 us -> 50 us  [swap(): return lax.ppermute(values, axis, [(i, i ^ mask) for i in range(count)])]
    pallas_call x3, Pallas kernels: 48.8 us -> 26 us  [attend_forward(): pl.pallas_call(partial(attend_forward_kernel, blocks), grid=(seqs, span /...]
    pallas_call x3, Pallas kernels: 70.5 us -> 53.6 us  [attend_backward(): pl.pallas_call(partial(attend_backward_kernel, blocks), grid=(seqs, span...]
    ppermute x24 -> x0, waiting for transfers between devices: 11.6 us -> none  [cycle(): lax.ppermute(values, axis, [(i, (i + shift) % count) for i in range(count)])]
    slice x13 -> x2, local copies, waits for them, and re-layouts: 7.2 us -> 0.58 us  [the longest x1 0.58 us: body(): extra_rows[:, 0]]
    unnamed x98 -> x92, local copies, waits for them, and re-layouts: 30.8 us -> 26.9 us
  transfers between devices with their start and end apart: 53 -> 52, of which waited for: 10 -> 15; matrix products, arithmetic and copies ran while one was open for 14% -> 12% of each run, Pallas kernels for 39% -> 32%
where the time goes in v4:
time: 404 us; the launch traced here: 397 us
  Pallas kernels  181 us (45%)
  starting transfers between devices  82.6 us (20%)
  local copies, waits for them, and re-layouts  58.9 us (15%)
  waiting for transfers between devices  50.1 us (12%)
  between operations  15.1 us (4%)
  other arithmetic  9.46 us (2%)
    ppermute x44, starting transfers between devices, swap(): return lax.ppermute(values, axis, [(i, i ^ mask) for i in range(count)])  71.1 us
    pallas_call x1, Pallas kernels, dense(): pl.pallas_call(partial(dense_kernel, chunks, steps), grid=(2 * steps,), i...  53.7 us
    pallas_call x3, Pallas kernels, attend_backward(): pl.pallas_call(partial(attend_backward_kernel, blocks), grid=(seqs, span...  53.6 us
    ppermute x44, waiting for transfers between devices, swap(): return lax.ppermute(values, axis, [(i, i ^ mask) for i in range(count)])  50 us
    unnamed x92, local copies, waits for them, and re-layouts  26.9 us
    pallas_call x3, Pallas kernels, attend_forward(): pl.pallas_call(partial(attend_forward_kernel, blocks), grid=(seqs, span /...  26 us
    pallas_call x2, Pallas kernels, gather_back(): pl.pallas_call(partial(gather_back_kernel, blocks, chunks, len(group_size...  21.7 us
    pallas_call x3, Pallas kernels, project(): pl.pallas_call(partial(project_kernel, len(pieces)), grid_spec=pltpu.Pref...  15.6 us
  transfers between devices with their start and end apart: 52, of which 15 were waited for; matrix products, arithmetic and copies ran while one was open for 12% of the time, Pallas kernels for 32%

profile of v4, /device:TPU:0, one launch (start us, length us, event | category | flops | bytes accessed | tf_op | source)
XLA Modules:
  0.0 397.1 jit_solution(8168517153468419854)
XLA Ops:
  12.2 5.1 %collective-permute-start = (bf16[109,768]{0,1:T(8,128)(2,1)S(1)}, bf16[109,768]{0,1:T(8,128)(2,1)S(1)}, u32[]{:S(2)}, u32[]{:S(2)}) collective-permute-start(bf16[109,768]{0,1:T(8,128)(2,1)S(1)} %pad_maximum_fusion.2), channel_id=1, source_target_pairs={{0,3},{1,2},{2,1},{3,0},{4,7},{5,6},{6,5},{7,4},{8,11},{9,10},{10,... | collective-permute-start | bytes 502280 | tf_op jit(solution)/shard_map/ppermute | solution.py:809
  18.0 2.7 copy.279
  21.8 4.0 %collective-permute-start.5 = (bf16[64,2,768]{2,0,1:T(8,128)(2,1)S(1)}, bf16[64,2,768]{2,0,1:T(8,128)(2,1)}, u32[]{:S(2)}, u32[]{:S(2)}) collective-permute-start(bf16[64,2,768]{2,0,1:T(8,128)(2,1)S(1)} %get-tuple-element.320), channel_id=1, source_target_pairs={{0,1},{1,2},{2,3},{4,5},{5,6},{6,7},{8,9},{9,10},{10,11},{12,13},{... | collective-permute-start | bytes 589832 | tf_op jit(solution)/shard_map/ppermute | solution.py:814
  25.7 1.3 collective-permute-start.6
  32.9 2.1 collective-permute-done.1
  36.2 1.6 collective-permute-start.3
  37.7 1.5 collective-permute-start.4
  41.3 1.7 maximum_bitcast_fusion.refs_10_.refs_6_
  43.0 6.7 %collective-permute-done.3.refs_1_ = bf16[96,3072]{1,0:T(8,128)(2,1)S(1)} collective-permute-done((bf16[96,3072]{1,0:T(8,128)(2,1)S(1)}, bf16[96,3072]{1,0:T(8,128)(2,1)S(1)}, u32[]{:S(2)}, u32[]{:S(2)}) %collective-permute-start.3) | collective-permute-done | bytes 589856 | tf_op jit(solution)/shard_map/ppermute | solution.py:809
  49.7 1.6 collective-permute-start.7
  54.3 3.0 collective-permute-done.7.refs_3_
  57.3 2.6 collective-permute-done.8.refs_4_
  60.1 1.8 collective-permute-done.13.refs_9_
  61.9 5.4 %shard_map.220 = (bf16[3,2,640,256]{3,2,1,0:T(8,128)(2,1)S(1)}, bf16[2,2,128,256]{3,2,1,0:T(8,128)(2,1)}, bf16[4,768,256]{2,1,0:T(8,128)(2,1)S(1)}) custom-call(s32[10]{0:T(128)S(1)} %stack.97.offs, bf16[96,3072]{1,0:T(8,128)(2,1)S(1)} %copy.291.refs_0_, bf16[96,3072]{1,0:T(8,128)(2,1)S(1)} %collective-permute-done.3.refs_1_, ...), custom_call_target="tpu_custom_call" | custom-call | flops 1 | bytes 1 | tf_op jit(solution)/shard_map/pallas_call | solution.py:100
  70.6 2.9 collective-permute-start.15
  74.5 5.5 %shard_map.222 = (bf16[3,2,640,256]{3,2,1,0:T(8,128)(2,1)S(1)}, bf16[2,2,128,256]{3,2,1,0:T(8,128)(2,1)}, bf16[4,768,256]{2,1,0:T(8,128)(2,1)S(1)}) custom-call(s32[10]{0:T(128)S(1)} %stack.97.offs, bf16[96,3072]{1,0:T(8,128)(2,1)S(1)} %copy.291.refs_0_, bf16[96,3072]{1,0:T(8,128)(2,1)S(1)} %collective-permute-done.3.refs_1_, ...), custom_call_target="tpu_custom_call" | custom-call | flops 1 | bytes 1 | tf_op jit(solution)/shard_map/pallas_call | solution.py:100
  79.9 1.4 copy-done.2
  82.1 4.7 %shard_map.223 = (bf16[3,2,640,256]{3,2,1,0:T(8,128)(2,1)S(1)}, bf16[2,2,128,256]{3,2,1,0:T(8,128)(2,1)S(1)}, bf16[4,768,256]{2,1,0:T(8,128)(2,1)S(1)}) custom-call(s32[10]{0:T(128)S(1)} %stack.97.offs, bf16[96,3072]{1,0:T(8,128)(2,1)S(1)} %copy.291.refs_0_, bf16[96,3072]{1,0:T(8,128)(2,1)S(1)} %collective-permute-done.3.refs_1_, ...), custom_call_target="tpu_custom_call" | custom-call | flops 1 | bytes 1 | tf_op jit(solution)/shard_map/pallas_call | solution.py:100
  86.9 1.3 copy-done
  90.1 2.1 collective-permute-done.15.refs_2_.refs_6_
  93.6 4.7 %collective-permute-start.17 = (bf16[2,2,128,256]{3,2,1,0:T(8,128)(2,1)}, bf16[2,2,128,256]{3,2,1,0:T(8,128)(2,1)S(1)}, u32[]{:S(2)}, u32[]{:S(2)}) collective-permute-start(bf16[2,2,128,256]{3,2,1,0:T(8,128)(2,1)} %get-tuple-element.130.refs_0_.refs_4_), channel_id=1, source_target_pairs={{0,1},{1,0},{2,3},{3,2},{4,5},{5,4},{6,7},{7,6},{8,9},{9,8},{10,11... | collective-permute-start | bytes 786440 | tf_op jit(solution)/shard_map/ppermute | solution.py:809
  98.3 1.7 copy.292.refs_8_
  101.0 1.5 collective-permute-start.19
  102.6 8.7 %shard_map.221.refs_0_ = bf16[2,512,256]{2,1,0:T(8,128)(2,1)} custom-call(bf16[3,2,640,256]{3,2,1,0:T(8,128)(2,1)} %copy-done.1, bf16[3,2,640,256]{3,2,1,0:T(8,128)(2,1)} %copy-done.1, bf16[3,2,640,256]{3,2,1,0:T(8,128)(2,1)} %copy-done.1, bf16[2,2,128,256]{3,2,1,0:T(8,128)(2,1)} %get-tuple-element.124.refs_0_.refs_4_, bf16[2,2,128,256]{3,2,1,0:T(8,128)(2,1)} %copy-done.13, ...), custom_call_target="tpu_custom_call" | custom-call | flops 1 | bytes 1 | tf_op jit(solution)/shard_map/pallas_call | solution.py:315
  112.3 1.8 collective-permute-start.21
  114.1 1.6 collective-permute-start.22
  117.8 2.4 copy.306
  120.2 2.8 copy.313
  123.0 8.6 %shard_map.224.refs_1_ = bf16[2,512,256]{2,1,0:T(8,128)(2,1)} custom-call(bf16[3,2,640,256]{3,2,1,0:T(8,128)(2,1)} %copy-done.2, bf16[3,2,640,256]{3,2,1,0:T(8,128)(2,1)} %copy-done.2, bf16[3,2,640,256]{3,2,1,0:T(8,128)(2,1)} %copy-done.2, bf16[2,2,128,256]{3,2,1,0:T(8,128)(2,1)} %get-tuple-element.130.refs_0_.refs_4_, bf16[2,2,128,256]{3,2,1,0:T(8,128)(2,1)} %copy-done.17, ...), custom_call_target="tpu_custom_call" | custom-call | flops 1 | bytes 1 | tf_op jit(solution)/shard_map/pallas_call | solution.py:315
  131.7 12.4 %collective-permute-done.21.refs_2_.refs_6_ = bf16[2,2,128,256]{3,2,1,0:T(8,128)(2,1)S(1)} collective-permute-done((bf16[2,2,128,256]{3,2,1,0:T(8,128)(2,1)S(1)}, bf16[2,2,128,256]{3,2,1,0:T(8,128)(2,1)S(1)}, u32[]{:S(2)}, u32[]{:S(2)}) %collective-permute-start.21) | collective-permute-done | bytes 262176 | tf_op jit(solution)/shard_map/ppermute | solution.py:809
  144.9 8.7 %shard_map.225.refs_2_ = bf16[2,512,256]{2,1,0:T(8,128)(2,1)} custom-call(bf16[3,2,640,256]{3,2,1,0:T(8,128)(2,1)} %copy-done, bf16[3,2,640,256]{3,2,1,0:T(8,128)(2,1)} %copy-done, bf16[3,2,640,256]{3,2,1,0:T(8,128)(2,1)} %copy-done, bf16[2,2,128,256]{3,2,1,0:T(8,128)(2,1)} %copy-done.8, bf16[2,2,128,256]{3,2,1,0:T(8,128)(2,1)} %copy-done.11, ...), custom_call_target="tpu_custom_call" | custom-call | flops 1 | bytes 1 | tf_op jit(solution)/shard_map/pallas_call | solution.py:315
  153.6 53.7 %shard_map.226 = (bf16[2,512,768]{2,1,0:T(8,128)(2,1)}, f32[2,512,768]{2,1,0:T(8,128)}, bf16[2,512,256]{2,1,0:T(8,128)(2,1)}, bf16[2,512,256]{2,1,0:T(8,128)(2,1...) custom-call(bf16[2,512,256]{2,1,0:T(8,128)(2,1)} %shard_map.221.refs, ...), custom_call_target="tpu_custom_call" | custom-call | flops 1 | bytes 1 | tf_op jit(solution)/shard_map/pallas_call | solution.py:519
  207.4 17.9 %shard_map.227 = (bf16[2,512,256]{2,1,0:T(8,128)(2,1)}, f32[2,640,256]{2,1,0:T(8,128)}, f32[2,640,256]{2,1,0:T(8,128)}, bf16[2,2,128,256]{3,2,1,0:T(8,128)(2,1)}...) custom-call(bf16[3,2,640,256]{3,2,1,0:T(8,128)(2,1)} %copy-done.1, ...), custom_call_target="tpu_custom_call" | custom-call | flops 1 | bytes 1 | tf_op jit(solution)/shard_map/pallas_call | solution.py:337
  225.3 4.2 %collective-permute-start.23 = (bf16[2,2,128,256]{3,2,1,0:T(8,128)(2,1)}, bf16[2,2,128,256]{3,2,1,0:T(8,128)(2,1)S(1)}, u32[]{:S(2)}, u32[]{:S(2)}) collective-permute-start(bf16[2,2,128,256]{3,2,1,0:T(8,128)(2,1)} %get-tuple-element.147), channel_id=1, source_target_pairs={{0,1},{1,0},{2,3},{3,2},{4,5},{5,4},{6,7},{7,6},{8,9},{9,8},{10,11... | collective-permute-start | bytes 786440 | tf_op jit(solution)/shard_map/ppermute | solution.py:809
  230.5 1.5 collective-permute-start.25
  232.0 17.9 %shard_map.228 = (bf16[2,512,256]{2,1,0:T(8,128)(2,1)}, f32[2,640,256]{2,1,0:T(8,128)}, f32[2,640,256]{2,1,0:T(8,128)}, bf16[2,2,128,256]{3,2,1,0:T(8,128)(2,1)}...) custom-call(bf16[3,2,640,256]{3,2,1,0:T(8,128)(2,1)} %copy-done.2, ...), custom_call_target="tpu_custom_call" | custom-call | flops 1 | bytes 1 | tf_op jit(solution)/shard_map/pallas_call | solution.py:337
  250.8 1.9 collective-permute-start.28
  252.8 12.5 %collective-permute-start.27 = (bf16[2,2,128,256]{3,2,1,0:T(8,128)(2,1)}, bf16[2,2,128,256]{3,2,1,0:T(8,128)(2,1)S(1)}, u32[]{:S(2)}, u32[]{:S(2)}) collective-permute-start(bf16[2,2,128,256]{3,2,1,0:T(8,128)(2,1)} %get-tuple-element.165), channel_id=1, source_target_pairs={{0,2},{1,3},{2,0},{3,1},{4,6},{5,7},{6,4},{7,5},{8,10},{9,11},{10,... | collective-permute-start | bytes 786440 | tf_op jit(solution)/shard_map/ppermute | solution.py:809
  265.9 17.9 %shard_map.229 = (bf16[2,512,256]{2,1,0:T(8,128)(2,1)}, f32[2,640,256]{2,1,0:T(8,128)}, f32[2,640,256]{2,1,0:T(8,128)}, bf16[2,2,128,256]{3,2,1,0:T(8,128)(2,1)}...) custom-call(bf16[3,2,640,256]{3,2,1,0:T(8,128)(2,1)} %copy-done, ...), custom_call_target="tpu_custom_call" | custom-call | flops 1 | bytes 1 | tf_op jit(solution)/shard_map/pallas_call | solution.py:337
  283.8 2.5 collective-permute-start.31
  286.9 1.4 collective-permute-start.29
  290.1 13.5 %shard_map.230 = (bf16[4,4,112,512]{3,2,1,0:T(8,128)(2,1)}, bf16[4,4,112,512]{3,2,1,0:T(8,128)(2,1)}, bf16[2,2,640,256]{3,2,1,0:T(8,128)(2,1)}, bf16[2,2,640,256]{3,2,1,0:T(8,128)(2,1)}) custom-call(s32[8]{0:T(128)} %stack.111.offs, f32[2,640,256]{2,1,0:T(8,128)} %get-tuple-element.154.refs_0_, f32[2,640,256]{2,1,0:T(8,128)} %get-tuple-element.155.refs_1_, ...), custom_call_target="tpu_custom_call" | custom-call | flops 1 | bytes 1 | tf_op jit(solution)/shard_map/pallas_call | solution.py:669
  304.6 3.2 collective-permute-done.33
  307.8 2.1 add_convert_fusion
  309.9 3.0 reshape_reduce_scatter.3
  314.8 8.2 %shard_map.231 = (bf16[4,4,112,256]{3,2,1,0:T(8,128)(2,1)}, bf16[4,4,112,256]{3,2,1,0:T(8,128)(2,1)}, bf16[2,2,640,256]{3,2,1,0:T(8,128)(2,1)}) custom-call(s32[8]{0:T(128)} %stack.111.offs, f32[2,640,256]{2,1,0:T(8,128)} %get-tuple-element.174.refs_0_, f32[2,640,256]{2,1,0:T(8,128)} %get-tuple-element.175.refs_1_, ...), custom_call_target="tpu_custom_call" | custom-call | flops 1 | bytes 1 | tf_op jit(solution)/shard_map/pallas_call | solution.py:669
  325.9 2.0 collective-permute-start.36
  327.8 9.5 %shard_map.232 = (f32[2,512,768]{2,1,0:T(8,128)}, bf16[2,64,768]{2,1,0:T(8,128)(2,1)}, bf16[2,64,768]{2,1,0:T(8,128)(2,1)}) custom-call(bf16[2,512,256]{2,1,0:T(8,128)(2,1)} %get-tuple-element.143.refs_2_.refs_0_, bf16[2,2,640,256]{3,2,1,0:T(8,128)(2,1)} %get-tuple-element.170.refs_1_, bf16[4,768,256]{2,1,0:T(8,128)(2,1)} %copy-done.4, ...), custom_call_target="tpu_custom_call" | custom-call | flops 1 | bytes 1 | tf_op jit(solution)/shard_map/pallas_call | solution.py:736
  338.5 9.6 %collective-permute-done.36 = bf16[4,112,512]{2,1,0:T(8,128)(2,1)S(1)} collective-permute-done((bf16[4,112,512]{2,1,0:T(8,128)(2,1)S(1)}, bf16[4,112,512]{2,1,0:T(8,128)(2,1)S(1)}, u32[]{:S(2)}, u32[]{:S(2)}) %collective-permute-start.36) | collective-permute-done | bytes 458784 | tf_op jit(solution)/shard_map/ppermute | solution.py:809
  349.6 1.5 collective-permute-start.38
  353.0 2.4 collective-permute-start.43
  355.3 2.0 collective-permute-done.37
  357.3 2.4 collective-permute-start.44
  359.7 1.3 collective-permute-done.38
  361.9 2.4 collective-permute-start.46
  364.2 1.4 collective-permute-start.47
  365.7 2.8 copy.303
  368.6 1.3 collective-permute-start.41
  369.9 4.6 %collective-permute-start.40 = (bf16[2,64,768]{2,1,0:T(8,128)(2,1)}, bf16[2,64,768]{2,1,0:T(8,128)(2,1)S(1)}, u32[]{:S(2)}, u32[]{:S(2)}) collective-permute-start(bf16[2,64,768]{2,1,0:T(8,128)(2,1)} %get-tuple-element.199), channel_id=1, source_target_pairs={{0,1},{1,2},{2,3},{4,5},{5,6},{6,7},{8,9},{9,10},{10,11},{12,13},{... | collective-permute-start | bytes 589832 | tf_op jit(solution)/shard_map/ppermute | solution.py:814
  376.6 1.3 slice.215
  377.9 1.3 slice.220
  379.2 1.3 slice.222
  381.1 1.3 copy.315
  383.5 4.1 %copy.304 = f32[512,2,768]{2,1,0:T(2,128)} copy(f32[512,2,768]{2,0,1:T(8,128)S(1)} %fusion.3) | data formatting | bytes 6291456
  (242 shorter events, 54.5 us)
Async XLA Ops:
  7.2 62.5 %all-gather.5.cloned.1.call-start = ((), (), s32[]{:S(2)}) async-start(), calls=%async_computation.4 | async-start | bytes 1474560 | tf_op jit(solution)/shard_map/all_gather | solution.py:983
  12.2 14.9 %copy-start.34 = (bf16[96,768]{1,0:T(8,128)(2,1)S(1)}, bf16[96,768]{1,0:T(8,128)(2,1)}, u32[]{:S(2)}) copy-start(bf16[96,768]{1,0:T(8,128)(2,1)} %param.26) | copy-start | bytes 442372
  12.2 15.7 %copy-start.33 = (s32[2048,2]{0,1:T(2,128)S(1)}, s32[2048,2]{0,1:T(2,128)}, u32[]{:S(2)}) copy-start(s32[2048,2]{0,1:T(2,128)} %param.18) | copy-start | bytes 49156
  12.2 20.7 %collective-permute-start = (bf16[109,768]{0,1:T(8,128)(2,1)S(1)}, bf16[109,768]{0,1:T(8,128)(2,1)S(1)}, u32[]{:S(2)}, u32[]{:S(2)}) collective-permute-start(bf16[109,768]{0,1:T(8,128)(2,1)S(1)} %pad_maximum_fusion.2), channel_id=1, source_target_pairs={{0,3},{1,2},{2,1},{3,0},{4,7},{5,6},{6,5},{7,4},{8,11},{9,10},{10,... | collective-permute-start | bytes 502280 | tf_op jit(solution)/shard_map/ppermute | solution.py:809
  17.3 17.7 %collective-permute-start.1 = (bf16[109,768]{0,1:T(8,128)(2,1)S(1)}, bf16[109,768]{0,1:T(8,128)(2,1)S(1)}, u32[]{:S(2)}, u32[]{:S(2)}) collective-permute-start(bf16[109,768]{0,1:T(8,128)(2,1)S(1)} %pad_maximum_fusion.2), channel_id=1, source_target_pairs={{0,2},{1,3},{2,0},{3,1},{4,6},{5,7},{6,4},{7,5},{8,10},{9,11},{10,... | collective-permute-start | bytes 502280 | tf_op jit(solution)/shard_map/ppermute | solution.py:809
  17.3 17.7 %collective-permute-start.2 = (bf16[109,768]{0,1:T(8,128)(2,1)S(1)}, bf16[109,768]{0,1:T(8,128)(2,1)S(1)}, u32[]{:S(2)}, u32[]{:S(2)}) collective-permute-start(bf16[109,768]{0,1:T(8,128)(2,1)S(1)} %pad_maximum_fusion.2), channel_id=1, source_target_pairs={{0,1},{1,0},{2,3},{3,2},{4,5},{5,4},{6,7},{7,6},{8,9},{9,8},{10,11... | collective-permute-start | bytes 502280 | tf_op jit(solution)/shard_map/ppermute | solution.py:809
  21.8 19.1 %collective-permute-start.5 = (bf16[64,2,768]{2,0,1:T(8,128)(2,1)S(1)}, bf16[64,2,768]{2,0,1:T(8,128)(2,1)}, u32[]{:S(2)}, u32[]{:S(2)}) collective-permute-start(bf16[64,2,768]{2,0,1:T(8,128)(2,1)S(1)} %get-tuple-element.320), channel_id=1, source_target_pairs={{0,1},{1,2},{2,3},{4,5},{5,6},{6,7},{8,9},{9,10},{10,11},{12,13},{... | collective-permute-start | bytes 589832 | tf_op jit(solution)/shard_map/ppermute | solution.py:814
  25.7 15.6 %collective-permute-start.6 = (bf16[64,2,768]{2,0,1:T(8,128)(2,1)S(1)}, bf16[64,2,768]{2,0,1:T(8,128)(2,1)}, u32[]{:S(2)}, u32[]{:S(2)}) collective-permute-start(bf16[64,2,768]{2,0,1:T(8,128)(2,1)S(1)} %get-tuple-element.321), channel_id=1, source_target_pairs={{1,0},{2,1},{3,2},{5,4},{6,5},{7,6},{9,8},{10,9},{11,10},{13,12},{... | collective-permute-start | bytes 589832 | tf_op jit(solution)/shard_map/ppermute | solution.py:819
  27.8 125.8 %all-gather.7.cloned.1.call-start = ((), (), s32[]{:S(2)}) async-start(), calls=%async_computation.5 | async-start | bytes 10616832 | tf_op jit(solution)/shard_map/all_gather | solution.py:1003
  32.3 49.0 %copy-start.7 = (f32[2,128,8]{2,1,0:T(8,128)}, f32[2,128,8]{2,1,0:T(8,128)S(1)}, u32[]{:S(2)}) copy-start(f32[2,128,8]{2,1,0:T(8,128)S(1)} %convert_element_type.88.refs_13_.refs_21_.refs_11_) | copy-start | bytes 24580
  36.2 13.5 %collective-permute-start.3 = (bf16[96,3072]{1,0:T(8,128)(2,1)S(1)}, bf16[96,3072]{1,0:T(8,128)(2,1)S(1)}, u32[]{:S(2)}, u32[]{:S(2)}) collective-permute-start(bf16[96,3072]{1,0:T(8,128)(2,1)S(1)} %copy.291.refs_0_), channel_id=1, source_target_pairs={{0,8},{4,12},{8,0},{12,4},{16,24},{20,28},{24,16},{28,20},{1,9},{5... | collective-permute-start | bytes 1769480 | tf_op jit(solution)/shard_map/ppermute | solution.py:809
  37.7 14.3 %collective-permute-start.4 = (bf16[96,3072]{1,0:T(8,128)(2,1)S(1)}, bf16[96,3072]{1,0:T(8,128)(2,1)}, u32[]{:S(2)}, u32[]{:S(2)}) collective-permute-start(bf16[96,3072]{1,0:T(8,128)(2,1)S(1)} %copy.291.refs_0_), channel_id=1, source_target_pairs={{0,16},{4,20},{8,24},{12,28},{16,0},{20,4},{24,8},{28,12},{1,17},{... | collective-permute-start | bytes 1769480 | tf_op jit(solution)/shard_map/ppermute | solution.py:809
  40.6 19.5 %collective-permute-start.9 = (bf16[96,3072]{1,0:T(8,128)(2,1)S(1)}, bf16[96,3072]{1,0:T(8,128)(2,1)}, u32[]{:S(2)}, u32[]{:S(2)}) collective-permute-start(bf16[96,3072]{1,0:T(8,128)(2,1)S(1)} %copy.291.refs_0_), channel_id=1, source_target_pairs={{0,4},{4,0},{8,12},{12,8},{16,20},{20,16},{24,28},{28,24},{1,5},{5... | collective-permute-start | bytes 1769480 | tf_op jit(solution)/shard_map/ppermute | solution.py:809
  40.7 33.8 %copy-start.9 = (f32[2,8,768]{2,1,0:T(8,128)}, f32[2,8,768]{2,1,0:T(8,128)S(1)}, u32[]{:S(2)}) copy-start(f32[2,8,768]{2,1,0:T(8,128)S(1)} %pad.22.refs_12_) | copy-start | bytes 147460
  43.0 74.9 %copy-start.3 = (bf16[2,640,768]{2,1,0:T(8,128)(2,1)}, bf16[2,640,768]{2,1,0:T(8,128)(2,1)S(1)}, u32[]{:S(2)}) copy-start(bf16[2,640,768]{2,1,0:T(8,128)(2,1)S(1)} %maximum_bitcast_fusion.refs_10_.refs_6_) | copy-start | bytes 5898244
  49.7 7.6 %collective-permute-start.7 = (bf16[48,3072]{1,0:T(8,128)(2,1)S(1)}, bf16[48,3072]{1,0:T(8,128)(2,1)}, u32[]{:S(2)}, u32[]{:S(2)}) collective-permute-start(bf16[48,3072]{1,0:T(8,128)(2,1)S(1)} %slice.224), channel_id=1, source_target_pairs={{0,16},{4,20},{8,24},{12,28},{16,0},{20,4},{24,8},{28,12},{1,17},{... | collective-permute-start | bytes 884744 | tf_op jit(solution)/shard_map/ppermute | solution.py:809
  53.1 6.9 %collective-permute-start.8 = (bf16[48,3072]{1,0:T(8,128)(2,1)S(1)}, bf16[48,3072]{1,0:T(8,128)(2,1)}, u32[]{:S(2)}, u32[]{:S(2)}) collective-permute-start(bf16[48,3072]{1,0:T(8,128)(2,1)S(1)} %slice.232), channel_id=1, source_target_pairs={{0,8},{4,12},{8,0},{12,4},{16,24},{20,28},{24,16},{28,20},{1,9},{5... | collective-permute-start | bytes 884744 | tf_op jit(solution)/shard_map/ppermute | solution.py:809
  53.8 8.1 %collective-permute-start.10 = (bf16[96,3072]{1,0:T(8,128)(2,1)S(1)}, bf16[96,3072]{1,0:T(8,128)(2,1)}, u32[]{:S(2)}, u32[]{:S(2)}) collective-permute-start(bf16[96,3072]{1,0:T(8,128)(2,1)S(1)} %collective-permute-done.3.refs_1_), channel_id=1, source_target_pairs={{0,4},{4,0},{8,12},{12,8},{16,20},{20,16},{24,28},{28,24},{1,5},{5... | collective-permute-start | bytes 1769480 | tf_op jit(solution)/shard_map/ppermute | solution.py:809
  53.8 8.1 %collective-permute-start.11 = (bf16[96,3072]{1,0:T(8,128)(2,1)}, bf16[96,3072]{1,0:T(8,128)(2,1)}, u32[]{:S(2)}, u32[]{:S(2)}) collective-permute-start(bf16[96,3072]{1,0:T(8,128)(2,1)} %collective-permute-done.4.refs_2_), channel_id=1, source_target_pairs={{0,4},{4,0},{8,12},{12,8},{16,20},{20,16},{24,28},{28,24},{1,5},{5... | collective-permute-start | bytes 1769480 | tf_op jit(solution)/shard_map/ppermute | solution.py:809
  57.3 2.7 collective-permute-start.12
  60.0 1.9 collective-permute-start.13
  69.7 240.2 %reduce-scatter.3.cloned.1.call-start = ((), (), s32[]{:S(2)}) async-start(), calls=%async_computation.2 | async-start | bytes 12386304 | tf_op jit(solution)/shard_map/reduce_scatter | solution.py:1023
  70.0 19.3 %collective-permute-start.14 = (bf16[2,2,128,256]{3,2,1,0:T(8,128)(2,1)}, bf16[2,2,128,256]{3,2,1,0:T(8,128)(2,1)S(1)}, u32[]{:S(2)}, u32[]{:S(2)}) collective-permute-start(bf16[2,2,128,256]{3,2,1,0:T(8,128)(2,1)} %get-tuple-element.124.refs_0_.refs_4_), channel_id=1, source_target_pairs={{0,1},{1,0},{2,3},{3,2},{4,5},{5,4},{6,7},{7,6},{8,9},{9,8},{10,11... | collective-permute-start | bytes 786440 | tf_op jit(solution)/shard_map/ppermute | solution.py:809
  70.6 21.6 %collective-permute-start.15 = (bf16[2,2,128,256]{3,2,1,0:T(8,128)(2,1)}, bf16[2,2,128,256]{3,2,1,0:T(8,128)(2,1)S(1)}, u32[]{:S(2)}, u32[]{:S(2)}) collective-permute-start(bf16[2,2,128,256]{3,2,1,0:T(8,128)(2,1)} %get-tuple-element.124.refs_0_.refs_4_), channel_id=1, source_target_pairs={{0,2},{1,3},{2,0},{3,1},{4,6},{5,7},{6,4},{7,5},{8,10},{9,11},{10,... | collective-permute-start | bytes 786440 | tf_op jit(solution)/shard_map/ppermute | solution.py:809
  73.6 19.4 %collective-permute-start.16 = (bf16[2,2,128,256]{3,2,1,0:T(8,128)(2,1)}, bf16[2,2,128,256]{3,2,1,0:T(8,128)(2,1)S(1)}, u32[]{:S(2)}, u32[]{:S(2)}) collective-permute-start(bf16[2,2,128,256]{3,2,1,0:T(8,128)(2,1)} %get-tuple-element.124.refs_0_.refs_4_), channel_id=1, source_target_pairs={{0,3},{1,2},{2,1},{3,0},{4,7},{5,6},{6,5},{7,4},{8,11},{9,10},{10,... | collective-permute-start | bytes 786440 | tf_op jit(solution)/shard_map/ppermute | solution.py:809
  89.3 24.8 %copy-start.8 = (bf16[2,2,128,256]{3,2,1,0:T(8,128)(2,1)}, bf16[2,2,128,256]{3,2,1,0:T(8,128)(2,1)S(1)}, u32[]{:S(2)}) copy-start(bf16[2,2,128,256]{3,2,1,0:T(8,128)(2,1)S(1)} %get-tuple-element.135.refs_0_.refs_4_) | copy-start | bytes 786436
  93.6 20.5 %collective-permute-start.17 = (bf16[2,2,128,256]{3,2,1,0:T(8,128)(2,1)}, bf16[2,2,128,256]{3,2,1,0:T(8,128)(2,1)S(1)}, u32[]{:S(2)}, u32[]{:S(2)}) collective-permute-start(bf16[2,2,128,256]{3,2,1,0:T(8,128)(2,1)} %get-tuple-element.130.refs_0_.refs_4_), channel_id=1, source_target_pairs={{0,1},{1,0},{2,3},{3,2},{4,5},{5,4},{6,7},{7,6},{8,9},{9,8},{10,11... | collective-permute-start | bytes 786440 | tf_op jit(solution)/shard_map/ppermute | solution.py:809
  100.1 23.0 %collective-permute-start.18 = (bf16[2,2,128,256]{3,2,1,0:T(8,128)(2,1)}, bf16[2,2,128,256]{3,2,1,0:T(8,128)(2,1)}, u32[]{:S(2)}, u32[]{:S(2)}) collective-permute-start(bf16[2,2,128,256]{3,2,1,0:T(8,128)(2,1)} %get-tuple-element.130.refs_0_.refs_4_), channel_id=1, source_target_pairs={{0,2},{1,3},{2,0},{3,1},{4,6},{5,7},{6,4},{7,5},{8,10},{9,11},{10,... | collective-permute-start | bytes 786440 | tf_op jit(solution)/shard_map/ppermute | solution.py:809
  101.0 22.0 %collective-permute-start.19 = (bf16[2,2,128,256]{3,2,1,0:T(8,128)(2,1)}, bf16[2,2,128,256]{3,2,1,0:T(8,128)(2,1)}, u32[]{:S(2)}, u32[]{:S(2)}) collective-permute-start(bf16[2,2,128,256]{3,2,1,0:T(8,128)(2,1)} %get-tuple-element.130.refs_0_.refs_4_), channel_id=1, source_target_pairs={{0,3},{1,2},{2,1},{3,0},{4,7},{5,6},{6,5},{7,4},{8,11},{9,10},{10,... | collective-permute-start | bytes 786440 | tf_op jit(solution)/shard_map/ppermute | solution.py:809
  111.2 20.5 %collective-permute-start.20 = (bf16[2,2,128,256]{3,2,1,0:T(8,128)(2,1)S(1)}, bf16[2,2,128,256]{3,2,1,0:T(8,128)(2,1)S(1)}, u32[]{:S(2)}, u32[]{:S(2)}) collective-permute-start(bf16[2,2,128,256]{3,2,1,0:T(8,128)(2,1)S(1)} %get-tuple-element.135.refs_0_.refs_4_), channel_id=1, source_target_pairs={{0,1},{1,0},{2,3},{3,2},{4,5},{5,4},{6,7},{7,6},{8,9},{9,8},{10,11... | collective-permute-start | bytes 786440 | tf_op jit(solution)/shard_map/ppermute | solution.py:809
  112.3 31.8 %collective-permute-start.21 = (bf16[2,2,128,256]{3,2,1,0:T(8,128)(2,1)S(1)}, bf16[2,2,128,256]{3,2,1,0:T(8,128)(2,1)S(1)}, u32[]{:S(2)}, u32[]{:S(2)}) collective-permute-start(bf16[2,2,128,256]{3,2,1,0:T(8,128)(2,1)S(1)} %get-tuple-element.135.refs_0_.refs_4_), channel_id=1, source_target_pairs={{0,2},{1,3},{2,0},{3,1},{4,6},{5,7},{6,4},{7,5},{8,10},{9,11},{10,... | collective-permute-start | bytes 786440 | tf_op jit(solution)/shard_map/ppermute | solution.py:809
  114.1 30.0 %collective-permute-start.22 = (bf16[2,2,128,256]{3,2,1,0:T(8,128)(2,1)S(1)}, bf16[2,2,128,256]{3,2,1,0:T(8,128)(2,1)S(1)}, u32[]{:S(2)}, u32[]{:S(2)}) collective-permute-start(bf16[2,2,128,256]{3,2,1,0:T(8,128)(2,1)S(1)} %get-tuple-element.135.refs_0_.refs_4_), channel_id=1, source_target_pairs={{0,3},{1,2},{2,1},{3,0},{4,7},{5,6},{6,5},{7,4},{8,11},{9,10},{10,... | collective-permute-start | bytes 786440 | tf_op jit(solution)/shard_map/ppermute | solution.py:809
  207.4 180.3 %reduce-scatter.5.cloned.1.call-start = ((), (), s32[]{:S(2)}) async-start(), calls=%async_computation.3 | async-start | bytes 1720320 | tf_op jit(solution)/shard_map/reduce_scatter | solution.py:1025
  225.3 24.5 %collective-permute-start.23 = (bf16[2,2,128,256]{3,2,1,0:T(8,128)(2,1)}, bf16[2,2,128,256]{3,2,1,0:T(8,128)(2,1)S(1)}, u32[]{:S(2)}, u32[]{:S(2)}) collective-permute-start(bf16[2,2,128,256]{3,2,1,0:T(8,128)(2,1)} %get-tuple-element.147), channel_id=1, source_target_pairs={{0,1},{1,0},{2,3},{3,2},{4,5},{5,4},{6,7},{7,6},{8,9},{9,8},{10,11... | collective-permute-start | bytes 786440 | tf_op jit(solution)/shard_map/ppermute | solution.py:809
  229.5 21.3 %collective-permute-start.24 = (bf16[2,2,128,256]{3,2,1,0:T(8,128)(2,1)}, bf16[2,2,128,256]{3,2,1,0:T(8,128)(2,1)S(1)}, u32[]{:S(2)}, u32[]{:S(2)}) collective-permute-start(bf16[2,2,128,256]{3,2,1,0:T(8,128)(2,1)} %get-tuple-element.148), channel_id=1, source_target_pairs={{0,2},{1,3},{2,0},{3,1},{4,6},{5,7},{6,4},{7,5},{8,10},{9,11},{10,... | collective-permute-start | bytes 786440 | tf_op jit(solution)/shard_map/ppermute | solution.py:809
  230.5 20.3 %collective-permute-start.25 = (bf16[2,2,128,256]{3,2,1,0:T(8,128)(2,1)}, bf16[2,2,128,256]{3,2,1,0:T(8,128)(2,1)S(1)}, u32[]{:S(2)}, u32[]{:S(2)}) collective-permute-start(bf16[2,2,128,256]{3,2,1,0:T(8,128)(2,1)} %get-tuple-element.149), channel_id=1, source_target_pairs={{0,3},{1,2},{2,1},{3,0},{4,7},{5,6},{6,5},{7,4},{8,11},{9,10},{10,... | collective-permute-start | bytes 786440 | tf_op jit(solution)/shard_map/ppermute | solution.py:809
  249.8 33.9 %copy-start.23 = (bf16[2,2,128,256]{3,2,1,0:T(8,128)(2,1)}, bf16[2,2,128,256]{3,2,1,0:T(8,128)(2,1)S(1)}, u32[]{:S(2)}) copy-start(bf16[2,2,128,256]{3,2,1,0:T(8,128)(2,1)S(1)} %collective-permute-done.23.refs_4_) | copy-start | bytes 786436
  250.8 32.9 %copy-start.24 = (bf16[2,2,128,256]{3,2,1,0:T(8,128)(2,1)}, bf16[2,2,128,256]{3,2,1,0:T(8,128)(2,1)S(1)}, u32[]{:S(2)}) copy-start(bf16[2,2,128,256]{3,2,1,0:T(8,128)(2,1)S(1)} %collective-permute-done.24.refs_5_) | copy-start | bytes 786436
  250.8 32.9 %copy-start.25 = (bf16[2,2,128,256]{3,2,1,0:T(8,128)(2,1)}, bf16[2,2,128,256]{3,2,1,0:T(8,128)(2,1)S(1)}, u32[]{:S(2)}) copy-start(bf16[2,2,128,256]{3,2,1,0:T(8,128)(2,1)S(1)} %collective-permute-done.25.refs_6_) | copy-start | bytes 786436
  250.8 32.9 %collective-permute-start.28 = (bf16[2,2,128,256]{3,2,1,0:T(8,128)(2,1)}, bf16[2,2,128,256]{3,2,1,0:T(8,128)(2,1)S(1)}, u32[]{:S(2)}, u32[]{:S(2)}) collective-permute-start(bf16[2,2,128,256]{3,2,1,0:T(8,128)(2,1)} %get-tuple-element.167), channel_id=1, source_target_pairs={{0,3},{1,2},{2,1},{3,0},{4,7},{5,6},{6,5},{7,4},{8,11},{9,10},{10,... | collective-permute-start | bytes 786440 | tf_op jit(solution)/shard_map/ppermute | solution.py:809
  252.8 31.0 %collective-permute-start.27 = (bf16[2,2,128,256]{3,2,1,0:T(8,128)(2,1)}, bf16[2,2,128,256]{3,2,1,0:T(8,128)(2,1)S(1)}, u32[]{:S(2)}, u32[]{:S(2)}) collective-permute-start(bf16[2,2,128,256]{3,2,1,0:T(8,128)(2,1)} %get-tuple-element.165), channel_id=1, source_target_pairs={{0,2},{1,3},{2,0},{3,1},{4,6},{5,7},{6,4},{7,5},{8,10},{9,11},{10,... | collective-permute-start | bytes 786440 | tf_op jit(solution)/shard_map/ppermute | solution.py:809
  265.3 18.5 %collective-permute-start.26 = (bf16[2,2,128,256]{3,2,1,0:T(8,128)(2,1)}, bf16[2,2,128,256]{3,2,1,0:T(8,128)(2,1)S(1)}, u32[]{:S(2)}, u32[]{:S(2)}) collective-permute-start(bf16[2,2,128,256]{3,2,1,0:T(8,128)(2,1)} %get-tuple-element.163), channel_id=1, source_target_pairs={{0,1},{1,0},{2,3},{3,2},{4,5},{5,4},{6,7},{7,6},{8,9},{9,8},{10,11... | collective-permute-start | bytes 786440 | tf_op jit(solution)/shard_map/ppermute | solution.py:809
  265.9 23.0 %copy-start.22 = (f32[2,5,768]{2,1,0:T(8,128)S(1)}, f32[2,5,768]{2,1,0:T(8,128)}, u32[]{:S(2)}) copy-start(f32[2,5,768]{2,1,0:T(8,128)} %copy-done.21) | copy-start | bytes 92164
  265.9 23.6 %copy-start.36 = (f32[8,768]{1,0:T(8,128)S(1)}, f32[8,768]{1,0:T(8,128)}, u32[]{:S(2)}) copy-start(f32[8,768]{1,0:T(8,128)} %get-tuple-element.169) | copy-start | bytes 73732
  283.8 19.9 %collective-permute-start.31 = (bf16[2,2,128,256]{3,2,1,0:T(8,128)(2,1)}, bf16[2,2,128,256]{3,2,1,0:T(8,128)(2,1)S(1)}, u32[]{:S(2)}, u32[]{:S(2)}) collective-permute-start(bf16[2,2,128,256]{3,2,1,0:T(8,128)(2,1)} %get-tuple-element.183), channel_id=1, source_target_pairs={{0,3},{1,2},{2,1},{3,0},{4,7},{5,6},{6,5},{7,4},{8,11},{9,10},{10,... | collective-permute-start | bytes 786440 | tf_op jit(solution)/shard_map/ppermute | solution.py:809
  286.3 17.4 %collective-permute-start.30 = (bf16[2,2,128,256]{3,2,1,0:T(8,128)(2,1)}, bf16[2,2,128,256]{3,2,1,0:T(8,128)(2,1)S(1)}, u32[]{:S(2)}, u32[]{:S(2)}) collective-permute-start(bf16[2,2,128,256]{3,2,1,0:T(8,128)(2,1)} %get-tuple-element.181), channel_id=1, source_target_pairs={{0,2},{1,3},{2,0},{3,1},{4,6},{5,7},{6,4},{7,5},{8,10},{9,11},{10,... | collective-permute-start | bytes 786440 | tf_op jit(solution)/shard_map/ppermute | solution.py:809
  286.9 16.8 %collective-permute-start.29 = (bf16[2,2,128,256]{3,2,1,0:T(8,128)(2,1)}, bf16[2,2,128,256]{3,2,1,0:T(8,128)(2,1)S(1)}, u32[]{:S(2)}, u32[]{:S(2)}) collective-permute-start(bf16[2,2,128,256]{3,2,1,0:T(8,128)(2,1)} %get-tuple-element.179), channel_id=1, source_target_pairs={{0,1},{1,0},{2,3},{3,2},{4,5},{5,4},{6,7},{7,6},{8,9},{9,8},{10,11... | collective-permute-start | bytes 786440 | tf_op jit(solution)/shard_map/ppermute | solution.py:809
  303.8 4.1 %collective-permute-start.33 = (bf16[4,4,112,512]{3,2,1,0:T(8,128)(2,1)}, bf16[4,4,112,512]{3,2,1,0:T(8,128)(2,1)S(1)}, u32[]{:S(2)}, u32[]{:S(2)}) collective-permute-start(bf16[4,4,112,512]{3,2,1,0:T(8,128)(2,1)} %get-tuple-element.196), channel_id=1, source_target_pairs={{0,4},{4,0},{8,12},{12,8},{16,20},{20,16},{24,28},{28,24},{1,5},{5... | collective-permute-start | bytes 5505032 | tf_op jit(solution)/shard_map/ppermute | solution.py:809
  323.0 25.3 %collective-permute-start.32 = (bf16[4,4,112,256]{3,2,1,0:T(8,128)(2,1)}, bf16[4,4,112,256]{3,2,1,0:T(8,128)(2,1)S(1)}, u32[]{:S(2)}, u32[]{:S(2)}) collective-permute-start(bf16[4,4,112,256]{3,2,1,0:T(8,128)(2,1)} %get-tuple-element.192), channel_id=1, source_target_pairs={{0,4},{4,0},{8,12},{12,8},{16,20},{20,16},{24,28},{28,24},{1,5},{5... | collective-permute-start | bytes 2752520 | tf_op jit(solution)/shard_map/ppermute | solution.py:809
  324.3 13.6 %collective-permute-start.34 = (bf16[4,112,512]{2,1,0:T(8,128)(2,1)}, bf16[4,112,512]{2,1,0:T(8,128)(2,1)S(1)}, u32[]{:S(2)}, u32[]{:S(2)}) collective-permute-start(bf16[4,112,512]{2,1,0:T(8,128)(2,1)} %get-tuple-element.319), channel_id=1, source_target_pairs={{0,8},{4,12},{8,0},{12,4},{16,24},{20,28},{24,16},{28,20},{1,9},{5... | collective-permute-start | bytes 1376264 | tf_op jit(solution)/shard_map/ppermute | solution.py:809
  325.4 13.1 %collective-permute-start.35 = (bf16[4,112,512]{2,1,0:T(8,128)(2,1)}, bf16[4,112,512]{2,1,0:T(8,128)(2,1)S(1)}, u32[]{:S(2)}, u32[]{:S(2)}) collective-permute-start(bf16[4,112,512]{2,1,0:T(8,128)(2,1)} %get-tuple-element.318), channel_id=1, source_target_pairs={{0,16},{4,20},{8,24},{12,28},{16,0},{20,4},{24,8},{28,12},{1,17},{... | collective-permute-start | bytes 1376264 | tf_op jit(solution)/shard_map/ppermute | solution.py:809
  325.9 22.2 %collective-permute-start.36 = (bf16[4,112,512]{2,1,0:T(8,128)(2,1)S(1)}, bf16[4,112,512]{2,1,0:T(8,128)(2,1)S(1)}, u32[]{:S(2)}, u32[]{:S(2)}) collective-permute-start(bf16[4,112,512]{2,1,0:T(8,128)(2,1)S(1)} %get-tuple-element.317), channel_id=1, source_target_pairs={{0,24},{4,28},{8,16},{12,20},{16,8},{20,12},{24,0},{28,4},{1,25},{... | collective-permute-start | bytes 1376264 | tf_op jit(solution)/shard_map/ppermute | solution.py:809
  348.6 17.0 %copy-start.19 = (bf16[2,512,768]{2,1,0:T(8,128)(2,1)S(1)}, bf16[2,512,768]{2,1,0:T(8,128)(2,1)}, u32[]{:S(2)}) copy-start(bf16[2,512,768]{2,1,0:T(8,128)(2,1)} %get-tuple-element.141) | copy-start | bytes 4718596
  348.7 8.6 %collective-permute-start.37 = (bf16[4,112,256]{2,1,0:T(8,128)(2,1)S(1)}, bf16[4,112,256]{2,1,0:T(8,128)(2,1)S(1)}, u32[]{:S(2)}, u32[]{:S(2)}) collective-permute-start(bf16[4,112,256]{2,1,0:T(8,128)(2,1)S(1)} %get-tuple-element.322), channel_id=1, source_target_pairs={{0,8},{4,12},{8,0},{12,4},{16,24},{20,28},{24,16},{28,20},{1,9},{5... | collective-permute-start | bytes 688136 | tf_op jit(solution)/shard_map/ppermute | solution.py:809
  349.6 11.4 %collective-permute-start.38 = (bf16[4,112,256]{2,1,0:T(8,128)(2,1)S(1)}, bf16[4,112,256]{2,1,0:T(8,128)(2,1)S(1)}, u32[]{:S(2)}, u32[]{:S(2)}) collective-permute-start(bf16[4,112,256]{2,1,0:T(8,128)(2,1)S(1)} %get-tuple-element.324), channel_id=1, source_target_pairs={{0,16},{4,20},{8,24},{12,28},{16,0},{20,4},{24,8},{28,12},{1,17},{... | collective-permute-start | bytes 688136 | tf_op jit(solution)/shard_map/ppermute | solution.py:809
  351.1 9.9 %collective-permute-start.39 = (bf16[4,112,256]{2,1,0:T(8,128)(2,1)S(1)}, bf16[4,112,256]{2,1,0:T(8,128)(2,1)S(1)}, u32[]{:S(2)}, u32[]{:S(2)}) collective-permute-start(bf16[4,112,256]{2,1,0:T(8,128)(2,1)S(1)} %get-tuple-element.323), channel_id=1, source_target_pairs={{0,24},{4,28},{8,16},{12,20},{16,8},{20,12},{24,0},{28,4},{1,25},{... | collective-permute-start | bytes 688136 | tf_op jit(solution)/shard_map/ppermute | solution.py:809
  352.3 11.9 %collective-permute-start.42 = (bf16[112,512]{1,0:T(8,128)(2,1)S(1)}, bf16[112,512]{1,0:T(8,128)(2,1)S(1)}, u32[]{:S(2)}, u32[]{:S(2)}) collective-permute-start(bf16[112,512]{1,0:T(8,128)(2,1)S(1)} %get-tuple-element.333), channel_id=1, source_target_pairs={{0,1},{1,0},{2,3},{3,2},{4,5},{5,4},{6,7},{7,6},{8,9},{9,8},{10,11... | collective-permute-start | bytes 344072 | tf_op jit(solution)/shard_map/ppermute | solution.py:809
  353.0 15.7 %collective-permute-start.43 = (bf16[112,512]{1,0:T(8,128)(2,1)S(1)}, bf16[112,512]{1,0:T(8,128)(2,1)S(1)}, u32[]{:S(2)}, u32[]{:S(2)}) collective-permute-start(bf16[112,512]{1,0:T(8,128)(2,1)S(1)} %get-tuple-element.332), channel_id=1, source_target_pairs={{0,2},{1,3},{2,0},{3,1},{4,6},{5,7},{6,4},{7,5},{8,10},{9,11},{10,... | collective-permute-start | bytes 344072 | tf_op jit(solution)/shard_map/ppermute | solution.py:809
  357.3 12.6 %collective-permute-start.44 = (bf16[112,512]{1,0:T(8,128)(2,1)S(1)}, bf16[112,512]{1,0:T(8,128)(2,1)S(1)}, u32[]{:S(2)}, u32[]{:S(2)}) collective-permute-start(bf16[112,512]{1,0:T(8,128)(2,1)S(1)} %get-tuple-element.331), channel_id=1, source_target_pairs={{0,3},{1,2},{2,1},{3,0},{4,7},{5,6},{6,5},{7,4},{8,11},{9,10},{10,... | collective-permute-start | bytes 344072 | tf_op jit(solution)/shard_map/ppermute | solution.py:809
  361.2 13.3 %collective-permute-start.45 = (bf16[112,256]{1,0:T(8,128)(2,1)S(1)}, bf16[112,256]{1,0:T(8,128)(2,1)S(1)}, u32[]{:S(2)}, u32[]{:S(2)}) collective-permute-start(bf16[112,256]{1,0:T(8,128)(2,1)S(1)} %get-tuple-element.337), channel_id=1, source_target_pairs={{0,1},{1,0},{2,3},{3,2},{4,5},{5,4},{6,7},{7,6},{8,9},{9,8},{10,11... | collective-permute-start | bytes 172040 | tf_op jit(solution)/shard_map/ppermute | solution.py:809
  361.9 12.6 %collective-permute-start.46 = (bf16[112,256]{1,0:T(8,128)(2,1)S(1)}, bf16[112,256]{1,0:T(8,128)(2,1)S(1)}, u32[]{:S(2)}, u32[]{:S(2)}) collective-permute-start(bf16[112,256]{1,0:T(8,128)(2,1)S(1)} %get-tuple-element.336), channel_id=1, source_target_pairs={{0,2},{1,3},{2,0},{3,1},{4,6},{5,7},{6,4},{7,5},{8,10},{9,11},{10,... | collective-permute-start | bytes 172040 | tf_op jit(solution)/shard_map/ppermute | solution.py:809
  364.2 10.3 %collective-permute-start.47 = (bf16[112,256]{1,0:T(8,128)(2,1)S(1)}, bf16[112,256]{1,0:T(8,128)(2,1)S(1)}, u32[]{:S(2)}, u32[]{:S(2)}) collective-permute-start(bf16[112,256]{1,0:T(8,128)(2,1)S(1)} %get-tuple-element.335), channel_id=1, source_target_pairs={{0,3},{1,2},{2,1},{3,0},{4,7},{5,6},{6,5},{7,4},{8,11},{9,10},{10,... | collective-permute-start | bytes 172040 | tf_op jit(solution)/shard_map/ppermute | solution.py:809
  368.6 14.8 %collective-permute-start.41 = (bf16[2,64,768]{2,1,0:T(8,128)(2,1)}, bf16[2,64,768]{2,1,0:T(8,128)(2,1)S(1)}, u32[]{:S(2)}, u32[]{:S(2)}) collective-permute-start(bf16[2,64,768]{2,1,0:T(8,128)(2,1)} %get-tuple-element.201), channel_id=1, source_target_pairs={{1,0},{2,1},{3,2},{5,4},{6,5},{7,6},{9,8},{10,9},{11,10},{13,12},{... | collective-permute-start | bytes 589832 | tf_op jit(solution)/shard_map/ppermute | solution.py:819
  369.9 12.5 %collective-permute-start.40 = (bf16[2,64,768]{2,1,0:T(8,128)(2,1)}, bf16[2,64,768]{2,1,0:T(8,128)(2,1)S(1)}, u32[]{:S(2)}, u32[]{:S(2)}) collective-permute-start(bf16[2,64,768]{2,1,0:T(8,128)(2,1)} %get-tuple-element.199), channel_id=1, source_target_pairs={{0,1},{1,2},{2,3},{4,5},{5,6},{6,7},{8,9},{9,10},{10,11},{12,13},{... | collective-permute-start | bytes 589832 | tf_op jit(solution)/shard_map/ppermute | solution.py:814
  (28 other events, 135.8 us)
Sparse Core Ops, SparseCore 0:
  27.9 33.0 all-gather.4
  69.9 58.4 all-gather.6
  207.5 85.7 reduce-scatter.2
  314.3 31.2 reduce-scatter.4

commit v5 on v4

--- a/solution.py
+++ b/solution.py
@@ -217,11 +217,11 @@
 def attend_backward_kernel(blocks, q_ref, k_ref, v_ref, *refs):
     pk, pv = refs[:blocks], refs[blocks : 2 * blocks]
     segq, segk, cen, grad_ref, dq_ref, dk_ref, dv_ref = refs[2 * blocks : 2 * blocks + 7]
-    dp_refs = refs[2 * blocks + 7 : 3 * blocks + 7]
+    dp_refs = refs[2 * blocks + 7 : 2 * blocks + 9]
     (
         near_bias, far_bias, far_keys, far_values,
         query, far_scores, far_probs, grad, far_dots, far_grads,
-    ) = refs[3 * blocks + 7 :]
+    ) = refs[2 * blocks + 9 :]
 
     @pl.when(pl.program_id(1) == 0)
     def _():
@@ -269,10 +269,11 @@
         dq_ref[0, first : first + QB, :] = jnp.where(head_mask(0), both[:QB], both[QB:]).astype(BF)
     dpk = nn(query[...].T, far_grads[...]).T.astype(BF)
     dpv = nn(grad[...].T, far_probs[...]).T.astype(BF)
-    far_rows = dp_refs[0].shape[2]
-    for n, ref in enumerate(dp_refs):
-        ref[0, 0] = dpk[n * far_rows : (n + 1) * far_rows]
-        ref[1, 0] = dpv[n * far_rows : (n + 1) * far_rows]
+    far_rows = dp_refs[0].shape[3]
+    for n in range(blocks):
+        span = slice(n * far_rows, (n + 1) * far_rows)
+        dp_refs[n % 2][n // 2, 0, 0] = dpk[span]
+        dp_refs[n % 2][n // 2, 1, 0] = dpv[span]
 
 
 def attention_specs(wide, blocks, far_rows):
@@ -332,15 +333,15 @@
     own_spec = pl.BlockSpec((1, rows, PAIR), lambda s, h: (s, 0, h))
     wide_spec = pl.BlockSpec((1, wide, PAIR), lambda s, h: (s, 0, h))
     wide_shape = jax.ShapeDtypeStruct((seqs, wide, span), F32)
-    far_spec = pl.BlockSpec((2, 1, far_rows, PAIR), lambda s, h: (0, s, 0, h))
-    far_shape = jax.ShapeDtypeStruct((2, seqs, far_rows, span), BF)
+    far_spec = pl.BlockSpec((blocks // 2, 2, 1, far_rows, PAIR), lambda s, h: (0, 0, s, 0, h))
+    far_shape = jax.ShapeDtypeStruct((blocks // 2, 2, seqs, far_rows, span), BF)
     out = pl.pallas_call(
         partial(attend_backward_kernel, blocks),
         grid=(seqs, span // PAIR),
         in_specs=attention_specs(wide, blocks, far_rows) + [own_spec],
-        out_specs=[own_spec, wide_spec, wide_spec] + [far_spec] * blocks,
+        out_specs=[own_spec, wide_spec, wide_spec] + [far_spec] * 2,
         out_shape=[jax.ShapeDtypeStruct((seqs, rows, span), BF), wide_shape, wide_shape]
-        + [far_shape] * blocks,
+        + [far_shape] * 2,
         scratch_shapes=attention_scratch(rows, blocks * far_rows)
         + [
             pltpu.VMEM((2 * rows, PAIR), BF),
@@ -455,15 +456,15 @@
             gpre[block, :] = low
             bias_sum = bias_sum + column_sum(low)
             acc[block, :] += nt(low, up_ref)
-        height = gud_ref.shape[2] - EXTRA
+        height = gud_ref.shape[3] - EXTRA
         lead = (gud_ref.shape[0], height, units)
-        gud_ref[:, 0, :height] = nn(flow_t[...], gpre[...]).astype(BF).reshape(lead)
-        gud_ref[:, 1, :height] = nn(gffn_t[...], hidden[which]).astype(BF).reshape(lead)
+        gud_ref[:, 0, 0, :height] = nn(flow_t[...], gpre[...]).astype(BF).reshape(lead)
+        gud_ref[:, 0, 1, :height] = nn(gffn_t[...], hidden[which]).astype(BF).reshape(lead)
         head = lax.broadcasted_iota(jnp.int32, (EXTRA, 1), 0) == 0
         extra = jnp.where(head, bias_sum, 0.0).astype(BF)
         for m in range(gud_ref.shape[0]):
-            gud_ref[m, 0, height:] = extra
-            gud_ref[m, 1, height:] = jnp.zeros((EXTRA, units), BF)
+            gud_ref[m, 0, 0, height:] = extra
+            gud_ref[m, 0, 1, height:] = jnp.zeros((EXTRA, units), BF)
 
     @pl.when(step == 2 * steps - 1)
     def _():
@@ -508,12 +509,14 @@
         + [jax.ShapeDtypeStruct((seqs, rows, span), BF)] * chunks
         + [jax.ShapeDtypeStruct((width, span), BF)] * chunks
         + [
-            jax.ShapeDtypeStruct((row_blocks, 2, height + EXTRA, steps * units), BF),
+            jax.ShapeDtypeStruct((row_blocks, steps, 2, height + EXTRA, units), BF),
             jax.ShapeDtypeStruct((8, width), F32),
         ]
     )
     out_specs = [once(o.shape) for o in out_shape[: 2 + 2 * chunks]] + [
-        pl.BlockSpec((row_blocks, 2, height + EXTRA, units), lambda i: (0, 0, 0, back(i))),
+        pl.BlockSpec(
+            (row_blocks, 1, 2, height + EXTRA, units), lambda i: (0, back(i), 0, 0, 0)
+        ),
         once((8, width)),
     ]
     out = pl.pallas_call(
@@ -848,7 +851,14 @@
 
 
 def spread_line(values):
-    return [swap(values, "tp", d) for d in range(1, lax.axis_size("tp"))]
+    two = swap(values, "tp", 2)
+    return [swap(values, "tp", 1), two, swap(two, "tp", 1)]
+
+
+def merge_line(own, other, *waits):
+    sent = after(other, *waits) if waits else other
+    merged = add_low(own, swap(sent, "tp", 1)).astype(BF)
+    return [merged[0], swap(merged[1], "tp", 2)]
 
 
 def add_low(first, *others):
@@ -993,12 +1003,12 @@
 
     for j in range(chunks):
         if j:
-            offs = after(offs, made[-1][1])
+            offs = after(offs, made[-1][1], *([slots[0][2]] if j > 1 else []))
         made.append(project(j, chunks, pieces, offs, x_wide, bias_qkv, taps, same, far_rows))
         if j == 0:
             send_pooled(0)
-    if chunks > 1:
-        send_pooled(1, made[-1][1], *slots[0][1:])
+        if j == 1:
+            send_pooled(1, slots[0][2])
     weights = after(weights, made[0][1])
     weights = lax.all_gather(weights, "fsdp", axis=0, tiled=False)
     for j in range(chunks):
@@ -1010,7 +1020,7 @@
             order = segs[:2] + (after(segs[2], att[-1], x_cols, cot),)
         att.append(attend_forward(made[j][0], slots[j], order))
         if j + 2 < chunks:
-            send_pooled(j + 2, att[j])
+            send_pooled(j + 2, att[j], slots[j + 1][2])
     if shard_rows % 16:
         weights = weights.transpose(1, 0, 2, 3).reshape(1, tp, width, -1)
 
@@ -1019,10 +1029,10 @@
         att, [m[2] for m in made], x_wide, cot, weights, bias_up, misc
     )
     if gud.shape[0] == 1:
-        gud = spread_rows(gud[0], fsdp)
+        gud = spread_rows(gud.reshape(2 * tp, -1, hidden_local), fsdp)
+        gud = gud.reshape(fsdp, tp, 2, -1, hidden_local)
     gud = lax.psum_scatter(gud, "fsdp", scatter_dimension=0, tiled=False)
-    gud_parts = gud.reshape(2, shard_rows + EXTRA, tp, hidden_local).transpose(2, 0, 1, 3)
-    gud = lax.psum_scatter(gud_parts, "tp", scatter_dimension=0, tiled=False).astype(F32)
+    grad_up_down = lax.psum_scatter(gud, "tp", scatter_dimension=0, tiled=False).astype(F32)
 
     if fast:
         mine = lax.axis_index("fsdp")
@@ -1037,12 +1047,11 @@
     for j in range(chunks):
         order = segs
         if j:
-            waits = (backs[-1][0],) + (tuple(backs[-2][3][1:]) if j > 1 else ())
+            waits = (backs[-1][0],) + (tuple(backs[-2][3][:1]) if j > 1 else ())
             order = segs[:2] + (after(segs[2], *waits),)
         dq, dk, dv, dps = attend_backward(made[j][0], slots[j], order, grad_att[j])
-        if j:
-            dps = [after(d, *backs[-1][3][1:]) for d in dps]
-        arrived = [dps[0]] + [swap(dps[d], "tp", d) for d in range(1, tp)]
+        waits = (backs[-1][3][:1] if j else []) + (backs[-2][3][1:] if j > 1 else [])
+        arrived = merge_line(*dps, *waits)
         backs.append((dq, dk, dv, arrived, made[j][0], grad_out[j]))
     totals, lows, merged = [], [], []
     for low, high in ((0, chunks - 1), (chunks - 1, chunks)):
@@ -1055,7 +1064,7 @@
             lines = -(-flat.size // cols)
             flat = jnp.pad(flat, (0, lines * cols - flat.size)).reshape(lines, cols)
             more = jnp.pad(flat, ((TAPS + 1, EXTRA - TAPS - 1 - lines), (0, 0)))
-        waits = [backs[-1][0]] + ([gud_parts] if merged else [])
+        waits = [backs[-1][0], backs[-1][3][0]] + ([gud] if merged else [])
         groups, low_kv = gather_back(
             low, after(out_offs, *waits), group_sizes, backs[low:high], taps, same, x_cols, more
         )
@@ -1098,9 +1107,9 @@
         extra_rows[1:, 1 : TAPS + 1],
         grad_w_out,
         sums[0:2],
-        gud[0, :shard_rows],
-        gud[0, shard_rows],
-        gud[1, :shard_rows],
+        grad_up_down[0, :shard_rows],
+        grad_up_down[0, shard_rows],
+        grad_up_down[1, :shard_rows],
         sums[2:4],
         sums[4:6],
     )

time: 404 us -> 393 us (0.973)
  starting transfers between devices: 82.6 us -> 55.7 us
  waiting for transfers between devices: 50.1 us -> 69.4 us
    ppermute x44 -> x41, starting transfers between devices: 71.1 us -> 44.3 us  [swap(): return lax.ppermute(values, axis, [(i, i ^ mask) for i in range(count)])]
    ppermute x44 -> x41, waiting for transfers between devices: 50 us -> 69.3 us  [swap(): return lax.ppermute(values, axis, [(i, i ^ mask) for i in range(count)])]
    another operation x2 -> x0, local copies, waits for them, and re-layouts: 4.25 us -> none  [body(): gud.reshape(2, shard_rows + EXTRA, tp, hidden_local).transpose(2, 0, 1, 3)]
    unnamed x92 -> x84, local copies, waits for them, and re-layouts: 26.9 us -> 26.7 us
  transfers between devices with their start and end apart: 52 -> 49, of which waited for: 15 -> 17; matrix products, arithmetic and copies ran while one was open for 12% -> 12% of each run, Pallas kernels for 32% -> 33%
where the time goes in v5:
time: 393 us; the launch traced here: 386 us
  Pallas kernels  181 us (46%)
  waiting for transfers between devices  69.4 us (18%)
  starting transfers between devices  55.7 us (14%)
  local copies, waits for them, and re-layouts  55.3 us (14%)
  between operations  15.1 us (4%)
  other arithmetic  9.83 us (3%)
    ppermute x41, waiting for transfers between devices, swap(): return lax.ppermute(values, axis, [(i, i ^ mask) for i in range(count)])  69.3 us
    pallas_call x3, Pallas kernels, attend_backward(): pl.pallas_call(partial(attend_backward_kernel, blocks), grid=(seqs, span...  53.7 us
    pallas_call x1, Pallas kernels, dense(): pl.pallas_call(partial(dense_kernel, chunks, steps), grid=(2 * steps,), i...  53.7 us
    ppermute x41, starting transfers between devices, swap(): return lax.ppermute(values, axis, [(i, i ^ mask) for i in range(count)])  44.3 us
    unnamed x84, local copies, waits for them, and re-layouts  26.7 us
    pallas_call x3, Pallas kernels, attend_forward(): pl.pallas_call(partial(attend_forward_kernel, blocks), grid=(seqs, span /...  26.3 us
    pallas_call x2, Pallas kernels, gather_back(): pl.pallas_call(partial(gather_back_kernel, blocks, chunks, len(group_size...  21 us
    pallas_call x3, Pallas kernels, project(): pl.pallas_call(partial(project_kernel, len(pieces)), grid_spec=pltpu.Pref...  15.6 us
  transfers between devices with their start and end apart: 49, of which 17 were waited for; matrix products, arithmetic and copies ran while one was open for 12% of the time, Pallas kernels for 33%

profile of v5, /device:TPU:0, one launch (start us, length us, event | category | flops | bytes accessed | tf_op | source)
XLA Modules:
  0.0 386.0 jit_solution(12936119494904151838)
XLA Ops:
  12.2 5.1 %collective-permute-start = (bf16[109,768]{0,1:T(8,128)(2,1)S(1)}, bf16[109,768]{0,1:T(8,128)(2,1)S(1)}, u32[]{:S(2)}, u32[]{:S(2)}) collective-permute-start(bf16[109,768]{0,1:T(8,128)(2,1)S(1)} %pad_maximum_fusion.2), channel_id=1, source_target_pairs={{0,3},{1,2},{2,1},{3,0},{4,7},{5,6},{6,5},{7,4},{8,11},{9,10},{10,... | collective-permute-start | bytes 502280 | tf_op jit(solution)/shard_map/ppermute | solution.py:812
  18.0 2.7 copy.271
  21.8 4.0 %collective-permute-start.5 = (bf16[64,2,768]{2,0,1:T(8,128)(2,1)S(1)}, bf16[64,2,768]{2,0,1:T(8,128)(2,1)}, u32[]{:S(2)}, u32[]{:S(2)}) collective-permute-start(bf16[64,2,768]{2,0,1:T(8,128)(2,1)S(1)} %get-tuple-element.296), channel_id=1, source_target_pairs={{0,1},{1,2},{2,3},{4,5},{5,6},{6,7},{8,9},{9,10},{10,11},{12,13},{... | collective-permute-start | bytes 589832 | tf_op jit(solution)/shard_map/ppermute | solution.py:817
  25.7 1.3 collective-permute-start.6
  32.3 2.7 collective-permute-done.1
  36.2 1.6 collective-permute-start.3
  37.7 1.5 collective-permute-start.4
  41.3 1.7 maximum_bitcast_fusion.refs_10_.refs_6_
  43.0 6.7 %collective-permute-done.3.refs_1_ = bf16[96,3072]{1,0:T(8,128)(2,1)S(1)} collective-permute-done((bf16[96,3072]{1,0:T(8,128)(2,1)S(1)}, bf16[96,3072]{1,0:T(8,128)(2,1)S(1)}, u32[]{:S(2)}, u32[]{:S(2)}) %collective-permute-start.3) | collective-permute-done | bytes 589856 | tf_op jit(solution)/shard_map/ppermute | solution.py:812
  49.7 1.6 collective-permute-start.7
  54.3 3.0 collective-permute-done.7.refs_3_
  57.3 2.6 collective-permute-done.8.refs_4_
  60.1 1.8 collective-permute-done.13.refs_9_
  61.9 5.4 %shard_map.220 = (bf16[3,2,640,256]{3,2,1,0:T(8,128)(2,1)S(1)}, bf16[2,2,128,256]{3,2,1,0:T(8,128)(2,1)}, bf16[4,768,256]{2,1,0:T(8,128)(2,1)S(1)}) custom-call(s32[10]{0:T(128)S(1)} %stack.97.offs, bf16[96,3072]{1,0:T(8,128)(2,1)S(1)} %copy.283.refs_0_, bf16[96,3072]{1,0:T(8,128)(2,1)S(1)} %collective-permute-done.3.refs_1_, ...), custom_call_target="tpu_custom_call" | custom-call | flops 1 | bytes 1 | tf_op jit(solution)/shard_map/pallas_call | solution.py:100
  67.3 1.3 copy-done.1
  70.3 3.0 collective-permute-start.14
  73.4 5.4 %shard_map.222 = (bf16[3,2,640,256]{3,2,1,0:T(8,128)(2,1)S(1)}, bf16[2,2,128,256]{3,2,1,0:T(8,128)(2,1)}, bf16[4,768,256]{2,1,0:T(8,128)(2,1)S(1)}) custom-call(s32[10]{0:T(128)S(1)} %stack.97.offs, bf16[96,3072]{1,0:T(8,128)(2,1)S(1)} %copy.283.refs_0_, bf16[96,3072]{1,0:T(8,128)(2,1)S(1)} %collective-permute-done.3.refs_1_, ...), custom_call_target="tpu_custom_call" | custom-call | flops 1 | bytes 1 | tf_op jit(solution)/shard_map/pallas_call | solution.py:100
  78.8 1.3 copy-done.2
  80.1 1.2 copy-done.5
  81.2 4.2 %collective-permute-done.15.refs_2_.refs_6_ = bf16[2,2,128,256]{3,2,1,0:T(8,128)(2,1)} collective-permute-done((bf16[2,2,128,256]{3,2,1,0:T(8,128)(2,1)}, bf16[2,2,128,256]{3,2,1,0:T(8,128)(2,1)}, u32[]{:S(2)}, u32[]{:S(2)}) %collective-permute-start.15) | collective-permute-done | bytes 262176 | tf_op jit(solution)/shard_map/ppermute | solution.py:812
  85.4 1.7 collective-permute-start.18
  89.0 4.7 %shard_map.224 = (bf16[3,2,640,256]{3,2,1,0:T(8,128)(2,1)S(1)}, bf16[2,2,128,256]{3,2,1,0:T(8,128)(2,1)S(1)}, bf16[4,768,256]{2,1,0:T(8,128)(2,1)S(1)}) custom-call(s32[10]{0:T(128)S(1)} %stack.97.offs, bf16[96,3072]{1,0:T(8,128)(2,1)S(1)} %copy.283.refs_0_, bf16[96,3072]{1,0:T(8,128)(2,1)S(1)} %collective-permute-done.3.refs_1_, ...), custom_call_target="tpu_custom_call" | custom-call | flops 1 | bytes 1 | tf_op jit(solution)/shard_map/pallas_call | solution.py:100
  93.8 1.3 copy-done
  95.1 1.1 copy-done.6
  96.2 1.9 collective-permute-done.16.refs_3_.refs_7_
  98.1 9.0 %shard_map.221.refs_0_ = bf16[2,512,256]{2,1,0:T(8,128)(2,1)} custom-call(bf16[3,2,640,256]{3,2,1,0:T(8,128)(2,1)} %copy-done.1, bf16[3,2,640,256]{3,2,1,0:T(8,128)(2,1)} %copy-done.1, bf16[3,2,640,256]{3,2,1,0:T(8,128)(2,1)} %copy-done.1, bf16[2,2,128,256]{3,2,1,0:T(8,128)(2,1)} %get-tuple-element.112.refs_0_.refs_4_, ...), custom_call_target="tpu_custom_call" | custom-call | flops 1 | bytes 1 | tf_op jit(solution)/shard_map/pallas_call | solution.py:316
  107.4 2.5 collective-permute-start.17
  110.0 1.9 collective-permute-start.19
  111.9 8.6 %collective-permute-done.21.refs_2_.refs_6_ = bf16[2,2,128,256]{3,2,1,0:T(8,128)(2,1)S(1)} collective-permute-done((bf16[2,2,128,256]{3,2,1,0:T(8,128)(2,1)S(1)}, bf16[2,2,128,256]{3,2,1,0:T(8,128)(2,1)S(1)}, u32[]{:S(2)}, u32[]{:S(2)}) %collective-permute-start.21) | collective-permute-done | bytes 262176 | tf_op jit(solution)/shard_map/ppermute | solution.py:812
  122.7 2.3 copy.297
  124.9 2.8 copy.303
  127.7 6.4 %collective-permute-done.19.refs_3_.refs_7_ = bf16[2,2,128,256]{3,2,1,0:T(8,128)(2,1)} collective-permute-done((bf16[2,2,128,256]{3,2,1,0:T(8,128)(2,1)}, bf16[2,2,128,256]{3,2,1,0:T(8,128)(2,1)}, u32[]{:S(2)}, u32[]{:S(2)}) %collective-permute-start.19) | collective-permute-done | bytes 262176 | tf_op jit(solution)/shard_map/ppermute | solution.py:812
  134.2 8.6 %shard_map.223.refs_1_ = bf16[2,512,256]{2,1,0:T(8,128)(2,1)} custom-call(bf16[3,2,640,256]{3,2,1,0:T(8,128)(2,1)} %copy-done.2, bf16[3,2,640,256]{3,2,1,0:T(8,128)(2,1)} %copy-done.2, bf16[3,2,640,256]{3,2,1,0:T(8,128)(2,1)} %copy-done.2, bf16[2,2,128,256]{3,2,1,0:T(8,128)(2,1)} %get-tuple-element.116.refs_0_.refs_4_, bf16[2,2,128,256]{3,2,1,0:T(8,128)(2,1)} %copy-done.14, ...), custom_call_target="tpu_custom_call" | custom-call | flops 1 | bytes 1 | tf_op jit(solution)/shard_map/pallas_call | solution.py:316
  143.6 8.7 %shard_map.225.refs_2_ = bf16[2,512,256]{2,1,0:T(8,128)(2,1)} custom-call(bf16[3,2,640,256]{3,2,1,0:T(8,128)(2,1)} %copy-done, bf16[3,2,640,256]{3,2,1,0:T(8,128)(2,1)} %copy-done, bf16[3,2,640,256]{3,2,1,0:T(8,128)(2,1)} %copy-done, bf16[2,2,128,256]{3,2,1,0:T(8,128)(2,1)} %copy-done.8, bf16[2,2,128,256]{3,2,1,0:T(8,128)(2,1)} %copy-done.12, ...), custom_call_target="tpu_custom_call" | custom-call | flops 1 | bytes 1 | tf_op jit(solution)/shard_map/pallas_call | solution.py:316
  152.3 53.7 %shard_map.226 = (bf16[2,512,768]{2,1,0:T(8,128)(2,1)}, f32[2,512,768]{2,1,0:T(8,128)}, bf16[2,512,256]{2,1,0:T(8,128)(2,1)}, bf16[2,512,256]{2,1,0:T(8,128)(2,1...) custom-call(bf16[2,512,256]{2,1,0:T(8,128)(2,1)} %shard_map.221.refs, ...), custom_call_target="tpu_custom_call" | custom-call | flops 1 | bytes 1 | tf_op jit(solution)/shard_map/pallas_call | solution.py:522
  206.1 17.8 %shard_map.227 = (bf16[2,512,256]{2,1,0:T(8,128)(2,1)}, f32[2,640,256]{2,1,0:T(8,128)}, f32[2,640,256]{2,1,0:T(8,128)}, bf16[2,2,2,128,256]{4,3,2,1,0:T(8,128)(2,1)}, bf16[2,2,2,128,256]{4,3,2,1,0:T(8,128)(2,1)}) custom-call(bf16[3,2,640,256]{3,2,1,0:T(8,128)(2,1)} %copy-done.1, bf16[3,2,640,256]{3,2,1,0:T(8,128)(2,1)} %copy-done.1, ...), custom_call_target="tpu_custom_call" | custom-call | flops 1 | bytes 1 | tf_op jit(solution)/shard_map/pallas_call | solution.py:338
  224.0 17.8 %shard_map.228 = (bf16[2,512,256]{2,1,0:T(8,128)(2,1)}, f32[2,640,256]{2,1,0:T(8,128)}, f32[2,640,256]{2,1,0:T(8,128)}, bf16[2,2,2,128,256]{4,3,2,1,0:T(8,128)(2,1)}, bf16[2,2,2,128,256]{4,3,2,1,0:T(8,128)(2,1)}) custom-call(bf16[3,2,640,256]{3,2,1,0:T(8,128)(2,1)} %copy-done.2, bf16[3,2,640,256]{3,2,1,0:T(8,128)(2,1)} %copy-done.2, ...), custom_call_target="tpu_custom_call" | custom-call | flops 1 | bytes 1 | tf_op jit(solution)/shard_map/pallas_call | solution.py:338
  242.9 2.1 collective-permute-start.24
  245.4 18.1 %shard_map.229 = (bf16[2,512,256]{2,1,0:T(8,128)(2,1)}, f32[2,640,256]{2,1,0:T(8,128)}, f32[2,640,256]{2,1,0:T(8,128)}, bf16[2,2,2,128,256]{4,3,2,1,0:T(8,128)(2,1)}, bf16[2,2,2,128,256]{4,3,2,1,0:T(8,128)(2,1)}) custom-call(bf16[3,2,640,256]{3,2,1,0:T(8,128)(2,1)} %copy-done, bf16[3,2,640,256]{3,2,1,0:T(8,128)(2,1)} %copy-done, ...), custom_call_target="tpu_custom_call" | custom-call | flops 1 | bytes 1 | tf_op jit(solution)/shard_map/pallas_call | solution.py:338
  264.5 2.1 collective-permute-start.26
  267.3 12.3 %collective-permute-done.26 = bf16[2,2,2,128,256]{4,3,2,1,0:T(8,128)(2,1)S(1)} collective-permute-done((bf16[2,2,2,128,256]{4,3,2,1,0:T(8,128)(2,1)S(1)}, bf16[2,2,2,128,256]{4,3,2,1,0:T(8,128)(2,1)S(1)}, u32[]{:S(2)}, u32[]{:S(2)}) %collective-permute-start.26) | collective-permute-done | bytes 524320 | tf_op jit(solution)/shard_map/ppermute | solution.py:812
  283.6 13.0 %shard_map.230 = (bf16[4,4,112,512]{3,2,1,0:T(8,128)(2,1)}, bf16[4,4,112,512]{3,2,1,0:T(8,128)(2,1)}, bf16[2,2,640,256]{3,2,1,0:T(8,128)(2,1)}, bf16[2,2,640,256]{3,2,1,0:T(8,128)(2,1)}) custom-call(s32[8]{0:T(128)} %stack.111.offs, f32[2,640,256]{2,1,0:T(8,128)} %get-tuple-element.147.refs_0_, f32[2,640,256]{2,1,0:T(8,128)} %get-tuple-element.148.refs_1_, ...), custom_call_target="tpu_custom_call" | custom-call | flops 1 | bytes 1 | tf_op jit(solution)/shard_map/pallas_call | solution.py:672
  297.4 3.4 collective-permute-done.30
  300.7 2.1 add_convert_fusion
  303.5 8.0 %shard_map.231 = (bf16[4,4,112,256]{3,2,1,0:T(8,128)(2,1)}, bf16[4,4,112,256]{3,2,1,0:T(8,128)(2,1)}, bf16[2,2,640,256]{3,2,1,0:T(8,128)(2,1)}) custom-call(s32[8]{0:T(128)} %stack.111.offs, f32[2,640,256]{2,1,0:T(8,128)} %get-tuple-element.158.refs_0_, f32[2,640,256]{2,1,0:T(8,128)} %get-tuple-element.159.refs_1_, ...), custom_call_target="tpu_custom_call" | custom-call | flops 1 | bytes 1 | tf_op jit(solution)/shard_map/pallas_call | solution.py:672
  314.6 1.7 collective-permute-start.33
  316.3 9.5 %shard_map.232 = (f32[2,512,768]{2,1,0:T(8,128)}, bf16[2,64,768]{2,1,0:T(8,128)(2,1)}, bf16[2,64,768]{2,1,0:T(8,128)(2,1)}) custom-call(bf16[2,512,256]{2,1,0:T(8,128)(2,1)} %get-tuple-element.131.refs_2_.refs_0_, bf16[2,2,640,256]{3,2,1,0:T(8,128)(2,1)} %get-tuple-element.154.refs_1_, bf16[4,768,256]{2,1,0:T(8,128)(2,1)} %copy-done.4, ...), custom_call_target="tpu_custom_call" | custom-call | flops 1 | bytes 1 | tf_op jit(solution)/shard_map/pallas_call | solution.py:739
  327.1 9.5 %collective-permute-done.33 = bf16[4,112,512]{2,1,0:T(8,128)(2,1)S(1)} collective-permute-done((bf16[4,112,512]{2,1,0:T(8,128)(2,1)S(1)}, bf16[4,112,512]{2,1,0:T(8,128)(2,1)S(1)}, u32[]{:S(2)}, u32[]{:S(2)}) %collective-permute-start.33) | collective-permute-done | bytes 458784 | tf_op jit(solution)/shard_map/ppermute | solution.py:812
  338.1 1.5 collective-permute-start.35
  339.6 1.2 collective-permute-start.36
  340.8 2.5 collective-permute-start.39
  343.4 2.4 collective-permute-done.34
  345.8 2.0 collective-permute-start.41
  347.8 1.5 collective-permute-done.35
  349.5 2.6 collective-permute-start.42
  352.3 2.3 collective-permute-start.44
  354.6 2.8 copy.294
  357.6 1.3 collective-permute-start.38
  358.9 4.6 %collective-permute-start.37 = (bf16[2,64,768]{2,1,0:T(8,128)(2,1)}, bf16[2,64,768]{2,1,0:T(8,128)(2,1)S(1)}, u32[]{:S(2)}, u32[]{:S(2)}) collective-permute-start(bf16[2,64,768]{2,1,0:T(8,128)(2,1)} %get-tuple-element.175), channel_id=1, source_target_pairs={{0,1},{1,2},{2,3},{4,5},{5,6},{6,7},{8,9},{9,10},{10,11},{12,13},{... | collective-permute-start | bytes 589832 | tf_op jit(solution)/shard_map/ppermute | solution.py:817
  365.5 1.3 slice.239
  366.8 1.3 slice.244
  368.2 1.3 slice.246
  370.1 1.3 copy.304
  372.5 4.1 %copy.295 = f32[512,2,768]{2,1,0:T(2,128)} copy(f32[512,2,768]{2,0,1:T(8,128)S(1)} %fusion.3) | data formatting | bytes 6291456
  (232 shorter events, 46.0 us)
Async XLA Ops:
  7.2 62.6 %all-gather.5.cloned.1.call-start = ((), (), s32[]{:S(2)}) async-start(), calls=%async_computation.4 | async-start | bytes 1474560 | tf_op jit(solution)/shard_map/all_gather | solution.py:993
  12.2 14.9 %copy-start.28 = (bf16[96,768]{1,0:T(8,128)(2,1)S(1)}, bf16[96,768]{1,0:T(8,128)(2,1)}, u32[]{:S(2)}) copy-start(bf16[96,768]{1,0:T(8,128)(2,1)} %param.26) | copy-start | bytes 442372
  12.2 15.7 %copy-start.27 = (s32[2048,2]{0,1:T(2,128)S(1)}, s32[2048,2]{0,1:T(2,128)}, u32[]{:S(2)}) copy-start(s32[2048,2]{0,1:T(2,128)} %param.18) | copy-start | bytes 49156
  12.2 20.1 %collective-permute-start = (bf16[109,768]{0,1:T(8,128)(2,1)S(1)}, bf16[109,768]{0,1:T(8,128)(2,1)S(1)}, u32[]{:S(2)}, u32[]{:S(2)}) collective-permute-start(bf16[109,768]{0,1:T(8,128)(2,1)S(1)} %pad_maximum_fusion.2), channel_id=1, source_target_pairs={{0,3},{1,2},{2,1},{3,0},{4,7},{5,6},{6,5},{7,4},{8,11},{9,10},{10,... | collective-permute-start | bytes 502280 | tf_op jit(solution)/shard_map/ppermute | solution.py:812
  17.3 17.7 %collective-permute-start.1 = (bf16[109,768]{0,1:T(8,128)(2,1)S(1)}, bf16[109,768]{0,1:T(8,128)(2,1)S(1)}, u32[]{:S(2)}, u32[]{:S(2)}) collective-permute-start(bf16[109,768]{0,1:T(8,128)(2,1)S(1)} %pad_maximum_fusion.2), channel_id=1, source_target_pairs={{0,2},{1,3},{2,0},{3,1},{4,6},{5,7},{6,4},{7,5},{8,10},{9,11},{10,... | collective-permute-start | bytes 502280 | tf_op jit(solution)/shard_map/ppermute | solution.py:812
  17.3 17.7 %collective-permute-start.2 = (bf16[109,768]{0,1:T(8,128)(2,1)S(1)}, bf16[109,768]{0,1:T(8,128)(2,1)S(1)}, u32[]{:S(2)}, u32[]{:S(2)}) collective-permute-start(bf16[109,768]{0,1:T(8,128)(2,1)S(1)} %pad_maximum_fusion.2), channel_id=1, source_target_pairs={{0,1},{1,0},{2,3},{3,2},{4,5},{5,4},{6,7},{7,6},{8,9},{9,8},{10,11... | collective-permute-start | bytes 502280 | tf_op jit(solution)/shard_map/ppermute | solution.py:812
  21.8 19.0 %collective-permute-start.5 = (bf16[64,2,768]{2,0,1:T(8,128)(2,1)S(1)}, bf16[64,2,768]{2,0,1:T(8,128)(2,1)}, u32[]{:S(2)}, u32[]{:S(2)}) collective-permute-start(bf16[64,2,768]{2,0,1:T(8,128)(2,1)S(1)} %get-tuple-element.296), channel_id=1, source_target_pairs={{0,1},{1,2},{2,3},{4,5},{5,6},{6,7},{8,9},{9,10},{10,11},{12,13},{... | collective-permute-start | bytes 589832 | tf_op jit(solution)/shard_map/ppermute | solution.py:817
  25.7 15.6 %collective-permute-start.6 = (bf16[64,2,768]{2,0,1:T(8,128)(2,1)S(1)}, bf16[64,2,768]{2,0,1:T(8,128)(2,1)}, u32[]{:S(2)}, u32[]{:S(2)}) collective-permute-start(bf16[64,2,768]{2,0,1:T(8,128)(2,1)S(1)} %get-tuple-element.297), channel_id=1, source_target_pairs={{1,0},{2,1},{3,2},{5,4},{6,5},{7,6},{9,8},{10,9},{11,10},{13,12},{... | collective-permute-start | bytes 589832 | tf_op jit(solution)/shard_map/ppermute | solution.py:822
  27.8 124.5 %all-gather.7.cloned.1.call-start = ((), (), s32[]{:S(2)}) async-start(), calls=%async_computation.5 | async-start | bytes 10616832 | tf_op jit(solution)/shard_map/all_gather | solution.py:1013
  31.7 56.5 %copy-start.7 = (f32[2,128,8]{2,1,0:T(8,128)}, f32[2,128,8]{2,1,0:T(8,128)S(1)}, u32[]{:S(2)}) copy-start(f32[2,128,8]{2,1,0:T(8,128)S(1)} %convert_element_type.115.refs_13_.refs_17_.refs_9_) | copy-start | bytes 24580
  36.2 13.5 %collective-permute-start.3 = (bf16[96,3072]{1,0:T(8,128)(2,1)S(1)}, bf16[96,3072]{1,0:T(8,128)(2,1)S(1)}, u32[]{:S(2)}, u32[]{:S(2)}) collective-permute-start(bf16[96,3072]{1,0:T(8,128)(2,1)S(1)} %copy.283.refs_0_), channel_id=1, source_target_pairs={{0,8},{4,12},{8,0},{12,4},{16,24},{20,28},{24,16},{28,20},{1,9},{5... | collective-permute-start | bytes 1769480 | tf_op jit(solution)/shard_map/ppermute | solution.py:812
  37.7 14.3 %collective-permute-start.4 = (bf16[96,3072]{1,0:T(8,128)(2,1)S(1)}, bf16[96,3072]{1,0:T(8,128)(2,1)}, u32[]{:S(2)}, u32[]{:S(2)}) collective-permute-start(bf16[96,3072]{1,0:T(8,128)(2,1)S(1)} %copy.283.refs_0_), channel_id=1, source_target_pairs={{0,16},{4,20},{8,24},{12,28},{16,0},{20,4},{24,8},{28,12},{1,17},{... | collective-permute-start | bytes 1769480 | tf_op jit(solution)/shard_map/ppermute | solution.py:812
  40.5 19.5 %collective-permute-start.9 = (bf16[96,3072]{1,0:T(8,128)(2,1)S(1)}, bf16[96,3072]{1,0:T(8,128)(2,1)}, u32[]{:S(2)}, u32[]{:S(2)}) collective-permute-start(bf16[96,3072]{1,0:T(8,128)(2,1)S(1)} %copy.283.refs_0_), channel_id=1, source_target_pairs={{0,4},{4,0},{8,12},{12,8},{16,20},{20,16},{24,28},{28,24},{1,5},{5... | collective-permute-start | bytes 1769480 | tf_op jit(solution)/shard_map/ppermute | solution.py:812
  40.7 32.7 %copy-start.9 = (f32[2,8,768]{2,1,0:T(8,128)}, f32[2,8,768]{2,1,0:T(8,128)S(1)}, u32[]{:S(2)}) copy-start(f32[2,8,768]{2,1,0:T(8,128)S(1)} %pad.22.refs_12_) | copy-start | bytes 147460
  42.9 79.7 %copy-start.3 = (bf16[2,640,768]{2,1,0:T(8,128)(2,1)}, bf16[2,640,768]{2,1,0:T(8,128)(2,1)S(1)}, u32[]{:S(2)}) copy-start(bf16[2,640,768]{2,1,0:T(8,128)(2,1)S(1)} %maximum_bitcast_fusion.refs_10_.refs_6_) | copy-start | bytes 5898244
  49.7 7.6 %collective-permute-start.7 = (bf16[48,3072]{1,0:T(8,128)(2,1)S(1)}, bf16[48,3072]{1,0:T(8,128)(2,1)}, u32[]{:S(2)}, u32[]{:S(2)}) collective-permute-start(bf16[48,3072]{1,0:T(8,128)(2,1)S(1)} %slice.248), channel_id=1, source_target_pairs={{0,16},{4,20},{8,24},{12,28},{16,0},{20,4},{24,8},{28,12},{1,17},{... | collective-permute-start | bytes 884744 | tf_op jit(solution)/shard_map/ppermute | solution.py:812
  53.1 6.9 %collective-permute-start.8 = (bf16[48,3072]{1,0:T(8,128)(2,1)S(1)}, bf16[48,3072]{1,0:T(8,128)(2,1)}, u32[]{:S(2)}, u32[]{:S(2)}) collective-permute-start(bf16[48,3072]{1,0:T(8,128)(2,1)S(1)} %slice.256), channel_id=1, source_target_pairs={{0,8},{4,12},{8,0},{12,4},{16,24},{20,28},{24,16},{28,20},{1,9},{5... | collective-permute-start | bytes 884744 | tf_op jit(solution)/shard_map/ppermute | solution.py:812
  53.8 8.1 %collective-permute-start.10 = (bf16[96,3072]{1,0:T(8,128)(2,1)S(1)}, bf16[96,3072]{1,0:T(8,128)(2,1)}, u32[]{:S(2)}, u32[]{:S(2)}) collective-permute-start(bf16[96,3072]{1,0:T(8,128)(2,1)S(1)} %collective-permute-done.3.refs_1_), channel_id=1, source_target_pairs={{0,4},{4,0},{8,12},{12,8},{16,20},{20,16},{24,28},{28,24},{1,5},{5... | collective-permute-start | bytes 1769480 | tf_op jit(solution)/shard_map/ppermute | solution.py:812
  53.8 8.1 %collective-permute-start.11 = (bf16[96,3072]{1,0:T(8,128)(2,1)}, bf16[96,3072]{1,0:T(8,128)(2,1)}, u32[]{:S(2)}, u32[]{:S(2)}) collective-permute-start(bf16[96,3072]{1,0:T(8,128)(2,1)} %collective-permute-done.4.refs_2_), channel_id=1, source_target_pairs={{0,4},{4,0},{8,12},{12,8},{16,20},{20,16},{24,28},{28,24},{1,5},{5... | collective-permute-start | bytes 1769480 | tf_op jit(solution)/shard_map/ppermute | solution.py:812
  57.3 2.7 collective-permute-start.12
  59.9 1.9 collective-permute-start.13
  69.8 233.0 %reduce-scatter.3.cloned.1.call-start = ((), (), s32[]{:S(2)}) async-start(), calls=%async_computation.2 | async-start | bytes 12386304 | tf_op jit(solution)/shard_map/reduce_scatter | solution.py:1034
  70.1 15.3 %collective-permute-start.15 = (bf16[2,2,128,256]{3,2,1,0:T(8,128)(2,1)}, bf16[2,2,128,256]{3,2,1,0:T(8,128)(2,1)}, u32[]{:S(2)}, u32[]{:S(2)}) collective-permute-start(bf16[2,2,128,256]{3,2,1,0:T(8,128)(2,1)} %get-tuple-element.112.refs_0_.refs_4_), channel_id=1, source_target_pairs={{0,2},{1,3},{2,0},{3,1},{4,6},{5,7},{6,4},{7,5},{8,10},{9,11},{10,... | collective-permute-start | bytes 786440 | tf_op jit(solution)/shard_map/ppermute | solution.py:812
  70.3 25.9 %collective-permute-start.14 = (bf16[2,2,128,256]{3,2,1,0:T(8,128)(2,1)}, bf16[2,2,128,256]{3,2,1,0:T(8,128)(2,1)}, u32[]{:S(2)}, u32[]{:S(2)}) collective-permute-start(bf16[2,2,128,256]{3,2,1,0:T(8,128)(2,1)} %get-tuple-element.112.refs_0_.refs_4_), channel_id=1, source_target_pairs={{0,1},{1,0},{2,3},{3,2},{4,5},{5,4},{6,7},{7,6},{8,9},{9,8},{10,11... | collective-permute-start | bytes 786440 | tf_op jit(solution)/shard_map/ppermute | solution.py:812
  85.4 12.7 %collective-permute-start.16 = (bf16[2,2,128,256]{3,2,1,0:T(8,128)(2,1)}, bf16[2,2,128,256]{3,2,1,0:T(8,128)(2,1)}, u32[]{:S(2)}, u32[]{:S(2)}) collective-permute-start(bf16[2,2,128,256]{3,2,1,0:T(8,128)(2,1)} %collective-permute-done.15.refs_2_.refs_6_), channel_id=1, source_target_pairs={{0,1},{1,0},{2,3},{3,2},{4,5},{5,4},{6,7},{7,6},{8,9},{9,8},{10,11... | collective-permute-start | bytes 786440 | tf_op jit(solution)/shard_map/ppermute | solution.py:812
  85.4 21.7 %collective-permute-start.18 = (bf16[2,2,128,256]{3,2,1,0:T(8,128)(2,1)}, bf16[2,2,128,256]{3,2,1,0:T(8,128)(2,1)}, u32[]{:S(2)}, u32[]{:S(2)}) collective-permute-start(bf16[2,2,128,256]{3,2,1,0:T(8,128)(2,1)} %get-tuple-element.116.refs_0_.refs_4_), channel_id=1, source_target_pairs={{0,2},{1,3},{2,0},{3,1},{4,6},{5,7},{6,4},{7,5},{8,10},{9,11},{10,... | collective-permute-start | bytes 786440 | tf_op jit(solution)/shard_map/ppermute | solution.py:812
  98.1 22.4 %copy-start.31 = (f32[2,768]{1,0:T(2,128)S(1)}, f32[2,768]{1,0:T(2,128)}, u32[]{:S(2)}) copy-start(f32[2,768]{1,0:T(2,128)} %param.28) | copy-start | bytes 18436
  98.1 22.4 %copy-start.32 = (f32[2,768]{1,0:T(2,128)S(1)}, f32[2,768]{1,0:T(2,128)}, u32[]{:S(2)}) copy-start(f32[2,768]{1,0:T(2,128)} %param.27) | copy-start | bytes 18436
  98.1 22.4 %copy-start.33 = (f32[2,768]{1,0:T(2,128)S(1)}, f32[2,768]{1,0:T(2,128)}, u32[]{:S(2)}) copy-start(f32[2,768]{1,0:T(2,128)} %param.23) | copy-start | bytes 18436
  107.2 13.4 %collective-permute-start.21 = (bf16[2,2,128,256]{3,2,1,0:T(8,128)(2,1)S(1)}, bf16[2,2,128,256]{3,2,1,0:T(8,128)(2,1)S(1)}, u32[]{:S(2)}, u32[]{:S(2)}) collective-permute-start(bf16[2,2,128,256]{3,2,1,0:T(8,128)(2,1)S(1)} %get-tuple-element.123.refs_0_.refs_4_), channel_id=1, source_target_pairs={{0,2},{1,3},{2,0},{3,1},{4,6},{5,7},{6,4},{7,5},{8,10},{9,11},{10,... | collective-permute-start | bytes 786440 | tf_op jit(solution)/shard_map/ppermute | solution.py:812
  107.4 20.3 %collective-permute-start.17 = (bf16[2,2,128,256]{3,2,1,0:T(8,128)(2,1)}, bf16[2,2,128,256]{3,2,1,0:T(8,128)(2,1)S(1)}, u32[]{:S(2)}, u32[]{:S(2)}) collective-permute-start(bf16[2,2,128,256]{3,2,1,0:T(8,128)(2,1)} %get-tuple-element.116.refs_0_.refs_4_), channel_id=1, source_target_pairs={{0,1},{1,0},{2,3},{3,2},{4,5},{5,4},{6,7},{7,6},{8,9},{9,8},{10,11... | collective-permute-start | bytes 786440 | tf_op jit(solution)/shard_map/ppermute | solution.py:812
  109.9 32.9 %collective-permute-start.20 = (bf16[2,2,128,256]{3,2,1,0:T(8,128)(2,1)S(1)}, bf16[2,2,128,256]{3,2,1,0:T(8,128)(2,1)S(1)}, u32[]{:S(2)}, u32[]{:S(2)}) collective-permute-start(bf16[2,2,128,256]{3,2,1,0:T(8,128)(2,1)S(1)} %get-tuple-element.123.refs_0_.refs_4_), channel_id=1, source_target_pairs={{0,1},{1,0},{2,3},{3,2},{4,5},{5,4},{6,7},{7,6},{8,9},{9,8},{10,11... | collective-permute-start | bytes 786440 | tf_op jit(solution)/shard_map/ppermute | solution.py:812
  110.0 24.2 %collective-permute-start.19 = (bf16[2,2,128,256]{3,2,1,0:T(8,128)(2,1)}, bf16[2,2,128,256]{3,2,1,0:T(8,128)(2,1)}, u32[]{:S(2)}, u32[]{:S(2)}) collective-permute-start(bf16[2,2,128,256]{3,2,1,0:T(8,128)(2,1)} %collective-permute-done.18.refs_2_.refs_6_), channel_id=1, source_target_pairs={{0,1},{1,0},{2,3},{3,2},{4,5},{5,4},{6,7},{7,6},{8,9},{9,8},{10,11... | collective-permute-start | bytes 786440 | tf_op jit(solution)/shard_map/ppermute | solution.py:812
  120.6 22.3 %collective-permute-start.22 = (bf16[2,2,128,256]{3,2,1,0:T(8,128)(2,1)S(1)}, bf16[2,2,128,256]{3,2,1,0:T(8,128)(2,1)S(1)}, u32[]{:S(2)}, u32[]{:S(2)}) collective-permute-start(bf16[2,2,128,256]{3,2,1,0:T(8,128)(2,1)S(1)} %collective-permute-done.21.refs_2_.refs_6_), channel_id=1, source_target_pairs={{0,1},{1,0},{2,3},{3,2},{4,5},{5,4},{6,7},{7,6},{8,9},{9,8},{10,11... | collective-permute-start | bytes 786440 | tf_op jit(solution)/shard_map/ppermute | solution.py:812
  206.1 170.5 %reduce-scatter.5.cloned.1.call-start = ((), (), s32[]{:S(2)}) async-start(), calls=%async_computation.3 | async-start | bytes 1720320 | tf_op jit(solution)/shard_map/reduce_scatter | solution.py:1035
  224.0 17.9 %collective-permute-start.23 = (bf16[2,2,2,128,256]{4,3,2,1,0:T(8,128)(2,1)}, bf16[2,2,2,128,256]{4,3,2,1,0:T(8,128)(2,1)S(1)}, u32[]{:S(2)}, u32[]{:S(2)}) collective-permute-start(bf16[2,2,2,128,256]{4,3,2,1,0:T(8,128)(2,1)} %get-tuple-element.136), channel_id=1, source_target_pairs={{0,1},{1,0},{2,3},{3,2},{4,5},{5,4},{6,7},{7,6},{8,9},{9,8},{10,11... | collective-permute-start | bytes 1572872 | tf_op jit(solution)/shard_map/ppermute | solution.py:812
  224.0 17.8 %copy-start.22 = (bf16[2,2,2,128,256]{4,3,2,1,0:T(8,128)(2,1)S(1)}, bf16[2,2,2,128,256]{4,3,2,1,0:T(8,128)(2,1)}, u32[]{:S(2)}) copy-start(bf16[2,2,2,128,256]{4,3,2,1,0:T(8,128)(2,1)} %get-tuple-element.135) | copy-start | bytes 1572868
  242.9 20.6 %collective-permute-start.24 = (bf16[2,2,2,128,256]{4,3,2,1,0:T(8,128)(2,1)S(1)}, bf16[2,2,2,128,256]{4,3,2,1,0:T(8,128)(2,1)S(1)}, u32[]{:S(2)}, u32[]{:S(2)}) collective-permute-start(bf16[2,2,2,128,256]{4,3,2,1,0:T(8,128)(2,1)S(1)} %copy-done.34), channel_id=1, source_target_pairs={{0,1},{1,0},{2,3},{3,2},{4,5},{5,4},{6,7},{7,6},{8,9},{9,8},{10,11... | collective-permute-start | bytes 1572872 | tf_op jit(solution)/shard_map/ppermute | solution.py:812
  245.1 19.4 %collective-permute-start.25 = (bf16[2,2,128,256]{3,2,1,0:T(8,128)(2,1)S(1)}, bf16[2,2,128,256]{3,2,1,0:T(8,128)(2,1)S(1)}, u32[]{:S(2)}, u32[]{:S(2)}) collective-permute-start(bf16[2,2,128,256]{3,2,1,0:T(8,128)(2,1)S(1)} %get-tuple-element.311), channel_id=1, source_target_pairs={{0,2},{1,3},{2,0},{3,1},{4,6},{5,7},{6,4},{7,5},{8,10},{9,11},{10,... | collective-permute-start | bytes 786440 | tf_op jit(solution)/shard_map/ppermute | solution.py:812
  245.4 18.1 %copy-start.20 = (bf16[2,2,2,128,256]{4,3,2,1,0:T(8,128)(2,1)S(1)}, bf16[2,2,2,128,256]{4,3,2,1,0:T(8,128)(2,1)}, u32[]{:S(2)}) copy-start(bf16[2,2,2,128,256]{4,3,2,1,0:T(8,128)(2,1)} %get-tuple-element.142) | copy-start | bytes 1572868
  263.5 16.1 %copy-start.21 = (bf16[2,2,2,128,256]{4,3,2,1,0:T(8,128)(2,1)S(1)}, bf16[2,2,2,128,256]{4,3,2,1,0:T(8,128)(2,1)}, u32[]{:S(2)}) copy-start(bf16[2,2,2,128,256]{4,3,2,1,0:T(8,128)(2,1)} %get-tuple-element.140) | copy-start | bytes 1572868
  263.6 18.0 %copy-start.19 = (f32[2,5,768]{2,1,0:T(8,128)S(1)}, f32[2,5,768]{2,1,0:T(8,128)}, u32[]{:S(2)}) copy-start(f32[2,5,768]{2,1,0:T(8,128)} %copy-done.18) | copy-start | bytes 92164
  263.7 18.6 %copy-start.30 = (f32[8,768]{1,0:T(8,128)S(1)}, f32[8,768]{1,0:T(8,128)}, u32[]{:S(2)}) copy-start(f32[8,768]{1,0:T(8,128)} %get-tuple-element.153) | copy-start | bytes 73732
  264.4 18.5 %copy-start.23 = (bf16[2,2,128,256]{3,2,1,0:T(8,128)(2,1)}, bf16[2,2,128,256]{3,2,1,0:T(8,128)(2,1)S(1)}, u32[]{:S(2)}) copy-start(bf16[2,2,128,256]{3,2,1,0:T(8,128)(2,1)S(1)} %collective-permute-done.25.refs_4_) | copy-start | bytes 786436
  264.5 15.1 %collective-permute-start.26 = (bf16[2,2,2,128,256]{4,3,2,1,0:T(8,128)(2,1)S(1)}, bf16[2,2,2,128,256]{4,3,2,1,0:T(8,128)(2,1)S(1)}, u32[]{:S(2)}, u32[]{:S(2)}) collective-permute-start(bf16[2,2,2,128,256]{4,3,2,1,0:T(8,128)(2,1)S(1)} %copy-done.35), channel_id=1, source_target_pairs={{0,1},{1,0},{2,3},{3,2},{4,5},{5,4},{6,7},{7,6},{8,9},{9,8},{10,11... | collective-permute-start | bytes 1572872 | tf_op jit(solution)/shard_map/ppermute | solution.py:812
  266.6 16.3 %collective-permute-start.27 = (bf16[2,2,128,256]{3,2,1,0:T(8,128)(2,1)S(1)}, bf16[2,2,128,256]{3,2,1,0:T(8,128)(2,1)S(1)}, u32[]{:S(2)}, u32[]{:S(2)}) collective-permute-start(bf16[2,2,128,256]{3,2,1,0:T(8,128)(2,1)S(1)} %get-tuple-element.309), channel_id=1, source_target_pairs={{0,2},{1,3},{2,0},{3,1},{4,6},{5,7},{6,4},{7,5},{8,10},{9,11},{10,... | collective-permute-start | bytes 786440 | tf_op jit(solution)/shard_map/ppermute | solution.py:812
  280.5 16.1 %collective-permute-start.28 = (bf16[2,2,128,256]{3,2,1,0:T(8,128)(2,1)S(1)}, bf16[2,2,128,256]{3,2,1,0:T(8,128)(2,1)S(1)}, u32[]{:S(2)}, u32[]{:S(2)}) collective-permute-start(bf16[2,2,128,256]{3,2,1,0:T(8,128)(2,1)S(1)} %get-tuple-element.307), channel_id=1, source_target_pairs={{0,2},{1,3},{2,0},{3,1},{4,6},{5,7},{6,4},{7,5},{8,10},{9,11},{10,... | collective-permute-start | bytes 786440 | tf_op jit(solution)/shard_map/ppermute | solution.py:812
  296.7 4.1 %collective-permute-start.30 = (bf16[4,4,112,512]{3,2,1,0:T(8,128)(2,1)}, bf16[4,4,112,512]{3,2,1,0:T(8,128)(2,1)S(1)}, u32[]{:S(2)}, u32[]{:S(2)}) collective-permute-start(bf16[4,4,112,512]{3,2,1,0:T(8,128)(2,1)} %get-tuple-element.172), channel_id=1, source_target_pairs={{0,4},{4,0},{8,12},{12,8},{16,20},{20,16},{24,28},{28,24},{1,5},{5... | collective-permute-start | bytes 5505032 | tf_op jit(solution)/shard_map/ppermute | solution.py:812
  311.5 25.4 %collective-permute-start.29 = (bf16[4,4,112,256]{3,2,1,0:T(8,128)(2,1)}, bf16[4,4,112,256]{3,2,1,0:T(8,128)(2,1)S(1)}, u32[]{:S(2)}, u32[]{:S(2)}) collective-permute-start(bf16[4,4,112,256]{3,2,1,0:T(8,128)(2,1)} %get-tuple-element.168), channel_id=1, source_target_pairs={{0,4},{4,0},{8,12},{12,8},{16,20},{20,16},{24,28},{28,24},{1,5},{5... | collective-permute-start | bytes 2752520 | tf_op jit(solution)/shard_map/ppermute | solution.py:812
  312.8 13.6 %collective-permute-start.31 = (bf16[4,112,512]{2,1,0:T(8,128)(2,1)}, bf16[4,112,512]{2,1,0:T(8,128)(2,1)S(1)}, u32[]{:S(2)}, u32[]{:S(2)}) collective-permute-start(bf16[4,112,512]{2,1,0:T(8,128)(2,1)} %get-tuple-element.295), channel_id=1, source_target_pairs={{0,8},{4,12},{8,0},{12,4},{16,24},{20,28},{24,16},{28,20},{1,9},{5... | collective-permute-start | bytes 1376264 | tf_op jit(solution)/shard_map/ppermute | solution.py:812
  313.9 13.1 %collective-permute-start.32 = (bf16[4,112,512]{2,1,0:T(8,128)(2,1)}, bf16[4,112,512]{2,1,0:T(8,128)(2,1)S(1)}, u32[]{:S(2)}, u32[]{:S(2)}) collective-permute-start(bf16[4,112,512]{2,1,0:T(8,128)(2,1)} %get-tuple-element.294), channel_id=1, source_target_pairs={{0,16},{4,20},{8,24},{12,28},{16,0},{20,4},{24,8},{28,12},{1,17},{... | collective-permute-start | bytes 1376264 | tf_op jit(solution)/shard_map/ppermute | solution.py:812
  314.6 22.0 %collective-permute-start.33 = (bf16[4,112,512]{2,1,0:T(8,128)(2,1)S(1)}, bf16[4,112,512]{2,1,0:T(8,128)(2,1)S(1)}, u32[]{:S(2)}, u32[]{:S(2)}) collective-permute-start(bf16[4,112,512]{2,1,0:T(8,128)(2,1)S(1)} %get-tuple-element.293), channel_id=1, source_target_pairs={{0,24},{4,28},{8,16},{12,20},{16,8},{20,12},{24,0},{28,4},{1,25},{... | collective-permute-start | bytes 1376264 | tf_op jit(solution)/shard_map/ppermute | solution.py:812
  337.1 17.4 %copy-start.16 = (bf16[2,512,768]{2,1,0:T(8,128)(2,1)S(1)}, bf16[2,512,768]{2,1,0:T(8,128)(2,1)}, u32[]{:S(2)}) copy-start(bf16[2,512,768]{2,1,0:T(8,128)(2,1)} %get-tuple-element.129) | copy-start | bytes 4718596
  337.2 8.6 %collective-permute-start.34 = (bf16[4,112,256]{2,1,0:T(8,128)(2,1)S(1)}, bf16[4,112,256]{2,1,0:T(8,128)(2,1)S(1)}, u32[]{:S(2)}, u32[]{:S(2)}) collective-permute-start(bf16[4,112,256]{2,1,0:T(8,128)(2,1)S(1)} %get-tuple-element.298), channel_id=1, source_target_pairs={{0,8},{4,12},{8,0},{12,4},{16,24},{20,28},{24,16},{28,20},{1,9},{5... | collective-permute-start | bytes 688136 | tf_op jit(solution)/shard_map/ppermute | solution.py:812
  338.1 11.3 %collective-permute-start.35 = (bf16[4,112,256]{2,1,0:T(8,128)(2,1)S(1)}, bf16[4,112,256]{2,1,0:T(8,128)(2,1)S(1)}, u32[]{:S(2)}, u32[]{:S(2)}) collective-permute-start(bf16[4,112,256]{2,1,0:T(8,128)(2,1)S(1)} %get-tuple-element.300), channel_id=1, source_target_pairs={{0,16},{4,20},{8,24},{12,28},{16,0},{20,4},{24,8},{28,12},{1,17},{... | collective-permute-start | bytes 688136 | tf_op jit(solution)/shard_map/ppermute | solution.py:812
  339.6 9.8 %collective-permute-start.36 = (bf16[4,112,256]{2,1,0:T(8,128)(2,1)S(1)}, bf16[4,112,256]{2,1,0:T(8,128)(2,1)S(1)}, u32[]{:S(2)}, u32[]{:S(2)}) collective-permute-start(bf16[4,112,256]{2,1,0:T(8,128)(2,1)S(1)} %get-tuple-element.299), channel_id=1, source_target_pairs={{0,24},{4,28},{8,16},{12,20},{16,8},{20,12},{24,0},{28,4},{1,25},{... | collective-permute-start | bytes 688136 | tf_op jit(solution)/shard_map/ppermute | solution.py:812
  340.8 11.5 %collective-permute-start.39 = (bf16[112,512]{1,0:T(8,128)(2,1)S(1)}, bf16[112,512]{1,0:T(8,128)(2,1)S(1)}, u32[]{:S(2)}, u32[]{:S(2)}) collective-permute-start(bf16[112,512]{1,0:T(8,128)(2,1)S(1)} %get-tuple-element.315), channel_id=1, source_target_pairs={{0,1},{1,0},{2,3},{3,2},{4,5},{5,4},{6,7},{7,6},{8,9},{9,8},{10,11... | collective-permute-start | bytes 344072 | tf_op jit(solution)/shard_map/ppermute | solution.py:812
  343.3 14.2 %collective-permute-start.40 = (bf16[112,512]{1,0:T(8,128)(2,1)S(1)}, bf16[112,512]{1,0:T(8,128)(2,1)S(1)}, u32[]{:S(2)}, u32[]{:S(2)}) collective-permute-start(bf16[112,512]{1,0:T(8,128)(2,1)S(1)} %get-tuple-element.314), channel_id=1, source_target_pairs={{0,2},{1,3},{2,0},{3,1},{4,6},{5,7},{6,4},{7,5},{8,10},{9,11},{10,... | collective-permute-start | bytes 344072 | tf_op jit(solution)/shard_map/ppermute | solution.py:812
  345.8 13.1 %collective-permute-start.41 = (bf16[112,512]{1,0:T(8,128)(2,1)S(1)}, bf16[112,512]{1,0:T(8,128)(2,1)S(1)}, u32[]{:S(2)}, u32[]{:S(2)}) collective-permute-start(bf16[112,512]{1,0:T(8,128)(2,1)S(1)} %get-tuple-element.313), channel_id=1, source_target_pairs={{0,3},{1,2},{2,1},{3,0},{4,7},{5,6},{6,5},{7,4},{8,11},{9,10},{10,... | collective-permute-start | bytes 344072 | tf_op jit(solution)/shard_map/ppermute | solution.py:812
  349.5 13.9 %collective-permute-start.42 = (bf16[112,256]{1,0:T(8,128)(2,1)S(1)}, bf16[112,256]{1,0:T(8,128)(2,1)S(1)}, u32[]{:S(2)}, u32[]{:S(2)}) collective-permute-start(bf16[112,256]{1,0:T(8,128)(2,1)S(1)} %get-tuple-element.319), channel_id=1, source_target_pairs={{0,1},{1,0},{2,3},{3,2},{4,5},{5,4},{6,7},{7,6},{8,9},{9,8},{10,11... | collective-permute-start | bytes 172040 | tf_op jit(solution)/shard_map/ppermute | solution.py:812
  352.1 11.3 %collective-permute-start.43 = (bf16[112,256]{1,0:T(8,128)(2,1)S(1)}, bf16[112,256]{1,0:T(8,128)(2,1)S(1)}, u32[]{:S(2)}, u32[]{:S(2)}) collective-permute-start(bf16[112,256]{1,0:T(8,128)(2,1)S(1)} %get-tuple-element.318), channel_id=1, source_target_pairs={{0,2},{1,3},{2,0},{3,1},{4,6},{5,7},{6,4},{7,5},{8,10},{9,11},{10,... | collective-permute-start | bytes 172040 | tf_op jit(solution)/shard_map/ppermute | solution.py:812
  352.3 11.2 %collective-permute-start.44 = (bf16[112,256]{1,0:T(8,128)(2,1)S(1)}, bf16[112,256]{1,0:T(8,128)(2,1)S(1)}, u32[]{:S(2)}, u32[]{:S(2)}) collective-permute-start(bf16[112,256]{1,0:T(8,128)(2,1)S(1)} %get-tuple-element.317), channel_id=1, source_target_pairs={{0,3},{1,2},{2,1},{3,0},{4,7},{5,6},{6,5},{7,4},{8,11},{9,10},{10,... | collective-permute-start | bytes 172040 | tf_op jit(solution)/shard_map/ppermute | solution.py:812
  357.6 14.8 %collective-permute-start.38 = (bf16[2,64,768]{2,1,0:T(8,128)(2,1)}, bf16[2,64,768]{2,1,0:T(8,128)(2,1)S(1)}, u32[]{:S(2)}, u32[]{:S(2)}) collective-permute-start(bf16[2,64,768]{2,1,0:T(8,128)(2,1)} %get-tuple-element.177), channel_id=1, source_target_pairs={{1,0},{2,1},{3,2},{5,4},{6,5},{7,6},{9,8},{10,9},{11,10},{13,12},{... | collective-permute-start | bytes 589832 | tf_op jit(solution)/shard_map/ppermute | solution.py:822
  358.9 12.5 %collective-permute-start.37 = (bf16[2,64,768]{2,1,0:T(8,128)(2,1)}, bf16[2,64,768]{2,1,0:T(8,128)(2,1)S(1)}, u32[]{:S(2)}, u32[]{:S(2)}) collective-permute-start(bf16[2,64,768]{2,1,0:T(8,128)(2,1)} %get-tuple-element.175), channel_id=1, source_target_pairs={{0,1},{1,2},{2,3},{4,5},{5,6},{6,7},{8,9},{9,10},{10,11},{12,13},{... | collective-permute-start | bytes 589832 | tf_op jit(solution)/shard_map/ppermute | solution.py:817
  (21 other events, 78.2 us)
Sparse Core Ops, SparseCore 0:
  27.9 33.0 all-gather.4
  69.9 58.1 all-gather.6
  206.2 82.4 reduce-scatter.2
  303.0 31.4 reduce-scatter.4

commit v6 on v5

--- a/solution.py
+++ b/solution.py
@@ -1091,25 +1091,29 @@
             blocks = after(blocks, merged[-1])
         totals.append(scatter_tp(blocks))
 
-    first, last = after(first, chips[-1]), after(last, chips[-1])
+    first, last = after(first, chips[0]), after(last, chips[0])
     to_left = shift_left(first).transpose(1, 0, 2)
     to_right = shift_right(last).transpose(1, 0, 2)
     grad_inputs = middle.at[:HALF].add(to_right.astype(F32))
     grad_inputs = grad_inputs.at[rows - HALF :].add(to_left.astype(F32))
 
+    out_rows = outputs.transpose(1, 0, 2)
+    grad_up, grad_down = grad_up_down[0, :shard_rows], grad_up_down[1, :shard_rows]
+    grad_up_bias = grad_up_down[0, shard_rows]
+    totals[-1][0] = after(totals[-1][0], grad_inputs, out_rows, grad_up, grad_down, grad_up_bias)
     grad_w_qkv, grad_w_out, extra_rows, sums = finish(totals, chunks)
     sums = sums[TAPS + 1 :].reshape(-1)[: 6 * width].reshape(6, width)
     return (
-        outputs.transpose(1, 0, 2),
+        out_rows,
         grad_inputs,
         grad_w_qkv.transpose(1, 0, 2),
         extra_rows[:, 0],
         extra_rows[1:, 1 : TAPS + 1],
         grad_w_out,
         sums[0:2],
-        grad_up_down[0, :shard_rows],
-        grad_up_down[0, shard_rows],
-        grad_up_down[1, :shard_rows],
+        grad_up,
+        grad_up_bias,
+        grad_down,
         sums[2:4],
         sums[4:6],
     )

time: 393 us -> 382 us (0.972)
  waiting for transfers between devices: 69.4 us -> 64 us
  local copies, waits for them, and re-layouts: 55.3 us -> 51 us
    ppermute x41, waiting for transfers between devices: 69.3 us -> 61.2 us  [swap(): return lax.ppermute(values, axis, [(i, i ^ mask) for i in range(count)])]
    unnamed x84 -> x88, local copies, waits for them, and re-layouts: 26.7 us -> 26.8 us
  transfers between devices with their start and end apart: 49 -> 49, of which waited for: 17 -> 16; matrix products, arithmetic and copies ran while one was open for 12% -> 11% of each run, Pallas kernels for 33% -> 34%
where the time goes in v6:
time: 382 us; the launch traced here: 376 us
  Pallas kernels  181 us (47%)
  waiting for transfers between devices  64 us (17%)
  starting transfers between devices  55.1 us (14%)
  local copies, waits for them, and re-layouts  51 us (13%)
  between operations  15.1 us (4%)
  other arithmetic  9.82 us (3%)
    ppermute x41, waiting for transfers between devices, swap(): return lax.ppermute(values, axis, [(i, i ^ mask) for i in range(count)])  61.2 us
    pallas_call x3, Pallas kernels, attend_backward(): pl.pallas_call(partial(attend_backward_kernel, blocks), grid=(seqs, span...  53.8 us
    pallas_call x1, Pallas kernels, dense(): pl.pallas_call(partial(dense_kernel, chunks, steps), grid=(2 * steps,), i...  53.7 us
    ppermute x41, starting transfers between devices, swap(): return lax.ppermute(values, axis, [(i, i ^ mask) for i in range(count)])  43.4 us
    unnamed x88, local copies, waits for them, and re-layouts  26.8 us
    pallas_call x3, Pallas kernels, attend_forward(): pl.pallas_call(partial(attend_forward_kernel, blocks), grid=(seqs, span /...  26.3 us
    pallas_call x2, Pallas kernels, gather_back(): pl.pallas_call(partial(gather_back_kernel, blocks, chunks, len(group_size...  21 us
    pallas_call x3, Pallas kernels, project(): pl.pallas_call(partial(project_kernel, len(pieces)), grid_spec=pltpu.Pref...  15.6 us
  transfers between devices with their start and end apart: 49, of which 16 were waited for; matrix products, arithmetic and copies ran while one was open for 11% of the time, Pallas kernels for 34%

profile of v6, /device:TPU:0, one launch (start us, length us, event | category | flops | bytes accessed | tf_op | source)
XLA Modules:
  0.0 375.6 jit_solution(5259715890330891352)
XLA Ops:
  10.0 1.1 copy.264
  12.2 5.1 %collective-permute-start = (bf16[109,768]{0,1:T(8,128)(2,1)S(1)}, bf16[109,768]{0,1:T(8,128)(2,1)S(1)}, u32[]{:S(2)}, u32[]{:S(2)}) collective-permute-start(bf16[109,768]{0,1:T(8,128)(2,1)S(1)} %pad_maximum_fusion.2), channel_id=1, source_target_pairs={{0,3},{1,2},{2,1},{3,0},{4,7},{5,6},{6,5},{7,4},{8,11},{9,10},{10,... | collective-permute-start | bytes 502280 | tf_op jit(solution)/shard_map/ppermute | solution.py:812
  18.0 2.7 copy.271
  20.7 1.0 fusion.5
  21.8 4.0 %collective-permute-start.5 = (bf16[64,2,768]{2,0,1:T(8,128)(2,1)S(1)}, bf16[64,2,768]{2,0,1:T(8,128)(2,1)}, u32[]{:S(2)}, u32[]{:S(2)}) collective-permute-start(bf16[64,2,768]{2,0,1:T(8,128)(2,1)S(1)} %get-tuple-element.298), channel_id=1, source_target_pairs={{0,1},{1,2},{2,3},{4,5},{5,6},{6,7},{8,9},{9,10},{10,11},{12,13},{... | collective-permute-start | bytes 589832 | tf_op jit(solution)/shard_map/ppermute | solution.py:817
  25.7 1.3 collective-permute-start.6
  32.3 2.7 collective-permute-done.1
  36.2 1.6 collective-permute-start.3
  37.7 1.5 collective-permute-start.4
  41.3 1.7 maximum_bitcast_fusion.refs_10_.refs_6_
  42.9 6.7 %collective-permute-done.3.refs_1_ = bf16[96,3072]{1,0:T(8,128)(2,1)S(1)} collective-permute-done((bf16[96,3072]{1,0:T(8,128)(2,1)S(1)}, bf16[96,3072]{1,0:T(8,128)(2,1)S(1)}, u32[]{:S(2)}, u32[]{:S(2)}) %collective-permute-start.3) | collective-permute-done | bytes 589856 | tf_op jit(solution)/shard_map/ppermute | solution.py:812
  49.7 1.6 collective-permute-start.7
  54.3 3.0 collective-permute-done.7.refs_3_
  57.3 2.6 collective-permute-done.8.refs_4_
  60.1 1.8 collective-permute-done.13.refs_9_
  61.9 5.4 %shard_map.220 = (bf16[3,2,640,256]{3,2,1,0:T(8,128)(2,1)S(1)}, bf16[2,2,128,256]{3,2,1,0:T(8,128)(2,1)}, bf16[4,768,256]{2,1,0:T(8,128)(2,1)S(1)}) custom-call(s32[10]{0:T(128)S(1)} %stack.97.offs, bf16[96,3072]{1,0:T(8,128)(2,1)S(1)} %copy.283.refs_0_, bf16[96,3072]{1,0:T(8,128)(2,1)S(1)} %collective-permute-done.3.refs_1_, ...), custom_call_target="tpu_custom_call" | custom-call | flops 1 | bytes 1 | tf_op jit(solution)/shard_map/pallas_call | solution.py:100
  67.3 1.3 copy-done.1
  68.6 1.1 copy-done.4
  70.3 3.0 collective-permute-start.14
  73.4 5.4 %shard_map.222 = (bf16[3,2,640,256]{3,2,1,0:T(8,128)(2,1)S(1)}, bf16[2,2,128,256]{3,2,1,0:T(8,128)(2,1)}, bf16[4,768,256]{2,1,0:T(8,128)(2,1)S(1)}) custom-call(s32[10]{0:T(128)S(1)} %stack.97.offs, bf16[96,3072]{1,0:T(8,128)(2,1)S(1)} %copy.283.refs_0_, bf16[96,3072]{1,0:T(8,128)(2,1)S(1)} %collective-permute-done.3.refs_1_, ...), custom_call_target="tpu_custom_call" | custom-call | flops 1 | bytes 1 | tf_op jit(solution)/shard_map/pallas_call | solution.py:100
  78.8 1.3 copy-done.2
  80.0 1.2 copy-done.5
  81.2 4.2 %collective-permute-done.15.refs_2_.refs_6_ = bf16[2,2,128,256]{3,2,1,0:T(8,128)(2,1)} collective-permute-done((bf16[2,2,128,256]{3,2,1,0:T(8,128)(2,1)}, bf16[2,2,128,256]{3,2,1,0:T(8,128)(2,1)}, u32[]{:S(2)}, u32[]{:S(2)}) %collective-permute-start.15) | collective-permute-done | bytes 262176 | tf_op jit(solution)/shard_map/ppermute | solution.py:812
  85.4 1.7 collective-permute-start.18
  89.0 4.7 %shard_map.224 = (bf16[3,2,640,256]{3,2,1,0:T(8,128)(2,1)S(1)}, bf16[2,2,128,256]{3,2,1,0:T(8,128)(2,1)S(1)}, bf16[4,768,256]{2,1,0:T(8,128)(2,1)S(1)}) custom-call(s32[10]{0:T(128)S(1)} %stack.97.offs, bf16[96,3072]{1,0:T(8,128)(2,1)S(1)} %copy.283.refs_0_, bf16[96,3072]{1,0:T(8,128)(2,1)S(1)} %collective-permute-done.3.refs_1_, ...), custom_call_target="tpu_custom_call" | custom-call | flops 1 | bytes 1 | tf_op jit(solution)/shard_map/pallas_call | solution.py:100
  93.7 1.3 copy-done
  95.1 1.1 copy-done.6
  96.2 1.9 collective-permute-done.16.refs_3_.refs_7_
  98.1 9.0 %shard_map.221.refs_0_ = bf16[2,512,256]{2,1,0:T(8,128)(2,1)} custom-call(bf16[3,2,640,256]{3,2,1,0:T(8,128)(2,1)} %copy-done.1, bf16[3,2,640,256]{3,2,1,0:T(8,128)(2,1)} %copy-done.1, bf16[3,2,640,256]{3,2,1,0:T(8,128)(2,1)} %copy-done.1, bf16[2,2,128,256]{3,2,1,0:T(8,128)(2,1)} %get-tuple-element.113.refs_0_.refs_4_, ...), custom_call_target="tpu_custom_call" | custom-call | flops 1 | bytes 1 | tf_op jit(solution)/shard_map/pallas_call | solution.py:316
  107.4 2.5 collective-permute-start.17
  110.0 1.9 collective-permute-start.19
  111.9 8.6 %collective-permute-done.21.refs_2_.refs_6_ = bf16[2,2,128,256]{3,2,1,0:T(8,128)(2,1)S(1)} collective-permute-done((bf16[2,2,128,256]{3,2,1,0:T(8,128)(2,1)S(1)}, bf16[2,2,128,256]{3,2,1,0:T(8,128)(2,1)S(1)}, u32[]{:S(2)}, u32[]{:S(2)}) %collective-permute-start.21) | collective-permute-done | bytes 262176 | tf_op jit(solution)/shard_map/ppermute | solution.py:812
  122.7 2.3 copy.297
  124.9 2.8 copy.303
  127.7 6.5 %collective-permute-done.19.refs_3_.refs_7_ = bf16[2,2,128,256]{3,2,1,0:T(8,128)(2,1)} collective-permute-done((bf16[2,2,128,256]{3,2,1,0:T(8,128)(2,1)}, bf16[2,2,128,256]{3,2,1,0:T(8,128)(2,1)}, u32[]{:S(2)}, u32[]{:S(2)}) %collective-permute-start.19) | collective-permute-done | bytes 262176 | tf_op jit(solution)/shard_map/ppermute | solution.py:812
  134.2 8.6 %shard_map.223.refs_1_ = bf16[2,512,256]{2,1,0:T(8,128)(2,1)} custom-call(bf16[3,2,640,256]{3,2,1,0:T(8,128)(2,1)} %copy-done.2, bf16[3,2,640,256]{3,2,1,0:T(8,128)(2,1)} %copy-done.2, bf16[3,2,640,256]{3,2,1,0:T(8,128)(2,1)} %copy-done.2, bf16[2,2,128,256]{3,2,1,0:T(8,128)(2,1)} %get-tuple-element.117.refs_0_.refs_4_, bf16[2,2,128,256]{3,2,1,0:T(8,128)(2,1)} %copy-done.14, ...), custom_call_target="tpu_custom_call" | custom-call | flops 1 | bytes 1 | tf_op jit(solution)/shard_map/pallas_call | solution.py:316
  143.6 8.7 %shard_map.225.refs_2_ = bf16[2,512,256]{2,1,0:T(8,128)(2,1)} custom-call(bf16[3,2,640,256]{3,2,1,0:T(8,128)(2,1)} %copy-done, bf16[3,2,640,256]{3,2,1,0:T(8,128)(2,1)} %copy-done, bf16[3,2,640,256]{3,2,1,0:T(8,128)(2,1)} %copy-done, bf16[2,2,128,256]{3,2,1,0:T(8,128)(2,1)} %copy-done.8, bf16[2,2,128,256]{3,2,1,0:T(8,128)(2,1)} %copy-done.12, ...), custom_call_target="tpu_custom_call" | custom-call | flops 1 | bytes 1 | tf_op jit(solution)/shard_map/pallas_call | solution.py:316
  152.3 53.7 %shard_map.226 = (bf16[2,512,768]{2,1,0:T(8,128)(2,1)}, f32[2,512,768]{2,1,0:T(8,128)}, bf16[2,512,256]{2,1,0:T(8,128)(2,1)}, bf16[2,512,256]{2,1,0:T(8,128)(2,1...) custom-call(bf16[2,512,256]{2,1,0:T(8,128)(2,1)} %shard_map.221.refs, ...), custom_call_target="tpu_custom_call" | custom-call | flops 1 | bytes 1 | tf_op jit(solution)/shard_map/pallas_call | solution.py:522
  206.1 17.9 %shard_map.227 = (bf16[2,512,256]{2,1,0:T(8,128)(2,1)}, f32[2,640,256]{2,1,0:T(8,128)}, f32[2,640,256]{2,1,0:T(8,128)}, bf16[2,2,2,128,256]{4,3,2,1,0:T(8,128)(2,1)}, bf16[2,2,2,128,256]{4,3,2,1,0:T(8,128)(2,1)}) custom-call(bf16[3,2,640,256]{3,2,1,0:T(8,128)(2,1)} %copy-done.1, bf16[3,2,640,256]{3,2,1,0:T(8,128)(2,1)} %copy-done.1, ...), custom_call_target="tpu_custom_call" | custom-call | flops 1 | bytes 1 | tf_op jit(solution)/shard_map/pallas_call | solution.py:338
  224.1 17.8 %shard_map.228 = (bf16[2,512,256]{2,1,0:T(8,128)(2,1)}, f32[2,640,256]{2,1,0:T(8,128)}, f32[2,640,256]{2,1,0:T(8,128)}, bf16[2,2,2,128,256]{4,3,2,1,0:T(8,128)(2,1)}, bf16[2,2,2,128,256]{4,3,2,1,0:T(8,128)(2,1)}) custom-call(bf16[3,2,640,256]{3,2,1,0:T(8,128)(2,1)} %copy-done.2, bf16[3,2,640,256]{3,2,1,0:T(8,128)(2,1)} %copy-done.2, ...), custom_call_target="tpu_custom_call" | custom-call | flops 1 | bytes 1 | tf_op jit(solution)/shard_map/pallas_call | solution.py:338
  243.0 2.1 collective-permute-start.24
  245.4 18.1 %shard_map.229 = (bf16[2,512,256]{2,1,0:T(8,128)(2,1)}, f32[2,640,256]{2,1,0:T(8,128)}, f32[2,640,256]{2,1,0:T(8,128)}, bf16[2,2,2,128,256]{4,3,2,1,0:T(8,128)(2,1)}, bf16[2,2,2,128,256]{4,3,2,1,0:T(8,128)(2,1)}) custom-call(bf16[3,2,640,256]{3,2,1,0:T(8,128)(2,1)} %copy-done, bf16[3,2,640,256]{3,2,1,0:T(8,128)(2,1)} %copy-done, ...), custom_call_target="tpu_custom_call" | custom-call | flops 1 | bytes 1 | tf_op jit(solution)/shard_map/pallas_call | solution.py:338
  264.5 2.1 collective-permute-start.26
  267.3 12.3 %collective-permute-done.26 = bf16[2,2,2,128,256]{4,3,2,1,0:T(8,128)(2,1)S(1)} collective-permute-done((bf16[2,2,2,128,256]{4,3,2,1,0:T(8,128)(2,1)S(1)}, bf16[2,2,2,128,256]{4,3,2,1,0:T(8,128)(2,1)S(1)}, u32[]{:S(2)}, u32[]{:S(2)}) %collective-permute-start.26) | collective-permute-done | bytes 524320 | tf_op jit(solution)/shard_map/ppermute | solution.py:812
  283.6 13.0 %shard_map.230 = (bf16[4,4,112,512]{3,2,1,0:T(8,128)(2,1)}, bf16[4,4,112,512]{3,2,1,0:T(8,128)(2,1)}, bf16[2,2,640,256]{3,2,1,0:T(8,128)(2,1)}, bf16[2,2,640,256]{3,2,1,0:T(8,128)(2,1)}) custom-call(s32[8]{0:T(128)} %stack.111.offs, f32[2,640,256]{2,1,0:T(8,128)} %get-tuple-element.148.refs_0_, f32[2,640,256]{2,1,0:T(8,128)} %get-tuple-element.149.refs_1_, ...), custom_call_target="tpu_custom_call" | custom-call | flops 1 | bytes 1 | tf_op jit(solution)/shard_map/pallas_call | solution.py:672
  296.7 4.0 %collective-permute-done.29 = bf16[4,4,112,512]{3,2,1,0:T(8,128)(2,1)S(1)} collective-permute-done((bf16[4,4,112,512]{3,2,1,0:T(8,128)(2,1)}, bf16[4,4,112,512]{3,2,1,0:T(8,128)(2,1)S(1)}, u32[]{:S(2)}, u32[]{:S(2)}) %collective-permute-start.29) | collective-permute-done | bytes 1835040 | tf_op jit(solution)/shard_map/ppermute | solution.py:812
  300.7 2.1 add_convert_fusion
  303.0 1.2 collective-permute-start.30
  304.9 1.7 collective-permute-start.32
  307.8 8.0 %shard_map.231 = (bf16[4,4,112,256]{3,2,1,0:T(8,128)(2,1)}, bf16[4,4,112,256]{3,2,1,0:T(8,128)(2,1)}, bf16[2,2,640,256]{3,2,1,0:T(8,128)(2,1)}) custom-call(s32[8]{0:T(128)} %stack.111.offs, f32[2,640,256]{2,1,0:T(8,128)} %get-tuple-element.159.refs_0_, f32[2,640,256]{2,1,0:T(8,128)} %get-tuple-element.160.refs_1_, ...), custom_call_target="tpu_custom_call" | custom-call | flops 1 | bytes 1 | tf_op jit(solution)/shard_map/pallas_call | solution.py:672
  315.9 9.3 %shard_map.232 = (f32[2,512,768]{2,1,0:T(8,128)}, bf16[2,64,768]{2,1,0:T(8,128)(2,1)}, bf16[2,64,768]{2,1,0:T(8,128)(2,1)}) custom-call(bf16[2,512,256]{2,1,0:T(8,128)(2,1)} %get-tuple-element.132.refs_2_.refs_0_, bf16[2,2,640,256]{3,2,1,0:T(8,128)(2,1)} %get-tuple-element.155.refs_1_, bf16[4,768,256]{2,1,0:T(8,128)(2,1)} %copy-done.4, ...), custom_call_target="tpu_custom_call" | custom-call | flops 1 | bytes 1 | tf_op jit(solution)/shard_map/pallas_call | solution.py:739
  325.2 1.4 collective-permute-done.32
  326.5 1.3 add_convert_fusion.5
  327.8 4.9 %collective-permute-start.33 = (bf16[2,64,768]{2,1,0:T(8,128)(2,1)S(1)}, bf16[2,64,768]{2,1,0:T(8,128)(2,1)S(1)}, u32[]{:S(2)}, u32[]{:S(2)}) collective-permute-start(bf16[2,64,768]{2,1,0:T(8,128)(2,1)S(1)} %copy-done.37), channel_id=1, source_target_pairs={{0,1},{1,2},{2,3},{4,5},{5,6},{6,7},{8,9},{9,10},{10,11},{12,13},{... | collective-permute-start | bytes 589832 | tf_op jit(solution)/shard_map/ppermute | solution.py:817
  332.7 2.8 copy.294
  336.4 1.3 collective-permute-start.34
  338.7 1.6 collective-permute-start.40
  340.3 1.3 collective-permute-start.41
  341.6 2.7 collective-permute-done.34
  344.4 4.1 %copy.295 = f32[512,2,768]{2,1,0:T(2,128)} copy(f32[512,2,768]{2,0,1:T(8,128)S(1)} %fusion.3) | data formatting | bytes 6291456
  349.1 3.8 %collective-permute-start.38 = (bf16[112,512]{1,0:T(8,128)(2,1)S(1)}, bf16[112,512]{1,0:T(8,128)(2,1)S(1)}, u32[]{:S(2)}, u32[]{:S(2)}) collective-permute-start(bf16[112,512]{1,0:T(8,128)(2,1)S(1)} %get-tuple-element.315), channel_id=1, source_target_pairs={{0,3},{1,2},{2,1},{3,0},{4,7},{5,6},{6,5},{7,4},{8,11},{9,10},{10,... | collective-permute-start | bytes 344072 | tf_op jit(solution)/shard_map/ppermute | solution.py:812
  355.6 3.8 %collective-permute-start.44 = (bf16[112,256]{1,0:T(8,128)(2,1)S(1)}, bf16[112,256]{1,0:T(8,128)(2,1)S(1)}, u32[]{:S(2)}, u32[]{:S(2)}) collective-permute-start(bf16[112,256]{1,0:T(8,128)(2,1)S(1)} %get-tuple-element.319), channel_id=1, source_target_pairs={{0,3},{1,2},{2,1},{3,0},{4,7},{5,6},{6,5},{7,4},{8,11},{9,10},{10,... | collective-permute-start | bytes 172040 | tf_op jit(solution)/shard_map/ppermute | solution.py:812
  360.1 2.2 collective-permute-done.37.refs_2_
  362.3 2.4 collective-permute-done.43.refs_6_
  (236 shorter events, 40.7 us)
Async XLA Ops:
  7.2 62.6 %all-gather.5.cloned.1.call-start = ((), (), s32[]{:S(2)}) async-start(), calls=%async_computation.4 | async-start | bytes 1474560 | tf_op jit(solution)/shard_map/all_gather | solution.py:993
  12.2 14.9 %copy-start.28 = (bf16[96,768]{1,0:T(8,128)(2,1)S(1)}, bf16[96,768]{1,0:T(8,128)(2,1)}, u32[]{:S(2)}) copy-start(bf16[96,768]{1,0:T(8,128)(2,1)} %param.26) | copy-start | bytes 442372
  12.2 14.9 %copy-start.29 = (bf16[96,768]{1,0:T(8,128)(2,1)S(1)}, bf16[96,768]{1,0:T(8,128)(2,1)}, u32[]{:S(2)}) copy-start(bf16[96,768]{1,0:T(8,128)(2,1)} %param.24) | copy-start | bytes 442372
  12.2 15.7 %copy-start.27 = (s32[2048,2]{0,1:T(2,128)S(1)}, s32[2048,2]{0,1:T(2,128)}, u32[]{:S(2)}) copy-start(s32[2048,2]{0,1:T(2,128)} %param.18) | copy-start | bytes 49156
  12.2 20.1 %collective-permute-start = (bf16[109,768]{0,1:T(8,128)(2,1)S(1)}, bf16[109,768]{0,1:T(8,128)(2,1)S(1)}, u32[]{:S(2)}, u32[]{:S(2)}) collective-permute-start(bf16[109,768]{0,1:T(8,128)(2,1)S(1)} %pad_maximum_fusion.2), channel_id=1, source_target_pairs={{0,3},{1,2},{2,1},{3,0},{4,7},{5,6},{6,5},{7,4},{8,11},{9,10},{10,... | collective-permute-start | bytes 502280 | tf_op jit(solution)/shard_map/ppermute | solution.py:812
  17.3 17.7 %collective-permute-start.1 = (bf16[109,768]{0,1:T(8,128)(2,1)S(1)}, bf16[109,768]{0,1:T(8,128)(2,1)S(1)}, u32[]{:S(2)}, u32[]{:S(2)}) collective-permute-start(bf16[109,768]{0,1:T(8,128)(2,1)S(1)} %pad_maximum_fusion.2), channel_id=1, source_target_pairs={{0,2},{1,3},{2,0},{3,1},{4,6},{5,7},{6,4},{7,5},{8,10},{9,11},{10,... | collective-permute-start | bytes 502280 | tf_op jit(solution)/shard_map/ppermute | solution.py:812
  17.3 17.7 %collective-permute-start.2 = (bf16[109,768]{0,1:T(8,128)(2,1)S(1)}, bf16[109,768]{0,1:T(8,128)(2,1)S(1)}, u32[]{:S(2)}, u32[]{:S(2)}) collective-permute-start(bf16[109,768]{0,1:T(8,128)(2,1)S(1)} %pad_maximum_fusion.2), channel_id=1, source_target_pairs={{0,1},{1,0},{2,3},{3,2},{4,5},{5,4},{6,7},{7,6},{8,9},{9,8},{10,11... | collective-permute-start | bytes 502280 | tf_op jit(solution)/shard_map/ppermute | solution.py:812
  21.8 19.0 %collective-permute-start.5 = (bf16[64,2,768]{2,0,1:T(8,128)(2,1)S(1)}, bf16[64,2,768]{2,0,1:T(8,128)(2,1)}, u32[]{:S(2)}, u32[]{:S(2)}) collective-permute-start(bf16[64,2,768]{2,0,1:T(8,128)(2,1)S(1)} %get-tuple-element.298), channel_id=1, source_target_pairs={{0,1},{1,2},{2,3},{4,5},{5,6},{6,7},{8,9},{9,10},{10,11},{12,13},{... | collective-permute-start | bytes 589832 | tf_op jit(solution)/shard_map/ppermute | solution.py:817
  25.7 15.5 %collective-permute-start.6 = (bf16[64,2,768]{2,0,1:T(8,128)(2,1)S(1)}, bf16[64,2,768]{2,0,1:T(8,128)(2,1)}, u32[]{:S(2)}, u32[]{:S(2)}) collective-permute-start(bf16[64,2,768]{2,0,1:T(8,128)(2,1)S(1)} %get-tuple-element.299), channel_id=1, source_target_pairs={{1,0},{2,1},{3,2},{5,4},{6,5},{7,6},{9,8},{10,9},{11,10},{13,12},{... | collective-permute-start | bytes 589832 | tf_op jit(solution)/shard_map/ppermute | solution.py:822
  27.8 124.5 %all-gather.7.cloned.1.call-start = ((), (), s32[]{:S(2)}) async-start(), calls=%async_computation.5 | async-start | bytes 10616832 | tf_op jit(solution)/shard_map/all_gather | solution.py:1013
  31.7 56.5 %copy-start.7 = (f32[2,128,8]{2,1,0:T(8,128)}, f32[2,128,8]{2,1,0:T(8,128)S(1)}, u32[]{:S(2)}) copy-start(f32[2,128,8]{2,1,0:T(8,128)S(1)} %convert_element_type.115.refs_13_.refs_17_.refs_9_) | copy-start | bytes 24580
  36.2 13.5 %collective-permute-start.3 = (bf16[96,3072]{1,0:T(8,128)(2,1)S(1)}, bf16[96,3072]{1,0:T(8,128)(2,1)S(1)}, u32[]{:S(2)}, u32[]{:S(2)}) collective-permute-start(bf16[96,3072]{1,0:T(8,128)(2,1)S(1)} %copy.283.refs_0_), channel_id=1, source_target_pairs={{0,8},{4,12},{8,0},{12,4},{16,24},{20,28},{24,16},{28,20},{1,9},{5... | collective-permute-start | bytes 1769480 | tf_op jit(solution)/shard_map/ppermute | solution.py:812
  37.7 14.3 %collective-permute-start.4 = (bf16[96,3072]{1,0:T(8,128)(2,1)S(1)}, bf16[96,3072]{1,0:T(8,128)(2,1)}, u32[]{:S(2)}, u32[]{:S(2)}) collective-permute-start(bf16[96,3072]{1,0:T(8,128)(2,1)S(1)} %copy.283.refs_0_), channel_id=1, source_target_pairs={{0,16},{4,20},{8,24},{12,28},{16,0},{20,4},{24,8},{28,12},{1,17},{... | collective-permute-start | bytes 1769480 | tf_op jit(solution)/shard_map/ppermute | solution.py:812
  40.5 19.5 %collective-permute-start.9 = (bf16[96,3072]{1,0:T(8,128)(2,1)S(1)}, bf16[96,3072]{1,0:T(8,128)(2,1)}, u32[]{:S(2)}, u32[]{:S(2)}) collective-permute-start(bf16[96,3072]{1,0:T(8,128)(2,1)S(1)} %copy.283.refs_0_), channel_id=1, source_target_pairs={{0,4},{4,0},{8,12},{12,8},{16,20},{20,16},{24,28},{28,24},{1,5},{5... | collective-permute-start | bytes 1769480 | tf_op jit(solution)/shard_map/ppermute | solution.py:812
  40.7 32.7 %copy-start.9 = (f32[2,8,768]{2,1,0:T(8,128)}, f32[2,8,768]{2,1,0:T(8,128)S(1)}, u32[]{:S(2)}) copy-start(f32[2,8,768]{2,1,0:T(8,128)S(1)} %pad.22.refs_12_) | copy-start | bytes 147460
  42.9 79.7 %copy-start.3 = (bf16[2,640,768]{2,1,0:T(8,128)(2,1)}, bf16[2,640,768]{2,1,0:T(8,128)(2,1)S(1)}, u32[]{:S(2)}) copy-start(bf16[2,640,768]{2,1,0:T(8,128)(2,1)S(1)} %maximum_bitcast_fusion.refs_10_.refs_6_) | copy-start | bytes 5898244
  49.7 7.6 %collective-permute-start.7 = (bf16[48,3072]{1,0:T(8,128)(2,1)S(1)}, bf16[48,3072]{1,0:T(8,128)(2,1)}, u32[]{:S(2)}, u32[]{:S(2)}) collective-permute-start(bf16[48,3072]{1,0:T(8,128)(2,1)S(1)} %slice.248), channel_id=1, source_target_pairs={{0,16},{4,20},{8,24},{12,28},{16,0},{20,4},{24,8},{28,12},{1,17},{... | collective-permute-start | bytes 884744 | tf_op jit(solution)/shard_map/ppermute | solution.py:812
  53.1 6.9 %collective-permute-start.8 = (bf16[48,3072]{1,0:T(8,128)(2,1)S(1)}, bf16[48,3072]{1,0:T(8,128)(2,1)}, u32[]{:S(2)}, u32[]{:S(2)}) collective-permute-start(bf16[48,3072]{1,0:T(8,128)(2,1)S(1)} %slice.256), channel_id=1, source_target_pairs={{0,8},{4,12},{8,0},{12,4},{16,24},{20,28},{24,16},{28,20},{1,9},{5... | collective-permute-start | bytes 884744 | tf_op jit(solution)/shard_map/ppermute | solution.py:812
  53.8 8.1 %collective-permute-start.10 = (bf16[96,3072]{1,0:T(8,128)(2,1)S(1)}, bf16[96,3072]{1,0:T(8,128)(2,1)}, u32[]{:S(2)}, u32[]{:S(2)}) collective-permute-start(bf16[96,3072]{1,0:T(8,128)(2,1)S(1)} %collective-permute-done.3.refs_1_), channel_id=1, source_target_pairs={{0,4},{4,0},{8,12},{12,8},{16,20},{20,16},{24,28},{28,24},{1,5},{5... | collective-permute-start | bytes 1769480 | tf_op jit(solution)/shard_map/ppermute | solution.py:812
  53.8 8.1 %collective-permute-start.11 = (bf16[96,3072]{1,0:T(8,128)(2,1)}, bf16[96,3072]{1,0:T(8,128)(2,1)}, u32[]{:S(2)}, u32[]{:S(2)}) collective-permute-start(bf16[96,3072]{1,0:T(8,128)(2,1)} %collective-permute-done.4.refs_2_), channel_id=1, source_target_pairs={{0,4},{4,0},{8,12},{12,8},{16,20},{20,16},{24,28},{28,24},{1,5},{5... | collective-permute-start | bytes 1769480 | tf_op jit(solution)/shard_map/ppermute | solution.py:812
  57.3 2.7 collective-permute-start.12
  59.9 1.9 collective-permute-start.13
  69.8 233.0 %reduce-scatter.3.cloned.1.call-start = ((), (), s32[]{:S(2)}) async-start(), calls=%async_computation.2 | async-start | bytes 12386304 | tf_op jit(solution)/shard_map/reduce_scatter | solution.py:1034
  70.1 15.3 %collective-permute-start.15 = (bf16[2,2,128,256]{3,2,1,0:T(8,128)(2,1)}, bf16[2,2,128,256]{3,2,1,0:T(8,128)(2,1)}, u32[]{:S(2)}, u32[]{:S(2)}) collective-permute-start(bf16[2,2,128,256]{3,2,1,0:T(8,128)(2,1)} %get-tuple-element.113.refs_0_.refs_4_), channel_id=1, source_target_pairs={{0,2},{1,3},{2,0},{3,1},{4,6},{5,7},{6,4},{7,5},{8,10},{9,11},{10,... | collective-permute-start | bytes 786440 | tf_op jit(solution)/shard_map/ppermute | solution.py:812
  70.3 25.9 %collective-permute-start.14 = (bf16[2,2,128,256]{3,2,1,0:T(8,128)(2,1)}, bf16[2,2,128,256]{3,2,1,0:T(8,128)(2,1)}, u32[]{:S(2)}, u32[]{:S(2)}) collective-permute-start(bf16[2,2,128,256]{3,2,1,0:T(8,128)(2,1)} %get-tuple-element.113.refs_0_.refs_4_), channel_id=1, source_target_pairs={{0,1},{1,0},{2,3},{3,2},{4,5},{5,4},{6,7},{7,6},{8,9},{9,8},{10,11... | collective-permute-start | bytes 786440 | tf_op jit(solution)/shard_map/ppermute | solution.py:812
  85.4 12.7 %collective-permute-start.16 = (bf16[2,2,128,256]{3,2,1,0:T(8,128)(2,1)}, bf16[2,2,128,256]{3,2,1,0:T(8,128)(2,1)}, u32[]{:S(2)}, u32[]{:S(2)}) collective-permute-start(bf16[2,2,128,256]{3,2,1,0:T(8,128)(2,1)} %collective-permute-done.15.refs_2_.refs_6_), channel_id=1, source_target_pairs={{0,1},{1,0},{2,3},{3,2},{4,5},{5,4},{6,7},{7,6},{8,9},{9,8},{10,11... | collective-permute-start | bytes 786440 | tf_op jit(solution)/shard_map/ppermute | solution.py:812
  85.4 21.7 %collective-permute-start.18 = (bf16[2,2,128,256]{3,2,1,0:T(8,128)(2,1)}, bf16[2,2,128,256]{3,2,1,0:T(8,128)(2,1)}, u32[]{:S(2)}, u32[]{:S(2)}) collective-permute-start(bf16[2,2,128,256]{3,2,1,0:T(8,128)(2,1)} %get-tuple-element.117.refs_0_.refs_4_), channel_id=1, source_target_pairs={{0,2},{1,3},{2,0},{3,1},{4,6},{5,7},{6,4},{7,5},{8,10},{9,11},{10,... | collective-permute-start | bytes 786440 | tf_op jit(solution)/shard_map/ppermute | solution.py:812
  98.1 22.4 %copy-start.31 = (f32[2,768]{1,0:T(2,128)S(1)}, f32[2,768]{1,0:T(2,128)}, u32[]{:S(2)}) copy-start(f32[2,768]{1,0:T(2,128)} %param.28) | copy-start | bytes 18436
  98.1 22.4 %copy-start.32 = (f32[2,768]{1,0:T(2,128)S(1)}, f32[2,768]{1,0:T(2,128)}, u32[]{:S(2)}) copy-start(f32[2,768]{1,0:T(2,128)} %param.27) | copy-start | bytes 18436
  98.1 22.4 %copy-start.33 = (f32[2,768]{1,0:T(2,128)S(1)}, f32[2,768]{1,0:T(2,128)}, u32[]{:S(2)}) copy-start(f32[2,768]{1,0:T(2,128)} %param.23) | copy-start | bytes 18436
  107.2 13.4 %collective-permute-start.21 = (bf16[2,2,128,256]{3,2,1,0:T(8,128)(2,1)S(1)}, bf16[2,2,128,256]{3,2,1,0:T(8,128)(2,1)S(1)}, u32[]{:S(2)}, u32[]{:S(2)}) collective-permute-start(bf16[2,2,128,256]{3,2,1,0:T(8,128)(2,1)S(1)} %get-tuple-element.124.refs_0_.refs_4_), channel_id=1, source_target_pairs={{0,2},{1,3},{2,0},{3,1},{4,6},{5,7},{6,4},{7,5},{8,10},{9,11},{10,... | collective-permute-start | bytes 786440 | tf_op jit(solution)/shard_map/ppermute | solution.py:812
  107.4 20.3 %collective-permute-start.17 = (bf16[2,2,128,256]{3,2,1,0:T(8,128)(2,1)}, bf16[2,2,128,256]{3,2,1,0:T(8,128)(2,1)S(1)}, u32[]{:S(2)}, u32[]{:S(2)}) collective-permute-start(bf16[2,2,128,256]{3,2,1,0:T(8,128)(2,1)} %get-tuple-element.117.refs_0_.refs_4_), channel_id=1, source_target_pairs={{0,1},{1,0},{2,3},{3,2},{4,5},{5,4},{6,7},{7,6},{8,9},{9,8},{10,11... | collective-permute-start | bytes 786440 | tf_op jit(solution)/shard_map/ppermute | solution.py:812
  109.9 32.9 %collective-permute-start.20 = (bf16[2,2,128,256]{3,2,1,0:T(8,128)(2,1)S(1)}, bf16[2,2,128,256]{3,2,1,0:T(8,128)(2,1)S(1)}, u32[]{:S(2)}, u32[]{:S(2)}) collective-permute-start(bf16[2,2,128,256]{3,2,1,0:T(8,128)(2,1)S(1)} %get-tuple-element.124.refs_0_.refs_4_), channel_id=1, source_target_pairs={{0,1},{1,0},{2,3},{3,2},{4,5},{5,4},{6,7},{7,6},{8,9},{9,8},{10,11... | collective-permute-start | bytes 786440 | tf_op jit(solution)/shard_map/ppermute | solution.py:812
  110.0 24.2 %collective-permute-start.19 = (bf16[2,2,128,256]{3,2,1,0:T(8,128)(2,1)}, bf16[2,2,128,256]{3,2,1,0:T(8,128)(2,1)}, u32[]{:S(2)}, u32[]{:S(2)}) collective-permute-start(bf16[2,2,128,256]{3,2,1,0:T(8,128)(2,1)} %collective-permute-done.18.refs_2_.refs_6_), channel_id=1, source_target_pairs={{0,1},{1,0},{2,3},{3,2},{4,5},{5,4},{6,7},{7,6},{8,9},{9,8},{10,11... | collective-permute-start | bytes 786440 | tf_op jit(solution)/shard_map/ppermute | solution.py:812
  120.6 22.3 %collective-permute-start.22 = (bf16[2,2,128,256]{3,2,1,0:T(8,128)(2,1)S(1)}, bf16[2,2,128,256]{3,2,1,0:T(8,128)(2,1)S(1)}, u32[]{:S(2)}, u32[]{:S(2)}) collective-permute-start(bf16[2,2,128,256]{3,2,1,0:T(8,128)(2,1)S(1)} %collective-permute-done.21.refs_2_.refs_6_), channel_id=1, source_target_pairs={{0,1},{1,0},{2,3},{3,2},{4,5},{5,4},{6,7},{7,6},{8,9},{9,8},{10,11... | collective-permute-start | bytes 786440 | tf_op jit(solution)/shard_map/ppermute | solution.py:812
  206.1 147.7 %reduce-scatter.5.cloned.1.call-start = ((), (), s32[]{:S(2)}) async-start(), calls=%async_computation.3 | async-start | bytes 1720320 | tf_op jit(solution)/shard_map/reduce_scatter | solution.py:1035
  224.0 17.9 %collective-permute-start.23 = (bf16[2,2,2,128,256]{4,3,2,1,0:T(8,128)(2,1)}, bf16[2,2,2,128,256]{4,3,2,1,0:T(8,128)(2,1)S(1)}, u32[]{:S(2)}, u32[]{:S(2)}) collective-permute-start(bf16[2,2,2,128,256]{4,3,2,1,0:T(8,128)(2,1)} %get-tuple-element.137), channel_id=1, source_target_pairs={{0,1},{1,0},{2,3},{3,2},{4,5},{5,4},{6,7},{7,6},{8,9},{9,8},{10,11... | collective-permute-start | bytes 1572872 | tf_op jit(solution)/shard_map/ppermute | solution.py:812
  224.1 17.8 %copy-start.22 = (bf16[2,2,2,128,256]{4,3,2,1,0:T(8,128)(2,1)S(1)}, bf16[2,2,2,128,256]{4,3,2,1,0:T(8,128)(2,1)}, u32[]{:S(2)}) copy-start(bf16[2,2,2,128,256]{4,3,2,1,0:T(8,128)(2,1)} %get-tuple-element.136) | copy-start | bytes 1572868
  243.0 20.5 %collective-permute-start.24 = (bf16[2,2,2,128,256]{4,3,2,1,0:T(8,128)(2,1)S(1)}, bf16[2,2,2,128,256]{4,3,2,1,0:T(8,128)(2,1)S(1)}, u32[]{:S(2)}, u32[]{:S(2)}) collective-permute-start(bf16[2,2,2,128,256]{4,3,2,1,0:T(8,128)(2,1)S(1)} %copy-done.34), channel_id=1, source_target_pairs={{0,1},{1,0},{2,3},{3,2},{4,5},{5,4},{6,7},{7,6},{8,9},{9,8},{10,11... | collective-permute-start | bytes 1572872 | tf_op jit(solution)/shard_map/ppermute | solution.py:812
  245.1 19.3 %collective-permute-start.25 = (bf16[2,2,128,256]{3,2,1,0:T(8,128)(2,1)S(1)}, bf16[2,2,128,256]{3,2,1,0:T(8,128)(2,1)S(1)}, u32[]{:S(2)}, u32[]{:S(2)}) collective-permute-start(bf16[2,2,128,256]{3,2,1,0:T(8,128)(2,1)S(1)} %get-tuple-element.313), channel_id=1, source_target_pairs={{0,2},{1,3},{2,0},{3,1},{4,6},{5,7},{6,4},{7,5},{8,10},{9,11},{10,... | collective-permute-start | bytes 786440 | tf_op jit(solution)/shard_map/ppermute | solution.py:812
  245.4 18.1 %copy-start.20 = (bf16[2,2,2,128,256]{4,3,2,1,0:T(8,128)(2,1)S(1)}, bf16[2,2,2,128,256]{4,3,2,1,0:T(8,128)(2,1)}, u32[]{:S(2)}) copy-start(bf16[2,2,2,128,256]{4,3,2,1,0:T(8,128)(2,1)} %get-tuple-element.143) | copy-start | bytes 1572868
  263.5 16.1 %copy-start.21 = (bf16[2,2,2,128,256]{4,3,2,1,0:T(8,128)(2,1)S(1)}, bf16[2,2,2,128,256]{4,3,2,1,0:T(8,128)(2,1)}, u32[]{:S(2)}) copy-start(bf16[2,2,2,128,256]{4,3,2,1,0:T(8,128)(2,1)} %get-tuple-element.141) | copy-start | bytes 1572868
  263.6 18.0 %copy-start.19 = (f32[2,5,768]{2,1,0:T(8,128)S(1)}, f32[2,5,768]{2,1,0:T(8,128)}, u32[]{:S(2)}) copy-start(f32[2,5,768]{2,1,0:T(8,128)} %copy-done.18) | copy-start | bytes 92164
  263.7 18.6 %copy-start.30 = (f32[8,768]{1,0:T(8,128)S(1)}, f32[8,768]{1,0:T(8,128)}, u32[]{:S(2)}) copy-start(f32[8,768]{1,0:T(8,128)} %get-tuple-element.154) | copy-start | bytes 73732
  264.4 18.5 %copy-start.23 = (bf16[2,2,128,256]{3,2,1,0:T(8,128)(2,1)}, bf16[2,2,128,256]{3,2,1,0:T(8,128)(2,1)S(1)}, u32[]{:S(2)}) copy-start(bf16[2,2,128,256]{3,2,1,0:T(8,128)(2,1)S(1)} %collective-permute-done.25.refs_4_) | copy-start | bytes 786436
  264.5 15.1 %collective-permute-start.26 = (bf16[2,2,2,128,256]{4,3,2,1,0:T(8,128)(2,1)S(1)}, bf16[2,2,2,128,256]{4,3,2,1,0:T(8,128)(2,1)S(1)}, u32[]{:S(2)}, u32[]{:S(2)}) collective-permute-start(bf16[2,2,2,128,256]{4,3,2,1,0:T(8,128)(2,1)S(1)} %copy-done.35), channel_id=1, source_target_pairs={{0,1},{1,0},{2,3},{3,2},{4,5},{5,4},{6,7},{7,6},{8,9},{9,8},{10,11... | collective-permute-start | bytes 1572872 | tf_op jit(solution)/shard_map/ppermute | solution.py:812
  266.6 16.3 %collective-permute-start.27 = (bf16[2,2,128,256]{3,2,1,0:T(8,128)(2,1)S(1)}, bf16[2,2,128,256]{3,2,1,0:T(8,128)(2,1)S(1)}, u32[]{:S(2)}, u32[]{:S(2)}) collective-permute-start(bf16[2,2,128,256]{3,2,1,0:T(8,128)(2,1)S(1)} %get-tuple-element.311), channel_id=1, source_target_pairs={{0,2},{1,3},{2,0},{3,1},{4,6},{5,7},{6,4},{7,5},{8,10},{9,11},{10,... | collective-permute-start | bytes 786440 | tf_op jit(solution)/shard_map/ppermute | solution.py:812
  280.5 16.1 %collective-permute-start.28 = (bf16[2,2,128,256]{3,2,1,0:T(8,128)(2,1)S(1)}, bf16[2,2,128,256]{3,2,1,0:T(8,128)(2,1)S(1)}, u32[]{:S(2)}, u32[]{:S(2)}) collective-permute-start(bf16[2,2,128,256]{3,2,1,0:T(8,128)(2,1)S(1)} %get-tuple-element.309), channel_id=1, source_target_pairs={{0,2},{1,3},{2,0},{3,1},{4,6},{5,7},{6,4},{7,5},{8,10},{9,11},{10,... | collective-permute-start | bytes 786440 | tf_op jit(solution)/shard_map/ppermute | solution.py:812
  296.6 4.1 %collective-permute-start.29 = (bf16[4,4,112,512]{3,2,1,0:T(8,128)(2,1)}, bf16[4,4,112,512]{3,2,1,0:T(8,128)(2,1)S(1)}, u32[]{:S(2)}, u32[]{:S(2)}) collective-permute-start(bf16[4,4,112,512]{3,2,1,0:T(8,128)(2,1)} %get-tuple-element.169), channel_id=1, source_target_pairs={{0,4},{4,0},{8,12},{12,8},{16,20},{20,16},{24,28},{28,24},{1,5},{5... | collective-permute-start | bytes 5505032 | tf_op jit(solution)/shard_map/ppermute | solution.py:812
  303.0 22.2 %collective-permute-start.30 = (bf16[4,112,512]{2,1,0:T(8,128)(2,1)S(1)}, bf16[4,112,512]{2,1,0:T(8,128)(2,1)S(1)}, u32[]{:S(2)}, u32[]{:S(2)}) collective-permute-start(bf16[4,112,512]{2,1,0:T(8,128)(2,1)S(1)} %get-tuple-element.297), channel_id=1, source_target_pairs={{0,8},{4,12},{8,0},{12,4},{16,24},{20,28},{24,16},{28,20},{1,9},{5... | collective-permute-start | bytes 1376264 | tf_op jit(solution)/shard_map/ppermute | solution.py:812
  304.2 21.0 %collective-permute-start.31 = (bf16[4,112,512]{2,1,0:T(8,128)(2,1)S(1)}, bf16[4,112,512]{2,1,0:T(8,128)(2,1)S(1)}, u32[]{:S(2)}, u32[]{:S(2)}) collective-permute-start(bf16[4,112,512]{2,1,0:T(8,128)(2,1)S(1)} %get-tuple-element.296), channel_id=1, source_target_pairs={{0,16},{4,20},{8,24},{12,28},{16,0},{20,4},{24,8},{28,12},{1,17},{... | collective-permute-start | bytes 1376264 | tf_op jit(solution)/shard_map/ppermute | solution.py:812
  304.9 21.7 %collective-permute-start.32 = (bf16[4,112,512]{2,1,0:T(8,128)(2,1)S(1)}, bf16[4,112,512]{2,1,0:T(8,128)(2,1)}, u32[]{:S(2)}, u32[]{:S(2)}) collective-permute-start(bf16[4,112,512]{2,1,0:T(8,128)(2,1)S(1)} %get-tuple-element.295), channel_id=1, source_target_pairs={{0,24},{4,28},{8,16},{12,20},{16,8},{20,12},{24,0},{28,4},{1,25},{... | collective-permute-start | bytes 1376264 | tf_op jit(solution)/shard_map/ppermute | solution.py:812
  315.8 22.0 %collective-permute-start.35 = (bf16[4,4,112,256]{3,2,1,0:T(8,128)(2,1)}, bf16[4,4,112,256]{3,2,1,0:T(8,128)(2,1)S(1)}, u32[]{:S(2)}, u32[]{:S(2)}) collective-permute-start(bf16[4,4,112,256]{3,2,1,0:T(8,128)(2,1)} %get-tuple-element.177), channel_id=1, source_target_pairs={{0,4},{4,0},{8,12},{12,8},{16,20},{20,16},{24,28},{28,24},{1,5},{5... | collective-permute-start | bytes 2752520 | tf_op jit(solution)/shard_map/ppermute | solution.py:812
  327.8 9.9 %collective-permute-start.33 = (bf16[2,64,768]{2,1,0:T(8,128)(2,1)S(1)}, bf16[2,64,768]{2,1,0:T(8,128)(2,1)S(1)}, u32[]{:S(2)}, u32[]{:S(2)}) collective-permute-start(bf16[2,64,768]{2,1,0:T(8,128)(2,1)S(1)} %copy-done.37), channel_id=1, source_target_pairs={{0,1},{1,2},{2,3},{4,5},{5,6},{6,7},{8,9},{9,10},{10,11},{12,13},{... | collective-permute-start | bytes 589832 | tf_op jit(solution)/shard_map/ppermute | solution.py:817
  336.4 7.9 %collective-permute-start.34 = (bf16[2,64,768]{2,1,0:T(8,128)(2,1)S(1)}, bf16[2,64,768]{2,1,0:T(8,128)(2,1)S(1)}, u32[]{:S(2)}, u32[]{:S(2)}) collective-permute-start(bf16[2,64,768]{2,1,0:T(8,128)(2,1)S(1)} %copy-done.36), channel_id=1, source_target_pairs={{1,0},{2,1},{3,2},{5,4},{6,5},{7,6},{9,8},{10,9},{11,10},{13,12},{... | collective-permute-start | bytes 589832 | tf_op jit(solution)/shard_map/ppermute | solution.py:822
  338.1 11.1 %collective-permute-start.39 = (bf16[4,112,256]{2,1,0:T(8,128)(2,1)S(1)}, bf16[4,112,256]{2,1,0:T(8,128)(2,1)S(1)}, u32[]{:S(2)}, u32[]{:S(2)}) collective-permute-start(bf16[4,112,256]{2,1,0:T(8,128)(2,1)S(1)} %get-tuple-element.300), channel_id=1, source_target_pairs={{0,8},{4,12},{8,0},{12,4},{16,24},{20,28},{24,16},{28,20},{1,9},{5... | collective-permute-start | bytes 688136 | tf_op jit(solution)/shard_map/ppermute | solution.py:812
  338.7 14.2 %collective-permute-start.40 = (bf16[4,112,256]{2,1,0:T(8,128)(2,1)S(1)}, bf16[4,112,256]{2,1,0:T(8,128)(2,1)S(1)}, u32[]{:S(2)}, u32[]{:S(2)}) collective-permute-start(bf16[4,112,256]{2,1,0:T(8,128)(2,1)S(1)} %get-tuple-element.302), channel_id=1, source_target_pairs={{0,16},{4,20},{8,24},{12,28},{16,0},{20,4},{24,8},{28,12},{1,17},{... | collective-permute-start | bytes 688136 | tf_op jit(solution)/shard_map/ppermute | solution.py:812
  340.3 12.6 %collective-permute-start.41 = (bf16[4,112,256]{2,1,0:T(8,128)(2,1)S(1)}, bf16[4,112,256]{2,1,0:T(8,128)(2,1)S(1)}, u32[]{:S(2)}, u32[]{:S(2)}) collective-permute-start(bf16[4,112,256]{2,1,0:T(8,128)(2,1)S(1)} %get-tuple-element.301), channel_id=1, source_target_pairs={{0,24},{4,28},{8,16},{12,20},{16,8},{20,12},{24,0},{28,4},{1,25},{... | collective-permute-start | bytes 688136 | tf_op jit(solution)/shard_map/ppermute | solution.py:812
  348.5 7.2 %collective-permute-start.36 = (bf16[112,512]{1,0:T(8,128)(2,1)S(1)}, bf16[112,512]{1,0:T(8,128)(2,1)S(1)}, u32[]{:S(2)}, u32[]{:S(2)}) collective-permute-start(bf16[112,512]{1,0:T(8,128)(2,1)S(1)} %get-tuple-element.317), channel_id=1, source_target_pairs={{0,1},{1,0},{2,3},{3,2},{4,5},{5,4},{6,7},{7,6},{8,9},{9,8},{10,11... | collective-permute-start | bytes 344072 | tf_op jit(solution)/shard_map/ppermute | solution.py:812
  349.1 13.2 %collective-permute-start.37 = (bf16[112,512]{1,0:T(8,128)(2,1)S(1)}, bf16[112,512]{1,0:T(8,128)(2,1)S(1)}, u32[]{:S(2)}, u32[]{:S(2)}) collective-permute-start(bf16[112,512]{1,0:T(8,128)(2,1)S(1)} %get-tuple-element.316), channel_id=1, source_target_pairs={{0,2},{1,3},{2,0},{3,1},{4,6},{5,7},{6,4},{7,5},{8,10},{9,11},{10,... | collective-permute-start | bytes 344072 | tf_op jit(solution)/shard_map/ppermute | solution.py:812
  349.1 13.2 %collective-permute-start.38 = (bf16[112,512]{1,0:T(8,128)(2,1)S(1)}, bf16[112,512]{1,0:T(8,128)(2,1)S(1)}, u32[]{:S(2)}, u32[]{:S(2)}) collective-permute-start(bf16[112,512]{1,0:T(8,128)(2,1)S(1)} %get-tuple-element.315), channel_id=1, source_target_pairs={{0,3},{1,2},{2,1},{3,0},{4,7},{5,6},{6,5},{7,4},{8,11},{9,10},{10,... | collective-permute-start | bytes 344072 | tf_op jit(solution)/shard_map/ppermute | solution.py:812
  353.1 9.2 %collective-permute-start.42 = (bf16[112,256]{1,0:T(8,128)(2,1)S(1)}, bf16[112,256]{1,0:T(8,128)(2,1)S(1)}, u32[]{:S(2)}, u32[]{:S(2)}) collective-permute-start(bf16[112,256]{1,0:T(8,128)(2,1)S(1)} %get-tuple-element.321), channel_id=1, source_target_pairs={{0,1},{1,0},{2,3},{3,2},{4,5},{5,4},{6,7},{7,6},{8,9},{9,8},{10,11... | collective-permute-start | bytes 172040 | tf_op jit(solution)/shard_map/ppermute | solution.py:812
  353.2 11.5 %collective-permute-start.43 = (bf16[112,256]{1,0:T(8,128)(2,1)S(1)}, bf16[112,256]{1,0:T(8,128)(2,1)S(1)}, u32[]{:S(2)}, u32[]{:S(2)}) collective-permute-start(bf16[112,256]{1,0:T(8,128)(2,1)S(1)} %get-tuple-element.320), channel_id=1, source_target_pairs={{0,2},{1,3},{2,0},{3,1},{4,6},{5,7},{6,4},{7,5},{8,10},{9,11},{10,... | collective-permute-start | bytes 172040 | tf_op jit(solution)/shard_map/ppermute | solution.py:812
  355.6 9.1 %collective-permute-start.44 = (bf16[112,256]{1,0:T(8,128)(2,1)S(1)}, bf16[112,256]{1,0:T(8,128)(2,1)S(1)}, u32[]{:S(2)}, u32[]{:S(2)}) collective-permute-start(bf16[112,256]{1,0:T(8,128)(2,1)S(1)} %get-tuple-element.319), channel_id=1, source_target_pairs={{0,3},{1,2},{2,1},{3,0},{4,7},{5,6},{6,5},{7,4},{8,11},{9,10},{10,... | collective-permute-start | bytes 172040 | tf_op jit(solution)/shard_map/ppermute | solution.py:812
  (23 other events, 65.5 us)
Sparse Core Ops, SparseCore 0:
  27.9 33.0 all-gather.4
  69.9 58.1 all-gather.6
  206.2 82.4 reduce-scatter.2
  303.0 31.4 reduce-scatter.4

commit v7 on v6

--- a/solution.py
+++ b/solution.py
@@ -852,7 +852,7 @@
 
 def spread_line(values):
     two = swap(values, "tp", 2)
-    return [swap(values, "tp", 1), two, swap(two, "tp", 1)]
+    return [swap(after(values, two), "tp", 1), two, swap(two, "tp", 1)]
 
 
 def merge_line(own, other, *waits):
@@ -1007,17 +1007,17 @@
         made.append(project(j, chunks, pieces, offs, x_wide, bias_qkv, taps, same, far_rows))
         if j == 0:
             send_pooled(0)
-        if j == 1:
-            send_pooled(1, slots[0][2])
+    if chunks > 1:
+        send_pooled(1, slots[0][2], made[-1][1])
     weights = after(weights, made[0][1])
     weights = lax.all_gather(weights, "fsdp", axis=0, tiled=False)
     for j in range(chunks):
-        order = segs
+        waits = att[-1:]
         if j == 1:
             x_cols = after(x_wide, att[0]).reshape(seqs * wide, width).T
             cot = after(cotangent, att[0]).transpose(1, 0, 2)
-        if j:
-            order = segs[:2] + (after(segs[2], att[-1], x_cols, cot),)
+            waits += [x_cols, cot]
+        order = segs[:2] + (after(segs[2], *waits) if waits else segs[2],)
         att.append(attend_forward(made[j][0], slots[j], order))
         if j + 2 < chunks:
             send_pooled(j + 2, att[j], slots[j + 1][2])

time: 382 us -> 383 us (level)
  waiting for transfers between devices: 64 us -> 70 us
  starting transfers between devices: 55.1 us -> 50.9 us
    ppermute x41, waiting for transfers between devices: 61.2 us -> 67.3 us  [swap(): return lax.ppermute(values, axis, [(i, i ^ mask) for i in range(count)])]
    unnamed x88 -> x92, local copies, waits for them, and re-layouts: 26.8 us -> 25.8 us
  transfers between devices with their start and end apart: 49 -> 49, of which waited for: 16 -> 17; matrix products, arithmetic and copies ran while one was open for 11% -> 11% of each run, Pallas kernels for 34% -> 33%
where the time goes in v7:
time: 383 us; the launch traced here: 377 us
  Pallas kernels  180 us (47%)
  waiting for transfers between devices  70 us (18%)
  starting transfers between devices  50.9 us (13%)
  local copies, waits for them, and re-layouts  50.3 us (13%)
  between operations  15.1 us (4%)
  other arithmetic  9.82 us (3%)
    ppermute x41, waiting for transfers between devices, swap(): return lax.ppermute(values, axis, [(i, i ^ mask) for i in range(count)])  67.3 us
    pallas_call x3, Pallas kernels, attend_backward(): pl.pallas_call(partial(attend_backward_kernel, blocks), grid=(seqs, span...  53.9 us
    pallas_call x1, Pallas kernels, dense(): pl.pallas_call(partial(dense_kernel, chunks, steps), grid=(2 * steps,), i...  53.7 us
    ppermute x41, starting transfers between devices, swap(): return lax.ppermute(values, axis, [(i, i ^ mask) for i in range(count)])  39.9 us
    pallas_call x3, Pallas kernels, attend_forward(): pl.pallas_call(partial(attend_forward_kernel, blocks), grid=(seqs, span /...  26 us
    unnamed x92, local copies, waits for them, and re-layouts  25.8 us
    pallas_call x2, Pallas kernels, gather_back(): pl.pallas_call(partial(gather_back_kernel, blocks, chunks, len(group_size...  21.1 us
    pallas_call x3, Pallas kernels, project(): pl.pallas_call(partial(project_kernel, len(pieces)), grid_spec=pltpu.Pref...  15.6 us
  transfers between devices with their start and end apart: 49, of which 17 were waited for; matrix products, arithmetic and copies ran while one was open for 11% of the time, Pallas kernels for 33%

profile of v7, /device:TPU:0, one launch (start us, length us, event | category | flops | bytes accessed | tf_op | source)
XLA Modules:
  0.0 376.6 jit_solution(3040661039044247653)
XLA Ops:
  10.0 1.1 copy.264
  12.2 5.1 %collective-permute-start = (bf16[109,768]{0,1:T(8,128)(2,1)S(1)}, bf16[109,768]{0,1:T(8,128)(2,1)S(1)}, u32[]{:S(2)}, u32[]{:S(2)}) collective-permute-start(bf16[109,768]{0,1:T(8,128)(2,1)S(1)} %pad_maximum_fusion.2), channel_id=1, source_target_pairs={{0,3},{1,2},{2,1},{3,0},{4,7},{5,6},{6,5},{7,4},{8,11},{9,10},{10,... | collective-permute-start | bytes 502280 | tf_op jit(solution)/shard_map/ppermute | solution.py:812
  18.0 1.6 copy.271
  19.6 1.1 copy-done.11
  20.7 3.3 collective-permute-start.5
  24.0 1.3 collective-permute-start.6
  31.2 3.8 %collective-permute-done.1 = bf16[109,768]{0,1:T(8,128)(2,1)S(1)} collective-permute-done((bf16[109,768]{0,1:T(8,128)(2,1)S(1)}, bf16[109,768]{0,1:T(8,128)(2,1)S(1)}, u32[]{:S(2)}, u32[]{:S(2)}) %collective-permute-start.1) | collective-permute-done | bytes 167456 | tf_op jit(solution)/shard_map/ppermute | solution.py:812
  36.2 1.6 collective-permute-start.3
  37.7 1.5 collective-permute-start.4
  40.9 1.7 maximum_bitcast_fusion.refs_10_.refs_6_
  42.6 7.1 %collective-permute-done.3.refs_1_ = bf16[96,3072]{1,0:T(8,128)(2,1)S(1)} collective-permute-done((bf16[96,3072]{1,0:T(8,128)(2,1)S(1)}, bf16[96,3072]{1,0:T(8,128)(2,1)S(1)}, u32[]{:S(2)}, u32[]{:S(2)}) %collective-permute-start.3) | collective-permute-done | bytes 589856 | tf_op jit(solution)/shard_map/ppermute | solution.py:812
  49.7 1.6 collective-permute-start.7
  54.3 3.0 collective-permute-done.7.refs_3_
  57.3 2.6 collective-permute-done.8.refs_4_
  60.1 1.8 collective-permute-done.13.refs_9_
  61.9 5.4 %shard_map.220 = (bf16[3,2,640,256]{3,2,1,0:T(8,128)(2,1)S(1)}, bf16[2,2,128,256]{3,2,1,0:T(8,128)(2,1)}, bf16[4,768,256]{2,1,0:T(8,128)(2,1)S(1)}) custom-call(s32[10]{0:T(128)S(1)} %stack.97.offs, bf16[96,3072]{1,0:T(8,128)(2,1)S(1)} %copy.283.refs_0_, bf16[96,3072]{1,0:T(8,128)(2,1)S(1)} %collective-permute-done.3.refs_1_, ...), custom_call_target="tpu_custom_call" | custom-call | flops 1 | bytes 1 | tf_op jit(solution)/shard_map/pallas_call | solution.py:100
  67.3 1.3 copy-done.1
  68.7 1.1 copy-done.4
  70.2 5.4 %shard_map.222 = (bf16[3,2,640,256]{3,2,1,0:T(8,128)(2,1)S(1)}, bf16[2,2,128,256]{3,2,1,0:T(8,128)(2,1)}, bf16[4,768,256]{2,1,0:T(8,128)(2,1)S(1)}) custom-call(s32[10]{0:T(128)S(1)} %stack.97.offs, bf16[96,3072]{1,0:T(8,128)(2,1)S(1)} %copy.283.refs_0_, bf16[96,3072]{1,0:T(8,128)(2,1)S(1)} %collective-permute-done.3.refs_1_, ...), custom_call_target="tpu_custom_call" | custom-call | flops 1 | bytes 1 | tf_op jit(solution)/shard_map/pallas_call | solution.py:100
  75.6 1.3 copy-done.2
  76.9 8.5 %collective-permute-done.14.refs_2_.refs_6_ = bf16[2,2,128,256]{3,2,1,0:T(8,128)(2,1)} collective-permute-done((bf16[2,2,128,256]{3,2,1,0:T(8,128)(2,1)}, bf16[2,2,128,256]{3,2,1,0:T(8,128)(2,1)}, u32[]{:S(2)}, u32[]{:S(2)}) %collective-permute-start.14) | collective-permute-done | bytes 262176 | tf_op jit(solution)/shard_map/ppermute | solution.py:812
  85.3 2.0 collective-permute-start.16
  88.2 4.7 %shard_map.223 = (bf16[3,2,640,256]{3,2,1,0:T(8,128)(2,1)S(1)}, bf16[2,2,128,256]{3,2,1,0:T(8,128)(2,1)S(1)}, bf16[4,768,256]{2,1,0:T(8,128)(2,1)S(1)}) custom-call(s32[10]{0:T(128)S(1)} %stack.97.offs, bf16[96,3072]{1,0:T(8,128)(2,1)S(1)} %copy.283.refs_0_, bf16[96,3072]{1,0:T(8,128)(2,1)S(1)} %collective-permute-done.3.refs_1_, ...), custom_call_target="tpu_custom_call" | custom-call | flops 1 | bytes 1 | tf_op jit(solution)/shard_map/pallas_call | solution.py:100
  92.9 1.3 copy-done
  94.2 1.1 copy-done.6
  95.4 1.7 copy.284.refs_8_
  97.1 2.9 collective-permute-done.16.refs_3_.refs_7_
  100.0 8.7 %shard_map.221.refs_0_ = bf16[2,512,256]{2,1,0:T(8,128)(2,1)} custom-call(bf16[3,2,640,256]{3,2,1,0:T(8,128)(2,1)} %copy-done.1, bf16[3,2,640,256]{3,2,1,0:T(8,128)(2,1)} %copy-done.1, bf16[3,2,640,256]{3,2,1,0:T(8,128)(2,1)} %copy-done.1, bf16[2,2,128,256]{3,2,1,0:T(8,128)(2,1)} %get-tuple-element.117.refs_0_.refs_4_, ...), custom_call_target="tpu_custom_call" | custom-call | flops 1 | bytes 1 | tf_op jit(solution)/shard_map/pallas_call | solution.py:316
  109.8 2.5 collective-permute-start.18
  112.3 10.0 %collective-permute-done.20.refs_2_.refs_6_ = bf16[2,2,128,256]{3,2,1,0:T(8,128)(2,1)S(1)} collective-permute-done((bf16[2,2,128,256]{3,2,1,0:T(8,128)(2,1)S(1)}, bf16[2,2,128,256]{3,2,1,0:T(8,128)(2,1)S(1)}, u32[]{:S(2)}, u32[]{:S(2)}) %collective-permute-start.20) | collective-permute-done | bytes 262176 | tf_op jit(solution)/shard_map/ppermute | solution.py:812
  122.3 2.0 collective-permute-start.22
  126.4 2.3 copy.297
  128.7 2.8 copy.303
  132.2 8.6 %shard_map.224.refs_1_ = bf16[2,512,256]{2,1,0:T(8,128)(2,1)} custom-call(bf16[3,2,640,256]{3,2,1,0:T(8,128)(2,1)} %copy-done.2, bf16[3,2,640,256]{3,2,1,0:T(8,128)(2,1)} %copy-done.2, bf16[3,2,640,256]{3,2,1,0:T(8,128)(2,1)} %copy-done.2, bf16[2,2,128,256]{3,2,1,0:T(8,128)(2,1)} %get-tuple-element.124.refs_0_.refs_4_, bf16[2,2,128,256]{3,2,1,0:T(8,128)(2,1)} %copy-done.16, ...), custom_call_target="tpu_custom_call" | custom-call | flops 1 | bytes 1 | tf_op jit(solution)/shard_map/pallas_call | solution.py:316
  141.6 8.7 %shard_map.225.refs_2_ = bf16[2,512,256]{2,1,0:T(8,128)(2,1)} custom-call(bf16[3,2,640,256]{3,2,1,0:T(8,128)(2,1)} %copy-done, bf16[3,2,640,256]{3,2,1,0:T(8,128)(2,1)} %copy-done, bf16[3,2,640,256]{3,2,1,0:T(8,128)(2,1)} %copy-done, bf16[2,2,128,256]{3,2,1,0:T(8,128)(2,1)} %copy-done.8, bf16[2,2,128,256]{3,2,1,0:T(8,128)(2,1)} %copy-done.14, ...), custom_call_target="tpu_custom_call" | custom-call | flops 1 | bytes 1 | tf_op jit(solution)/shard_map/pallas_call | solution.py:316
  150.3 53.7 %shard_map.226 = (bf16[2,512,768]{2,1,0:T(8,128)(2,1)}, f32[2,512,768]{2,1,0:T(8,128)}, bf16[2,512,256]{2,1,0:T(8,128)(2,1)}, bf16[2,512,256]{2,1,0:T(8,128)(2,1...) custom-call(bf16[2,512,256]{2,1,0:T(8,128)(2,1)} %shard_map.221.refs, ...), custom_call_target="tpu_custom_call" | custom-call | flops 1 | bytes 1 | tf_op jit(solution)/shard_map/pallas_call | solution.py:522
  204.1 17.9 %shard_map.227 = (bf16[2,512,256]{2,1,0:T(8,128)(2,1)}, f32[2,640,256]{2,1,0:T(8,128)}, f32[2,640,256]{2,1,0:T(8,128)}, bf16[2,2,2,128,256]{4,3,2,1,0:T(8,128)(2,1)}, bf16[2,2,2,128,256]{4,3,2,1,0:T(8,128)(2,1)}) custom-call(bf16[3,2,640,256]{3,2,1,0:T(8,128)(2,1)} %copy-done.1, bf16[3,2,640,256]{3,2,1,0:T(8,128)(2,1)} %copy-done.1, ...), custom_call_target="tpu_custom_call" | custom-call | flops 1 | bytes 1 | tf_op jit(solution)/shard_map/pallas_call | solution.py:338
  222.1 17.8 %shard_map.228 = (bf16[2,512,256]{2,1,0:T(8,128)(2,1)}, f32[2,640,256]{2,1,0:T(8,128)}, f32[2,640,256]{2,1,0:T(8,128)}, bf16[2,2,2,128,256]{4,3,2,1,0:T(8,128)(2,1)}, bf16[2,2,2,128,256]{4,3,2,1,0:T(8,128)(2,1)}) custom-call(bf16[3,2,640,256]{3,2,1,0:T(8,128)(2,1)} %copy-done.2, bf16[3,2,640,256]{3,2,1,0:T(8,128)(2,1)} %copy-done.2, ...), custom_call_target="tpu_custom_call" | custom-call | flops 1 | bytes 1 | tf_op jit(solution)/shard_map/pallas_call | solution.py:338
  241.0 1.9 collective-permute-start.24
  243.0 1.1 collective-permute-start.25
  244.0 18.1 %shard_map.229 = (bf16[2,512,256]{2,1,0:T(8,128)(2,1)}, f32[2,640,256]{2,1,0:T(8,128)}, f32[2,640,256]{2,1,0:T(8,128)}, bf16[2,2,2,128,256]{4,3,2,1,0:T(8,128)(2,1)}, bf16[2,2,2,128,256]{4,3,2,1,0:T(8,128)(2,1)}) custom-call(bf16[3,2,640,256]{3,2,1,0:T(8,128)(2,1)} %copy-done, bf16[3,2,640,256]{3,2,1,0:T(8,128)(2,1)} %copy-done, ...), custom_call_target="tpu_custom_call" | custom-call | flops 1 | bytes 1 | tf_op jit(solution)/shard_map/pallas_call | solution.py:338
  263.2 2.0 collective-permute-start.26
  265.2 15.6 %collective-permute-done.26 = bf16[2,2,2,128,256]{4,3,2,1,0:T(8,128)(2,1)S(1)} collective-permute-done((bf16[2,2,2,128,256]{4,3,2,1,0:T(8,128)(2,1)S(1)}, bf16[2,2,2,128,256]{4,3,2,1,0:T(8,128)(2,1)S(1)}, u32[]{:S(2)}, u32[]{:S(2)}) %collective-permute-start.26) | collective-permute-done | bytes 524320 | tf_op jit(solution)/shard_map/ppermute | solution.py:812
  284.4 13.0 %shard_map.230 = (bf16[4,4,112,512]{3,2,1,0:T(8,128)(2,1)}, bf16[4,4,112,512]{3,2,1,0:T(8,128)(2,1)}, bf16[2,2,640,256]{3,2,1,0:T(8,128)(2,1)}, bf16[2,2,640,256]{3,2,1,0:T(8,128)(2,1)}) custom-call(s32[8]{0:T(128)} %stack.111.offs, f32[2,640,256]{2,1,0:T(8,128)} %get-tuple-element.154.refs_0_, f32[2,640,256]{2,1,0:T(8,128)} %get-tuple-element.155.refs_1_, ...), custom_call_target="tpu_custom_call" | custom-call | flops 1 | bytes 1 | tf_op jit(solution)/shard_map/pallas_call | solution.py:672
  297.6 4.0 %collective-permute-done.29 = bf16[4,4,112,512]{3,2,1,0:T(8,128)(2,1)S(1)} collective-permute-done((bf16[4,4,112,512]{3,2,1,0:T(8,128)(2,1)}, bf16[4,4,112,512]{3,2,1,0:T(8,128)(2,1)S(1)}, u32[]{:S(2)}, u32[]{:S(2)}) %collective-permute-start.29) | collective-permute-done | bytes 1835040 | tf_op jit(solution)/shard_map/ppermute | solution.py:812
  301.6 2.1 add_convert_fusion
  303.9 1.4 collective-permute-start.30
  305.7 1.7 collective-permute-start.32
  308.6 8.1 %shard_map.231 = (bf16[4,4,112,256]{3,2,1,0:T(8,128)(2,1)}, bf16[4,4,112,256]{3,2,1,0:T(8,128)(2,1)}, bf16[2,2,640,256]{3,2,1,0:T(8,128)(2,1)}) custom-call(s32[8]{0:T(128)} %stack.111.offs, f32[2,640,256]{2,1,0:T(8,128)} %get-tuple-element.165.refs_0_, f32[2,640,256]{2,1,0:T(8,128)} %get-tuple-element.166.refs_1_, ...), custom_call_target="tpu_custom_call" | custom-call | flops 1 | bytes 1 | tf_op jit(solution)/shard_map/pallas_call | solution.py:672
  316.8 9.3 %shard_map.232 = (f32[2,512,768]{2,1,0:T(8,128)}, bf16[2,64,768]{2,1,0:T(8,128)(2,1)}, bf16[2,64,768]{2,1,0:T(8,128)(2,1)}) custom-call(bf16[2,512,256]{2,1,0:T(8,128)(2,1)} %get-tuple-element.138.refs_2_.refs_0_, bf16[2,2,640,256]{3,2,1,0:T(8,128)(2,1)} %get-tuple-element.161.refs_1_, bf16[4,768,256]{2,1,0:T(8,128)(2,1)} %copy-done.4, ...), custom_call_target="tpu_custom_call" | custom-call | flops 1 | bytes 1 | tf_op jit(solution)/shard_map/pallas_call | solution.py:739
  326.1 1.3 collective-permute-done.31
  327.4 1.3 add_convert_fusion.5
  328.7 4.8 %collective-permute-start.33 = (bf16[2,64,768]{2,1,0:T(8,128)(2,1)S(1)}, bf16[2,64,768]{2,1,0:T(8,128)(2,1)S(1)}, u32[]{:S(2)}, u32[]{:S(2)}) collective-permute-start(bf16[2,64,768]{2,1,0:T(8,128)(2,1)S(1)} %copy-done.39), channel_id=1, source_target_pairs={{0,1},{1,2},{2,3},{4,5},{5,6},{6,7},{8,9},{9,10},{10,11},{12,13},{... | collective-permute-start | bytes 589832 | tf_op jit(solution)/shard_map/ppermute | solution.py:817
  333.5 2.8 copy.294
  337.2 1.3 collective-permute-start.34
  339.7 1.5 collective-permute-start.40
  341.2 1.3 collective-permute-start.41
  342.4 2.6 collective-permute-done.34
  345.1 4.1 %copy.295 = f32[512,2,768]{2,1,0:T(2,128)} copy(f32[512,2,768]{2,0,1:T(8,128)S(1)} %fusion.3) | data formatting | bytes 6291456
  350.2 3.5 collective-permute-start.38
  354.9 1.0 bitcast_convert_fusion
  356.8 3.5 collective-permute-start.44
  360.8 2.2 collective-permute-done.37.refs_2_
  363.0 2.7 collective-permute-done.43.refs_6_
  (240 shorter events, 39.5 us)
Async XLA Ops:
  7.2 62.6 %all-gather.5.cloned.1.call-start = ((), (), s32[]{:S(2)}) async-start(), calls=%async_computation.4 | async-start | bytes 1474560 | tf_op jit(solution)/shard_map/all_gather | solution.py:993
  12.2 19.0 %collective-permute-start = (bf16[109,768]{0,1:T(8,128)(2,1)S(1)}, bf16[109,768]{0,1:T(8,128)(2,1)S(1)}, u32[]{:S(2)}, u32[]{:S(2)}) collective-permute-start(bf16[109,768]{0,1:T(8,128)(2,1)S(1)} %pad_maximum_fusion.2), channel_id=1, source_target_pairs={{0,3},{1,2},{2,1},{3,0},{4,7},{5,6},{6,5},{7,4},{8,11},{9,10},{10,... | collective-permute-start | bytes 502280 | tf_op jit(solution)/shard_map/ppermute | solution.py:812
  17.3 17.7 %collective-permute-start.1 = (bf16[109,768]{0,1:T(8,128)(2,1)S(1)}, bf16[109,768]{0,1:T(8,128)(2,1)S(1)}, u32[]{:S(2)}, u32[]{:S(2)}) collective-permute-start(bf16[109,768]{0,1:T(8,128)(2,1)S(1)} %pad_maximum_fusion.2), channel_id=1, source_target_pairs={{0,2},{1,3},{2,0},{3,1},{4,6},{5,7},{6,4},{7,5},{8,10},{9,11},{10,... | collective-permute-start | bytes 502280 | tf_op jit(solution)/shard_map/ppermute | solution.py:812
  17.3 17.7 %collective-permute-start.2 = (bf16[109,768]{0,1:T(8,128)(2,1)S(1)}, bf16[109,768]{0,1:T(8,128)(2,1)S(1)}, u32[]{:S(2)}, u32[]{:S(2)}) collective-permute-start(bf16[109,768]{0,1:T(8,128)(2,1)S(1)} %pad_maximum_fusion.2), channel_id=1, source_target_pairs={{0,1},{1,0},{2,3},{3,2},{4,5},{5,4},{6,7},{7,6},{8,9},{9,8},{10,11... | collective-permute-start | bytes 502280 | tf_op jit(solution)/shard_map/ppermute | solution.py:812
  20.7 19.7 %collective-permute-start.5 = (bf16[64,2,768]{2,0,1:T(8,128)(2,1)S(1)}, bf16[64,2,768]{2,0,1:T(8,128)(2,1)S(1)}, u32[]{:S(2)}, u32[]{:S(2)}) collective-permute-start(bf16[64,2,768]{2,0,1:T(8,128)(2,1)S(1)} %get-tuple-element.304), channel_id=1, source_target_pairs={{0,1},{1,2},{2,3},{4,5},{5,6},{6,7},{8,9},{9,10},{10,11},{12,13},{... | collective-permute-start | bytes 589832 | tf_op jit(solution)/shard_map/ppermute | solution.py:817
  24.0 16.9 %collective-permute-start.6 = (bf16[64,2,768]{2,0,1:T(8,128)(2,1)S(1)}, bf16[64,2,768]{2,0,1:T(8,128)(2,1)}, u32[]{:S(2)}, u32[]{:S(2)}) collective-permute-start(bf16[64,2,768]{2,0,1:T(8,128)(2,1)S(1)} %get-tuple-element.305), channel_id=1, source_target_pairs={{1,0},{2,1},{3,2},{5,4},{6,5},{7,6},{9,8},{10,9},{11,10},{13,12},{... | collective-permute-start | bytes 589832 | tf_op jit(solution)/shard_map/ppermute | solution.py:822
  26.1 124.1 %all-gather.7.cloned.1.call-start = ((), (), s32[]{:S(2)}) async-start(), calls=%async_computation.5 | async-start | bytes 10616832 | tf_op jit(solution)/shard_map/all_gather | solution.py:1013
  30.6 56.8 %copy-start.7 = (f32[2,128,8]{2,1,0:T(8,128)}, f32[2,128,8]{2,1,0:T(8,128)S(1)}, u32[]{:S(2)}) copy-start(f32[2,128,8]{2,1,0:T(8,128)S(1)} %convert_element_type.115.refs_13_.refs_17_.refs_9_) | copy-start | bytes 24580
  36.2 13.5 %collective-permute-start.3 = (bf16[96,3072]{1,0:T(8,128)(2,1)S(1)}, bf16[96,3072]{1,0:T(8,128)(2,1)S(1)}, u32[]{:S(2)}, u32[]{:S(2)}) collective-permute-start(bf16[96,3072]{1,0:T(8,128)(2,1)S(1)} %copy.283.refs_0_), channel_id=1, source_target_pairs={{0,8},{4,12},{8,0},{12,4},{16,24},{20,28},{24,16},{28,20},{1,9},{5... | collective-permute-start | bytes 1769480 | tf_op jit(solution)/shard_map/ppermute | solution.py:812
  37.7 14.3 %collective-permute-start.4 = (bf16[96,3072]{1,0:T(8,128)(2,1)S(1)}, bf16[96,3072]{1,0:T(8,128)(2,1)}, u32[]{:S(2)}, u32[]{:S(2)}) collective-permute-start(bf16[96,3072]{1,0:T(8,128)(2,1)S(1)} %copy.283.refs_0_), channel_id=1, source_target_pairs={{0,16},{4,20},{8,24},{12,28},{16,0},{20,4},{24,8},{28,12},{1,17},{... | collective-permute-start | bytes 1769480 | tf_op jit(solution)/shard_map/ppermute | solution.py:812
  40.1 19.9 %collective-permute-start.9 = (bf16[96,3072]{1,0:T(8,128)(2,1)S(1)}, bf16[96,3072]{1,0:T(8,128)(2,1)}, u32[]{:S(2)}, u32[]{:S(2)}) collective-permute-start(bf16[96,3072]{1,0:T(8,128)(2,1)S(1)} %copy.283.refs_0_), channel_id=1, source_target_pairs={{0,4},{4,0},{8,12},{12,8},{16,20},{20,16},{24,28},{28,24},{1,5},{5... | collective-permute-start | bytes 1769480 | tf_op jit(solution)/shard_map/ppermute | solution.py:812
  40.3 29.9 %copy-start.9 = (f32[2,8,768]{2,1,0:T(8,128)}, f32[2,8,768]{2,1,0:T(8,128)S(1)}, u32[]{:S(2)}) copy-start(f32[2,8,768]{2,1,0:T(8,128)S(1)} %pad.22.refs_12_) | copy-start | bytes 147460
  42.6 83.8 %copy-start.3 = (bf16[2,640,768]{2,1,0:T(8,128)(2,1)}, bf16[2,640,768]{2,1,0:T(8,128)(2,1)S(1)}, u32[]{:S(2)}) copy-start(bf16[2,640,768]{2,1,0:T(8,128)(2,1)S(1)} %maximum_bitcast_fusion.refs_10_.refs_6_) | copy-start | bytes 5898244
  49.7 7.6 %collective-permute-start.7 = (bf16[48,3072]{1,0:T(8,128)(2,1)S(1)}, bf16[48,3072]{1,0:T(8,128)(2,1)}, u32[]{:S(2)}, u32[]{:S(2)}) collective-permute-start(bf16[48,3072]{1,0:T(8,128)(2,1)S(1)} %slice.248), channel_id=1, source_target_pairs={{0,16},{4,20},{8,24},{12,28},{16,0},{20,4},{24,8},{28,12},{1,17},{... | collective-permute-start | bytes 884744 | tf_op jit(solution)/shard_map/ppermute | solution.py:812
  53.1 6.9 %collective-permute-start.8 = (bf16[48,3072]{1,0:T(8,128)(2,1)S(1)}, bf16[48,3072]{1,0:T(8,128)(2,1)}, u32[]{:S(2)}, u32[]{:S(2)}) collective-permute-start(bf16[48,3072]{1,0:T(8,128)(2,1)S(1)} %slice.256), channel_id=1, source_target_pairs={{0,8},{4,12},{8,0},{12,4},{16,24},{20,28},{24,16},{28,20},{1,9},{5... | collective-permute-start | bytes 884744 | tf_op jit(solution)/shard_map/ppermute | solution.py:812
  53.8 8.0 %collective-permute-start.10 = (bf16[96,3072]{1,0:T(8,128)(2,1)S(1)}, bf16[96,3072]{1,0:T(8,128)(2,1)}, u32[]{:S(2)}, u32[]{:S(2)}) collective-permute-start(bf16[96,3072]{1,0:T(8,128)(2,1)S(1)} %collective-permute-done.3.refs_1_), channel_id=1, source_target_pairs={{0,4},{4,0},{8,12},{12,8},{16,20},{20,16},{24,28},{28,24},{1,5},{5... | collective-permute-start | bytes 1769480 | tf_op jit(solution)/shard_map/ppermute | solution.py:812
  53.8 8.0 %collective-permute-start.11 = (bf16[96,3072]{1,0:T(8,128)(2,1)}, bf16[96,3072]{1,0:T(8,128)(2,1)}, u32[]{:S(2)}, u32[]{:S(2)}) collective-permute-start(bf16[96,3072]{1,0:T(8,128)(2,1)} %collective-permute-done.4.refs_2_), channel_id=1, source_target_pairs={{0,4},{4,0},{8,12},{12,8},{16,20},{20,16},{24,28},{28,24},{1,5},{5... | collective-permute-start | bytes 1769480 | tf_op jit(solution)/shard_map/ppermute | solution.py:812
  57.3 2.7 collective-permute-start.12
  59.9 1.9 collective-permute-start.13
  69.8 233.9 %reduce-scatter.3.cloned.1.call-start = ((), (), s32[]{:S(2)}) async-start(), calls=%async_computation.2 | async-start | bytes 12386304 | tf_op jit(solution)/shard_map/reduce_scatter | solution.py:1034
  70.1 15.2 %collective-permute-start.14 = (bf16[2,2,128,256]{3,2,1,0:T(8,128)(2,1)}, bf16[2,2,128,256]{3,2,1,0:T(8,128)(2,1)}, u32[]{:S(2)}, u32[]{:S(2)}) collective-permute-start(bf16[2,2,128,256]{3,2,1,0:T(8,128)(2,1)} %get-tuple-element.117.refs_0_.refs_4_), channel_id=1, source_target_pairs={{0,2},{1,3},{2,0},{3,1},{4,6},{5,7},{6,4},{7,5},{8,10},{9,11},{10,... | collective-permute-start | bytes 786440 | tf_op jit(solution)/shard_map/ppermute | solution.py:812
  76.9 16.0 %copy-start.5 = (bf16[4,768,256]{2,1,0:T(8,128)(2,1)}, bf16[4,768,256]{2,1,0:T(8,128)(2,1)S(1)}, u32[]{:S(2)}) copy-start(bf16[4,768,256]{2,1,0:T(8,128)(2,1)S(1)} %get-tuple-element.133.refs_4_.refs_5_) | copy-start | bytes 4718596
  85.3 11.8 %collective-permute-start.15 = (bf16[2,2,128,256]{3,2,1,0:T(8,128)(2,1)}, bf16[2,2,128,256]{3,2,1,0:T(8,128)(2,1)}, u32[]{:S(2)}, u32[]{:S(2)}) collective-permute-start(bf16[2,2,128,256]{3,2,1,0:T(8,128)(2,1)} %get-tuple-element.117.refs_0_.refs_4_), channel_id=1, source_target_pairs={{0,1},{1,0},{2,3},{3,2},{4,5},{5,4},{6,7},{7,6},{8,9},{9,8},{10,11... | collective-permute-start | bytes 786440 | tf_op jit(solution)/shard_map/ppermute | solution.py:812
  85.3 14.7 %collective-permute-start.16 = (bf16[2,2,128,256]{3,2,1,0:T(8,128)(2,1)}, bf16[2,2,128,256]{3,2,1,0:T(8,128)(2,1)}, u32[]{:S(2)}, u32[]{:S(2)}) collective-permute-start(bf16[2,2,128,256]{3,2,1,0:T(8,128)(2,1)} %collective-permute-done.14.refs_2_.refs_6_), channel_id=1, source_target_pairs={{0,1},{1,0},{2,3},{3,2},{4,5},{5,4},{6,7},{7,6},{8,9},{9,8},{10,11... | collective-permute-start | bytes 786440 | tf_op jit(solution)/shard_map/ppermute | solution.py:812
  95.4 26.9 %copy-start.8 = (bf16[2,2,128,256]{3,2,1,0:T(8,128)(2,1)}, bf16[2,2,128,256]{3,2,1,0:T(8,128)(2,1)S(1)}, u32[]{:S(2)}) copy-start(bf16[2,2,128,256]{3,2,1,0:T(8,128)(2,1)S(1)} %get-tuple-element.130.refs_0_.refs_4_) | copy-start | bytes 786436
  95.4 14.3 %collective-permute-start.17 = (bf16[2,2,128,256]{3,2,1,0:T(8,128)(2,1)}, bf16[2,2,128,256]{3,2,1,0:T(8,128)(2,1)S(1)}, u32[]{:S(2)}, u32[]{:S(2)}) collective-permute-start(bf16[2,2,128,256]{3,2,1,0:T(8,128)(2,1)} %get-tuple-element.124.refs_0_.refs_4_), channel_id=1, source_target_pairs={{0,2},{1,3},{2,0},{3,1},{4,6},{5,7},{6,4},{7,5},{8,10},{9,11},{10,... | collective-permute-start | bytes 786440 | tf_op jit(solution)/shard_map/ppermute | solution.py:812
  100.0 24.3 %copy-start.33 = (f32[2,768]{1,0:T(2,128)S(1)}, f32[2,768]{1,0:T(2,128)}, u32[]{:S(2)}) copy-start(f32[2,768]{1,0:T(2,128)} %param.28) | copy-start | bytes 18436
  100.0 24.3 %copy-start.34 = (f32[2,768]{1,0:T(2,128)S(1)}, f32[2,768]{1,0:T(2,128)}, u32[]{:S(2)}) copy-start(f32[2,768]{1,0:T(2,128)} %param.27) | copy-start | bytes 18436
  100.0 24.3 %copy-start.35 = (f32[2,768]{1,0:T(2,128)S(1)}, f32[2,768]{1,0:T(2,128)}, u32[]{:S(2)}) copy-start(f32[2,768]{1,0:T(2,128)} %param.23) | copy-start | bytes 18436
  109.7 19.0 %copy-start.13 = (bf16[2,2,128,256]{3,2,1,0:T(8,128)(2,1)}, bf16[2,2,128,256]{3,2,1,0:T(8,128)(2,1)S(1)}, u32[]{:S(2)}) copy-start(bf16[2,2,128,256]{3,2,1,0:T(8,128)(2,1)S(1)} %collective-permute-done.17.refs_2_.refs_6_) | copy-start | bytes 786436
  109.7 12.6 %collective-permute-start.20 = (bf16[2,2,128,256]{3,2,1,0:T(8,128)(2,1)S(1)}, bf16[2,2,128,256]{3,2,1,0:T(8,128)(2,1)S(1)}, u32[]{:S(2)}, u32[]{:S(2)}) collective-permute-start(bf16[2,2,128,256]{3,2,1,0:T(8,128)(2,1)S(1)} %get-tuple-element.130.refs_0_.refs_4_), channel_id=1, source_target_pairs={{0,2},{1,3},{2,0},{3,1},{4,6},{5,7},{6,4},{7,5},{8,10},{9,11},{10,... | collective-permute-start | bytes 786440 | tf_op jit(solution)/shard_map/ppermute | solution.py:812
  109.8 21.7 %collective-permute-start.18 = (bf16[2,2,128,256]{3,2,1,0:T(8,128)(2,1)}, bf16[2,2,128,256]{3,2,1,0:T(8,128)(2,1)S(1)}, u32[]{:S(2)}, u32[]{:S(2)}) collective-permute-start(bf16[2,2,128,256]{3,2,1,0:T(8,128)(2,1)} %get-tuple-element.124.refs_0_.refs_4_), channel_id=1, source_target_pairs={{0,1},{1,0},{2,3},{3,2},{4,5},{5,4},{6,7},{7,6},{8,9},{9,8},{10,11... | collective-permute-start | bytes 786440 | tf_op jit(solution)/shard_map/ppermute | solution.py:812
  112.2 19.2 %collective-permute-start.19 = (bf16[2,2,128,256]{3,2,1,0:T(8,128)(2,1)S(1)}, bf16[2,2,128,256]{3,2,1,0:T(8,128)(2,1)}, u32[]{:S(2)}, u32[]{:S(2)}) collective-permute-start(bf16[2,2,128,256]{3,2,1,0:T(8,128)(2,1)S(1)} %collective-permute-done.17.refs_2_.refs_6_), channel_id=1, source_target_pairs={{0,1},{1,0},{2,3},{3,2},{4,5},{5,4},{6,7},{7,6},{8,9},{9,8},{10,11... | collective-permute-start | bytes 786440 | tf_op jit(solution)/shard_map/ppermute | solution.py:812
  122.3 18.5 %collective-permute-start.21 = (bf16[2,2,128,256]{3,2,1,0:T(8,128)(2,1)S(1)}, bf16[2,2,128,256]{3,2,1,0:T(8,128)(2,1)S(1)}, u32[]{:S(2)}, u32[]{:S(2)}) collective-permute-start(bf16[2,2,128,256]{3,2,1,0:T(8,128)(2,1)S(1)} %get-tuple-element.130.refs_0_.refs_4_), channel_id=1, source_target_pairs={{0,1},{1,0},{2,3},{3,2},{4,5},{5,4},{6,7},{7,6},{8,9},{9,8},{10,11... | collective-permute-start | bytes 786440 | tf_op jit(solution)/shard_map/ppermute | solution.py:812
  122.3 18.5 %collective-permute-start.22 = (bf16[2,2,128,256]{3,2,1,0:T(8,128)(2,1)S(1)}, bf16[2,2,128,256]{3,2,1,0:T(8,128)(2,1)S(1)}, u32[]{:S(2)}, u32[]{:S(2)}) collective-permute-start(bf16[2,2,128,256]{3,2,1,0:T(8,128)(2,1)S(1)} %collective-permute-done.20.refs_2_.refs_6_), channel_id=1, source_target_pairs={{0,1},{1,0},{2,3},{3,2},{4,5},{5,4},{6,7},{7,6},{8,9},{9,8},{10,11... | collective-permute-start | bytes 786440 | tf_op jit(solution)/shard_map/ppermute | solution.py:812
  204.0 150.9 %reduce-scatter.5.cloned.1.call-start = ((), (), s32[]{:S(2)}) async-start(), calls=%async_computation.3 | async-start | bytes 1720320 | tf_op jit(solution)/shard_map/reduce_scatter | solution.py:1035
  222.0 18.0 %collective-permute-start.23 = (bf16[2,2,2,128,256]{4,3,2,1,0:T(8,128)(2,1)}, bf16[2,2,2,128,256]{4,3,2,1,0:T(8,128)(2,1)S(1)}, u32[]{:S(2)}, u32[]{:S(2)}) collective-permute-start(bf16[2,2,2,128,256]{4,3,2,1,0:T(8,128)(2,1)} %get-tuple-element.143), channel_id=1, source_target_pairs={{0,1},{1,0},{2,3},{3,2},{4,5},{5,4},{6,7},{7,6},{8,9},{9,8},{10,11... | collective-permute-start | bytes 1572872 | tf_op jit(solution)/shard_map/ppermute | solution.py:812
  222.1 17.9 %copy-start.24 = (bf16[2,2,2,128,256]{4,3,2,1,0:T(8,128)(2,1)S(1)}, bf16[2,2,2,128,256]{4,3,2,1,0:T(8,128)(2,1)}, u32[]{:S(2)}) copy-start(bf16[2,2,2,128,256]{4,3,2,1,0:T(8,128)(2,1)} %get-tuple-element.142) | copy-start | bytes 1572868
  241.0 21.2 %collective-permute-start.24 = (bf16[2,2,2,128,256]{4,3,2,1,0:T(8,128)(2,1)S(1)}, bf16[2,2,2,128,256]{4,3,2,1,0:T(8,128)(2,1)S(1)}, u32[]{:S(2)}, u32[]{:S(2)}) collective-permute-start(bf16[2,2,2,128,256]{4,3,2,1,0:T(8,128)(2,1)S(1)} %copy-done.36), channel_id=1, source_target_pairs={{0,1},{1,0},{2,3},{3,2},{4,5},{5,4},{6,7},{7,6},{8,9},{9,8},{10,11... | collective-permute-start | bytes 1572872 | tf_op jit(solution)/shard_map/ppermute | solution.py:812
  243.0 20.1 %collective-permute-start.25 = (bf16[2,2,128,256]{3,2,1,0:T(8,128)(2,1)S(1)}, bf16[2,2,128,256]{3,2,1,0:T(8,128)(2,1)S(1)}, u32[]{:S(2)}, u32[]{:S(2)}) collective-permute-start(bf16[2,2,128,256]{3,2,1,0:T(8,128)(2,1)S(1)} %get-tuple-element.319), channel_id=1, source_target_pairs={{0,2},{1,3},{2,0},{3,1},{4,6},{5,7},{6,4},{7,5},{8,10},{9,11},{10,... | collective-permute-start | bytes 786440 | tf_op jit(solution)/shard_map/ppermute | solution.py:812
  244.0 18.2 %copy-start.22 = (bf16[2,2,2,128,256]{4,3,2,1,0:T(8,128)(2,1)S(1)}, bf16[2,2,2,128,256]{4,3,2,1,0:T(8,128)(2,1)}, u32[]{:S(2)}) copy-start(bf16[2,2,2,128,256]{4,3,2,1,0:T(8,128)(2,1)} %get-tuple-element.149) | copy-start | bytes 1572868
  262.2 18.7 %copy-start.23 = (bf16[2,2,2,128,256]{4,3,2,1,0:T(8,128)(2,1)S(1)}, bf16[2,2,2,128,256]{4,3,2,1,0:T(8,128)(2,1)}, u32[]{:S(2)}) copy-start(bf16[2,2,2,128,256]{4,3,2,1,0:T(8,128)(2,1)} %get-tuple-element.147) | copy-start | bytes 1572868
  262.3 20.1 %copy-start.21 = (f32[2,5,768]{2,1,0:T(8,128)S(1)}, f32[2,5,768]{2,1,0:T(8,128)}, u32[]{:S(2)}) copy-start(f32[2,5,768]{2,1,0:T(8,128)} %copy-done.20) | copy-start | bytes 92164
  262.3 20.7 %copy-start.32 = (f32[8,768]{1,0:T(8,128)S(1)}, f32[8,768]{1,0:T(8,128)}, u32[]{:S(2)}) copy-start(f32[8,768]{1,0:T(8,128)} %get-tuple-element.160) | copy-start | bytes 73732
  263.1 20.6 %copy-start.25 = (bf16[2,2,128,256]{3,2,1,0:T(8,128)(2,1)}, bf16[2,2,128,256]{3,2,1,0:T(8,128)(2,1)S(1)}, u32[]{:S(2)}) copy-start(bf16[2,2,128,256]{3,2,1,0:T(8,128)(2,1)S(1)} %collective-permute-done.25.refs_4_) | copy-start | bytes 786436
  263.2 17.7 %collective-permute-start.26 = (bf16[2,2,2,128,256]{4,3,2,1,0:T(8,128)(2,1)S(1)}, bf16[2,2,2,128,256]{4,3,2,1,0:T(8,128)(2,1)S(1)}, u32[]{:S(2)}, u32[]{:S(2)}) collective-permute-start(bf16[2,2,2,128,256]{4,3,2,1,0:T(8,128)(2,1)S(1)} %copy-done.37), channel_id=1, source_target_pairs={{0,1},{1,0},{2,3},{3,2},{4,5},{5,4},{6,7},{7,6},{8,9},{9,8},{10,11... | collective-permute-start | bytes 1572872 | tf_op jit(solution)/shard_map/ppermute | solution.py:812
  265.2 18.5 %collective-permute-start.27 = (bf16[2,2,128,256]{3,2,1,0:T(8,128)(2,1)S(1)}, bf16[2,2,128,256]{3,2,1,0:T(8,128)(2,1)S(1)}, u32[]{:S(2)}, u32[]{:S(2)}) collective-permute-start(bf16[2,2,128,256]{3,2,1,0:T(8,128)(2,1)S(1)} %get-tuple-element.317), channel_id=1, source_target_pairs={{0,2},{1,3},{2,0},{3,1},{4,6},{5,7},{6,4},{7,5},{8,10},{9,11},{10,... | collective-permute-start | bytes 786440 | tf_op jit(solution)/shard_map/ppermute | solution.py:812
  281.8 15.7 %collective-permute-start.28 = (bf16[2,2,128,256]{3,2,1,0:T(8,128)(2,1)S(1)}, bf16[2,2,128,256]{3,2,1,0:T(8,128)(2,1)S(1)}, u32[]{:S(2)}, u32[]{:S(2)}) collective-permute-start(bf16[2,2,128,256]{3,2,1,0:T(8,128)(2,1)S(1)} %get-tuple-element.315), channel_id=1, source_target_pairs={{0,2},{1,3},{2,0},{3,1},{4,6},{5,7},{6,4},{7,5},{8,10},{9,11},{10,... | collective-permute-start | bytes 786440 | tf_op jit(solution)/shard_map/ppermute | solution.py:812
  297.5 4.1 %collective-permute-start.29 = (bf16[4,4,112,512]{3,2,1,0:T(8,128)(2,1)}, bf16[4,4,112,512]{3,2,1,0:T(8,128)(2,1)S(1)}, u32[]{:S(2)}, u32[]{:S(2)}) collective-permute-start(bf16[4,4,112,512]{3,2,1,0:T(8,128)(2,1)} %get-tuple-element.175), channel_id=1, source_target_pairs={{0,4},{4,0},{8,12},{12,8},{16,20},{20,16},{24,28},{28,24},{1,5},{5... | collective-permute-start | bytes 5505032 | tf_op jit(solution)/shard_map/ppermute | solution.py:812
  303.9 22.2 %collective-permute-start.30 = (bf16[4,112,512]{2,1,0:T(8,128)(2,1)S(1)}, bf16[4,112,512]{2,1,0:T(8,128)(2,1)S(1)}, u32[]{:S(2)}, u32[]{:S(2)}) collective-permute-start(bf16[4,112,512]{2,1,0:T(8,128)(2,1)S(1)} %get-tuple-element.303), channel_id=1, source_target_pairs={{0,8},{4,12},{8,0},{12,4},{16,24},{20,28},{24,16},{28,20},{1,9},{5... | collective-permute-start | bytes 1376264 | tf_op jit(solution)/shard_map/ppermute | solution.py:812
  305.3 22.1 %collective-permute-start.31 = (bf16[4,112,512]{2,1,0:T(8,128)(2,1)S(1)}, bf16[4,112,512]{2,1,0:T(8,128)(2,1)S(1)}, u32[]{:S(2)}, u32[]{:S(2)}) collective-permute-start(bf16[4,112,512]{2,1,0:T(8,128)(2,1)S(1)} %get-tuple-element.302), channel_id=1, source_target_pairs={{0,16},{4,20},{8,24},{12,28},{16,0},{20,4},{24,8},{28,12},{1,17},{... | collective-permute-start | bytes 1376264 | tf_op jit(solution)/shard_map/ppermute | solution.py:812
  305.7 21.7 %collective-permute-start.32 = (bf16[4,112,512]{2,1,0:T(8,128)(2,1)S(1)}, bf16[4,112,512]{2,1,0:T(8,128)(2,1)}, u32[]{:S(2)}, u32[]{:S(2)}) collective-permute-start(bf16[4,112,512]{2,1,0:T(8,128)(2,1)S(1)} %get-tuple-element.301), channel_id=1, source_target_pairs={{0,24},{4,28},{8,16},{12,20},{16,8},{20,12},{24,0},{28,4},{1,25},{... | collective-permute-start | bytes 1376264 | tf_op jit(solution)/shard_map/ppermute | solution.py:812
  316.7 21.9 %collective-permute-start.35 = (bf16[4,4,112,256]{3,2,1,0:T(8,128)(2,1)}, bf16[4,4,112,256]{3,2,1,0:T(8,128)(2,1)S(1)}, u32[]{:S(2)}, u32[]{:S(2)}) collective-permute-start(bf16[4,4,112,256]{3,2,1,0:T(8,128)(2,1)} %get-tuple-element.183), channel_id=1, source_target_pairs={{0,4},{4,0},{8,12},{12,8},{16,20},{20,16},{24,28},{28,24},{1,5},{5... | collective-permute-start | bytes 2752520 | tf_op jit(solution)/shard_map/ppermute | solution.py:812
  328.7 9.8 %collective-permute-start.33 = (bf16[2,64,768]{2,1,0:T(8,128)(2,1)S(1)}, bf16[2,64,768]{2,1,0:T(8,128)(2,1)S(1)}, u32[]{:S(2)}, u32[]{:S(2)}) collective-permute-start(bf16[2,64,768]{2,1,0:T(8,128)(2,1)S(1)} %copy-done.39), channel_id=1, source_target_pairs={{0,1},{1,2},{2,3},{4,5},{5,6},{6,7},{8,9},{9,10},{10,11},{12,13},{... | collective-permute-start | bytes 589832 | tf_op jit(solution)/shard_map/ppermute | solution.py:817
  337.2 7.8 %collective-permute-start.34 = (bf16[2,64,768]{2,1,0:T(8,128)(2,1)S(1)}, bf16[2,64,768]{2,1,0:T(8,128)(2,1)S(1)}, u32[]{:S(2)}, u32[]{:S(2)}) collective-permute-start(bf16[2,64,768]{2,1,0:T(8,128)(2,1)S(1)} %copy-done.38), channel_id=1, source_target_pairs={{1,0},{2,1},{3,2},{5,4},{6,5},{7,6},{9,8},{10,9},{11,10},{13,12},{... | collective-permute-start | bytes 589832 | tf_op jit(solution)/shard_map/ppermute | solution.py:822
  338.9 11.4 %collective-permute-start.39 = (bf16[4,112,256]{2,1,0:T(8,128)(2,1)S(1)}, bf16[4,112,256]{2,1,0:T(8,128)(2,1)S(1)}, u32[]{:S(2)}, u32[]{:S(2)}) collective-permute-start(bf16[4,112,256]{2,1,0:T(8,128)(2,1)S(1)} %get-tuple-element.306), channel_id=1, source_target_pairs={{0,8},{4,12},{8,0},{12,4},{16,24},{20,28},{24,16},{28,20},{1,9},{5... | collective-permute-start | bytes 688136 | tf_op jit(solution)/shard_map/ppermute | solution.py:812
  339.7 14.0 %collective-permute-start.40 = (bf16[4,112,256]{2,1,0:T(8,128)(2,1)S(1)}, bf16[4,112,256]{2,1,0:T(8,128)(2,1)S(1)}, u32[]{:S(2)}, u32[]{:S(2)}) collective-permute-start(bf16[4,112,256]{2,1,0:T(8,128)(2,1)S(1)} %get-tuple-element.308), channel_id=1, source_target_pairs={{0,16},{4,20},{8,24},{12,28},{16,0},{20,4},{24,8},{28,12},{1,17},{... | collective-permute-start | bytes 688136 | tf_op jit(solution)/shard_map/ppermute | solution.py:812
  341.2 12.6 %collective-permute-start.41 = (bf16[4,112,256]{2,1,0:T(8,128)(2,1)S(1)}, bf16[4,112,256]{2,1,0:T(8,128)(2,1)S(1)}, u32[]{:S(2)}, u32[]{:S(2)}) collective-permute-start(bf16[4,112,256]{2,1,0:T(8,128)(2,1)S(1)} %get-tuple-element.307), channel_id=1, source_target_pairs={{0,24},{4,28},{8,16},{12,20},{16,8},{20,12},{24,0},{28,4},{1,25},{... | collective-permute-start | bytes 688136 | tf_op jit(solution)/shard_map/ppermute | solution.py:812
  349.3 7.5 %collective-permute-start.36 = (bf16[112,512]{1,0:T(8,128)(2,1)S(1)}, bf16[112,512]{1,0:T(8,128)(2,1)S(1)}, u32[]{:S(2)}, u32[]{:S(2)}) collective-permute-start(bf16[112,512]{1,0:T(8,128)(2,1)S(1)} %get-tuple-element.323), channel_id=1, source_target_pairs={{0,1},{1,0},{2,3},{3,2},{4,5},{5,4},{6,7},{7,6},{8,9},{9,8},{10,11... | collective-permute-start | bytes 344072 | tf_op jit(solution)/shard_map/ppermute | solution.py:812
  350.2 12.8 %collective-permute-start.37 = (bf16[112,512]{1,0:T(8,128)(2,1)S(1)}, bf16[112,512]{1,0:T(8,128)(2,1)S(1)}, u32[]{:S(2)}, u32[]{:S(2)}) collective-permute-start(bf16[112,512]{1,0:T(8,128)(2,1)S(1)} %get-tuple-element.322), channel_id=1, source_target_pairs={{0,2},{1,3},{2,0},{3,1},{4,6},{5,7},{6,4},{7,5},{8,10},{9,11},{10,... | collective-permute-start | bytes 344072 | tf_op jit(solution)/shard_map/ppermute | solution.py:812
  350.2 12.8 %collective-permute-start.38 = (bf16[112,512]{1,0:T(8,128)(2,1)S(1)}, bf16[112,512]{1,0:T(8,128)(2,1)S(1)}, u32[]{:S(2)}, u32[]{:S(2)}) collective-permute-start(bf16[112,512]{1,0:T(8,128)(2,1)S(1)} %get-tuple-element.321), channel_id=1, source_target_pairs={{0,3},{1,2},{2,1},{3,0},{4,7},{5,6},{6,5},{7,4},{8,11},{9,10},{10,... | collective-permute-start | bytes 344072 | tf_op jit(solution)/shard_map/ppermute | solution.py:812
  353.9 9.1 %collective-permute-start.42 = (bf16[112,256]{1,0:T(8,128)(2,1)S(1)}, bf16[112,256]{1,0:T(8,128)(2,1)S(1)}, u32[]{:S(2)}, u32[]{:S(2)}) collective-permute-start(bf16[112,256]{1,0:T(8,128)(2,1)S(1)} %get-tuple-element.327), channel_id=1, source_target_pairs={{0,1},{1,0},{2,3},{3,2},{4,5},{5,4},{6,7},{7,6},{8,9},{9,8},{10,11... | collective-permute-start | bytes 172040 | tf_op jit(solution)/shard_map/ppermute | solution.py:812
  354.0 11.7 %collective-permute-start.43 = (bf16[112,256]{1,0:T(8,128)(2,1)S(1)}, bf16[112,256]{1,0:T(8,128)(2,1)S(1)}, u32[]{:S(2)}, u32[]{:S(2)}) collective-permute-start(bf16[112,256]{1,0:T(8,128)(2,1)S(1)} %get-tuple-element.326), channel_id=1, source_target_pairs={{0,2},{1,3},{2,0},{3,1},{4,6},{5,7},{6,4},{7,5},{8,10},{9,11},{10,... | collective-permute-start | bytes 172040 | tf_op jit(solution)/shard_map/ppermute | solution.py:812
  356.8 8.9 %collective-permute-start.44 = (bf16[112,256]{1,0:T(8,128)(2,1)S(1)}, bf16[112,256]{1,0:T(8,128)(2,1)S(1)}, u32[]{:S(2)}, u32[]{:S(2)}) collective-permute-start(bf16[112,256]{1,0:T(8,128)(2,1)S(1)} %get-tuple-element.325), channel_id=1, source_target_pairs={{0,3},{1,2},{2,1},{3,0},{4,7},{5,6},{6,5},{7,4},{8,11},{9,10},{10,... | collective-permute-start | bytes 172040 | tf_op jit(solution)/shard_map/ppermute | solution.py:812
  (25 other events, 88.3 us)
Sparse Core Ops, SparseCore 0:
  26.2 33.7 all-gather.4
  70.0 58.1 all-gather.6
  204.1 83.1 reduce-scatter.2
  303.8 31.6 reduce-scatter.4
